TPU v7x, 32 devices: a whole 2x2x4 slice. The times are simulated.
32 devices in a mesh: frames: 8 (over y, x, core), book: 4 (over z).
Axes of the slice: x: 2, y: 2, z: 4, core: 2. Of those that a mesh axis runs over, the one named last changes fastest.
Arguments:
- gate_pre: bfloat16 [2048, 6144], P('frames', 'book'), may hold values from -6 to 6
- up_pre: bfloat16 [2048, 6144], P('frames', 'book'), may hold values from -6 to 6
- down_weight: bfloat16 [6144, 4096], P('book'), may hold values from -0.109375 to 0.109375
- residual: bfloat16 [2048, 4096], P('frames', 'book'), may hold values from -6 to 6
- out_gain: bfloat16 [4096], replicated, may hold values from 0.25 to 1.75
- in_proj: bfloat16 [4, 4096, 1024], P('book', 'frames'), may hold values from -0.09375 to 0.09375
- embedding: bfloat16 [4, 1024, 1024], P('book', 'frames'), may hold values from -6 to 6
- token_ids: int32 [2048, 4], P('frames', 'book'), may hold values from 0 to 1023
- depth_gain: bfloat16 [4, 1024], P('book'), may hold values from 0.25 to 1.75
- qkv_weight: bfloat16 [4, 1024, 1536], P('book', 'frames'), may hold values from -2 to 2
Outputs:
- context: bfloat16 [2048, 4, 512], P(('frames', 'book'))
All inputs are finite; a program needn't handle non-finite values.
Results may differ from a plain program's by a relative error of at most 0.019.
Values may be sent and summed in bfloat16 or wider, within the bound.
No kernel may reach another device: no remote copies, remote signals or barrier semaphores. Data moves between devices by JAX's collectives and lax.ppermute only.
A program may use at most 64 MiB of HBM per device.

v0:
```python
import jax
import jax.numpy as jnp
from jax import lax
from jax.sharding import PartitionSpec as P

H = 8
HD = 64


def rms_scale(values, gain):
    moment = jnp.mean(values * values, axis=-1, keepdims=True)
    return values * lax.rsqrt(moment + 1e-05) * gain


def attend_block(grouped):
    inner = grouped[0]
    frames_here = inner.shape[0]
    books = inner.shape[1]
    width = H * HD
    queries = inner[:, :, :width].reshape(frames_here, books, H, HD)
    keys_all = inner[:, :, width : 2 * width].reshape(frames_here, books, H, HD)
    values_all = inner[:, :, 2 * width :].reshape(frames_here, books, H, HD)
    scores = jnp.einsum(
        "nkhd,njhd->nhkj", queries, keys_all, preferred_element_type=jnp.float32
    ) * HD ** (-0.5)
    causal = lax.broadcasted_iota(jnp.int32, (books, books), 0) >= lax.broadcasted_iota(
        jnp.int32, (books, books), 1
    )
    scores = jnp.where(causal, scores, -1e30)
    peak = jnp.max(scores, axis=-1, keepdims=True)
    expo = jnp.exp(scores - peak)
    probability = (expo / jnp.sum(expo, axis=-1, keepdims=True)).astype(jnp.bfloat16)
    context = jnp.einsum(
        "nhkj,njhd->nkhd", probability, values_all, preferred_element_type=jnp.float32
    )
    return context.reshape(1, frames_here, books, width).astype(jnp.bfloat16)


def gather_embedding(embedding, token_column):
    table_piece = lax.all_gather(embedding, "frames", axis=1, tiled=True)
    columns = lax.broadcasted_iota(jnp.int32, (1, table_piece.shape[1]), 1)
    matches = (token_column[:, None] == columns).astype(jnp.bfloat16)
    return jnp.dot(matches, table_piece[0], preferred_element_type=jnp.float32)


def per_device(
    gate_pre,
    up_pre,
    down_weight,
    residual,
    out_gain,
    in_proj,
    embedding,
    token_ids,
    depth_gain,
    qkv_weight,
):
    tokens_here = gate_pre.shape[0]
    book_count = lax.axis_size("book")
    token_column = token_ids[:, 0]
    hidden = (jax.nn.silu(gate_pre.astype(jnp.float32)) * up_pre.astype(jnp.float32)).astype(
        jnp.bfloat16
    )
    partial_value = jnp.dot(hidden, down_weight, preferred_element_type=jnp.float32)
    share = lax.psum_scatter(partial_value, "book", scatter_dimension=1, tiled=True)
    temporal = (share + residual.astype(jnp.float32)).astype(jnp.bfloat16)
    whole = lax.all_gather(temporal, "book", axis=1, tiled=True)
    normed = rms_scale(whole.astype(jnp.float32), out_gain.astype(jnp.float32)).astype(jnp.bfloat16)
    looked = gather_embedding(embedding, token_column)
    columns = normed
    projected = jnp.dot(
        columns,
        lax.all_gather(in_proj, "frames", axis=1, tiled=True)[0],
        preferred_element_type=jnp.float32,
    )
    depth_in = (projected + looked).astype(jnp.bfloat16)
    depth_normed = rms_scale(
        depth_in.astype(jnp.float32), depth_gain[0].astype(jnp.float32)
    ).astype(jnp.bfloat16)
    columns = depth_normed
    packed = jnp.dot(
        columns,
        lax.all_gather(qkv_weight, "frames", axis=1, tiled=True)[0],
        preferred_element_type=jnp.float32,
    ).astype(jnp.bfloat16)
    grouped = packed.reshape(book_count, tokens_here // book_count, 1, packed.shape[1])
    context = attend_block(lax.all_to_all(grouped, "book", split_axis=0, concat_axis=2, tiled=True))
    return context.reshape(context.shape[1], context.shape[2], context.shape[3])


def solution(mesh):
    in_specs = (
        P("frames", "book"),
        P("frames", "book"),
        P("book", None),
        P("frames", "book"),
        P(),
        P("book", "frames", None),
        P("book", "frames", None),
        P("frames", "book"),
        P("book", None),
        P("book", "frames", None),
    )
    out_specs = P(("frames", "book"), None, None)
    return jax.shard_map(
        per_device, mesh=mesh, in_specs=in_specs, out_specs=out_specs, check_vma=False
    )
```

profile of v0, /device:TPU:0, one launch (start us, length us, event | category | flops | bytes accessed | tf_op | source)
XLA Modules:
  0.0 305.7 jit_solution(1780264627851407803)
XLA Ops:
  6.5 10.6 %fusion.30 = f32[256,4096]{1,0:T(8,128)} fusion(bf16[1536,4096]{1,0:T(8,128)(2,1)} %param.12, bf16[256,1536]{1,0:T(8,128)(2,1)} %param.11, bf16[256,1536]{1,0:T(8,128)(2,1)} %param.10), kind=kOutput, calls=%fused_computation.32 | convolution fusion | flops 3224371200 | bytes 18350080 | tf_op jit(solution)/shard_map/dot_general | solution.py:64
  17.2 79.5 %reduce-scatter.2.cloned.1.call-done = f32[256,1024]{1,0:T(8,128)} async-done(((f32[256,4096]{1,0:T(8,128)}), f32[256,1024]{1,0:T(8,128)}) %reduce-scatter.2.cloned.1.call-update) | async-done | bytes 1048592 | tf_op jit(solution)/shard_map/reduce_scatter | solution.py:65
  96.8 2.2 add_convert_fusion
  99.0 0.7 all-gather.7.cloned.1.call-update
  99.7 0.5 all-gather.9.cloned.1.call-update
  100.3 0.5 all-gather.11.cloned.1.call-update
  100.9 44.7 %all-gather.5.cloned.1.call-done = bf16[256,4096]{1,0:T(8,128)(2,1)} async-done(((bf16[256,1024]{1,0:T(8,128)(2,1)}), bf16[256,4096]{1,0:T(8,128)(2,1)}) %all-gather.5.cloned.1.call-update) | async-done | bytes 2097168 | tf_op jit(solution)/shard_map/all_gather | solution.py:67
  145.6 2.1 fusion.2
  147.7 53.1 %all-gather.7.cloned.1.call-done = bf16[1,4096,1024]{2,1,0:T(8,128)(2,1)} async-done(((bf16[1,512,1024]{2,1,0:T(8,128)(2,1)}), bf16[1,4096,1024]{2,1,0:T(8,128)(2,1)}) %all-gather.7.cloned.1.call-update) | async-done | bytes 8388624 | tf_op jit(solution)/shard_map/all_gather | solution.py:73
  200.7 6.4 %fusion = f32[256,1024]{1,0:T(8,128)S(1)} fusion(bf16[1,4096,1024]{2,1,0:T(8,128)(2,1)} %all-gather.7.cloned.1.call-done, bf16[256,4096]{1,0:T(8,128)(2,1)} %all-gather.5.cloned.1.call-done, f32[4096]{0:T(1024)S(1)} %convert_element_type.60, f32[256]{0:T(256)S(1)} %add_rsqrt_fusion.1), kind=kOutput, calls=%fused_computation | convolution fusion | flops 2151677952 | bytes 11551744 | tf_op jit(solution)/shard_map/dot_general | solution.py:71
  207.2 23.4 %all-gather.9.cloned.1.call-done = bf16[1,1024,1024]{2,1,0:T(8,128)(2,1)} async-done(((bf16[1,128,1024]{2,1,0:T(8,128)(2,1)}), bf16[1,1024,1024]{2,1,0:T(8,128)(2,1)}) %all-gather.9.cloned.1.call-update) | async-done | bytes 2097168 | tf_op jit(solution)/shard_map/all_gather | solution.py:40
  230.6 2.5 fusion.27
  233.0 31.8 %all-gather.11.cloned.1.call-done = bf16[1,1024,1536]{2,1,0:T(8,128)(2,1)} async-done(((bf16[1,128,1536]{2,1,0:T(8,128)(2,1)}), bf16[1,1024,1536]{2,1,0:T(8,128)(2,1)}) %all-gather.11.cloned.1.call-update) | async-done | bytes 3145744 | tf_op jit(solution)/shard_map/all_gather | solution.py:83
  264.8 3.8 %fusion.7 = bf16[256,1536]{1,0:T(8,128)(2,1)} fusion(bf16[1,1024,1536]{2,1,0:T(8,128)(2,1)} %all-gather.11.cloned.1.call-done, bf16[256,1024]{1,0:T(8,128)(2,1)S(1)} %get-tuple-element.9, f32[1024]{0:T(1024)S(1)} %bitcast.40, f32[256]{0:T(256)S(1)} %add_rsqrt_fusion), kind=kOutput, calls=%fused_computation.9 | convolution fusion | flops 806748160 | bytes 4461568 | tf_op jit(solution)/shard_map/dot_general | solution.py:81
  268.7 4.6 %all-to-all-start = ((bf16[4,64,1,1536]{3,1,2,0:T(8,128)(2,1)}), bf16[4,64,1,1536]{3,1,2,0:T(8,128)(2,1)S(1)}, u32[]{:S(2)}, u32[]{:S(2)}) async-start(bf16[4,64,1,1536]{3,1,2,0:T(8,128)(2,1)} %bitcast.6), calls=%async_computation.1 | async-start | bytes 1572864 | tf_op jit(solution)/shard_map/all_to_all | solution.py:87
  273.3 20.5 %all-to-all-done = bf16[4,64,1,1536]{3,1,2,0:T(8,128)(2,1)S(1)} async-done(((bf16[4,64,1,1536]{3,1,2,0:T(8,128)(2,1)}), bf16[4,64,1,1536]{3,1,2,0:T(8,128)(2,1)S(1)}, u32[]{:S(2)}, u32[]{:S(2)}) %all-to-all-start) | async-done | bytes 786464 | tf_op jit(solution)/shard_map/all_to_all | solution.py:87
  293.9 0.3 reshape.41
  294.1 0.3 reshape.42
  294.4 0.8 fusion.35
  295.2 0.7 copy.28
  296.2 0.9 copy.30
  297.1 0.3 reshape.40
  297.4 0.7 fusion.26
  298.2 1.0 reshape.44
  (25 shorter events, 0.7 us)
Async XLA Ops:
  6.5 90.2 %reduce-scatter.2.cloned.1.call-start = ((), (), s32[]{:S(2)}) async-start(), calls=%async_computation.2 | async-start | bytes 5242880 | tf_op jit(solution)/shard_map/reduce_scatter | solution.py:65
  17.1 79.6 %copy-start = (bf16[256,1024]{1,0:T(8,128)(2,1)S(1)}, bf16[256,1024]{1,0:T(8,128)(2,1)}, u32[]{:S(2)}) copy-start(bf16[256,1024]{1,0:T(8,128)(2,1)} %param.13) | copy-start | bytes 1572868
  17.1 83.7 %copy-start.1 = (bf16[4096]{0:T(1024)(128)(2,1)S(1)}, bf16[4096]{0:T(1024)(128)(2,1)}, u32[]{:S(2)}) copy-start(bf16[4096]{0:T(1024)(128)(2,1)} %param.14) | copy-start | bytes 24580
  17.1 83.7 %copy-start.2 = (bf16[1,1024]{1,0:T(2,128)(2,1)S(1)}, bf16[1,1024]{1,0:T(2,128)(2,1)}, u32[]{:S(2)}) copy-start(bf16[1,1024]{1,0:T(2,128)(2,1)} %param.18) | copy-start | bytes 6148
  17.2 128.4 %all-gather.5.cloned.1.call-start = ((), (), s32[]{:S(2)}) async-start(), calls=%async_computation.3 | async-start | bytes 2621440 | tf_op jit(solution)/shard_map/all_gather | solution.py:67
  99.0 101.8 %all-gather.7.cloned.1.call-start = ((), (), s32[]{:S(2)}) async-start(), calls=%async_computation.4 | async-start | bytes 9437184 | tf_op jit(solution)/shard_map/all_gather | solution.py:73
  99.7 130.9 %all-gather.9.cloned.1.call-start = ((), (), s32[]{:S(2)}) async-start(), calls=%async_computation.5 | async-start | bytes 2359296 | tf_op jit(solution)/shard_map/all_gather | solution.py:40
  100.3 164.5 %all-gather.11.cloned.1.call-start = ((), (), s32[]{:S(2)}) async-start(), calls=%async_computation.6 | async-start | bytes 3538944 | tf_op jit(solution)/shard_map/all_gather | solution.py:83
  147.7 82.9 %copy-start.3 = (s32[256,1]{0,1:T(1,128)S(1)}, s32[256,1]{0,1:T(1,128)}, u32[]{:S(2)}) copy-start(s32[256,1]{0,1:T(1,128)} %param.17) | copy-start | bytes 3076
  268.7 25.1 %all-to-all-start = ((bf16[4,64,1,1536]{3,1,2,0:T(8,128)(2,1)}), bf16[4,64,1,1536]{3,1,2,0:T(8,128)(2,1)S(1)}, u32[]{:S(2)}, u32[]{:S(2)}) async-start(bf16[4,64,1,1536]{3,1,2,0:T(8,128)(2,1)} %bitcast.6), calls=%async_computation.1 | async-start | bytes 1572864 | tf_op jit(solution)/shard_map/all_to_all | solution.py:87
Sparse Core Ops, SparseCore 0:
  17.3 79.4 reduce-scatter.1
  99.1 46.4 all-gather.4
  147.6 53.0 all-gather.6
  202.6 27.8 all-gather.8
  232.5 32.3 all-gather.10
where the time goes:
time: 306 us
  waiting for transfers between devices  255 us (83%)
  matrix products  24.8 us (8%)
  between operations  13.3 us (4%)
  starting transfers between devices  4.76 us (2%)
  other arithmetic  4.57 us (1%)
  local copies, waits for them, and re-layouts  3.57 us (1%)
    reduce_scatter x1, waiting for transfers between devices, per_device(): lax.psum_scatter(partial_value, 'book', scatter_dimension=1, tiled=True)  79.5 us
    all_gather x1, waiting for transfers between devices, per_device(): lax.all_gather(in_proj, 'frames', axis=1, tiled=True)[0]  53.1 us
    all_gather x1, waiting for transfers between devices, per_device(): whole = lax.all_gather(temporal, 'book', axis=1, tiled=True)  44.7 us
    all_gather x1, waiting for transfers between devices, per_device(): lax.all_gather(qkv_weight, 'frames', axis=1, tiled=True)[0]  31.8 us
    all_gather x1, waiting for transfers between devices, gather_embedding(): table_piece = lax.all_gather(embedding, 'frames', axis=1, tiled=True)  23.4 us
    all_to_all x1, waiting for transfers between devices, per_device(): lax.all_to_all(grouped, 'book', split_axis=0, concat_axis=2, tiled=True)  20.5 us
    dot_general x1, matrix products, per_device(): jnp.dot(hidden, down_weight, preferred_element_type=jnp.float32)  10.6 us
    dot_general x1, matrix products, per_device(): jnp.dot(columns, lax.all_gather(in_proj, 'frames', axis=1, tiled=True)[0]...  6.4 us
  transfers between devices with their start and end apart: 6, of which 6 were waited for; matrix products, arithmetic and copies ran while one was open for 4% of the time, Pallas kernels for 0%

commit v1 on v0

v1 whole, which is shorter than its diff:
```python
import jax
import jax.numpy as jnp
from jax import lax
from jax.sharding import PartitionSpec as P

H = 8
HD = 64
CHUNKS = 2


def attend_block(grouped):
    inner = grouped[0]
    frames_here = inner.shape[0]
    books = inner.shape[1]
    width = H * HD
    queries = inner[:, :, :width].reshape(frames_here, books, H, HD)
    keys_all = inner[:, :, width : 2 * width].reshape(frames_here, books, H, HD)
    values_all = inner[:, :, 2 * width :].reshape(frames_here, books, H, HD)
    scores = jnp.einsum(
        "nkhd,njhd->nhkj", queries, keys_all, preferred_element_type=jnp.float32
    ) * HD ** (-0.5)
    causal = lax.broadcasted_iota(jnp.int32, (books, books), 0) >= lax.broadcasted_iota(
        jnp.int32, (books, books), 1
    )
    scores = jnp.where(causal, scores, -1e30)
    peak = jnp.max(scores, axis=-1, keepdims=True)
    expo = jnp.exp(scores - peak)
    probability = (expo / jnp.sum(expo, axis=-1, keepdims=True)).astype(jnp.bfloat16)
    context = jnp.einsum(
        "nhkj,njhd->nkhd", probability, values_all, preferred_element_type=jnp.float32
    )
    return context.reshape(1, frames_here, books, width).astype(jnp.bfloat16)


def to_right(value, first, last):
    return lax.ppermute(value, "book", [(i, i + 1) for i in range(first, last)])


def to_left(value, first, last):
    return lax.ppermute(value, "book", [(i, i - 1) for i in range(first, last)])


def per_device(
    gate_pre,
    up_pre,
    down_weight,
    residual,
    out_gain,
    in_proj,
    embedding,
    token_ids,
    depth_gain,
    qkv_weight,
):
    f32, bf16 = jnp.float32, jnp.bfloat16
    frames_here = gate_pre.shape[0]
    books = lax.axis_size("book")
    here = lax.axis_index("book")
    width = residual.shape[1]
    rows = frames_here // CHUNKS

    proj_all = lax.all_gather(in_proj[0], "frames", axis=0, tiled=True)
    table = lax.all_gather(embedding[0], "frames", axis=0, tiled=True)
    qkv_all = lax.all_gather(qkv_weight[0], "frames", axis=0, tiled=True)

    def block_of(step):
        return lax.rem(here + step, books) * width

    hidden = (jax.nn.silu(gate_pre.astype(f32)) * up_pre.astype(f32)).astype(bf16)
    sums = {}
    for far in range(1, books):
        for step in (far, books - far):
            if step not in sums:
                block = lax.dynamic_slice_in_dim(down_weight, block_of(step), width, 1)
                sums[step] = jnp.dot(hidden, block, preferred_element_type=f32)
    block = lax.dynamic_slice_in_dim(down_weight, block_of(0), width, 1)
    sums[0] = jnp.dot(hidden, block, preferred_element_type=f32)

    pieces = [slice(c * rows, (c + 1) * rows) for c in range(CHUNKS)]
    right = [None] * CHUNKS
    left = [None] * CHUNKS
    for step in range(1, books):
        for c, piece in enumerate(pieces):
            going = sums[books - step][piece]
            if step > 1:
                going = going + right[c].astype(f32)
            right[c] = to_right(going.astype(bf16), 0, step)
            going = sums[step][piece]
            if step > 1:
                going = going + left[c].astype(f32)
            left[c] = to_left(going.astype(bf16), books - step, books)

    outs = []
    for c, piece in enumerate(pieces):
        own = sums[0][piece] + residual[piece].astype(f32)
        own = (own + right[c].astype(f32) + left[c].astype(f32)).astype(bf16)
        outs.append(own)

    from_left = [[own] for own in outs]
    from_right = [[own] for own in outs]
    for step in range(1, books):
        for c in range(CHUNKS):
            from_left[c].append(to_right(from_left[c][-1], step - 1, books - 1))
            from_right[c].append(to_left(from_right[c][-1], 1, books - step + 1))

    token_column = token_ids[:, 0]
    columns = lax.broadcasted_iota(jnp.int32, (1, table.shape[0]), 1)
    matches = (token_column[:, None] == columns).astype(bf16)
    looked = jnp.dot(matches, table, preferred_element_type=f32)

    gain = out_gain.astype(f32)
    packed = []
    for c, piece in enumerate(pieces):
        square = 0.0
        projected = 0.0
        for step in range(books):
            if step == 0:
                part = outs[c]
            else:
                part = from_right[c][step] + from_left[c][books - step]
            part = part.astype(f32)
            square = square + jnp.sum(part * part, axis=-1, keepdims=True)
            scaled = (part * lax.dynamic_slice_in_dim(gain, block_of(step), width, 0)).astype(bf16)
            block = lax.dynamic_slice_in_dim(proj_all, block_of(step), width, 0)
            projected = projected + jnp.dot(scaled, block, preferred_element_type=f32)
        projected = projected * lax.rsqrt(square / (books * width) + 1e-05)
        depth_in = (projected + looked[piece]).astype(bf16).astype(f32)
        moment = jnp.mean(depth_in * depth_in, axis=-1, keepdims=True)
        depth_normed = depth_in * lax.rsqrt(moment + 1e-05) * depth_gain[0].astype(f32)
        packed.append(
            jnp.dot(depth_normed.astype(bf16), qkv_all, preferred_element_type=f32).astype(bf16)
        )
    packed = jnp.concatenate(packed, axis=0)
    grouped = packed.reshape(books, frames_here // books, 1, packed.shape[1])
    context = attend_block(lax.all_to_all(grouped, "book", split_axis=0, concat_axis=2, tiled=True))
    return context.reshape(context.shape[1], context.shape[2], context.shape[3])


def solution(mesh):
    in_specs = (
        P("frames", "book"),
        P("frames", "book"),
        P("book", None),
        P("frames", "book"),
        P(),
        P("book", "frames", None),
        P("book", "frames", None),
        P("frames", "book"),
        P("book", None),
        P("book", "frames", None),
    )
    out_specs = P(("frames", "book"), None, None)
    return jax.shard_map(
        per_device, mesh=mesh, in_specs=in_specs, out_specs=out_specs, check_vma=False
    )
```

time: 306 us -> 173 us (0.57)
  waiting for transfers between devices: 255 us -> 57.4 us
  starting transfers between devices: 4.76 us -> 58.6 us
  matrix products: 24.8 us -> 29.6 us
    all_gather x4 -> x3, waiting for transfers between devices: 153 us -> 3.45 us  [the longest x1 3.42 us: per_device(): qkv_all = lax.all_gather(qkv_weight[0], 'frames', axis=0, tiled=True)]
    reduce_scatter x1 -> x0, waiting for transfers between devices: 79.5 us -> none  [per_device(): lax.psum_scatter(partial_value, 'book', scatter_dimension=1, tiled=True)]
    ppermute x0 -> x24, starting transfers between devices: none -> 53.9 us  [the longest x12 39.2 us: to_right(): return lax.ppermute(value, 'book', [(i, i + 1) for i in range(first, last)])]
    ppermute x0 -> x24, waiting for transfers between devices: none -> 32.1 us  [the longest x12 28 us: to_left(): return lax.ppermute(value, 'book', [(i, i - 1) for i in range(first, last)])]
    dot_general x4 -> x15, matrix products: 23.3 us -> 28.1 us  [the longest x8 9.99 us: per_device(): projected = projected + jnp.dot(scaled, block, preferred_element_type=f32)]
  transfers between devices with their start and end apart: 6 -> 28, of which waited for: 6 -> 12; matrix products, arithmetic and copies ran while one was open for 4% -> 19% of each run, Pallas kernels for 0% -> 0%
where the time goes in v1:
time: 173 us; the launch traced here: 172 us
  starting transfers between devices  58.6 us (34%)
  waiting for transfers between devices  57.4 us (33%)
  matrix products  29.6 us (17%)
  between operations  13.7 us (8%)
  other arithmetic  7.08 us (4%)
  local copies, waits for them, and re-layouts  5.53 us (3%)
    ppermute x12, starting transfers between devices, to_right(): return lax.ppermute(value, 'book', [(i, i + 1) for i in range(first, last)])  39.2 us
    ppermute x12, waiting for transfers between devices, to_left(): return lax.ppermute(value, 'book', [(i, i - 1) for i in range(first, last)])  28 us
    all_to_all x1, waiting for transfers between devices, per_device(): lax.all_to_all(grouped, 'book', split_axis=0, concat_axis=2, tiled=True)  20.5 us
    ppermute x12, starting transfers between devices, to_left(): return lax.ppermute(value, 'book', [(i, i - 1) for i in range(first, last)])  14.7 us
    dot_general x8, matrix products, per_device(): projected = projected + jnp.dot(scaled, block, preferred_element_type=f32)  9.99 us
    dot_general x3, matrix products, per_device(): sums[step] = jnp.dot(hidden, block, preferred_element_type=f32)  8.61 us
    all_to_all x1, starting transfers between devices, per_device(): lax.all_to_all(grouped, 'book', split_axis=0, concat_axis=2, tiled=True)  4.59 us
    ppermute x12, waiting for transfers between devices, to_right(): return lax.ppermute(value, 'book', [(i, i + 1) for i in range(first, last)])  4.09 us
  transfers between devices with their start and end apart: 28, of which 12 were waited for; matrix products, arithmetic and copies ran while one was open for 19% of the time, Pallas kernels for 0%

profile of v1, /device:TPU:0, one launch (start us, length us, event | category | flops | bytes accessed | tf_op | source)
XLA Modules:
  0.0 171.9 jit_solution(8794942056585851690)
XLA Ops:
  9.9 2.9 %fusion.4 = f32[256,1024]{1,0:T(8,128)S(1)} fusion(bf16[256,1536]{1,0:T(8,128)(2,1)S(1)} %fusion.48, bf16[1536,4096]{1,0:T(8,128)(2,1)} %param.12, s32[]{:T(128)S(6)} %select_n.14), kind=kOutput, calls=%fused_computation.4 | convolution fusion | flops 805306368 | bytes 4980740 | tf_op jit(solution)/shard_map/dot_general | solution.py:75
  13.7 4.9 %collective-permute-start = (bf16[128,1024]{1,0:T(8,128)(2,1)}, bf16[128,1024]{1,0:T(8,128)(2,1)S(1)}, u32[]{:S(2)}, u32[]{:S(2)}) collective-permute-start(bf16[128,1024]{1,0:T(8,128)(2,1)} %get-tuple-element.17), channel_id=1, source_target_pairs={{0,1},{4,5},{8,9},{12,13},{16,17},{20,21},{24,25},{28,29}} | collective-permute-start | bytes 786440 | tf_op jit(solution)/shard_map/ppermute | solution.py:36
  19.9 2.9 %fusion.8 = f32[256,1024]{1,0:T(8,128)S(1)} fusion(bf16[256,1536]{1,0:T(8,128)(2,1)S(1)} %fusion.48, bf16[1536,4096]{1,0:T(8,128)(2,1)} %param.12, s32[]{:T(128)S(6)} %select_n.12), kind=kOutput, calls=%fused_computation.8 | convolution fusion | flops 805306368 | bytes 4980740 | tf_op jit(solution)/shard_map/dot_general | solution.py:75
  26.4 2.9 %fusion.6 = f32[256,1024]{1,0:T(8,128)S(1)} fusion(bf16[256,1536]{1,0:T(8,128)(2,1)S(1)} %fusion.48, bf16[1536,4096]{1,0:T(8,128)(2,1)} %param.12, s32[]{:T(128)S(6)} %select_n.13), kind=kOutput, calls=%fused_computation.6 | convolution fusion | flops 805306368 | bytes 4980740 | tf_op jit(solution)/shard_map/dot_general | solution.py:75
  32.3 4.2 %collective-permute-start.1 = (bf16[128,1024]{1,0:T(8,128)(2,1)}, bf16[128,1024]{1,0:T(8,128)(2,1)S(1)}, u32[]{:S(2)}, u32[]{:S(2)}) collective-permute-start(bf16[128,1024]{1,0:T(8,128)(2,1)} %get-tuple-element.13), channel_id=1, source_target_pairs={{0,1},{1,2},{4,5},{5,6},{8,9},{9,10},{12,13},{13,14},{16,17},{17,1... | collective-permute-start | bytes 786440 | tf_op jit(solution)/shard_map/ppermute | solution.py:36
  36.6 8.7 %collective-permute-start.13 = (bf16[128,1024]{1,0:T(8,128)(2,1)}, bf16[128,1024]{1,0:T(8,128)(2,1)S(1)}, u32[]{:S(2)}, u32[]{:S(2)}) collective-permute-start(bf16[128,1024]{1,0:T(8,128)(2,1)} %get-tuple-element.16), channel_id=1, source_target_pairs={{0,1},{1,2},{4,5},{5,6},{8,9},{9,10},{12,13},{13,14},{16,17},{17,1... | collective-permute-start | bytes 786440 | tf_op jit(solution)/shard_map/ppermute | solution.py:36
  46.7 3.3 %collective-permute-done.13 = bf16[128,1024]{1,0:T(8,128)(2,1)S(1)} collective-permute-done((bf16[128,1024]{1,0:T(8,128)(2,1)}, bf16[128,1024]{1,0:T(8,128)(2,1)S(1)}, u32[]{:S(2)}, u32[]{:S(2)}) %collective-permute-start.13) | collective-permute-done | bytes 262176 | tf_op jit(solution)/shard_map/ppermute | solution.py:36
  50.1 5.9 %collective-permute-start.14 = (bf16[128,1024]{1,0:T(8,128)(2,1)S(1)}, bf16[128,1024]{1,0:T(8,128)(2,1)S(1)}, u32[]{:S(2)}, u32[]{:S(2)}) collective-permute-start(bf16[128,1024]{1,0:T(8,128)(2,1)S(1)} %get-tuple-element.12), channel_id=1, source_target_pairs={{0,1},{1,2},{2,3},{4,5},{5,6},{6,7},{8,9},{9,10},{10,11},{12,13},{... | collective-permute-start | bytes 786440 | tf_op jit(solution)/shard_map/ppermute | solution.py:36
  56.1 4.3 %collective-permute-start.2 = (bf16[128,1024]{1,0:T(8,128)(2,1)S(1)}, bf16[128,1024]{1,0:T(8,128)(2,1)S(1)}, u32[]{:S(2)}, u32[]{:S(2)}) collective-permute-start(bf16[128,1024]{1,0:T(8,128)(2,1)S(1)} %get-tuple-element.11), channel_id=1, source_target_pairs={{0,1},{1,2},{2,3},{4,5},{5,6},{6,7},{8,9},{9,10},{10,11},{12,13},{... | collective-permute-start | bytes 786440 | tf_op jit(solution)/shard_map/ppermute | solution.py:36
  63.3 2.9 %fusion.10 = f32[256,1024]{1,0:T(8,128)S(1)} fusion(bf16[256,1536]{1,0:T(8,128)(2,1)S(1)} %fusion.48, bf16[1536,4096]{1,0:T(8,128)(2,1)} %param.12, s32[]{:T(128)S(6)} %select_n.11), kind=kOutput, calls=%fused_computation.10 | convolution fusion | flops 805306368 | bytes 4980740 | tf_op jit(solution)/shard_map/dot_general | solution.py:77
  66.2 4.9 %collective-permute-done.17 = bf16[128,1024]{1,0:T(8,128)(2,1)S(1)} collective-permute-done((bf16[128,1024]{1,0:T(8,128)(2,1)S(1)}, bf16[128,1024]{1,0:T(8,128)(2,1)S(1)}, u32[]{:S(2)}, u32[]{:S(2)}) %collective-permute-start.17) | collective-permute-done | bytes 262176 | tf_op jit(solution)/shard_map/ppermute | solution.py:40
  71.1 2.8 %collective-permute-done.5 = bf16[128,1024]{1,0:T(8,128)(2,1)S(1)} collective-permute-done((bf16[128,1024]{1,0:T(8,128)(2,1)S(1)}, bf16[128,1024]{1,0:T(8,128)(2,1)S(1)}, u32[]{:S(2)}, u32[]{:S(2)}) %collective-permute-start.5) | collective-permute-done | bytes 262176 | tf_op jit(solution)/shard_map/ppermute | solution.py:40
  78.2 4.6 %collective-permute-start.19 = (bf16[128,1024]{1,0:T(8,128)(2,1)S(1)}, bf16[128,1024]{1,0:T(8,128)(2,1)S(1)}, u32[]{:S(2)}, u32[]{:S(2)}) collective-permute-start(bf16[128,1024]{1,0:T(8,128)(2,1)S(1)} %get-tuple-element.10), channel_id=1, source_target_pairs={{0,1},{1,2},{2,3},{4,5},{5,6},{6,7},{8,9},{9,10},{10,11},{12,13},{... | collective-permute-start | bytes 786440 | tf_op jit(solution)/shard_map/ppermute | solution.py:36
  88.3 5.6 %collective-permute-done.18 = bf16[128,1024]{1,0:T(8,128)(2,1)S(1)} collective-permute-done((bf16[128,1024]{1,0:T(8,128)(2,1)S(1)}, bf16[128,1024]{1,0:T(8,128)(2,1)S(1)}, u32[]{:S(2)}, u32[]{:S(2)}) %collective-permute-start.18) | collective-permute-done | bytes 262176 | tf_op jit(solution)/shard_map/ppermute | solution.py:40
  95.9 3.6 %collective-permute-done.10 = bf16[128,1024]{1,0:T(8,128)(2,1)S(1)} collective-permute-done((bf16[128,1024]{1,0:T(8,128)(2,1)S(1)}, bf16[128,1024]{1,0:T(8,128)(2,1)S(1)}, u32[]{:S(2)}, u32[]{:S(2)}) %collective-permute-start.10) | collective-permute-done | bytes 262176 | tf_op jit(solution)/shard_map/ppermute | solution.py:40
  101.5 3.6 %collective-permute-done.22 = bf16[128,1024]{1,0:T(8,128)(2,1)S(1)} collective-permute-done((bf16[128,1024]{1,0:T(8,128)(2,1)S(1)}, bf16[128,1024]{1,0:T(8,128)(2,1)S(1)}, u32[]{:S(2)}, u32[]{:S(2)}) %collective-permute-start.22) | collective-permute-done | bytes 262176 | tf_op jit(solution)/shard_map/ppermute | solution.py:40
  107.1 3.3 %collective-permute-done.11 = bf16[128,1024]{1,0:T(8,128)(2,1)S(1)} collective-permute-done((bf16[128,1024]{1,0:T(8,128)(2,1)S(1)}, bf16[128,1024]{1,0:T(8,128)(2,1)S(1)}, u32[]{:S(2)}, u32[]{:S(2)}) %collective-permute-start.11) | collective-permute-done | bytes 262176 | tf_op jit(solution)/shard_map/ppermute | solution.py:40
  110.8 2.6 %collective-permute-done.23 = bf16[128,1024]{1,0:T(8,128)(2,1)S(1)} collective-permute-done((bf16[128,1024]{1,0:T(8,128)(2,1)S(1)}, bf16[128,1024]{1,0:T(8,128)(2,1)S(1)}, u32[]{:S(2)}, u32[]{:S(2)}) %collective-permute-start.23) | collective-permute-done | bytes 262176 | tf_op jit(solution)/shard_map/ppermute | solution.py:40
  113.6 3.3 %fusion.18 = f32[256,1024]{1,0:T(8,128)} fusion(bf16[1,1024,1024]{2,1,0:T(8,128)(2,1)} %all-gather.9.cloned.1.call-done, s32[256]{0:T(256)S(1)} %bitcast.92), kind=kOutput, calls=%fused_computation.14 | convolution fusion | flops 537133056 | bytes 3146752 | tf_op jit(solution)/shard_map/dot_general | solution.py:109
  119.3 2.9 %fusion.26 = f32[128,1024]{1,0:T(8,128)S(1)} fusion(bf16[1,4096,1024]{2,1,0:T(8,128)(2,1)} %all-gather.7.cloned.1.call-done, s32[]{:T(128)S(6)} %select_n.13, f32[1024]{0:T(1024)S(1)} %get-tuple-element.29, bf16[128,1024]{1,0:T(8,128)(2,1)} %copy-done.2, bf16[128,1024]{1,0:T(8,128)(2,1)S(1)} %collective-permute-done.8), kind=kOutput, calls=%fused_computation.22 | convolution fusion | flops 268959744 | bytes 3149828 | tf_op jit(solution)/shard_map/dot_general | solution.py:125
  127.0 3.4 %all-gather.11.cloned.1.call-done = bf16[1,1024,1536]{2,1,0:T(8,128)(2,1)} async-done(((bf16[1,128,1536]{2,1,0:T(8,128)(2,1)}), bf16[1,1024,1536]{2,1,0:T(8,128)(2,1)}) %all-gather.11.cloned.1.call-update) | async-done | bytes 3145744 | tf_op jit(solution)/shard_map/all_gather | solution.py:64
  130.4 2.7 %fusion.12 = bf16[128,1536]{1,0:T(8,128)(2,1)S(1)} fusion(bf16[1,1024,1536]{2,1,0:T(8,128)(2,1)} %all-gather.11.cloned.1.call-done, f32[128,1024]{1,0:T(8,128)S(1)} %get-tuple-element.33, f32[1024]{0:T(1024)S(1)} %bitcast.90, f32[128]{0:T(128)S(1)} %add_rsqrt_fusion.2), kind=kOutput, calls=%fused_computation.12 | convolution fusion | flops 403243008 | bytes 4067840 | tf_op jit(solution)/shard_map/dot_general | solution.py:131
  134.9 4.6 %all-to-all-start = ((bf16[4,64,1,1536]{3,1,2,0:T(8,128)(2,1)}), bf16[4,64,1,1536]{3,1,2,0:T(8,128)(2,1)S(1)}, u32[]{:S(2)}, u32[]{:S(2)}) async-start(bf16[4,64,1,1536]{3,1,2,0:T(8,128)(2,1)} %bitcast.9), calls=%async_computation | async-start | bytes 1572864 | tf_op jit(solution)/shard_map/all_to_all | solution.py:135
  139.5 20.5 %all-to-all-done = bf16[4,64,1,1536]{3,1,2,0:T(8,128)(2,1)S(1)} async-done(((bf16[4,64,1,1536]{3,1,2,0:T(8,128)(2,1)}), bf16[4,64,1,1536]{3,1,2,0:T(8,128)(2,1)S(1)}, u32[]{:S(2)}, u32[]{:S(2)}) %all-to-all-start) | async-done | bytes 786464 | tf_op jit(solution)/shard_map/all_to_all | solution.py:135
  (100 shorter events, 47.0 us)
Async XLA Ops:
  6.5 107.0 %all-gather.9.cloned.1.call-start = ((), (), s32[]{:S(2)}) async-start(), calls=%async_computation.2 | async-start | bytes 2359296 | tf_op jit(solution)/shard_map/all_gather | solution.py:63
  7.3 109.6 %all-gather.7.cloned.1.call-start = ((), (), s32[]{:S(2)}) async-start(), calls=%async_computation.1 | async-start | bytes 9437184 | tf_op jit(solution)/shard_map/all_gather | solution.py:62
  8.0 122.4 %all-gather.11.cloned.1.call-start = ((), (), s32[]{:S(2)}) async-start(), calls=%async_computation.3 | async-start | bytes 3538944 | tf_op jit(solution)/shard_map/all_gather | solution.py:64
  13.7 15.6 %collective-permute-start = (bf16[128,1024]{1,0:T(8,128)(2,1)}, bf16[128,1024]{1,0:T(8,128)(2,1)S(1)}, u32[]{:S(2)}, u32[]{:S(2)}) collective-permute-start(bf16[128,1024]{1,0:T(8,128)(2,1)} %get-tuple-element.17), channel_id=1, source_target_pairs={{0,1},{4,5},{8,9},{12,13},{16,17},{20,21},{24,25},{28,29}} | collective-permute-start | bytes 786440 | tf_op jit(solution)/shard_map/ppermute | solution.py:36
  18.6 11.5 %collective-permute-start.12 = (bf16[128,1024]{1,0:T(8,128)(2,1)}, bf16[128,1024]{1,0:T(8,128)(2,1)S(1)}, u32[]{:S(2)}, u32[]{:S(2)}) collective-permute-start(bf16[128,1024]{1,0:T(8,128)(2,1)} %get-tuple-element.18), channel_id=1, source_target_pairs={{0,1},{4,5},{8,9},{12,13},{16,17},{20,21},{24,25},{28,29}} | collective-permute-start | bytes 786440 | tf_op jit(solution)/shard_map/ppermute | solution.py:36
  32.3 14.4 %collective-permute-start.1 = (bf16[128,1024]{1,0:T(8,128)(2,1)}, bf16[128,1024]{1,0:T(8,128)(2,1)S(1)}, u32[]{:S(2)}, u32[]{:S(2)}) collective-permute-start(bf16[128,1024]{1,0:T(8,128)(2,1)} %get-tuple-element.13), channel_id=1, source_target_pairs={{0,1},{1,2},{4,5},{5,6},{8,9},{9,10},{12,13},{13,14},{16,17},{17,1... | collective-permute-start | bytes 786440 | tf_op jit(solution)/shard_map/ppermute | solution.py:36
  36.6 13.4 %collective-permute-start.13 = (bf16[128,1024]{1,0:T(8,128)(2,1)}, bf16[128,1024]{1,0:T(8,128)(2,1)S(1)}, u32[]{:S(2)}, u32[]{:S(2)}) collective-permute-start(bf16[128,1024]{1,0:T(8,128)(2,1)} %get-tuple-element.16), channel_id=1, source_target_pairs={{0,1},{1,2},{4,5},{5,6},{8,9},{9,10},{12,13},{13,14},{16,17},{17,1... | collective-permute-start | bytes 786440 | tf_op jit(solution)/shard_map/ppermute | solution.py:36
  45.3 15.0 %collective-permute-start.16 = (bf16[128,1024]{1,0:T(8,128)(2,1)}, bf16[128,1024]{1,0:T(8,128)(2,1)S(1)}, u32[]{:S(2)}, u32[]{:S(2)}) collective-permute-start(bf16[128,1024]{1,0:T(8,128)(2,1)} %get-tuple-element.15), channel_id=1, source_target_pairs={{2,1},{3,2},{6,5},{7,6},{10,9},{11,10},{14,13},{15,14},{18,17},{19... | collective-permute-start | bytes 786440 | tf_op jit(solution)/shard_map/ppermute | solution.py:40
  46.0 14.3 %collective-permute-start.4 = (bf16[128,1024]{1,0:T(8,128)(2,1)}, bf16[128,1024]{1,0:T(8,128)(2,1)S(1)}, u32[]{:S(2)}, u32[]{:S(2)}) collective-permute-start(bf16[128,1024]{1,0:T(8,128)(2,1)} %get-tuple-element.14), channel_id=1, source_target_pairs={{2,1},{3,2},{6,5},{7,6},{10,9},{11,10},{14,13},{15,14},{18,17},{19... | collective-permute-start | bytes 786440 | tf_op jit(solution)/shard_map/ppermute | solution.py:40
  50.1 16.1 %collective-permute-start.14 = (bf16[128,1024]{1,0:T(8,128)(2,1)S(1)}, bf16[128,1024]{1,0:T(8,128)(2,1)S(1)}, u32[]{:S(2)}, u32[]{:S(2)}) collective-permute-start(bf16[128,1024]{1,0:T(8,128)(2,1)S(1)} %get-tuple-element.12), channel_id=1, source_target_pairs={{0,1},{1,2},{2,3},{4,5},{5,6},{6,7},{8,9},{9,10},{10,11},{12,13},{... | collective-permute-start | bytes 786440 | tf_op jit(solution)/shard_map/ppermute | solution.py:36
  56.1 10.2 %collective-permute-start.2 = (bf16[128,1024]{1,0:T(8,128)(2,1)S(1)}, bf16[128,1024]{1,0:T(8,128)(2,1)S(1)}, u32[]{:S(2)}, u32[]{:S(2)}) collective-permute-start(bf16[128,1024]{1,0:T(8,128)(2,1)S(1)} %get-tuple-element.11), channel_id=1, source_target_pairs={{0,1},{1,2},{2,3},{4,5},{5,6},{6,7},{8,9},{9,10},{10,11},{12,13},{... | collective-permute-start | bytes 786440 | tf_op jit(solution)/shard_map/ppermute | solution.py:36
  60.6 10.5 %collective-permute-start.17 = (bf16[128,1024]{1,0:T(8,128)(2,1)S(1)}, bf16[128,1024]{1,0:T(8,128)(2,1)S(1)}, u32[]{:S(2)}, u32[]{:S(2)}) collective-permute-start(bf16[128,1024]{1,0:T(8,128)(2,1)S(1)} %get-tuple-element.20), channel_id=1, source_target_pairs={{1,0},{2,1},{3,2},{5,4},{6,5},{7,6},{9,8},{10,9},{11,10},{13,12},{... | collective-permute-start | bytes 786440 | tf_op jit(solution)/shard_map/ppermute | solution.py:40
  62.0 11.9 %collective-permute-start.5 = (bf16[128,1024]{1,0:T(8,128)(2,1)S(1)}, bf16[128,1024]{1,0:T(8,128)(2,1)S(1)}, u32[]{:S(2)}, u32[]{:S(2)}) collective-permute-start(bf16[128,1024]{1,0:T(8,128)(2,1)S(1)} %get-tuple-element.19), channel_id=1, source_target_pairs={{1,0},{2,1},{3,2},{5,4},{6,5},{7,6},{9,8},{10,9},{11,10},{13,12},{... | collective-permute-start | bytes 786440 | tf_op jit(solution)/shard_map/ppermute | solution.py:40
  74.3 9.8 %collective-permute-start.7 = (bf16[128,1024]{1,0:T(8,128)(2,1)S(1)}, bf16[128,1024]{1,0:T(8,128)(2,1)S(1)}, u32[]{:S(2)}, u32[]{:S(2)}) collective-permute-start(bf16[128,1024]{1,0:T(8,128)(2,1)S(1)} %get-tuple-element.6), channel_id=1, source_target_pairs={{0,1},{1,2},{2,3},{4,5},{5,6},{6,7},{8,9},{9,10},{10,11},{12,13},{... | collective-permute-start | bytes 786440 | tf_op jit(solution)/shard_map/ppermute | solution.py:36
  76.9 9.4 %collective-permute-start.6 = (bf16[128,1024]{1,0:T(8,128)(2,1)S(1)}, bf16[128,1024]{1,0:T(8,128)(2,1)S(1)}, u32[]{:S(2)}, u32[]{:S(2)}) collective-permute-start(bf16[128,1024]{1,0:T(8,128)(2,1)S(1)} %get-tuple-element.6), channel_id=1, source_target_pairs={{1,0},{2,1},{3,2},{5,4},{6,5},{7,6},{9,8},{10,9},{11,10},{13,12},{... | collective-permute-start | bytes 786440 | tf_op jit(solution)/shard_map/ppermute | solution.py:40
  82.7 11.1 %collective-permute-start.18 = (bf16[128,1024]{1,0:T(8,128)(2,1)S(1)}, bf16[128,1024]{1,0:T(8,128)(2,1)S(1)}, u32[]{:S(2)}, u32[]{:S(2)}) collective-permute-start(bf16[128,1024]{1,0:T(8,128)(2,1)S(1)} %get-tuple-element.10), channel_id=1, source_target_pairs={{1,0},{2,1},{3,2},{5,4},{6,5},{7,6},{9,8},{10,9},{11,10},{13,12},{... | collective-permute-start | bytes 786440 | tf_op jit(solution)/shard_map/ppermute | solution.py:40
  84.0 11.2 %collective-permute-start.8 = (bf16[128,1024]{1,0:T(8,128)(2,1)S(1)}, bf16[128,1024]{1,0:T(8,128)(2,1)S(1)}, u32[]{:S(2)}, u32[]{:S(2)}) collective-permute-start(bf16[128,1024]{1,0:T(8,128)(2,1)S(1)} %collective-permute-done.7), channel_id=1, source_target_pairs={{1,2},{2,3},{5,6},{6,7},{9,10},{10,11},{13,14},{14,15},{17,18},{18... | collective-permute-start | bytes 786440 | tf_op jit(solution)/shard_map/ppermute | solution.py:36
  86.3 13.2 %collective-permute-start.10 = (bf16[128,1024]{1,0:T(8,128)(2,1)S(1)}, bf16[128,1024]{1,0:T(8,128)(2,1)S(1)}, u32[]{:S(2)}, u32[]{:S(2)}) collective-permute-start(bf16[128,1024]{1,0:T(8,128)(2,1)S(1)} %collective-permute-done.6), channel_id=1, source_target_pairs={{1,0},{2,1},{5,4},{6,5},{9,8},{10,9},{13,12},{14,13},{17,16},{18,1... | collective-permute-start | bytes 786440 | tf_op jit(solution)/shard_map/ppermute | solution.py:40
  87.6 13.2 %collective-permute-start.20 = (bf16[128,1024]{1,0:T(8,128)(2,1)S(1)}, bf16[128,1024]{1,0:T(8,128)(2,1)S(1)}, u32[]{:S(2)}, u32[]{:S(2)}) collective-permute-start(bf16[128,1024]{1,0:T(8,128)(2,1)S(1)} %collective-permute-done.19), channel_id=1, source_target_pairs={{1,2},{2,3},{5,6},{6,7},{9,10},{10,11},{13,14},{14,15},{17,18},{18... | collective-permute-start | bytes 786440 | tf_op jit(solution)/shard_map/ppermute | solution.py:36
  93.9 11.2 %collective-permute-start.22 = (bf16[128,1024]{1,0:T(8,128)(2,1)S(1)}, bf16[128,1024]{1,0:T(8,128)(2,1)S(1)}, u32[]{:S(2)}, u32[]{:S(2)}) collective-permute-start(bf16[128,1024]{1,0:T(8,128)(2,1)S(1)} %collective-permute-done.18), channel_id=1, source_target_pairs={{1,0},{2,1},{5,4},{6,5},{9,8},{10,9},{13,12},{14,13},{17,16},{18,1... | collective-permute-start | bytes 786440 | tf_op jit(solution)/shard_map/ppermute | solution.py:40
  95.2 11.7 %collective-permute-start.9 = (bf16[128,1024]{1,0:T(8,128)(2,1)S(1)}, bf16[128,1024]{1,0:T(8,128)(2,1)S(1)}, u32[]{:S(2)}, u32[]{:S(2)}) collective-permute-start(bf16[128,1024]{1,0:T(8,128)(2,1)S(1)} %collective-permute-done.8), channel_id=1, source_target_pairs={{2,3},{6,7},{10,11},{14,15},{18,19},{22,23},{26,27},{30,31}} | collective-permute-start | bytes 786440 | tf_op jit(solution)/shard_map/ppermute | solution.py:36
  99.5 10.9 %collective-permute-start.11 = (bf16[128,1024]{1,0:T(8,128)(2,1)S(1)}, bf16[128,1024]{1,0:T(8,128)(2,1)S(1)}, u32[]{:S(2)}, u32[]{:S(2)}) collective-permute-start(bf16[128,1024]{1,0:T(8,128)(2,1)S(1)} %collective-permute-done.10), channel_id=1, source_target_pairs={{1,0},{5,4},{9,8},{13,12},{17,16},{21,20},{25,24},{29,28}} | collective-permute-start | bytes 786440 | tf_op jit(solution)/shard_map/ppermute | solution.py:40
  100.8 9.8 %collective-permute-start.21 = (bf16[128,1024]{1,0:T(8,128)(2,1)S(1)}, bf16[128,1024]{1,0:T(8,128)(2,1)S(1)}, u32[]{:S(2)}, u32[]{:S(2)}) collective-permute-start(bf16[128,1024]{1,0:T(8,128)(2,1)S(1)} %collective-permute-done.20), channel_id=1, source_target_pairs={{2,3},{6,7},{10,11},{14,15},{18,19},{22,23},{26,27},{30,31}} | collective-permute-start | bytes 786440 | tf_op jit(solution)/shard_map/ppermute | solution.py:36
  134.9 25.1 %all-to-all-start = ((bf16[4,64,1,1536]{3,1,2,0:T(8,128)(2,1)}), bf16[4,64,1,1536]{3,1,2,0:T(8,128)(2,1)S(1)}, u32[]{:S(2)}, u32[]{:S(2)}) async-start(bf16[4,64,1,1536]{3,1,2,0:T(8,128)(2,1)} %bitcast.9), calls=%async_computation | async-start | bytes 1572864 | tf_op jit(solution)/shard_map/all_to_all | solution.py:135
  (12 other events, 185.3 us)
Sparse Core Ops, SparseCore 0:
  9.2 30.5 all-gather.8
  41.8 54.3 all-gather.6
  98.1 32.3 all-gather.10

commit v2 on v0

v2 whole, which is shorter than its diff:
```python
import functools

import jax
import jax.numpy as jnp
from jax import lax
from jax.experimental import pallas as pl
from jax.experimental.pallas import tpu as pltpu
from jax.sharding import PartitionSpec as P

H = 8
HD = 64
f32, bf16 = jnp.float32, jnp.bfloat16


def tail_kernel(books, groups, place_ref, *refs):
    blocks = refs[:books]
    gain_ref, tokens_ref, depth_gain_ref, gathered = refs[books : books + 4]
    outs = refs[books + 4 : 2 * books + 4]
    proj, table, qkv, packed, sems = refs[2 * books + 4 :]
    place = place_ref[0]
    frames_here, width = blocks[0].shape
    depth = proj.shape[1]
    wide = qkv.shape[1]
    proj_rows = proj.shape[0] // groups
    table_rows = table.shape[0] // groups
    qkv_rows = qkv.shape[0] // groups
    per_book = groups // books
    half = qkv_rows // 2
    extra = wide - depth

    table_copies, proj_copies, qkv_copies = [], [], []

    def copy(source, target, into):
        number = len(table_copies) + len(proj_copies) + len(qkv_copies)
        made = pltpu.make_async_copy(source, target, sems.at[number])
        made.start()
        into.append(made)

    at_table = proj_rows
    at_qkv = proj_rows + table_rows
    at_extra = at_qkv + qkv_rows
    for g in range(groups):
        copy(
            gathered.at[g, pl.ds(at_table, table_rows)],
            table.at[pl.ds(g * table_rows, table_rows)],
            table_copies,
        )
    for m in range(books):
        for r in range(per_book):
            g = jnp.bitwise_xor(place, m) * per_book + r
            copy(
                gathered.at[g, pl.ds(0, proj_rows)],
                proj.at[pl.ds(pl.multiple_of(g * proj_rows, proj_rows), proj_rows)],
                proj_copies,
            )
    for g in range(groups):
        copy(
            gathered.at[g, pl.ds(at_qkv, qkv_rows)],
            qkv.at[pl.ds(g * qkv_rows, qkv_rows), pl.ds(0, depth)],
            qkv_copies,
        )
        for side in range(2):
            copy(
                gathered.at[g, pl.ds(at_extra, half), pl.ds(side * extra, extra)],
                qkv.at[pl.ds(g * qkv_rows + side * half, half), pl.ds(depth, extra)],
                qkv_copies,
            )

    columns = lax.broadcasted_iota(jnp.int32, (frames_here, table.shape[0]), 1)
    matches = (tokens_ref[...] == columns).astype(f32).astype(bf16)
    for made in table_copies:
        made.wait()
    looked = jnp.dot(matches, table[...], preferred_element_type=f32)

    square = jnp.zeros((frames_here, 1), f32)
    projected = jnp.zeros((frames_here, depth), f32)
    for m in range(books):
        start = pl.multiple_of(jnp.bitwise_xor(place, m) * width, width)
        part = blocks[m][...].astype(f32)
        square = square + jnp.sum(part * part, axis=-1, keepdims=True)
        scaled = (part * gain_ref[:, pl.ds(start, width)]).astype(bf16)
        for made in proj_copies[m * per_book : (m + 1) * per_book]:
            made.wait()
        projected = projected + jnp.dot(
            scaled, proj[pl.ds(start, width), :], preferred_element_type=f32
        )
    projected = projected * lax.rsqrt(square / (books * width) + 1e-05)
    depth_in = (projected + looked).astype(bf16).astype(f32)
    moment = jnp.mean(depth_in * depth_in, axis=-1, keepdims=True)
    depth_normed = (depth_in * lax.rsqrt(moment + 1e-05) * depth_gain_ref[...]).astype(bf16)
    for made in qkv_copies:
        made.wait()
    packed[...] = jnp.dot(depth_normed, qkv[...], preferred_element_type=f32).astype(bf16)
    rows = frames_here // books
    for m in range(books):
        start = pl.multiple_of(jnp.bitwise_xor(place, m) * rows, rows)
        outs[m][...] = packed[pl.ds(start, rows), :]


def tail(place, blocks, gain, tokens, depth_gain, gathered, sizes):
    books = len(blocks)
    groups = gathered.shape[0]
    features, codes, depth, wide = sizes
    frames_here = blocks[0].shape[0]
    vmem = pl.BlockSpec(memory_space=pltpu.VMEM)
    flops = 2 * frames_here * depth * (features + codes + wide)
    return pl.pallas_call(
        functools.partial(tail_kernel, books, groups),
        out_shape=[jax.ShapeDtypeStruct((frames_here // books, wide), bf16)] * books,
        in_specs=[pl.BlockSpec(memory_space=pltpu.SMEM)]
        + [vmem] * (books + 3)
        + [pl.BlockSpec(memory_space=pl.ANY)],
        out_specs=[vmem] * books,
        scratch_shapes=[
            pltpu.VMEM((features, depth), bf16),
            pltpu.VMEM((codes, depth), bf16),
            pltpu.VMEM((depth, wide), bf16),
            pltpu.VMEM((frames_here, wide), bf16),
            pltpu.SemaphoreType.DMA((5 * groups,)),
        ],
        compiler_params=pltpu.CompilerParams(vmem_limit_bytes=40 * 2**20),
        cost_estimate=pl.CostEstimate(
            flops=flops, bytes_accessed=gathered.size * 2, transcendentals=0
        ),
        name="project_lookup_qkv",
    )(place, *blocks, gain, tokens, depth_gain, gathered)


def attend_kernel(books, place_ref, *refs):
    arrived = refs[:books]
    out_ref, inner = refs[books:]
    place = place_ref[0]
    rows, wide = arrived[0].shape
    width = wide // 3
    for m in range(books):
        inner[jnp.bitwise_xor(place, m)] = arrived[m][...]
    head_of_row = lax.broadcasted_iota(jnp.int32, (width, width), 0) // HD
    head_of_column = lax.broadcasted_iota(jnp.int32, (width, width), 1) // HD
    same_head = (head_of_row == head_of_column).astype(f32).astype(bf16)
    keys_all = [inner[j, :, width : 2 * width].astype(f32) for j in range(books)]
    values_all = [inner[j, :, 2 * width :].astype(f32) for j in range(books)]
    contexts = []
    for k in range(books):
        query = inner[k, :, :width].astype(f32) * HD ** (-0.5)
        products = jnp.concatenate([query * keys_all[j] for j in range(k + 1)], axis=0)
        high = products.astype(bf16)
        low = (products - high.astype(f32)).astype(bf16)
        scores = jnp.dot(high, same_head, preferred_element_type=f32) + jnp.dot(
            low, same_head, preferred_element_type=f32
        )
        scores = [scores[j * rows : (j + 1) * rows] for j in range(k + 1)]
        peak = functools.reduce(jnp.maximum, scores)
        expo = [jnp.exp(score - peak) for score in scores]
        total = functools.reduce(jnp.add, expo)
        context = 0.0
        for j in range(k + 1):
            probability = (expo[j] / total).astype(bf16).astype(f32)
            context = context + probability * values_all[j]
        contexts.append(context)
    out_ref[...] = jnp.stack(contexts, axis=1).astype(bf16)


def attend(place, arrived):
    books = len(arrived)
    rows, wide = arrived[0].shape
    vmem = pl.BlockSpec(memory_space=pltpu.VMEM)
    return pl.pallas_call(
        functools.partial(attend_kernel, books),
        out_shape=jax.ShapeDtypeStruct((rows, books, wide // 3), bf16),
        in_specs=[pl.BlockSpec(memory_space=pltpu.SMEM)] + [vmem] * books,
        out_specs=vmem,
        scratch_shapes=[pltpu.VMEM((books, rows, wide), bf16)],
        compiler_params=pltpu.CompilerParams(vmem_limit_bytes=32 * 2**20),
        name="attend_books",
    )(place, *arrived)


def swap(value, distance):
    books = lax.axis_size("book")
    return lax.ppermute(value, "book", [(i, i ^ distance) for i in range(books)])


def per_device(
    gate_pre,
    up_pre,
    down_weight,
    residual,
    out_gain,
    in_proj,
    embedding,
    token_ids,
    depth_gain,
    qkv_weight,
):
    books = lax.axis_size("book")
    groups = lax.axis_size("frames")
    here = lax.axis_index("book").astype(jnp.int32)
    place = here[None]
    width = residual.shape[1]
    depth = in_proj.shape[2]
    wide = qkv_weight.shape[2]
    half = qkv_weight.shape[1] // 2

    beyond = qkv_weight[0, :, depth:]
    weights = jnp.concatenate(
        [
            in_proj[0],
            embedding[0],
            qkv_weight[0, :, :depth],
            jnp.concatenate([beyond[:half], beyond[half:]], axis=1),
        ],
        axis=0,
    )
    gathered = lax.all_gather(weights, "frames", axis=0)

    hidden = (jax.nn.silu(gate_pre.astype(f32)) * up_pre.astype(f32)).astype(bf16)

    def share(m):
        start = jnp.bitwise_xor(here, m) * width
        block = lax.dynamic_slice_in_dim(down_weight, start, width, 1)
        return jnp.dot(hidden, block, preferred_element_type=f32)

    sums = {books - 1: share(books - 1)}
    for m in range(books - 2, -1, -1):
        sums[m] = lax.optimization_barrier(share(m))
    sums[0] = sums[0] + residual.astype(f32)
    distance = 1
    while distance < books:
        for m in range(books - distance, 0, -2 * distance):
            came = swap(sums.pop(m).astype(bf16), distance)
            sums[m ^ distance] = sums[m ^ distance] + came.astype(f32)
        distance *= 2

    blocks = {0: sums[0].astype(bf16)}
    distance = books // 2
    while distance:
        for m in sorted(blocks):
            blocks[m ^ distance] = swap(blocks[m], distance)
        distance //= 2

    packed = tail(
        place,
        [blocks[m] for m in range(books)],
        out_gain.astype(f32)[None],
        token_ids,
        depth_gain.astype(f32),
        gathered,
        (books * width, groups * embedding.shape[1], depth, wide),
    )
    arrived = [packed[0]]
    far = {m: swap(packed[m], m) for m in range(books - 1, 0, -1)}
    arrived += [far[m] for m in range(1, books)]
    return attend(place, arrived)


def solution(mesh):
    in_specs = (
        P("frames", "book"),
        P("frames", "book"),
        P("book", None),
        P("frames", "book"),
        P(),
        P("book", "frames", None),
        P("book", "frames", None),
        P("frames", "book"),
        P("book", None),
        P("book", "frames", None),
    )
    out_specs = P(("frames", "book"), None, None)
    return jax.shard_map(
        per_device, mesh=mesh, in_specs=in_specs, out_specs=out_specs, check_vma=False
    )
```

time: 306 us -> 127 us (0.42)
  waiting for transfers between devices: 255 us -> 55.4 us
  starting transfers between devices: 4.76 us -> 29.7 us
  matrix products: 24.8 us -> 12.8 us
  Pallas kernels: 0 us -> 9.29 us
    all_gather x4 -> x1, waiting for transfers between devices: 153 us -> 1.18 us  [per_device(): gathered = lax.all_gather(weights, 'frames', axis=0)]
    reduce_scatter x1 -> x0, waiting for transfers between devices: 79.5 us -> none  [per_device(): lax.psum_scatter(partial_value, 'book', scatter_dimension=1, tiled=True)]
    ppermute x0 -> x9, waiting for transfers between devices: none -> 54.2 us  [swap(): lax.ppermute(value, 'book', [(i, i ^ distance) for i in range(books)])]
    ppermute x0 -> x9, starting transfers between devices: none -> 29.7 us  [swap(): lax.ppermute(value, 'book', [(i, i ^ distance) for i in range(books)])]
    all_to_all x1 -> x0, waiting for transfers between devices: 20.5 us -> none  [per_device(): lax.all_to_all(grouped, 'book', split_axis=0, concat_axis=2, tiled=True)]
    dot_general x6 -> x4, matrix products: 24.8 us -> 12.8 us  [share(): return jnp.dot(hidden, block, preferred_element_type=f32)]
    pallas_call x0 -> x2, Pallas kernels: none -> 9.29 us  [the longest x1 7.04 us: tail(): pl.pallas_call(functools.partial(tail_kernel, books, groups), out_shape=[...]
    all_to_all x1 -> x0, starting transfers between devices: 4.6 us -> none  [per_device(): lax.all_to_all(grouped, 'book', split_axis=0, concat_axis=2, tiled=True)]
  transfers between devices with their start and end apart: 6 -> 10, of which waited for: 6 -> 9; matrix products, arithmetic and copies ran while one was open for 4% -> 11% of each run, Pallas kernels for 0% -> 0%
where the time goes in v2:
time: 127 us
  waiting for transfers between devices  55.4 us (44%)
  starting transfers between devices  29.7 us (23%)
  between operations  13.5 us (11%)
  matrix products  12.8 us (10%)
  Pallas kernels  9.29 us (7%)
  other arithmetic  3.65 us (3%)
  local copies, waits for them, and re-layouts  2.13 us (2%)
    ppermute x9, waiting for transfers between devices, swap(): lax.ppermute(value, 'book', [(i, i ^ distance) for i in range(books)])  54.2 us
    ppermute x9, starting transfers between devices, swap(): lax.ppermute(value, 'book', [(i, i ^ distance) for i in range(books)])  29.7 us
    dot_general x4, matrix products, share(): return jnp.dot(hidden, block, preferred_element_type=f32)  12.8 us
    pallas_call x1, Pallas kernels, tail(): pl.pallas_call(functools.partial(tail_kernel, books, groups), out_shape=[...  7.04 us
    concatenate x1, other arithmetic, per_device(): jnp.concatenate([in_proj[0], embedding[0], qkv_weight[0, :, :depth], jnp....  2.65 us
  transfers between devices with their start and end apart: 10, of which 9 were waited for; matrix products, arithmetic and copies ran while one was open for 11% of the time, Pallas kernels for 0%

profile of v2, /device:TPU:0, one launch (start us, length us, event | category | flops | bytes accessed | tf_op | source)
XLA Modules:
  0.0 126.6 jit_solution(10347237265550012205)
XLA Ops:
  6.5 1.0 slice_bitcast_fusion.2
  7.5 1.0 slice_bitcast_fusion
  8.5 2.6 %maximum_maximum_fusion = bf16[832,1024]{1,0:T(8,128)(2,1)} fusion(bf16[64,512]{1,0:T(8,128)(2,1)S(1)} %get-tuple-element.14, bf16[64,512]{1,0:T(8,128)(2,1)S(1)} %get-tuple-element.13, bf16[128,1024]{1,0:T(8,128)(2,1)S(1)} %slice_bitcast_fusion, bf16[128,1024]{1,0:T(8,128)(2,1)} %bitcast.18, bf16[512,1024]{1,0:T(8,128)(2,1)} %bitcast.17), kind=kLoop, calls=%fused_computation.10 | loop fusion | flops 8519680 | bytes 3407872 | tf_op jit(solution)/shard_map/concatenate | solution.py:205
  11.7 2.9 %fusion.13 = bf16[256,1024]{1,0:T(8,128)(2,1)S(1)} fusion(bf16[256,1536]{1,0:T(8,128)(2,1)S(1)} %fusion.12, bf16[1536,4096]{1,0:T(8,128)(2,1)} %param.12, s32[]{:T(128)S(6)} %select_n.15), kind=kOutput, calls=%fused_computation.16 | convolution fusion | flops 805568512 | bytes 4456452 | tf_op jit(solution)/shard_map/dot_general | solution.py:221
  14.6 3.1 %collective-permute-start.1 = (bf16[256,1024]{1,0:T(8,128)(2,1)S(1)}, bf16[256,1024]{1,0:T(8,128)(2,1)S(1)}, u32[]{:S(2)}, u32[]{:S(2)}) collective-permute-start(bf16[256,1024]{1,0:T(8,128)(2,1)S(1)} %fusion.13), channel_id=1, source_target_pairs={{0,1},{1,0},{2,3},{3,2},{4,5},{5,4},{6,7},{7,6},{8,9},{9,8},{10,11... | collective-permute-start | bytes 1572872 | tf_op jit(solution)/shard_map/ppermute | solution.py:180
  17.7 3.7 %fusion.4 = bf16[256,1024]{1,0:T(8,128)(2,1)} fusion(bf16[256,1536]{1,0:T(8,128)(2,1)S(1)} %fusion.12, bf16[1536,4096]{1,0:T(8,128)(2,1)} %param.12, s32[]{:T(128)S(6)} %select_n.13), kind=kOutput, calls=%fused_computation.4 | convolution fusion | flops 805306368 | bytes 4456452 | tf_op jit(solution)/shard_map/dot_general | solution.py:221
  21.4 3.3 %fusion.2 = f32[256,1024]{1,0:T(8,128)S(1)} fusion(bf16[256,1536]{1,0:T(8,128)(2,1)S(1)} %fusion.12, bf16[1536,4096]{1,0:T(8,128)(2,1)} %param.12, s32[]{:T(128)S(6)} %select_n.14), kind=kOutput, calls=%fused_computation.2 | convolution fusion | flops 805306368 | bytes 4980740 | tf_op jit(solution)/shard_map/dot_general | solution.py:221
  24.7 5.7 %collective-permute-done.1 = bf16[256,1024]{1,0:T(8,128)(2,1)S(1)} collective-permute-done((bf16[256,1024]{1,0:T(8,128)(2,1)S(1)}, bf16[256,1024]{1,0:T(8,128)(2,1)S(1)}, u32[]{:S(2)}, u32[]{:S(2)}) %collective-permute-start.1) | collective-permute-done | bytes 524320 | tf_op jit(solution)/shard_map/ppermute | solution.py:180
  30.6 3.1 %collective-permute-start.2 = (bf16[256,1024]{1,0:T(8,128)(2,1)S(1)}, bf16[256,1024]{1,0:T(8,128)(2,1)S(1)}, u32[]{:S(2)}, u32[]{:S(2)}) collective-permute-start(bf16[256,1024]{1,0:T(8,128)(2,1)S(1)} %add_convert_fusion.1), channel_id=1, source_target_pairs={{0,2},{1,3},{2,0},{3,1},{4,6},{5,7},{6,4},{7,5},{8,10},{9,11},{10,... | collective-permute-start | bytes 1572872 | tf_op jit(solution)/shard_map/ppermute | solution.py:180
  33.8 2.9 %fusion.6 = f32[256,1024]{1,0:T(8,128)S(1)} fusion(bf16[256,1536]{1,0:T(8,128)(2,1)S(1)} %fusion.12, bf16[1536,4096]{1,0:T(8,128)(2,1)} %param.12, s32[]{:T(128)S(6)} %select_n.12), kind=kOutput, calls=%fused_computation.6 | convolution fusion | flops 805306368 | bytes 4980740 | tf_op jit(solution)/shard_map/dot_general | solution.py:221
  36.7 14.5 %collective-permute-done = bf16[256,1024]{1,0:T(8,128)(2,1)S(1)} collective-permute-done((bf16[256,1024]{1,0:T(8,128)(2,1)}, bf16[256,1024]{1,0:T(8,128)(2,1)S(1)}, u32[]{:S(2)}, u32[]{:S(2)}) %collective-permute-start) | collective-permute-done | bytes 524320 | tf_op jit(solution)/shard_map/ppermute | solution.py:180
  51.2 4.3 %collective-permute-done.2 = bf16[256,1024]{1,0:T(8,128)(2,1)S(1)} collective-permute-done((bf16[256,1024]{1,0:T(8,128)(2,1)S(1)}, bf16[256,1024]{1,0:T(8,128)(2,1)S(1)}, u32[]{:S(2)}, u32[]{:S(2)}) %collective-permute-start.2) | collective-permute-done | bytes 524320 | tf_op jit(solution)/shard_map/ppermute | solution.py:180
  55.9 14.8 %collective-permute-start.3 = (bf16[256,1024]{1,0:T(8,128)(2,1)S(1)}, bf16[256,1024]{1,0:T(8,128)(2,1)S(1)}, u32[]{:S(2)}, u32[]{:S(2)}) collective-permute-start(bf16[256,1024]{1,0:T(8,128)(2,1)S(1)} %add_convert_fusion.refs_0_), channel_id=1, source_target_pairs={{0,1},{1,0},{2,3},{3,2},{4,5},{5,4},{6,7},{7,6},{8,9},{9,8},{10,11... | collective-permute-start | bytes 1572872 | tf_op jit(solution)/shard_map/ppermute | solution.py:180
  70.7 7.2 %collective-permute-done.4.refs_2_ = bf16[256,1024]{1,0:T(8,128)(2,1)S(1)} collective-permute-done((bf16[256,1024]{1,0:T(8,128)(2,1)S(1)}, bf16[256,1024]{1,0:T(8,128)(2,1)S(1)}, u32[]{:S(2)}, u32[]{:S(2)}) %collective-permute-start.4) | collective-permute-done | bytes 524320 | tf_op jit(solution)/shard_map/ppermute | solution.py:180
  77.8 0.6 collective-permute-start.5
  78.6 2.7 %collective-permute-done.3.refs_1_ = bf16[256,1024]{1,0:T(8,128)(2,1)S(1)} collective-permute-done((bf16[256,1024]{1,0:T(8,128)(2,1)S(1)}, bf16[256,1024]{1,0:T(8,128)(2,1)S(1)}, u32[]{:S(2)}, u32[]{:S(2)}) %collective-permute-start.3) | collective-permute-done | bytes 524320 | tf_op jit(solution)/shard_map/ppermute | solution.py:180
  81.3 8.2 %collective-permute-done.5.refs_3_ = bf16[256,1024]{1,0:T(8,128)(2,1)S(1)} collective-permute-done((bf16[256,1024]{1,0:T(8,128)(2,1)S(1)}, bf16[256,1024]{1,0:T(8,128)(2,1)S(1)}, u32[]{:S(2)}, u32[]{:S(2)}) %collective-permute-start.5) | collective-permute-done | bytes 524320 | tf_op jit(solution)/shard_map/ppermute | solution.py:180
  89.4 1.2 all-gather.3.cloned.1.call-done
  90.6 7.0 %project_lookup_qkv.1 = (bf16[64,1536]{1,0:T(8,128)(2,1)S(1)}, bf16[64,1536]{1,0:T(8,128)(2,1)S(1)}, bf16[64,1536]{1,0:T(8,128)(2,1)S(1)}, bf16[64,1536]{1,0:T(8,128)(2,1)S(1)}) custom-call(s32[1]{0:T(128)} %bitcast.place_ref, bf16[256,1024]{1,0:T(8,128)(2,1)S(1)} %add_convert_fusion.refs_0_, bf16[256,1024]{1,0:T(8,128)(2,1)S(1)} %collective-permute-done.3.refs_1_, ...), custom_call_target="tpu_custom_call" | custom-call | flops 3489660928 | bytes 13631488 | tf_op jit(solution)/shard_map/project_lookup_qkv/pallas_call | solution.py:107
  97.7 1.6 %collective-permute-start.6 = (bf16[64,1536]{1,0:T(8,128)(2,1)S(1)}, bf16[64,1536]{1,0:T(8,128)(2,1)S(1)}, u32[]{:S(2)}, u32[]{:S(2)}) collective-permute-start(bf16[64,1536]{1,0:T(8,128)(2,1)S(1)} %get-tuple-element.10), channel_id=1, source_target_pairs={{0,1},{1,0},{2,3},{3,2},{4,5},{5,4},{6,7},{7,6},{8,9},{9,8},{10,11... | collective-permute-start | bytes 589832 | tf_op jit(solution)/shard_map/ppermute | solution.py:180
  99.2 6.5 %collective-permute-start.7 = (bf16[64,1536]{1,0:T(8,128)(2,1)S(1)}, bf16[64,1536]{1,0:T(8,128)(2,1)S(1)}, u32[]{:S(2)}, u32[]{:S(2)}) collective-permute-start(bf16[64,1536]{1,0:T(8,128)(2,1)S(1)} %get-tuple-element.11), channel_id=1, source_target_pairs={{0,2},{1,3},{2,0},{3,1},{4,6},{5,7},{6,4},{7,5},{8,10},{9,11},{10,... | collective-permute-start | bytes 589832 | tf_op jit(solution)/shard_map/ppermute | solution.py:180
  105.7 1.0 collective-permute-done.6.refs_1_
  106.7 10.8 %collective-permute-done.7.refs_2_ = bf16[64,1536]{1,0:T(8,128)(2,1)S(1)} collective-permute-done((bf16[64,1536]{1,0:T(8,128)(2,1)S(1)}, bf16[64,1536]{1,0:T(8,128)(2,1)S(1)}, u32[]{:S(2)}, u32[]{:S(2)}) %collective-permute-start.7) | collective-permute-done | bytes 196640 | tf_op jit(solution)/shard_map/ppermute | solution.py:180
  117.5 2.2 %attend_books.1 = bf16[64,4,512]{2,1,0:T(4,128)(2,1)} custom-call(s32[1]{0:T(128)} %bitcast.place_ref, bf16[64,1536]{1,0:T(8,128)(2,1)S(1)} %get-tuple-element.9.refs_0_, bf16[64,1536]{1,0:T(8,128)(2,1)S(1)} %collective-permute-done.6.refs_1_, bf16[64,1536]{1,0:T(8,128)(2,1)S(1)} %collective-permute-done.7.refs_2_, ...), custom_call_target="tpu_custom_call" | custom-call | tf_op jit(solution)/shard_map/attend_books/pallas_call | solution.py:167
  (24 shorter events, 1.3 us)
Async XLA Ops:
  6.5 4.7 %copy-start.1 = (bf16[256,1536]{1,0:T(8,128)(2,1)S(1)}, bf16[256,1536]{1,0:T(8,128)(2,1)}, u32[]{:S(2)}) copy-start(bf16[256,1536]{1,0:T(8,128)(2,1)} %param.10) | copy-start | bytes 2359300
  6.5 4.7 %copy-start = (bf16[256,1536]{1,0:T(8,128)(2,1)S(1)}, bf16[256,1536]{1,0:T(8,128)(2,1)}, u32[]{:S(2)}) copy-start(bf16[256,1536]{1,0:T(8,128)(2,1)} %param.11) | copy-start | bytes 2359300
  6.5 84.1 %all-gather.3.cloned.1.call-start = ((), (), s32[]{:S(2)}) async-start(), calls=%async_computation | async-start | bytes 15335424 | tf_op jit(solution)/shard_map/all_gather | solution.py:214
  14.6 15.8 %collective-permute-start.1 = (bf16[256,1024]{1,0:T(8,128)(2,1)S(1)}, bf16[256,1024]{1,0:T(8,128)(2,1)S(1)}, u32[]{:S(2)}, u32[]{:S(2)}) collective-permute-start(bf16[256,1024]{1,0:T(8,128)(2,1)S(1)} %fusion.13), channel_id=1, source_target_pairs={{0,1},{1,0},{2,3},{3,2},{4,5},{5,4},{6,7},{7,6},{8,9},{9,8},{10,11... | collective-permute-start | bytes 1572872 | tf_op jit(solution)/shard_map/ppermute | solution.py:180
  21.4 29.8 %collective-permute-start = (bf16[256,1024]{1,0:T(8,128)(2,1)}, bf16[256,1024]{1,0:T(8,128)(2,1)S(1)}, u32[]{:S(2)}, u32[]{:S(2)}) collective-permute-start(bf16[256,1024]{1,0:T(8,128)(2,1)} %fusion.4), channel_id=1, source_target_pairs={{0,1},{1,0},{2,3},{3,2},{4,5},{5,4},{6,7},{7,6},{8,9},{9,8},{10,11... | collective-permute-start | bytes 1572872 | tf_op jit(solution)/shard_map/ppermute | solution.py:180
  30.6 24.8 %copy-start.2 = (bf16[256,1024]{1,0:T(8,128)(2,1)S(1)}, bf16[256,1024]{1,0:T(8,128)(2,1)}, u32[]{:S(2)}) copy-start(bf16[256,1024]{1,0:T(8,128)(2,1)} %param.13) | copy-start | bytes 1572868
  30.6 24.8 %collective-permute-start.2 = (bf16[256,1024]{1,0:T(8,128)(2,1)S(1)}, bf16[256,1024]{1,0:T(8,128)(2,1)S(1)}, u32[]{:S(2)}, u32[]{:S(2)}) collective-permute-start(bf16[256,1024]{1,0:T(8,128)(2,1)S(1)} %add_convert_fusion.1), channel_id=1, source_target_pairs={{0,2},{1,3},{2,0},{3,1},{4,6},{5,7},{6,4},{7,5},{8,10},{9,11},{10,... | collective-permute-start | bytes 1572872 | tf_op jit(solution)/shard_map/ppermute | solution.py:180
  33.8 44.6 %copy-start.5 = (s32[256,1]{0,1:T(1,128)S(1)}, s32[256,1]{0,1:T(1,128)}, u32[]{:S(2)}) copy-start(s32[256,1]{0,1:T(1,128)} %param.17) | copy-start | bytes 3076
  33.8 44.8 %copy-start.3 = (bf16[4096]{0:T(1024)(128)(2,1)S(1)}, bf16[4096]{0:T(1024)(128)(2,1)}, u32[]{:S(2)}) copy-start(bf16[4096]{0:T(1024)(128)(2,1)} %param.14) | copy-start | bytes 24580
  33.8 44.8 %copy-start.4 = (bf16[1,1024]{1,0:T(2,128)(2,1)S(1)}, bf16[1,1024]{1,0:T(2,128)(2,1)}, u32[]{:S(2)}) copy-start(bf16[1,1024]{1,0:T(2,128)(2,1)} %param.18) | copy-start | bytes 6148
  55.8 22.0 %collective-permute-start.4 = (bf16[256,1024]{1,0:T(8,128)(2,1)S(1)}, bf16[256,1024]{1,0:T(8,128)(2,1)S(1)}, u32[]{:S(2)}, u32[]{:S(2)}) collective-permute-start(bf16[256,1024]{1,0:T(8,128)(2,1)S(1)} %add_convert_fusion.refs_0_), channel_id=1, source_target_pairs={{0,2},{1,3},{2,0},{3,1},{4,6},{5,7},{6,4},{7,5},{8,10},{9,11},{10,... | collective-permute-start | bytes 1572872 | tf_op jit(solution)/shard_map/ppermute | solution.py:180
  55.9 25.4 %collective-permute-start.3 = (bf16[256,1024]{1,0:T(8,128)(2,1)S(1)}, bf16[256,1024]{1,0:T(8,128)(2,1)S(1)}, u32[]{:S(2)}, u32[]{:S(2)}) collective-permute-start(bf16[256,1024]{1,0:T(8,128)(2,1)S(1)} %add_convert_fusion.refs_0_), channel_id=1, source_target_pairs={{0,1},{1,0},{2,3},{3,2},{4,5},{5,4},{6,7},{7,6},{8,9},{9,8},{10,11... | collective-permute-start | bytes 1572872 | tf_op jit(solution)/shard_map/ppermute | solution.py:180
  77.8 11.6 %collective-permute-start.5 = (bf16[256,1024]{1,0:T(8,128)(2,1)S(1)}, bf16[256,1024]{1,0:T(8,128)(2,1)S(1)}, u32[]{:S(2)}, u32[]{:S(2)}) collective-permute-start(bf16[256,1024]{1,0:T(8,128)(2,1)S(1)} %collective-permute-done.4.refs_2_), channel_id=1, source_target_pairs={{0,1},{1,0},{2,3},{3,2},{4,5},{5,4},{6,7},{7,6},{8,9},{9,8},{10,11... | collective-permute-start | bytes 1572872 | tf_op jit(solution)/shard_map/ppermute | solution.py:180
  97.7 9.0 %collective-permute-start.6 = (bf16[64,1536]{1,0:T(8,128)(2,1)S(1)}, bf16[64,1536]{1,0:T(8,128)(2,1)S(1)}, u32[]{:S(2)}, u32[]{:S(2)}) collective-permute-start(bf16[64,1536]{1,0:T(8,128)(2,1)S(1)} %get-tuple-element.10), channel_id=1, source_target_pairs={{0,1},{1,0},{2,3},{3,2},{4,5},{5,4},{6,7},{7,6},{8,9},{9,8},{10,11... | collective-permute-start | bytes 589832 | tf_op jit(solution)/shard_map/ppermute | solution.py:180
  99.2 18.3 %collective-permute-start.7 = (bf16[64,1536]{1,0:T(8,128)(2,1)S(1)}, bf16[64,1536]{1,0:T(8,128)(2,1)S(1)}, u32[]{:S(2)}, u32[]{:S(2)}) collective-permute-start(bf16[64,1536]{1,0:T(8,128)(2,1)S(1)} %get-tuple-element.11), channel_id=1, source_target_pairs={{0,2},{1,3},{2,0},{3,1},{4,6},{5,7},{6,4},{7,5},{8,10},{9,11},{10,... | collective-permute-start | bytes 589832 | tf_op jit(solution)/shard_map/ppermute | solution.py:180
  105.7 11.8 %collective-permute-start.8 = (bf16[64,1536]{1,0:T(8,128)(2,1)S(1)}, bf16[64,1536]{1,0:T(8,128)(2,1)S(1)}, u32[]{:S(2)}, u32[]{:S(2)}) collective-permute-start(bf16[64,1536]{1,0:T(8,128)(2,1)S(1)} %get-tuple-element.12), channel_id=1, source_target_pairs={{0,3},{1,2},{2,1},{3,0},{4,7},{5,6},{6,5},{7,4},{8,11},{9,10},{10,... | collective-permute-start | bytes 589832 | tf_op jit(solution)/shard_map/ppermute | solution.py:180
Sparse Core Ops, SparseCore 0:
  11.3 79.2 all-gather.2

commit v3 on v2

v3 whole, which is shorter than its diff:
```python
import functools

import jax
import jax.numpy as jnp
from jax import lax
from jax.experimental import pallas as pl
from jax.experimental.pallas import tpu as pltpu
from jax.sharding import PartitionSpec as P

H = 8
HD = 64
f32, bf16 = jnp.float32, jnp.bfloat16


def assemble_kernel(groups, sizes, place_ref, tokens_ref, *refs):
    parts = refs[:groups]
    looked_ref, qkv_ref, table, sems = refs[groups:]
    table_rows, qkv_rows = sizes
    half = qkv_rows // 2
    depth = table.shape[1]
    extra = qkv_ref.shape[1] - depth
    place = place_ref[0]
    table_copies, qkv_copies = [], []

    def copy(source, target, number, into):
        made = pltpu.make_async_copy(source, target, sems.at[number])
        made.start()
        into.append(made)

    for n in range(groups):
        g = jnp.bitwise_xor(place, n)
        start = pl.multiple_of(g * table_rows, table_rows)
        copy(
            parts[n].at[pl.ds(0, table_rows)], table.at[pl.ds(start, table_rows)], 4 * n, table_copies
        )
    for n in range(groups):
        g = jnp.bitwise_xor(place, n)
        start = pl.multiple_of(g * qkv_rows, qkv_rows)
        copy(
            parts[n].at[pl.ds(table_rows, qkv_rows)],
            qkv_ref.at[pl.ds(start, qkv_rows), pl.ds(0, depth)],
            4 * n + 1,
            qkv_copies,
        )
        for side in range(2):
            start = pl.multiple_of(g * qkv_rows + side * half, half)
            copy(
                parts[n].at[pl.ds(table_rows + qkv_rows, half), pl.ds(side * extra, extra)],
                qkv_ref.at[pl.ds(start, half), pl.ds(depth, extra)],
                4 * n + 2 + side,
                qkv_copies,
            )
    columns = lax.broadcasted_iota(jnp.int32, (tokens_ref.shape[0], table.shape[0]), 1)
    matches = (tokens_ref[...] == columns).astype(f32).astype(bf16)
    for made in table_copies:
        made.wait()
    looked_ref[...] = jnp.dot(matches, table[...], preferred_element_type=f32).astype(bf16)
    for made in qkv_copies:
        made.wait()


def assemble(place, tokens, parts, table_rows, qkv_rows, wide):
    groups = len(parts)
    frames_here = tokens.shape[0]
    depth = parts[0].shape[1]
    vmem = pl.BlockSpec(memory_space=pltpu.VMEM)
    return pl.pallas_call(
        functools.partial(assemble_kernel, groups, (table_rows, qkv_rows)),
        out_shape=[
            jax.ShapeDtypeStruct((frames_here, depth), bf16),
            jax.ShapeDtypeStruct((groups * qkv_rows, wide), bf16),
        ],
        in_specs=[pl.BlockSpec(memory_space=pltpu.SMEM), vmem]
        + [pl.BlockSpec(memory_space=pl.ANY)] * groups,
        out_specs=[vmem] * 2,
        scratch_shapes=[
            pltpu.VMEM((groups * table_rows, depth), bf16),
            pltpu.SemaphoreType.DMA((4 * groups,)),
        ],
        compiler_params=pltpu.CompilerParams(vmem_limit_bytes=24 * 2**20),
        cost_estimate=pl.CostEstimate(
            flops=2 * frames_here * groups * table_rows * depth,
            bytes_accessed=2 * groups * parts[0].size,
            transcendentals=0,
        ),
        name="lookup_and_qkv_rows",
    )(place, tokens, *parts)


def early_kernel(early, late, place_ref, gain_ref, *refs):
    count = len(early)
    blocks = dict(zip(early, refs[:count]))
    proj, projected_ref, square_ref, later, held, sems = refs[count:]
    place = place_ref[0]
    frames_here, width = refs[0].shape
    depth = proj.shape[1]

    def rows_of(m):
        return pl.ds(pl.multiple_of(jnp.bitwise_xor(place, m) * width, width), width)

    copies = []
    for number, m in enumerate(early):
        made = pltpu.make_async_copy(proj.at[rows_of(m)], held.at[number], sems.at[number])
        made.start()
        copies.append(made)
    for number, m in enumerate(late):
        made = pltpu.make_async_copy(
            proj.at[rows_of(m)], later.at[number], sems.at[count + number]
        )
        made.start()
        copies.append(made)
    square = jnp.zeros((frames_here, 1), f32)
    projected = jnp.zeros((frames_here, depth), f32)
    for number, m in enumerate(early):
        part = blocks[m][...].astype(f32)
        square = square + jnp.sum(part * part, axis=-1, keepdims=True)
        scaled = (part * gain_ref[:, rows_of(m)]).astype(bf16)
        copies[number].wait()
        projected = projected + jnp.dot(scaled, held[number], preferred_element_type=f32)
    projected_ref[...] = projected
    square_ref[...] = square
    for made in copies[count:]:
        made.wait()


def project_early(place, gain, blocks, early, late, proj):
    frames_here, width = blocks[0].shape
    depth = proj.shape[1]
    vmem = pl.BlockSpec(memory_space=pltpu.VMEM)
    return pl.pallas_call(
        functools.partial(early_kernel, early, late),
        out_shape=[
            jax.ShapeDtypeStruct((frames_here, depth), f32),
            jax.ShapeDtypeStruct((frames_here, 1), f32),
            jax.ShapeDtypeStruct((len(late), width, depth), bf16),
        ],
        in_specs=[pl.BlockSpec(memory_space=pltpu.SMEM), vmem]
        + [vmem] * len(early)
        + [pl.BlockSpec(memory_space=pltpu.HBM)],
        out_specs=[vmem] * 3,
        scratch_shapes=[
            pltpu.VMEM((len(early), width, depth), bf16),
            pltpu.SemaphoreType.DMA((len(early) + len(late),)),
        ],
        compiler_params=pltpu.CompilerParams(vmem_limit_bytes=42 * 2**20),
        cost_estimate=pl.CostEstimate(
            flops=2 * frames_here * depth * width * len(early),
            bytes_accessed=2 * proj.size,
            transcendentals=0,
        ),
        name="project_early_blocks",
    )(place, gain, *[blocks[m] for m in early], proj)


def late_kernel(books, late, place_ref, *refs):
    count = len(late)
    blocks = refs[:count]
    later, projected_ref, square_ref, looked_ref, gain_ref, depth_gain_ref, qkv_ref = refs[
        count : count + 7
    ]
    outs = refs[count + 7 : count + 7 + books]
    packed = refs[count + 7 + books]
    place = place_ref[0]
    frames_here, width = blocks[0].shape
    square = square_ref[...]
    projected = projected_ref[...]
    for number, m in enumerate(late):
        start = pl.multiple_of(jnp.bitwise_xor(place, m) * width, width)
        part = blocks[number][...].astype(f32)
        square = square + jnp.sum(part * part, axis=-1, keepdims=True)
        scaled = (part * gain_ref[:, pl.ds(start, width)]).astype(bf16)
        projected = projected + jnp.dot(scaled, later[number], preferred_element_type=f32)
    projected = projected * lax.rsqrt(square / (books * width) + 1e-05)
    depth_in = (projected + looked_ref[...].astype(f32)).astype(bf16).astype(f32)
    moment = jnp.mean(depth_in * depth_in, axis=-1, keepdims=True)
    depth_normed = (depth_in * lax.rsqrt(moment + 1e-05) * depth_gain_ref[...]).astype(bf16)
    packed[...] = jnp.dot(depth_normed, qkv_ref[...], preferred_element_type=f32).astype(bf16)
    rows = frames_here // books
    for m in range(books):
        start = pl.multiple_of(jnp.bitwise_xor(place, m) * rows, rows)
        outs[m][...] = packed[pl.ds(start, rows), :]


def project_late(place, blocks, late, later, projected, square, looked, gain, depth_gain, qkv):
    books = len(blocks)
    frames_here, width = blocks[0].shape
    depth, wide = qkv.shape
    vmem = pl.BlockSpec(memory_space=pltpu.VMEM)
    return pl.pallas_call(
        functools.partial(late_kernel, books, late),
        out_shape=[jax.ShapeDtypeStruct((frames_here // books, wide), bf16)] * books,
        in_specs=[pl.BlockSpec(memory_space=pltpu.SMEM)] + [vmem] * (len(late) + 7),
        out_specs=[vmem] * books,
        scratch_shapes=[pltpu.VMEM((frames_here, wide), bf16)],
        compiler_params=pltpu.CompilerParams(vmem_limit_bytes=32 * 2**20),
        cost_estimate=pl.CostEstimate(
            flops=2 * frames_here * depth * (width * len(late) + wide),
            bytes_accessed=2 * qkv.size,
            transcendentals=0,
        ),
        name="project_late_blocks_and_qkv",
    )(
        place,
        *[blocks[m] for m in late],
        later,
        projected,
        square,
        looked,
        gain,
        depth_gain,
        qkv,
    )


def attend_kernel(books, place_ref, *refs):
    arrived = refs[:books]
    out_ref, inner = refs[books:]
    place = place_ref[0]
    rows, wide = arrived[0].shape
    width = wide // 3
    for m in range(books):
        inner[jnp.bitwise_xor(place, m)] = arrived[m][...]
    head_of_row = lax.broadcasted_iota(jnp.int32, (width, width), 0) // HD
    head_of_column = lax.broadcasted_iota(jnp.int32, (width, width), 1) // HD
    same_head = (head_of_row == head_of_column).astype(f32).astype(bf16)
    keys_all = [inner[j, :, width : 2 * width].astype(f32) for j in range(books)]
    values_all = [inner[j, :, 2 * width :].astype(f32) for j in range(books)]
    contexts = []
    for k in range(books):
        query = inner[k, :, :width].astype(f32) * HD ** (-0.5)
        products = jnp.concatenate([query * keys_all[j] for j in range(k + 1)], axis=0)
        high = products.astype(bf16)
        low = (products - high.astype(f32)).astype(bf16)
        scores = jnp.dot(high, same_head, preferred_element_type=f32) + jnp.dot(
            low, same_head, preferred_element_type=f32
        )
        scores = [scores[j * rows : (j + 1) * rows] for j in range(k + 1)]
        peak = functools.reduce(jnp.maximum, scores)
        expo = [jnp.exp(score - peak) for score in scores]
        total = functools.reduce(jnp.add, expo)
        context = 0.0
        for j in range(k + 1):
            probability = (expo[j] / total).astype(bf16).astype(f32)
            context = context + probability * values_all[j]
        contexts.append(context)
    out_ref[...] = jnp.stack(contexts, axis=1).astype(bf16)


def attend(place, arrived):
    books = len(arrived)
    rows, wide = arrived[0].shape
    vmem = pl.BlockSpec(memory_space=pltpu.VMEM)
    return pl.pallas_call(
        functools.partial(attend_kernel, books),
        out_shape=jax.ShapeDtypeStruct((rows, books, wide // 3), bf16),
        in_specs=[pl.BlockSpec(memory_space=pltpu.SMEM)] + [vmem] * books,
        out_specs=vmem,
        scratch_shapes=[pltpu.VMEM((books, rows, wide), bf16)],
        compiler_params=pltpu.CompilerParams(vmem_limit_bytes=32 * 2**20),
        name="attend_books",
    )(place, *arrived)


def swap(value, axis, distance):
    return lax.ppermute(value, axis, [(i, i ^ distance) for i in range(lax.axis_size(axis))])


def after(value, *others):
    return lax.optimization_barrier((value, *others))[0]


def per_device(
    gate_pre,
    up_pre,
    down_weight,
    residual,
    out_gain,
    in_proj,
    embedding,
    token_ids,
    depth_gain,
    qkv_weight,
):
    books = lax.axis_size("book")
    groups = lax.axis_size("frames")
    here = lax.axis_index("book").astype(jnp.int32)
    place = here[None]
    width = residual.shape[1]
    depth = in_proj.shape[2]
    wide = qkv_weight.shape[2]
    table_rows = embedding.shape[1]
    qkv_rows = qkv_weight.shape[1]
    gain = out_gain.astype(f32)[None]

    proj = lax.all_gather(in_proj[0], "frames", axis=0, tiled=True)

    hidden = (jax.nn.silu(gate_pre.astype(f32)) * up_pre.astype(f32)).astype(bf16)

    def share(m, *others):
        start = jnp.bitwise_xor(here, m) * width
        block = lax.dynamic_slice_in_dim(down_weight, start, width, 1)
        factor = after(hidden, *others) if others else hidden
        return jnp.dot(factor, block, preferred_element_type=f32)

    sums = {books - 1: share(books - 1)}
    first = sums[books - 1].astype(bf16)

    table_mine, qkv_mine = after((embedding[0], qkv_weight[0]), first)
    beyond = qkv_mine[:, depth:]
    rows = jnp.concatenate(
        [
            table_mine,
            qkv_mine[:, :depth],
            jnp.concatenate([beyond[: qkv_rows // 2], beyond[qkv_rows // 2 :]], axis=1),
        ],
        axis=0,
    )
    parts = {0: rows}
    for n in range(2, groups, 2):
        parts[n] = swap(rows, "frames", n)

    sums[books - 2] = lax.optimization_barrier(share(books - 2, rows))
    distance = 1
    while distance < books:
        came = None
        for m in range(books - distance, 0, -2 * distance):
            going = sums.pop(m).astype(bf16)
            if came is not None:
                going = after(going, came)
            came = swap(going, "book", distance)
            if m == books - 1:
                for n in range(books - 3, -1, -1):
                    sums[n] = lax.optimization_barrier(share(n, came))
                sums[0] = sums[0] + residual.astype(f32)
            sums[m ^ distance] = sums[m ^ distance] + came.astype(f32)
        distance *= 2

    blocks = {0: sums[0].astype(bf16)}
    distance = books // 2
    while distance:
        for m in sorted(blocks):
            going = blocks[m] if m == 0 else after(blocks[m], blocks[distance])
            blocks[m ^ distance] = swap(going, "book", distance)
        distance //= 2

    for n in range(0, groups, 2):
        parts[n + 1] = swap(after(parts[n], blocks[0]), "frames", 1)
    looked, qkv = assemble(
        lax.axis_index("frames").astype(jnp.int32)[None],
        token_ids,
        [parts[n] for n in range(groups)],
        table_rows,
        qkv_rows,
        wide,
    )

    early = [m for m in range(books) if m % 2 == 0 or m == 1]
    late = [m for m in range(books) if m not in early]
    projected, square, later = project_early(place, gain, blocks, early, late, proj)
    packed = project_late(
        place,
        blocks,
        late,
        later,
        projected,
        square,
        looked,
        gain,
        depth_gain.astype(f32),
        qkv,
    )
    far = {m: swap(packed[m], "book", m) for m in range(books - 1, 0, -1)}
    return attend(place, [packed[0]] + [far[m] for m in range(1, books)])


def solution(mesh):
    in_specs = (
        P("frames", "book"),
        P("frames", "book"),
        P("book", None),
        P("frames", "book"),
        P(),
        P("book", "frames", None),
        P("book", "frames", None),
        P("frames", "book"),
        P("book", None),
        P("book", "frames", None),
    )
    out_specs = P(("frames", "book"), None, None)
    return jax.shard_map(
        per_device, mesh=mesh, in_specs=in_specs, out_specs=out_specs, check_vma=False
    )
```

time: 127 us -> 142 us (1.12)
  local copies, waits for them, and re-layouts: 2.13 us -> 13.6 us
  starting transfers between devices: 29.7 us -> 19.1 us
  waiting for transfers between devices: 55.4 us -> 63.7 us
  Pallas kernels: 9.29 us -> 12.8 us
    unnamed x13 -> x45, local copies, waits for them, and re-layouts: 0.16 us -> 13.5 us
    ppermute x9 -> x16, starting transfers between devices: 29.7 us -> 19.1 us  [swap(): lax.ppermute(value, axis, [(i, i ^ distance) for i in range(lax.axis_size...]
    ppermute x9 -> x16, waiting for transfers between devices: 54.2 us -> 63 us  [swap(): lax.ppermute(value, axis, [(i, i ^ distance) for i in range(lax.axis_size...]
    pallas_call x1 -> x3, Pallas kernels: 7.04 us -> 10.5 us  [the longest x1 5.3 us: project_early(): pl.pallas_call(functools.partial(early_kernel, early, late), out_shape=[j...]
    concatenate x1, other arithmetic: 2.65 us -> 0.05 us  [per_device(): jnp.concatenate([table_mine, qkv_mine[:, :depth], jnp.concatenate([beyond...]
  transfers between devices with their start and end apart: 10 -> 17, of which waited for: 9 -> 8; matrix products, arithmetic and copies ran while one was open for 11% -> 13% of each run, Pallas kernels for 0% -> 5%
where the time goes in v3:
time: 142 us; the launch traced here: 141 us
  waiting for transfers between devices  63.7 us (45%)
  starting transfers between devices  19.1 us (13%)
  local copies, waits for them, and re-layouts  13.6 us (10%)
  between operations  13.6 us (10%)
  matrix products  13.4 us (9%)
  Pallas kernels  12.8 us (9%)
  other arithmetic  4.42 us (3%)
    ppermute x16, waiting for transfers between devices, swap(): lax.ppermute(value, axis, [(i, i ^ distance) for i in range(lax.axis_size...  63 us
    ppermute x16, starting transfers between devices, swap(): lax.ppermute(value, axis, [(i, i ^ distance) for i in range(lax.axis_size...  19.1 us
    unnamed x45, local copies, waits for them, and re-layouts  13.5 us
    dot_general x4, matrix products, share(): return jnp.dot(factor, block, preferred_element_type=f32)  13.4 us
    pallas_call x1, Pallas kernels, project_early(): pl.pallas_call(functools.partial(early_kernel, early, late), out_shape=[j...  5.3 us
    pallas_call x1, Pallas kernels, project_late(): pl.pallas_call(functools.partial(late_kernel, books, late), out_shape=[ja...  3.02 us
  transfers between devices with their start and end apart: 17, of which 8 were waited for; matrix products, arithmetic and copies ran while one was open for 13% of the time, Pallas kernels for 5%

profile of v3, /device:TPU:0, one launch (start us, length us, event | category | flops | bytes accessed | tf_op | source)
XLA Modules:
  0.0 140.6 jit_solution(4493257026253666835)
XLA Ops:
  7.3 1.9 %fusion.12 = bf16[256,1536]{1,0:T(8,128)(2,1)S(1)} fusion(bf16[256,1536]{1,0:T(8,128)(2,1)} %param.11, bf16[256,1536]{1,0:T(8,128)(2,1)} %param.10), kind=kLoop, calls=%fused_computation.14 | loop fusion | flops 3145728 | bytes 2359296 | tf_op jit(solution)/shard_map/convert_element_type | solution.py:297
  9.1 3.7 %fusion.13 = bf16[256,1024]{1,0:T(8,128)(2,1)} fusion(bf16[256,1536]{1,0:T(8,128)(2,1)S(1)} %fusion.12, bf16[1536,4096]{1,0:T(8,128)(2,1)} %param.12, s32[]{:T(128)S(6)} %select_n.12), kind=kOutput, calls=%fused_computation.15 | convolution fusion | flops 805568512 | bytes 4456452 | tf_op jit(solution)/shard_map/dot_general | solution.py:303
  12.9 3.0 %collective-permute-start = (bf16[256,1024]{1,0:T(8,128)(2,1)}, bf16[256,1024]{1,0:T(8,128)(2,1)S(1)}, u32[]{:S(2)}, u32[]{:S(2)}) collective-permute-start(bf16[256,1024]{1,0:T(8,128)(2,1)} %fusion.13), channel_id=1, source_target_pairs={{0,1},{1,0},{2,3},{3,2},{4,5},{5,4},{6,7},{7,6},{8,9},{9,8},{10,11... | collective-permute-start | bytes 1572872 | tf_op jit(solution)/shard_map/ppermute | solution.py:265
  16.0 3.1 %fusion = f32[256,1024]{1,0:T(8,128)S(1)} fusion(bf16[256,1536]{1,0:T(8,128)(2,1)S(1)} %fusion.12, bf16[1536,4096]{1,0:T(8,128)(2,1)} %param.12, s32[]{:T(128)S(6)} %select_n.15), kind=kOutput, calls=%fused_computation | convolution fusion | flops 805306368 | bytes 4980740 | tf_op jit(solution)/shard_map/dot_general | solution.py:303
  19.2 8.9 %collective-permute-done = bf16[256,1024]{1,0:T(8,128)(2,1)S(1)} collective-permute-done((bf16[256,1024]{1,0:T(8,128)(2,1)}, bf16[256,1024]{1,0:T(8,128)(2,1)S(1)}, u32[]{:S(2)}, u32[]{:S(2)}) %collective-permute-start) | collective-permute-done | bytes 524320 | tf_op jit(solution)/shard_map/ppermute | solution.py:265
  29.0 2.8 %collective-permute-start.2 = (bf16[256,1024]{1,0:T(8,128)(2,1)}, bf16[256,1024]{1,0:T(8,128)(2,1)}, u32[]{:S(2)}, u32[]{:S(2)}) collective-permute-start(bf16[256,1024]{1,0:T(8,128)(2,1)} %add_convert_fusion.1), channel_id=1, source_target_pairs={{0,2},{1,3},{2,0},{3,1},{4,6},{5,7},{6,4},{7,5},{8,10},{9,11},{10,... | collective-permute-start | bytes 1572872 | tf_op jit(solution)/shard_map/ppermute | solution.py:265
  31.8 3.7 %fusion.2 = bf16[256,1024]{1,0:T(8,128)(2,1)} fusion(bf16[256,1536]{1,0:T(8,128)(2,1)S(1)} %fusion.12, bf16[1536,4096]{1,0:T(8,128)(2,1)} %param.12, s32[]{:T(128)S(6)} %select_n.14), kind=kOutput, calls=%fused_computation.2 | convolution fusion | flops 805306368 | bytes 4456452 | tf_op jit(solution)/shard_map/dot_general | solution.py:303
  35.4 1.6 %collective-permute-start.1 = (bf16[256,1024]{1,0:T(8,128)(2,1)}, bf16[256,1024]{1,0:T(8,128)(2,1)}, u32[]{:S(2)}, u32[]{:S(2)}) collective-permute-start(bf16[256,1024]{1,0:T(8,128)(2,1)} %fusion.2), channel_id=1, source_target_pairs={{0,1},{1,0},{2,3},{3,2},{4,5},{5,4},{6,7},{7,6},{8,9},{9,8},{10,11... | collective-permute-start | bytes 1572872 | tf_op jit(solution)/shard_map/ppermute | solution.py:265
  40.5 2.9 %fusion.4 = f32[256,1024]{1,0:T(8,128)S(1)} fusion(bf16[256,1536]{1,0:T(8,128)(2,1)S(1)} %fusion.12, bf16[1536,4096]{1,0:T(8,128)(2,1)} %param.12, s32[]{:T(128)S(6)} %select_n.13), kind=kOutput, calls=%fused_computation.4 | convolution fusion | flops 805306368 | bytes 4980740 | tf_op jit(solution)/shard_map/dot_general | solution.py:303
  43.4 11.3 %collective-permute-done.2 = bf16[256,1024]{1,0:T(8,128)(2,1)} collective-permute-done((bf16[256,1024]{1,0:T(8,128)(2,1)}, bf16[256,1024]{1,0:T(8,128)(2,1)}, u32[]{:S(2)}, u32[]{:S(2)}) %collective-permute-start.2) | collective-permute-done | bytes 524320 | tf_op jit(solution)/shard_map/ppermute | solution.py:265
  54.8 3.9 %collective-permute-done.1 = bf16[256,1024]{1,0:T(8,128)(2,1)} collective-permute-done((bf16[256,1024]{1,0:T(8,128)(2,1)}, bf16[256,1024]{1,0:T(8,128)(2,1)}, u32[]{:S(2)}, u32[]{:S(2)}) %collective-permute-start.1) | collective-permute-done | bytes 524320 | tf_op jit(solution)/shard_map/ppermute | solution.py:265
  58.6 1.5 %add_convert_fusion.refs_0_ = bf16[256,1024]{1,0:T(8,128)(2,1)S(1)} fusion(bf16[256,1024]{1,0:T(8,128)(2,1)} %collective-permute-done.2, bf16[256,1024]{1,0:T(8,128)(2,1)} %collective-permute-done.1, f32[256,1024]{1,0:T(8,128)S(1)} %fusion.4, bf16[256,1024]{1,0:T(8,128)(2,1)S(1)} %copy-done.16), kind=kLoop, calls=%fused_computation.16 | loop fusion | flops 1835008 | bytes 3145728 | tf_op jit(solution)/shard_map/convert_element_type | solution.py:338
  60.5 2.5 %collective-permute-start.4 = (bf16[256,1024]{1,0:T(8,128)(2,1)S(1)}, bf16[256,1024]{1,0:T(8,128)(2,1)S(1)}, u32[]{:S(2)}, u32[]{:S(2)}) collective-permute-start(bf16[256,1024]{1,0:T(8,128)(2,1)S(1)} %add_convert_fusion.refs_0_), channel_id=1, source_target_pairs={{0,1},{1,0},{2,3},{3,2},{4,5},{5,4},{6,7},{7,6},{8,9},{9,8},{10,11... | collective-permute-start | bytes 1572872 | tf_op jit(solution)/shard_map/ppermute | solution.py:265
  63.8 3.8 %collective-permute-done.7.refs_2_ = bf16[320,1024]{1,0:T(8,128)(2,1)S(1)} collective-permute-done((bf16[320,1024]{1,0:T(8,128)(2,1)S(1)}, bf16[320,1024]{1,0:T(8,128)(2,1)S(1)}, u32[]{:S(2)}, u32[]{:S(2)}) %collective-permute-start.7) | collective-permute-done | bytes 655392 | tf_op jit(solution)/shard_map/ppermute | solution.py:265
  67.6 4.5 %collective-permute-done.9.refs_4_ = bf16[320,1024]{1,0:T(8,128)(2,1)S(1)} collective-permute-done((bf16[320,1024]{1,0:T(8,128)(2,1)S(1)}, bf16[320,1024]{1,0:T(8,128)(2,1)S(1)}, u32[]{:S(2)}, u32[]{:S(2)}) %collective-permute-start.9) | collective-permute-done | bytes 655392 | tf_op jit(solution)/shard_map/ppermute | solution.py:265
  73.0 16.7 %collective-permute-done.11.refs_6_ = bf16[320,1024]{1,0:T(8,128)(2,1)S(1)} collective-permute-done((bf16[320,1024]{1,0:T(8,128)(2,1)S(1)}, bf16[320,1024]{1,0:T(8,128)(2,1)S(1)}, u32[]{:S(2)}, u32[]{:S(2)}) %collective-permute-start.11) | collective-permute-done | bytes 655392 | tf_op jit(solution)/shard_map/ppermute | solution.py:265
  99.7 2.2 %lookup_and_qkv_rows.1 = (bf16[256,1024]{1,0:T(8,128)(2,1)S(1)}, bf16[1024,1536]{1,0:T(8,128)(2,1)S(1)}) custom-call(s32[1]{0:T(128)} %bitcast.5.place_ref, s32[256,1]{1,0:T(8,128)S(1)} %copy.11.tokens_ref, bf16[320,1024]{1,0:T(8,128)(2,1)S(1)} %copy-done.1, bf16[320,1024]{1,0:T(8,128)(2,1)S(1)} %copy-done.11, bf16[320,1024]{1,0:T(8,128)(2,1)S(1)} %copy-done.5, ...), custom_call_target="tpu_custom_call" | custom-call | flops 536870912 | bytes 5242880 | tf_op jit(solution)/shard_map/lookup_and_qkv_rows/pallas_call | solution.py:67
  104.9 5.3 %project_early_blocks.1 = (f32[256,1024]{1,0:T(8,128)S(1)}, f32[256,1]{1,0:T(8,128)S(1)}, bf16[1,1024,1024]{2,1,0:T(8,128)(2,1)S(1)}) custom-call(s32[1]{0:T(128)} %bitcast.place_ref, f32[1,4096]{1,0:T(1,128)S(1)} %bitcast.10, bf16[256,1024]{1,0:T(8,128)(2,1)S(1)} %copy-done.3, bf16[256,1024]{1,0:T(8,128)(2,1)S(1)} %copy-done.13, ...), custom_call_target="tpu_custom_call" | custom-call | flops 1610612736 | bytes 8388608 | tf_op jit(solution)/shard_map/project_early_blocks/pallas_call | solution.py:130
  110.2 3.0 %project_late_blocks_and_qkv.1 = (bf16[64,1536]{1,0:T(8,128)(2,1)S(1)}, bf16[64,1536]{1,0:T(8,128)(2,1)S(1)}, bf16[64,1536]{1,0:T(8,128)(2,1)S(1)}, bf16[64,1536]{1,0:T(8,128)(2,1)S(1)}) custom-call(s32[1]{0:T(128)} %bitcast.place_ref, bf16[256,1024]{1,0:T(8,128)(2,1)} %collective-permute-done.5.refs_0_, ...), custom_call_target="tpu_custom_call" | custom-call | flops 1342177280 | bytes 3145728 | tf_op jit(solution)/shard_map/project_late_blocks_and_qkv/pallas_call | solution.py:189
  113.2 1.6 %collective-permute-start.13 = (bf16[64,1536]{1,0:T(8,128)(2,1)S(1)}, bf16[64,1536]{1,0:T(8,128)(2,1)S(1)}, u32[]{:S(2)}, u32[]{:S(2)}) collective-permute-start(bf16[64,1536]{1,0:T(8,128)(2,1)S(1)} %get-tuple-element.40), channel_id=1, source_target_pairs={{0,1},{1,0},{2,3},{3,2},{4,5},{5,4},{6,7},{7,6},{8,9},{9,8},{10,11... | collective-permute-start | bytes 589832 | tf_op jit(solution)/shard_map/ppermute | solution.py:265
  115.2 2.4 %collective-permute-start.15 = (bf16[64,1536]{1,0:T(8,128)(2,1)S(1)}, bf16[64,1536]{1,0:T(8,128)(2,1)S(1)}, u32[]{:S(2)}, u32[]{:S(2)}) collective-permute-start(bf16[64,1536]{1,0:T(8,128)(2,1)S(1)} %get-tuple-element.42), channel_id=1, source_target_pairs={{0,3},{1,2},{2,1},{3,0},{4,7},{5,6},{6,5},{7,4},{8,11},{9,10},{10,... | collective-permute-start | bytes 589832 | tf_op jit(solution)/shard_map/ppermute | solution.py:265
  117.7 4.0 %collective-permute-done.13.refs_1_ = bf16[64,1536]{1,0:T(8,128)(2,1)S(1)} collective-permute-done((bf16[64,1536]{1,0:T(8,128)(2,1)S(1)}, bf16[64,1536]{1,0:T(8,128)(2,1)S(1)}, u32[]{:S(2)}, u32[]{:S(2)}) %collective-permute-start.13) | collective-permute-done | bytes 196640 | tf_op jit(solution)/shard_map/ppermute | solution.py:265
  121.7 9.8 %collective-permute-done.14.refs_2_ = bf16[64,1536]{1,0:T(8,128)(2,1)S(1)} collective-permute-done((bf16[64,1536]{1,0:T(8,128)(2,1)S(1)}, bf16[64,1536]{1,0:T(8,128)(2,1)S(1)}, u32[]{:S(2)}, u32[]{:S(2)}) %collective-permute-start.14) | collective-permute-done | bytes 196640 | tf_op jit(solution)/shard_map/ppermute | solution.py:265
  131.5 2.2 %attend_books.1 = bf16[64,4,512]{2,1,0:T(4,128)(2,1)} custom-call(s32[1]{0:T(128)} %bitcast.place_ref, bf16[64,1536]{1,0:T(8,128)(2,1)S(1)} %get-tuple-element.39.refs_0_, bf16[64,1536]{1,0:T(8,128)(2,1)S(1)} %collective-permute-done.13.refs_1_, bf16[64,1536]{1,0:T(8,128)(2,1)S(1)} %collective-permute-done.14.refs_2_, ...), custom_call_target="tpu_custom_call" | custom-call | tf_op jit(solution)/shard_map/attend_books/pallas_call | solution.py:253
  (72 shorter events, 20.5 us)
Async XLA Ops:
  6.5 96.2 %all-gather.3.cloned.1.call-start = ((), (), s32[]{:S(2)}) async-start(), calls=%async_computation | async-start | bytes 9437184 | tf_op jit(solution)/shard_map/all_gather | solution.py:295
  9.1 6.8 %copy-start.17 = (bf16[1,128,1536]{2,1,0:T(8,128)(2,1)S(1)}, bf16[1,128,1536]{2,1,0:T(8,128)(2,1)}, u32[]{:S(2)}) copy-start(bf16[1,128,1536]{2,1,0:T(8,128)(2,1)} %param.19) | copy-start | bytes 1179652
  9.1 6.8 %copy-start.18 = (bf16[1,128,1024]{2,1,0:T(8,128)(2,1)S(1)}, bf16[1,128,1024]{2,1,0:T(8,128)(2,1)}, u32[]{:S(2)}) copy-start(bf16[1,128,1024]{2,1,0:T(8,128)(2,1)} %param.16) | copy-start | bytes 786436
  12.9 15.2 %collective-permute-start = (bf16[256,1024]{1,0:T(8,128)(2,1)}, bf16[256,1024]{1,0:T(8,128)(2,1)S(1)}, u32[]{:S(2)}, u32[]{:S(2)}) collective-permute-start(bf16[256,1024]{1,0:T(8,128)(2,1)} %fusion.13), channel_id=1, source_target_pairs={{0,1},{1,0},{2,3},{3,2},{4,5},{5,4},{6,7},{7,6},{8,9},{9,8},{10,11... | collective-permute-start | bytes 1572872 | tf_op jit(solution)/shard_map/ppermute | solution.py:265
  16.0 51.6 %copy-start = (bf16[320,1024]{1,0:T(8,128)(2,1)}, bf16[320,1024]{1,0:T(8,128)(2,1)S(1)}, u32[]{:S(2)}) copy-start(bf16[320,1024]{1,0:T(8,128)(2,1)S(1)} %maximum_maximum_fusion.refs_0_) | copy-start | bytes 1966084
  29.0 25.8 %collective-permute-start.2 = (bf16[256,1024]{1,0:T(8,128)(2,1)}, bf16[256,1024]{1,0:T(8,128)(2,1)}, u32[]{:S(2)}, u32[]{:S(2)}) collective-permute-start(bf16[256,1024]{1,0:T(8,128)(2,1)} %add_convert_fusion.1), channel_id=1, source_target_pairs={{0,2},{1,3},{2,0},{3,1},{4,6},{5,7},{6,4},{7,5},{8,10},{9,11},{10,... | collective-permute-start | bytes 1572872 | tf_op jit(solution)/shard_map/ppermute | solution.py:265
  35.4 23.2 %collective-permute-start.1 = (bf16[256,1024]{1,0:T(8,128)(2,1)}, bf16[256,1024]{1,0:T(8,128)(2,1)}, u32[]{:S(2)}, u32[]{:S(2)}) collective-permute-start(bf16[256,1024]{1,0:T(8,128)(2,1)} %fusion.2), channel_id=1, source_target_pairs={{0,1},{1,0},{2,3},{3,2},{4,5},{5,4},{6,7},{7,6},{8,9},{9,8},{10,11... | collective-permute-start | bytes 1572872 | tf_op jit(solution)/shard_map/ppermute | solution.py:265
  37.0 30.6 %collective-permute-start.7 = (bf16[320,1024]{1,0:T(8,128)(2,1)S(1)}, bf16[320,1024]{1,0:T(8,128)(2,1)S(1)}, u32[]{:S(2)}, u32[]{:S(2)}) collective-permute-start(bf16[320,1024]{1,0:T(8,128)(2,1)S(1)} %maximum_maximum_fusion.refs_0_), channel_id=1, source_target_pairs={{0,8},{4,12},{8,0},{12,4},{16,24},{20,28},{24,16},{28,20},{1,9},{5... | collective-permute-start | bytes 1966088 | tf_op jit(solution)/shard_map/ppermute | solution.py:265
  38.5 33.7 %collective-permute-start.9 = (bf16[320,1024]{1,0:T(8,128)(2,1)S(1)}, bf16[320,1024]{1,0:T(8,128)(2,1)S(1)}, u32[]{:S(2)}, u32[]{:S(2)}) collective-permute-start(bf16[320,1024]{1,0:T(8,128)(2,1)S(1)} %maximum_maximum_fusion.refs_0_), channel_id=1, source_target_pairs={{0,16},{4,20},{8,24},{12,28},{16,0},{20,4},{24,8},{28,12},{1,17},{... | collective-permute-start | bytes 1966088 | tf_op jit(solution)/shard_map/ppermute | solution.py:265
  40.0 49.7 %collective-permute-start.11 = (bf16[320,1024]{1,0:T(8,128)(2,1)S(1)}, bf16[320,1024]{1,0:T(8,128)(2,1)S(1)}, u32[]{:S(2)}, u32[]{:S(2)}) collective-permute-start(bf16[320,1024]{1,0:T(8,128)(2,1)S(1)} %maximum_maximum_fusion.refs_0_), channel_id=1, source_target_pairs={{0,24},{4,28},{8,16},{12,20},{16,8},{20,12},{24,0},{28,4},{1,25},{... | collective-permute-start | bytes 1966088 | tf_op jit(solution)/shard_map/ppermute | solution.py:265
  40.5 18.1 %copy-start.16 = (bf16[256,1024]{1,0:T(8,128)(2,1)S(1)}, bf16[256,1024]{1,0:T(8,128)(2,1)}, u32[]{:S(2)}) copy-start(bf16[256,1024]{1,0:T(8,128)(2,1)} %param.13) | copy-start | bytes 1572868
  40.5 52.7 %copy-start.19 = (bf16[4096]{0:T(1024)(128)(2,1)S(1)}, bf16[4096]{0:T(1024)(128)(2,1)}, u32[]{:S(2)}) copy-start(bf16[4096]{0:T(1024)(128)(2,1)} %param.14) | copy-start | bytes 24580
  40.5 52.7 %copy-start.21 = (s32[256,1]{0,1:T(1,128)S(1)}, s32[256,1]{0,1:T(1,128)}, u32[]{:S(2)}) copy-start(s32[256,1]{0,1:T(1,128)} %param.17) | copy-start | bytes 3076
  40.5 52.9 %copy-start.20 = (bf16[1,1024]{1,0:T(2,128)(2,1)S(1)}, bf16[1,1024]{1,0:T(2,128)(2,1)}, u32[]{:S(2)}) copy-start(bf16[1,1024]{1,0:T(2,128)(2,1)} %param.18) | copy-start | bytes 6148
  60.2 30.4 %collective-permute-start.3 = (bf16[256,1024]{1,0:T(8,128)(2,1)S(1)}, bf16[256,1024]{1,0:T(8,128)(2,1)}, u32[]{:S(2)}, u32[]{:S(2)}) collective-permute-start(bf16[256,1024]{1,0:T(8,128)(2,1)S(1)} %add_convert_fusion.refs_0_), channel_id=1, source_target_pairs={{0,2},{1,3},{2,0},{3,1},{4,6},{5,7},{6,4},{7,5},{8,10},{9,11},{10,... | collective-permute-start | bytes 1572872 | tf_op jit(solution)/shard_map/ppermute | solution.py:265
  60.5 31.4 %collective-permute-start.4 = (bf16[256,1024]{1,0:T(8,128)(2,1)S(1)}, bf16[256,1024]{1,0:T(8,128)(2,1)S(1)}, u32[]{:S(2)}, u32[]{:S(2)}) collective-permute-start(bf16[256,1024]{1,0:T(8,128)(2,1)S(1)} %add_convert_fusion.refs_0_), channel_id=1, source_target_pairs={{0,1},{1,0},{2,3},{3,2},{4,5},{5,4},{6,7},{7,6},{8,9},{9,8},{10,11... | collective-permute-start | bytes 1572872 | tf_op jit(solution)/shard_map/ppermute | solution.py:265
  67.6 25.8 %collective-permute-start.6 = (bf16[320,1024]{1,0:T(8,128)(2,1)S(1)}, bf16[320,1024]{1,0:T(8,128)(2,1)S(1)}, u32[]{:S(2)}, u32[]{:S(2)}) collective-permute-start(bf16[320,1024]{1,0:T(8,128)(2,1)S(1)} %maximum_maximum_fusion.refs_0_), channel_id=1, source_target_pairs={{0,4},{4,0},{8,12},{12,8},{16,20},{20,16},{24,28},{28,24},{1,5},{5... | collective-permute-start | bytes 1966088 | tf_op jit(solution)/shard_map/ppermute | solution.py:265
  72.2 22.1 %collective-permute-start.8 = (bf16[320,1024]{1,0:T(8,128)(2,1)S(1)}, bf16[320,1024]{1,0:T(8,128)(2,1)}, u32[]{:S(2)}, u32[]{:S(2)}) collective-permute-start(bf16[320,1024]{1,0:T(8,128)(2,1)S(1)} %collective-permute-done.7.refs_2_), channel_id=1, source_target_pairs={{0,4},{4,0},{8,12},{12,8},{16,20},{20,16},{24,28},{28,24},{1,5},{5... | collective-permute-start | bytes 1966088 | tf_op jit(solution)/shard_map/ppermute | solution.py:265
  89.7 4.6 %collective-permute-start.10 = (bf16[320,1024]{1,0:T(8,128)(2,1)S(1)}, bf16[320,1024]{1,0:T(8,128)(2,1)}, u32[]{:S(2)}, u32[]{:S(2)}) collective-permute-start(bf16[320,1024]{1,0:T(8,128)(2,1)S(1)} %collective-permute-done.9.refs_4_), channel_id=1, source_target_pairs={{0,4},{4,0},{8,12},{12,8},{16,20},{20,16},{24,28},{28,24},{1,5},{5... | collective-permute-start | bytes 1966088 | tf_op jit(solution)/shard_map/ppermute | solution.py:265
  90.5 3.7 %collective-permute-start.12 = (bf16[320,1024]{1,0:T(8,128)(2,1)S(1)}, bf16[320,1024]{1,0:T(8,128)(2,1)}, u32[]{:S(2)}, u32[]{:S(2)}) collective-permute-start(bf16[320,1024]{1,0:T(8,128)(2,1)S(1)} %collective-permute-done.11.refs_6_), channel_id=1, source_target_pairs={{0,4},{4,0},{8,12},{12,8},{16,20},{20,16},{24,28},{28,24},{1,5},{5... | collective-permute-start | bytes 1966088 | tf_op jit(solution)/shard_map/ppermute | solution.py:265
  92.8 17.4 %collective-permute-start.5 = (bf16[256,1024]{1,0:T(8,128)(2,1)}, bf16[256,1024]{1,0:T(8,128)(2,1)}, u32[]{:S(2)}, u32[]{:S(2)}) collective-permute-start(bf16[256,1024]{1,0:T(8,128)(2,1)} %collective-permute-done.3.refs_2_), channel_id=1, source_target_pairs={{0,1},{1,0},{2,3},{3,2},{4,5},{5,4},{6,7},{7,6},{8,9},{9,8},{10,11... | collective-permute-start | bytes 1572872 | tf_op jit(solution)/shard_map/ppermute | solution.py:265
  113.2 8.5 %collective-permute-start.13 = (bf16[64,1536]{1,0:T(8,128)(2,1)S(1)}, bf16[64,1536]{1,0:T(8,128)(2,1)S(1)}, u32[]{:S(2)}, u32[]{:S(2)}) collective-permute-start(bf16[64,1536]{1,0:T(8,128)(2,1)S(1)} %get-tuple-element.40), channel_id=1, source_target_pairs={{0,1},{1,0},{2,3},{3,2},{4,5},{5,4},{6,7},{7,6},{8,9},{9,8},{10,11... | collective-permute-start | bytes 589832 | tf_op jit(solution)/shard_map/ppermute | solution.py:265
  114.8 16.7 %collective-permute-start.14 = (bf16[64,1536]{1,0:T(8,128)(2,1)S(1)}, bf16[64,1536]{1,0:T(8,128)(2,1)S(1)}, u32[]{:S(2)}, u32[]{:S(2)}) collective-permute-start(bf16[64,1536]{1,0:T(8,128)(2,1)S(1)} %get-tuple-element.41), channel_id=1, source_target_pairs={{0,2},{1,3},{2,0},{3,1},{4,6},{5,7},{6,4},{7,5},{8,10},{9,11},{10,... | collective-permute-start | bytes 589832 | tf_op jit(solution)/shard_map/ppermute | solution.py:265
  115.2 16.3 %collective-permute-start.15 = (bf16[64,1536]{1,0:T(8,128)(2,1)S(1)}, bf16[64,1536]{1,0:T(8,128)(2,1)S(1)}, u32[]{:S(2)}, u32[]{:S(2)}) collective-permute-start(bf16[64,1536]{1,0:T(8,128)(2,1)S(1)} %get-tuple-element.42), channel_id=1, source_target_pairs={{0,3},{1,2},{2,1},{3,0},{4,7},{5,6},{6,5},{7,4},{8,11},{9,10},{10,... | collective-permute-start | bytes 589832 | tf_op jit(solution)/shard_map/ppermute | solution.py:265
  (15 other events, 18.7 us)
Sparse Core Ops, SparseCore 0:
  9.2 83.7 all-gather.2

commit v4 on v3

v4 whole, which is shorter than its diff:
```python
import functools

import jax
import jax.numpy as jnp
from jax import lax
from jax.experimental import pallas as pl
from jax.experimental.pallas import tpu as pltpu
from jax.sharding import PartitionSpec as P

H = 8
HD = 64
f32, bf16 = jnp.float32, jnp.bfloat16


def pack_kernel(proj_ref, table_ref, qkv_ref, packed_ref, sems):
    proj_rows, depth = proj_ref.shape
    table_rows = table_ref.shape[0]
    qkv_rows, wide = qkv_ref.shape
    half, extra = qkv_rows // 2, wide - depth
    at_qkv = proj_rows + table_rows
    at_extra = at_qkv + qkv_rows
    moves = [
        (proj_ref, packed_ref.at[pl.ds(0, proj_rows)]),
        (table_ref, packed_ref.at[pl.ds(proj_rows, table_rows)]),
        (qkv_ref.at[:, pl.ds(0, depth)], packed_ref.at[pl.ds(at_qkv, qkv_rows)]),
    ]
    for side in range(2):
        moves.append(
            (
                qkv_ref.at[pl.ds(side * half, half), pl.ds(depth, extra)],
                packed_ref.at[pl.ds(at_extra, half), pl.ds(side * extra, extra)],
            )
        )
    copies = [
        pltpu.make_async_copy(source, target, sems.at[number])
        for number, (source, target) in enumerate(moves)
    ]
    for made in copies:
        made.start()
    for made in copies:
        made.wait()


def pack(proj, table, qkv):
    depth = proj.shape[1]
    rows = proj.shape[0] + table.shape[0] + qkv.shape[0] + qkv.shape[0] // 2
    return pl.pallas_call(
        pack_kernel,
        out_shape=jax.ShapeDtypeStruct((rows, depth), bf16),
        in_specs=[pl.BlockSpec(memory_space=pl.ANY)] * 3,
        out_specs=pl.BlockSpec(memory_space=pltpu.VMEM),
        scratch_shapes=[pltpu.SemaphoreType.DMA((5,))],
        compiler_params=pltpu.CompilerParams(vmem_limit_bytes=4 * 2**20),
        name="pack_weight_rows",
    )(proj, table, qkv)


def assemble_kernel(groups, sizes, place_ref, tokens_ref, *refs):
    parts = refs[:groups]
    looked_ref, qkv_ref, table, sems = refs[groups:]
    table_rows, qkv_rows, firsts = sizes
    half = qkv_rows // 2
    depth = table.shape[1]
    extra = qkv_ref.shape[1] - depth
    place = place_ref[1]
    table_copies, qkv_copies = [], []

    def copy(source, target, number, into):
        made = pltpu.make_async_copy(source, target, sems.at[number])
        made.start()
        into.append(made)

    for n in range(groups):
        g = jnp.bitwise_xor(place, n)
        start = pl.multiple_of(g * table_rows, table_rows)
        copy(
            parts[n].at[pl.ds(firsts[n], table_rows)],
            table.at[pl.ds(start, table_rows)],
            4 * n,
            table_copies,
        )
    for n in range(groups):
        g = jnp.bitwise_xor(place, n)
        at_qkv = firsts[n] + table_rows
        start = pl.multiple_of(g * qkv_rows, qkv_rows)
        copy(
            parts[n].at[pl.ds(at_qkv, qkv_rows)],
            qkv_ref.at[pl.ds(start, qkv_rows), pl.ds(0, depth)],
            4 * n + 1,
            qkv_copies,
        )
        for side in range(2):
            start = pl.multiple_of(g * qkv_rows + side * half, half)
            copy(
                parts[n].at[pl.ds(at_qkv + qkv_rows, half), pl.ds(side * extra, extra)],
                qkv_ref.at[pl.ds(start, half), pl.ds(depth, extra)],
                4 * n + 2 + side,
                qkv_copies,
            )
    columns = lax.broadcasted_iota(jnp.int32, (tokens_ref.shape[0], table.shape[0]), 1)
    matches = (tokens_ref[...] == columns).astype(f32).astype(bf16)
    for made in table_copies:
        made.wait()
    looked_ref[...] = jnp.dot(matches, table[...], preferred_element_type=f32).astype(bf16)
    for made in qkv_copies:
        made.wait()


def assemble(place, tokens, parts, firsts, table_rows, qkv_rows, wide):
    groups = len(parts)
    frames_here = tokens.shape[0]
    depth = parts[0].shape[1]
    vmem = pl.BlockSpec(memory_space=pltpu.VMEM)
    return pl.pallas_call(
        functools.partial(assemble_kernel, groups, (table_rows, qkv_rows, firsts)),
        out_shape=[
            jax.ShapeDtypeStruct((frames_here, depth), bf16),
            jax.ShapeDtypeStruct((groups * qkv_rows, wide), bf16),
        ],
        in_specs=[pl.BlockSpec(memory_space=pltpu.SMEM)] + [vmem] * (1 + groups),
        out_specs=[vmem] * 2,
        scratch_shapes=[
            pltpu.VMEM((groups * table_rows, depth), bf16),
            pltpu.SemaphoreType.DMA((4 * groups,)),
        ],
        compiler_params=pltpu.CompilerParams(vmem_limit_bytes=24 * 2**20),
        name="lookup_and_qkv_rows",
    )(place, tokens, *parts)


def is_late(m):
    return (m % 2 == 1) & (m != 1)


def add_products(late, books, pieces, where, refs, held, projected_ref):
    here, group = where
    rows_each = held.shape[2] * books // (1 + max(n for n, _, _ in pieces))
    per_book = held.shape[2] // rows_each
    for (n, row, count), ref in zip(pieces, refs):
        owner = jnp.bitwise_xor(group, n)
        book = owner // per_book
        start = (owner % per_book) * rows_each + row

        @pl.when(is_late(jnp.bitwise_xor(here, book)) == late)
        def _():
            columns = pl.ds(pl.multiple_of(start, 128), count)
            projected_ref[...] += jnp.dot(
                held[book, :, columns], ref[:count, :], preferred_element_type=f32
            )


def hold_blocks(blocks, here, gain_ref, held):
    square = 0.0
    for m, ref in blocks.items():
        book = jnp.bitwise_xor(here, m)
        part = ref[...].astype(f32)
        square = square + jnp.sum(part * part, axis=-1, keepdims=True)
        width = part.shape[1]
        columns = pl.ds(pl.multiple_of(book * width, width), width)
        held[book] = (part * gain_ref[:, columns]).astype(bf16)
    return square


def early_kernel(books, early, pieces, place_ref, gain_ref, *refs):
    blocks = dict(zip(early, refs))
    proj = refs[len(early) : len(early) + len(pieces)]
    projected_ref, square_ref, held = refs[len(early) + len(pieces) :]
    where = place_ref[0], place_ref[1]
    square_ref[...] = hold_blocks(blocks, where[0], gain_ref, held)
    projected_ref[...] = jnp.zeros_like(projected_ref)
    add_products(False, books, pieces, where, proj, held, projected_ref)


def project_early(place, gain, blocks, early, pieces, proj):
    books = len(blocks)
    frames_here, width = blocks[0].shape
    depth = proj[0].shape[1]
    vmem = pl.BlockSpec(memory_space=pltpu.VMEM)
    return pl.pallas_call(
        functools.partial(early_kernel, books, early, pieces),
        out_shape=[
            jax.ShapeDtypeStruct((frames_here, depth), f32),
            jax.ShapeDtypeStruct((frames_here, 1), f32),
        ],
        in_specs=[pl.BlockSpec(memory_space=pltpu.SMEM)]
        + [vmem] * (1 + len(early) + len(pieces)),
        out_specs=[vmem] * 2,
        scratch_shapes=[pltpu.VMEM((books, frames_here, width), bf16)],
        compiler_params=pltpu.CompilerParams(vmem_limit_bytes=24 * 2**20),
        name="project_early_blocks",
    )(place, gain, *[blocks[m] for m in early], *proj)


def late_kernel(books, late, pieces, place_ref, gain_ref, *refs):
    blocks = dict(zip(late, refs))
    refs = refs[len(late) :]
    proj = refs[: len(pieces)]
    early_ref, square_ref, looked_ref, depth_gain_ref, qkv_ref = refs[
        len(pieces) : len(pieces) + 5
    ]
    refs = refs[len(pieces) + 5 :]
    outs = refs[:books]
    held, projected_ref, packed = refs[books:]
    where = place_ref[0], place_ref[1]
    frames_here, width = held.shape[1:]
    square = square_ref[...] + hold_blocks(blocks, where[0], gain_ref, held)
    projected_ref[...] = early_ref[...]
    add_products(True, books, pieces, where, proj, held, projected_ref)
    projected = projected_ref[...] * lax.rsqrt(square / (books * width) + 1e-05)
    depth_in = (projected + looked_ref[...].astype(f32)).astype(bf16).astype(f32)
    moment = jnp.mean(depth_in * depth_in, axis=-1, keepdims=True)
    depth_normed = (depth_in * lax.rsqrt(moment + 1e-05) * depth_gain_ref[...]).astype(bf16)
    packed[...] = jnp.dot(depth_normed, qkv_ref[...], preferred_element_type=f32).astype(bf16)
    rows = frames_here // books
    for m in range(books):
        start = pl.multiple_of(jnp.bitwise_xor(where[0], m) * rows, rows)
        outs[m][...] = packed[pl.ds(start, rows), :]


def project_late(
    place, gain, blocks, late, pieces, proj, projected, square, looked, depth_gain, qkv
):
    books = len(blocks)
    frames_here, width = blocks[0].shape
    depth, wide = qkv.shape
    vmem = pl.BlockSpec(memory_space=pltpu.VMEM)
    return pl.pallas_call(
        functools.partial(late_kernel, books, late, pieces),
        out_shape=[jax.ShapeDtypeStruct((frames_here // books, wide), bf16)] * books,
        in_specs=[pl.BlockSpec(memory_space=pltpu.SMEM)]
        + [vmem] * (1 + len(late) + len(pieces) + 5),
        out_specs=[vmem] * books,
        scratch_shapes=[
            pltpu.VMEM((books, frames_here, width), bf16),
            pltpu.VMEM((frames_here, depth), f32),
            pltpu.VMEM((frames_here, wide), bf16),
        ],
        compiler_params=pltpu.CompilerParams(vmem_limit_bytes=28 * 2**20),
        name="project_late_blocks_and_qkv",
    )(
        place,
        gain,
        *[blocks[m] for m in late],
        *proj,
        projected,
        square,
        looked,
        depth_gain,
        qkv,
    )


def attend_kernel(books, place_ref, *refs):
    arrived = refs[:books]
    out_ref, inner = refs[books:]
    place = place_ref[0]
    rows, wide = arrived[0].shape
    width = wide // 3
    for m in range(books):
        inner[jnp.bitwise_xor(place, m)] = arrived[m][...]
    head_of_row = lax.broadcasted_iota(jnp.int32, (width, width), 0) // HD
    head_of_column = lax.broadcasted_iota(jnp.int32, (width, width), 1) // HD
    same_head = (head_of_row == head_of_column).astype(f32).astype(bf16)
    keys_all = [inner[j, :, width : 2 * width].astype(f32) for j in range(books)]
    values_all = [inner[j, :, 2 * width :].astype(f32) for j in range(books)]
    contexts = []
    for k in range(books):
        query = inner[k, :, :width].astype(f32) * HD ** (-0.5)
        products = jnp.concatenate([query * keys_all[j] for j in range(k + 1)], axis=0)
        high = products.astype(bf16)
        low = (products - high.astype(f32)).astype(bf16)
        scores = jnp.dot(high, same_head, preferred_element_type=f32) + jnp.dot(
            low, same_head, preferred_element_type=f32
        )
        scores = [scores[j * rows : (j + 1) * rows] for j in range(k + 1)]
        peak = functools.reduce(jnp.maximum, scores)
        expo = [jnp.exp(score - peak) for score in scores]
        total = functools.reduce(jnp.add, expo)
        context = 0.0
        for j in range(k + 1):
            probability = (expo[j] / total).astype(bf16).astype(f32)
            context = context + probability * values_all[j]
        contexts.append(context)
    out_ref[...] = jnp.stack(contexts, axis=1).astype(bf16)


def attend(place, arrived):
    books = len(arrived)
    rows, wide = arrived[0].shape
    vmem = pl.BlockSpec(memory_space=pltpu.VMEM)
    return pl.pallas_call(
        functools.partial(attend_kernel, books),
        out_shape=jax.ShapeDtypeStruct((rows, books, wide // 3), bf16),
        in_specs=[pl.BlockSpec(memory_space=pltpu.SMEM)] + [vmem] * books,
        out_specs=vmem,
        scratch_shapes=[pltpu.VMEM((books, rows, wide), bf16)],
        compiler_params=pltpu.CompilerParams(vmem_limit_bytes=16 * 2**20),
        name="attend_books",
    )(place, *arrived)


def swap(value, axis, distance):
    return lax.ppermute(value, axis, [(i, i ^ distance) for i in range(lax.axis_size(axis))])


def after(value, *others):
    return lax.optimization_barrier((value, *others))[0]


def bits_of(number):
    return [1 << place for place in range(number.bit_length()) if number >> place & 1]


def per_device(
    gate_pre,
    up_pre,
    down_weight,
    residual,
    out_gain,
    in_proj,
    embedding,
    token_ids,
    depth_gain,
    qkv_weight,
):
    books = lax.axis_size("book")
    groups = lax.axis_size("frames")
    here = lax.axis_index("book").astype(jnp.int32)
    place = jnp.stack([here, lax.axis_index("frames").astype(jnp.int32)])
    width = residual.shape[1]
    depth = in_proj.shape[2]
    wide = qkv_weight.shape[2]
    proj_rows = in_proj.shape[1]
    table_rows = embedding.shape[1]
    qkv_rows = qkv_weight.shape[1]
    gain = out_gain.astype(f32)[None]

    hidden = (jax.nn.silu(gate_pre.astype(f32)) * up_pre.astype(f32)).astype(bf16)

    def share(m, *others):
        start = jnp.bitwise_xor(here, m) * width
        block = lax.dynamic_slice_in_dim(down_weight, start, width, 1)
        factor = after(hidden, *others) if others else hidden
        return jnp.dot(factor, block, preferred_element_type=f32)

    sums = {books - 1: share(books - 1)}
    first = sums[books - 1].astype(bf16)

    rows = pack(*after((in_proj[0], embedding[0], qkv_weight[0]), first))
    parts = {0: [(0, rows)]}
    near = [n for n in range(2, groups, 2) if len(bits_of(n)) == 1]
    for n in near:
        parts[n] = [(0, swap(rows, "frames", n))]

    sums[books - 2] = lax.optimization_barrier(share(books - 2, rows))
    distance = 1
    while distance < books:
        came = None
        for m in range(books - distance, 0, -2 * distance):
            going = sums.pop(m).astype(bf16)
            if came is not None:
                going = after(going, came, sums[m + distance])
            came = swap(going, "book", distance)
            if m == books - 1:
                for n in range(books - 3, -1, -1):
                    sums[n] = lax.optimization_barrier(share(n, came))
                sums[0] = sums[0] + residual.astype(f32)
            sums[m ^ distance] = sums[m ^ distance] + came.astype(f32)
        distance *= 2

    blocks = {0: sums[0].astype(bf16)}
    distance = books // 2
    while distance:
        for m in sorted(blocks):
            going = blocks[m] if m == 0 else after(blocks[m], blocks[distance])
            blocks[m ^ distance] = swap(going, "book", distance)
        distance //= 2

    arrived = after([parts[n][0][1] for n in near], blocks[0])
    for n, value in zip(near, arrived):
        parts[n] = [(0, value)]
    cut = rows.shape[0] // 2 // 128 * 128
    for n in range(2, groups, 2):
        sides = bits_of(n)
        if n in near:
            continue
        if len(sides) == 2 and 0 < cut < proj_rows:
            upper = swap(parts[n ^ sides[0]][0][1][:cut], "frames", sides[0])
            lower = swap(parts[n ^ sides[1]][0][1][cut:], "frames", sides[1])
            parts[n] = [(0, upper), (cut, lower)]
        else:
            parts[n] = [(0, swap(rows, "frames", n))]
    for n in range(0, groups, 2):
        parts[n + 1] = [(first, swap(value, "frames", 1)) for first, value in parts[n]]
    looked, qkv = assemble(
        place,
        token_ids,
        [parts[n][-1][1] for n in range(groups)],
        [proj_rows - parts[n][-1][0] for n in range(groups)],
        table_rows,
        qkv_rows,
        wide,
    )

    pieces, proj = [], []
    for n in range(groups):
        for first, value in parts[n]:
            pieces.append((n, first, min(value.shape[0], proj_rows - first)))
            proj.append(value)
    early = [m for m in range(books) if not is_late(m)]
    late = [m for m in range(books) if is_late(m)]
    projected, square = project_early(place, gain, blocks, early, pieces, proj)
    packed = project_late(
        place,
        gain,
        blocks,
        late,
        pieces,
        proj,
        projected,
        square,
        looked,
        depth_gain.astype(f32),
        qkv,
    )
    far = {m: swap(packed[m], "book", m) for m in range(books - 1, 0, -1)}
    return attend(place, [packed[0]] + [far[m] for m in range(1, books)])


def solution(mesh):
    in_specs = (
        P("frames", "book"),
        P("frames", "book"),
        P("book", None),
        P("frames", "book"),
        P(),
        P("book", "frames", None),
        P("book", "frames", None),
        P("frames", "book"),
        P("book", None),
        P("book", "frames", None),
    )
    out_specs = P(("frames", "book"), None, None)
    return jax.shard_map(
        per_device, mesh=mesh, in_specs=in_specs, out_specs=out_specs, check_vma=False
    )
```

time: 142 us -> 148 us (1.042)
  waiting for transfers between devices: 63.7 us -> 77.5 us
  between operations: 13.6 us -> 0.25 us
  Pallas kernels: 12.8 us -> 21.7 us
  local copies, waits for them, and re-layouts: 13.6 us -> 4.97 us
  starting transfers between devices: 19.1 us -> 21.1 us
  matrix products: 13.4 us -> 15.2 us
  other arithmetic: 4.42 us -> 6.09 us
    ppermute x16 -> x18, waiting for transfers between devices: 63 us -> 77.5 us  [swap(): lax.ppermute(value, axis, [(i, i ^ distance) for i in range(lax.axis_size...]
    unnamed x45 -> x33, local copies, waits for them, and re-layouts: 13.5 us -> 3.54 us
    pallas_call x2 -> x3, Pallas kernels: 8.32 us -> 14.1 us  [the longest x1 6.98 us: project_early(): pl.pallas_call(functools.partial(early_kernel, books, early, pieces), out...]
    pallas_call x1, Pallas kernels: 2.21 us -> 4.82 us  [assemble(): pl.pallas_call(functools.partial(assemble_kernel, groups, (table_rows, qk...]
    ppermute x16 -> x18, starting transfers between devices: 19.1 us -> 21.1 us  [swap(): lax.ppermute(value, axis, [(i, i ^ distance) for i in range(lax.axis_size...]
    add x0 -> x1, other arithmetic: none -> 2.02 us  [per_device(): sums[m ^ distance] = sums[m ^ distance] + came.astype(f32)]
    dot_general x4, matrix products: 13.4 us -> 15.2 us  [share(): return jnp.dot(factor, block, preferred_element_type=f32)]
  transfers between devices with their start and end apart: 17 -> 18, of which waited for: 8 -> 8; matrix products, arithmetic and copies ran while one was open for 13% -> 12% of each run, Pallas kernels for 5% -> 8%
where the time goes in v4:
time: 148 us; the launch traced here: 147 us
  waiting for transfers between devices  77.5 us (52%)
  Pallas kernels  21.7 us (15%)
  starting transfers between devices  21.1 us (14%)
  matrix products  15.2 us (10%)
  other arithmetic  6.09 us (4%)
  local copies, waits for them, and re-layouts  4.97 us (3%)
    ppermute x18, waiting for transfers between devices, swap(): lax.ppermute(value, axis, [(i, i ^ distance) for i in range(lax.axis_size...  77.5 us
    ppermute x18, starting transfers between devices, swap(): lax.ppermute(value, axis, [(i, i ^ distance) for i in range(lax.axis_size...  21.1 us
    dot_general x4, matrix products, share(): return jnp.dot(factor, block, preferred_element_type=f32)  15.2 us
    pallas_call x1, Pallas kernels, project_early(): pl.pallas_call(functools.partial(early_kernel, books, early, pieces), out...  6.98 us
    pallas_call x1, Pallas kernels, project_late(): pl.pallas_call(functools.partial(late_kernel, books, late, pieces), out_s...  6.91 us
    pallas_call x1, Pallas kernels, assemble(): pl.pallas_call(functools.partial(assemble_kernel, groups, (table_rows, qk...  4.82 us
    unnamed x33, local copies, waits for them, and re-layouts  3.54 us
  transfers between devices with their start and end apart: 18, of which 8 were waited for; matrix products, arithmetic and copies ran while one was open for 12% of the time, Pallas kernels for 8%

profile of v4, /device:TPU:0, one launch (start us, length us, event | category | flops | bytes accessed | tf_op | source)
XLA Modules:
  0.0 146.8 jit_solution(8734655024860061362)
XLA Ops:
  0.0 1.9 %fusion.12 = bf16[256,1536]{1,0:T(8,128)(2,1)S(1)} fusion(bf16[256,1536]{1,0:T(8,128)(2,1)} %param.11, bf16[256,1536]{1,0:T(8,128)(2,1)} %param.10), kind=kLoop, calls=%fused_computation.14 | loop fusion | flops 3145728 | bytes 2359296 | tf_op jit(solution)/shard_map/convert_element_type | solution.py:338
  1.9 4.0 %fusion.13 = bf16[256,1024]{1,0:T(8,128)(2,1)} fusion(bf16[256,1536]{1,0:T(8,128)(2,1)S(1)} %fusion.12, bf16[1536,4096]{1,0:T(8,128)(2,1)} %param.12, s32[]{:T(128)S(6)} %select_n.12), kind=kOutput, calls=%fused_computation.15 | convolution fusion | flops 805568512 | bytes 4456452 | tf_op jit(solution)/shard_map/dot_general | solution.py:344
  5.9 3.0 %collective-permute-start = (bf16[256,1024]{1,0:T(8,128)(2,1)}, bf16[256,1024]{1,0:T(8,128)(2,1)}, u32[]{:S(2)}, u32[]{:S(2)}) collective-permute-start(bf16[256,1024]{1,0:T(8,128)(2,1)} %fusion.13), channel_id=1, source_target_pairs={{0,1},{1,0},{2,3},{3,2},{4,5},{5,4},{6,7},{7,6},{8,9},{9,8},{10,11... | collective-permute-start | bytes 1572872 | tf_op jit(solution)/shard_map/ppermute | solution.py:303
  12.2 4.1 %fusion = f32[256,1024]{1,0:T(8,128)} fusion(bf16[256,1536]{1,0:T(8,128)(2,1)} %copy-done.12, bf16[1536,4096]{1,0:T(8,128)(2,1)} %param.12, s32[]{:T(128)S(6)} %select_n.15), kind=kOutput, calls=%fused_computation | convolution fusion | flops 805306368 | bytes 4980740 | tf_op jit(solution)/shard_map/dot_general | solution.py:344
  16.3 4.9 %collective-permute-done = bf16[256,1024]{1,0:T(8,128)(2,1)} collective-permute-done((bf16[256,1024]{1,0:T(8,128)(2,1)}, bf16[256,1024]{1,0:T(8,128)(2,1)}, u32[]{:S(2)}, u32[]{:S(2)}) %collective-permute-start) | collective-permute-done | bytes 524320 | tf_op jit(solution)/shard_map/ppermute | solution.py:303
  21.2 3.9 %fusion.2 = bf16[256,1024]{1,0:T(8,128)(2,1)} fusion(bf16[256,1536]{1,0:T(8,128)(2,1)} %copy-done.12, bf16[1536,4096]{1,0:T(8,128)(2,1)} %param.12, s32[]{:T(128)S(6)} %select_n.14), kind=kOutput, calls=%fused_computation.2 | convolution fusion | flops 805306368 | bytes 4456452 | tf_op jit(solution)/shard_map/dot_general | solution.py:344
  25.1 2.0 %convert_add_fusion = bf16[256,1024]{1,0:T(8,128)(2,1)} fusion(f32[256,1024]{1,0:T(8,128)S(1)} %copy-done.11, bf16[256,1024]{1,0:T(8,128)(2,1)} %collective-permute-done), kind=kLoop, calls=%fused_computation.17 | loop fusion | flops 786432 | bytes 2097152 | tf_op jit(solution)/shard_map/add | solution.py:368
  27.1 1.7 %collective-permute-start.1 = (bf16[256,1024]{1,0:T(8,128)(2,1)}, bf16[256,1024]{1,0:T(8,128)(2,1)}, u32[]{:S(2)}, u32[]{:S(2)}) collective-permute-start(bf16[256,1024]{1,0:T(8,128)(2,1)} %fusion.2), channel_id=1, source_target_pairs={{0,1},{1,0},{2,3},{3,2},{4,5},{5,4},{6,7},{7,6},{8,9},{9,8},{10,11... | collective-permute-start | bytes 1572872 | tf_op jit(solution)/shard_map/ppermute | solution.py:303
  28.9 2.6 %collective-permute-start.2 = (bf16[256,1024]{1,0:T(8,128)(2,1)}, bf16[256,1024]{1,0:T(8,128)(2,1)}, u32[]{:S(2)}, u32[]{:S(2)}) collective-permute-start(bf16[256,1024]{1,0:T(8,128)(2,1)} %convert_add_fusion), channel_id=1, source_target_pairs={{0,2},{1,3},{2,0},{3,1},{4,6},{5,7},{6,4},{7,5},{8,10},{9,11},{10,... | collective-permute-start | bytes 1572872 | tf_op jit(solution)/shard_map/ppermute | solution.py:303
  31.4 3.2 %fusion.4 = f32[256,1024]{1,0:T(8,128)S(1)} fusion(bf16[256,1536]{1,0:T(8,128)(2,1)} %copy-done.12, bf16[1536,4096]{1,0:T(8,128)(2,1)} %param.12, s32[]{:T(128)S(6)} %select_n.13), kind=kOutput, calls=%fused_computation.4 | convolution fusion | flops 805306368 | bytes 4980740 | tf_op jit(solution)/shard_map/dot_general | solution.py:344
  34.6 17.0 %collective-permute-done.1 = bf16[256,1024]{1,0:T(8,128)(2,1)} collective-permute-done((bf16[256,1024]{1,0:T(8,128)(2,1)}, bf16[256,1024]{1,0:T(8,128)(2,1)}, u32[]{:S(2)}, u32[]{:S(2)}) %collective-permute-start.1) | collective-permute-done | bytes 524320 | tf_op jit(solution)/shard_map/ppermute | solution.py:303
  51.7 2.2 %collective-permute-done.2 = bf16[256,1024]{1,0:T(8,128)(2,1)} collective-permute-done((bf16[256,1024]{1,0:T(8,128)(2,1)}, bf16[256,1024]{1,0:T(8,128)(2,1)}, u32[]{:S(2)}, u32[]{:S(2)}) %collective-permute-start.2) | collective-permute-done | bytes 524320 | tf_op jit(solution)/shard_map/ppermute | solution.py:303
  55.9 2.6 %collective-permute-start.3 = (bf16[256,1024]{1,0:T(8,128)(2,1)S(1)}, bf16[256,1024]{1,0:T(8,128)(2,1)}, u32[]{:S(2)}, u32[]{:S(2)}) collective-permute-start(bf16[256,1024]{1,0:T(8,128)(2,1)S(1)} %add_convert_fusion.refs_0_), channel_id=1, source_target_pairs={{0,2},{1,3},{2,0},{3,1},{4,6},{5,7},{6,4},{7,5},{8,10},{9,11},{10,... | collective-permute-start | bytes 1572872 | tf_op jit(solution)/shard_map/ppermute | solution.py:303
  60.2 13.0 %collective-permute-done.4.refs_1_ = bf16[256,1024]{1,0:T(8,128)(2,1)S(1)} collective-permute-done((bf16[256,1024]{1,0:T(8,128)(2,1)S(1)}, bf16[256,1024]{1,0:T(8,128)(2,1)S(1)}, u32[]{:S(2)}, u32[]{:S(2)}) %collective-permute-start.4) | collective-permute-done | bytes 524320 | tf_op jit(solution)/shard_map/ppermute | solution.py:303
  74.6 8.0 %collective-permute-done.3.refs_2_ = bf16[256,1024]{1,0:T(8,128)(2,1)} collective-permute-done((bf16[256,1024]{1,0:T(8,128)(2,1)S(1)}, bf16[256,1024]{1,0:T(8,128)(2,1)}, u32[]{:S(2)}, u32[]{:S(2)}) %collective-permute-start.3) | collective-permute-done | bytes 524320 | tf_op jit(solution)/shard_map/ppermute | solution.py:303
  84.1 17.8 %collective-permute-done.11.refs_9_.refs_7_ = bf16[384,1024]{1,0:T(8,128)(2,1)} collective-permute-done((bf16[384,1024]{1,0:T(8,128)(2,1)S(1)}, bf16[384,1024]{1,0:T(8,128)(2,1)}, u32[]{:S(2)}, u32[]{:S(2)}) %collective-permute-start.11) | collective-permute-done | bytes 786464 | tf_op jit(solution)/shard_map/ppermute | solution.py:303
  106.1 4.8 %lookup_and_qkv_rows.1 = (bf16[256,1024]{1,0:T(8,128)(2,1)S(1)}, bf16[1024,1536]{1,0:T(8,128)(2,1)S(1)}) custom-call(s32[2]{0:T(128)S(1)} %pad_add_fusion.place_ref, s32[256,1]{1,0:T(8,128)S(1)} %copy.11.tokens_ref, bf16[832,1024]{1,0:T(8,128)(2,1)S(1)} %pack_weight_rows.1.refs_3_.refs_0_.refs_1_, bf16[832,1024]{1,0:T(8,128)(2,1)S(1)} %copy-done.1, ...), custom_call_target="tpu_custom_call" | custom-call | tf_op jit(solution)/shard_map/lookup_and_qkv_rows/pallas_call | solution.py:114
  110.9 7.0 %project_early_blocks.1 = (f32[256,1024]{1,0:T(8,128)S(1)}, f32[256,1]{1,0:T(8,128)S(1)}) custom-call(s32[2]{0:T(128)S(1)} %pad_add_fusion.place_ref, f32[1,4096]{1,0:T(1,128)S(1)} %bitcast.13, bf16[256,1024]{1,0:T(8,128)(2,1)S(1)} %copy-done.4, bf16[256,1024]{1,0:T(8,128)(2,1)S(1)} %copy-done.7, bf16[256,1024]{1,0:T(8,128)(2,1)} %collective-permute-done.3.refs_2_, ...), custom_call_target="tpu_custom_call" | custom-call | tf_op jit(solution)/shard_map/project_early_blocks/pallas_call | solution.py:179
  118.0 6.9 %project_late_blocks_and_qkv.1 = (bf16[64,1536]{1,0:T(8,128)(2,1)S(1)}, bf16[64,1536]{1,0:T(8,128)(2,1)S(1)}, bf16[64,1536]{1,0:T(8,128)(2,1)S(1)}, bf16[64,1536]{1,0:T(8,128)(2,1)S(1)}) custom-call(s32[2]{0:T(128)S(1)} %pad_add_fusion.place_ref, f32[1,4096]{1,0:T(1,128)S(1)} %bitcast.14, bf16[256,1024]{1,0:T(8,128)(2,1)} %collective-permute-done.5.refs_0_, ...), custom_call_target="tpu_custom_call" | custom-call | tf_op jit(solution)/shard_map/project_late_blocks_and_qkv/pallas_call | solution.py:227
  124.9 2.1 %collective-permute-start.15 = (bf16[64,1536]{1,0:T(8,128)(2,1)S(1)}, bf16[64,1536]{1,0:T(8,128)(2,1)S(1)}, u32[]{:S(2)}, u32[]{:S(2)}) collective-permute-start(bf16[64,1536]{1,0:T(8,128)(2,1)S(1)} %get-tuple-element.36), channel_id=1, source_target_pairs={{0,1},{1,0},{2,3},{3,2},{4,5},{5,4},{6,7},{7,6},{8,9},{9,8},{10,11... | collective-permute-start | bytes 589832 | tf_op jit(solution)/shard_map/ppermute | solution.py:303
  127.6 1.8 %collective-permute-start.17 = (bf16[64,1536]{1,0:T(8,128)(2,1)S(1)}, bf16[64,1536]{1,0:T(8,128)(2,1)S(1)}, u32[]{:S(2)}, u32[]{:S(2)}) collective-permute-start(bf16[64,1536]{1,0:T(8,128)(2,1)S(1)} %get-tuple-element.38), channel_id=1, source_target_pairs={{0,3},{1,2},{2,1},{3,0},{4,7},{5,6},{6,5},{7,4},{8,11},{9,10},{10,... | collective-permute-start | bytes 589832 | tf_op jit(solution)/shard_map/ppermute | solution.py:303
  129.4 6.3 %collective-permute-done.15.refs_1_ = bf16[64,1536]{1,0:T(8,128)(2,1)S(1)} collective-permute-done((bf16[64,1536]{1,0:T(8,128)(2,1)S(1)}, bf16[64,1536]{1,0:T(8,128)(2,1)S(1)}, u32[]{:S(2)}, u32[]{:S(2)}) %collective-permute-start.15) | collective-permute-done | bytes 196640 | tf_op jit(solution)/shard_map/ppermute | solution.py:303
  135.7 8.4 %collective-permute-done.16.refs_2_ = bf16[64,1536]{1,0:T(8,128)(2,1)S(1)} collective-permute-done((bf16[64,1536]{1,0:T(8,128)(2,1)S(1)}, bf16[64,1536]{1,0:T(8,128)(2,1)S(1)}, u32[]{:S(2)}, u32[]{:S(2)}) %collective-permute-start.16) | collective-permute-done | bytes 196640 | tf_op jit(solution)/shard_map/ppermute | solution.py:303
  144.0 2.8 %attend_books.1 = bf16[64,4,512]{2,1,0:T(4,128)(2,1)} custom-call(s32[2]{0:T(128)S(1)} %pad_add_fusion.place_ref, bf16[64,1536]{1,0:T(8,128)(2,1)S(1)} %get-tuple-element.35.refs_0_, bf16[64,1536]{1,0:T(8,128)(2,1)S(1)} %collective-permute-done.15.refs_1_, bf16[64,1536]{1,0:T(8,128)(2,1)S(1)} %collective-permute-done.16.refs_2_, ...), custom_call_target="tpu_custom_call" | custom-call | tf_op jit(solution)/shard_map/attend_books/pallas_call | solution.py:291
  (62 shorter events, 14.8 us)
Async XLA Ops:
  5.9 15.3 %collective-permute-start = (bf16[256,1024]{1,0:T(8,128)(2,1)}, bf16[256,1024]{1,0:T(8,128)(2,1)}, u32[]{:S(2)}, u32[]{:S(2)}) collective-permute-start(bf16[256,1024]{1,0:T(8,128)(2,1)} %fusion.13), channel_id=1, source_target_pairs={{0,1},{1,0},{2,3},{3,2},{4,5},{5,4},{6,7},{7,6},{8,9},{9,8},{10,11... | collective-permute-start | bytes 1572872 | tf_op jit(solution)/shard_map/ppermute | solution.py:303
  9.1 49.4 %collective-permute-start.8 = (bf16[832,1024]{1,0:T(8,128)(2,1)S(1)}, bf16[832,1024]{1,0:T(8,128)(2,1)}, u32[]{:S(2)}, u32[]{:S(2)}) collective-permute-start(bf16[832,1024]{1,0:T(8,128)(2,1)S(1)} %pack_weight_rows.1.refs_3_.refs_0_.refs_1_), channel_id=1, source_target_pairs={{0,16},{4,20},{8,24},{12,28},{16,0},{20,4},{24,8},{28,12},{1,17},{... | collective-permute-start | bytes 5111816 | tf_op jit(solution)/shard_map/ppermute | solution.py:303
  10.7 47.8 %collective-permute-start.7 = (bf16[832,1024]{1,0:T(8,128)(2,1)S(1)}, bf16[832,1024]{1,0:T(8,128)(2,1)S(1)}, u32[]{:S(2)}, u32[]{:S(2)}) collective-permute-start(bf16[832,1024]{1,0:T(8,128)(2,1)S(1)} %pack_weight_rows.1.refs_3_.refs_0_.refs_1_), channel_id=1, source_target_pairs={{0,8},{4,12},{8,0},{12,4},{16,24},{20,28},{24,16},{28,20},{1,9},{5... | collective-permute-start | bytes 5111816 | tf_op jit(solution)/shard_map/ppermute | solution.py:303
  16.3 8.8 %copy-start.11 = (f32[256,1024]{1,0:T(8,128)S(1)}, f32[256,1024]{1,0:T(8,128)}, u32[]{:S(2)}) copy-start(f32[256,1024]{1,0:T(8,128)} %fusion) | copy-start | bytes 3145732
  27.1 24.6 %collective-permute-start.1 = (bf16[256,1024]{1,0:T(8,128)(2,1)}, bf16[256,1024]{1,0:T(8,128)(2,1)}, u32[]{:S(2)}, u32[]{:S(2)}) collective-permute-start(bf16[256,1024]{1,0:T(8,128)(2,1)} %fusion.2), channel_id=1, source_target_pairs={{0,1},{1,0},{2,3},{3,2},{4,5},{5,4},{6,7},{7,6},{8,9},{9,8},{10,11... | collective-permute-start | bytes 1572872 | tf_op jit(solution)/shard_map/ppermute | solution.py:303
  28.9 25.0 %collective-permute-start.2 = (bf16[256,1024]{1,0:T(8,128)(2,1)}, bf16[256,1024]{1,0:T(8,128)(2,1)}, u32[]{:S(2)}, u32[]{:S(2)}) collective-permute-start(bf16[256,1024]{1,0:T(8,128)(2,1)} %convert_add_fusion), channel_id=1, source_target_pairs={{0,2},{1,3},{2,0},{3,1},{4,6},{5,7},{6,4},{7,5},{8,10},{9,11},{10,... | collective-permute-start | bytes 1572872 | tf_op jit(solution)/shard_map/ppermute | solution.py:303
  31.4 22.4 %copy-start.13 = (bf16[256,1024]{1,0:T(8,128)(2,1)S(1)}, bf16[256,1024]{1,0:T(8,128)(2,1)}, u32[]{:S(2)}) copy-start(bf16[256,1024]{1,0:T(8,128)(2,1)} %param.13) | copy-start | bytes 1572868
  34.6 68.5 %copy-start.15 = (bf16[1,1024]{1,0:T(2,128)(2,1)S(1)}, bf16[1,1024]{1,0:T(2,128)(2,1)}, u32[]{:S(2)}) copy-start(bf16[1,1024]{1,0:T(2,128)(2,1)} %param.18) | copy-start | bytes 6148
  34.6 69.1 %copy-start.14 = (bf16[4096]{0:T(1024)(128)(2,1)S(1)}, bf16[4096]{0:T(1024)(128)(2,1)}, u32[]{:S(2)}) copy-start(bf16[4096]{0:T(1024)(128)(2,1)} %param.14) | copy-start | bytes 24580
  55.4 46.4 %copy-start.3 = (bf16[256,1024]{1,0:T(8,128)(2,1)}, bf16[256,1024]{1,0:T(8,128)(2,1)S(1)}, u32[]{:S(2)}) copy-start(bf16[256,1024]{1,0:T(8,128)(2,1)S(1)} %add_convert_fusion.refs_0_) | copy-start | bytes 1572868
  55.4 17.8 %collective-permute-start.4 = (bf16[256,1024]{1,0:T(8,128)(2,1)S(1)}, bf16[256,1024]{1,0:T(8,128)(2,1)S(1)}, u32[]{:S(2)}, u32[]{:S(2)}) collective-permute-start(bf16[256,1024]{1,0:T(8,128)(2,1)S(1)} %add_convert_fusion.refs_0_), channel_id=1, source_target_pairs={{0,1},{1,0},{2,3},{3,2},{4,5},{5,4},{6,7},{7,6},{8,9},{9,8},{10,11... | collective-permute-start | bytes 1572872 | tf_op jit(solution)/shard_map/ppermute | solution.py:303
  55.9 45.9 %collective-permute-start.6 = (bf16[832,1024]{1,0:T(8,128)(2,1)S(1)}, bf16[832,1024]{1,0:T(8,128)(2,1)S(1)}, u32[]{:S(2)}, u32[]{:S(2)}) collective-permute-start(bf16[832,1024]{1,0:T(8,128)(2,1)S(1)} %pack_weight_rows.1.refs_3_.refs_0_.refs_1_), channel_id=1, source_target_pairs={{0,4},{4,0},{8,12},{12,8},{16,20},{20,16},{24,28},{28,24},{1,5},{5... | collective-permute-start | bytes 5111816 | tf_op jit(solution)/shard_map/ppermute | solution.py:303
  55.9 26.6 %collective-permute-start.3 = (bf16[256,1024]{1,0:T(8,128)(2,1)S(1)}, bf16[256,1024]{1,0:T(8,128)(2,1)}, u32[]{:S(2)}, u32[]{:S(2)}) collective-permute-start(bf16[256,1024]{1,0:T(8,128)(2,1)S(1)} %add_convert_fusion.refs_0_), channel_id=1, source_target_pairs={{0,2},{1,3},{2,0},{3,1},{4,6},{5,7},{6,4},{7,5},{8,10},{9,11},{10,... | collective-permute-start | bytes 1572872 | tf_op jit(solution)/shard_map/ppermute | solution.py:303
  58.6 25.5 %collective-permute-start.12 = (bf16[448,1024]{1,0:T(8,128)(2,1)S(1)}, bf16[448,1024]{1,0:T(8,128)(2,1)}, u32[]{:S(2)}, u32[]{:S(2)}) collective-permute-start(bf16[448,1024]{1,0:T(8,128)(2,1)S(1)} %slice.7), channel_id=1, source_target_pairs={{0,16},{4,20},{8,24},{12,28},{16,0},{20,4},{24,8},{28,12},{1,17},{... | collective-permute-start | bytes 2752520 | tf_op jit(solution)/shard_map/ppermute | solution.py:303
  60.2 44.4 %collective-permute-start.9 = (bf16[832,1024]{1,0:T(8,128)(2,1)S(1)}, bf16[832,1024]{1,0:T(8,128)(2,1)}, u32[]{:S(2)}, u32[]{:S(2)}) collective-permute-start(bf16[832,1024]{1,0:T(8,128)(2,1)S(1)} %collective-permute-done.7.refs_5_.refs_2_.refs_3_), channel_id=1, source_target_pairs={{0,4},{4,0},{8,12},{12,8},{16,20},{20,16},{24,28},{28,24},{1,5},{5... | collective-permute-start | bytes 5111816 | tf_op jit(solution)/shard_map/ppermute | solution.py:303
  73.2 28.7 %copy-start.6 = (bf16[256,1024]{1,0:T(8,128)(2,1)}, bf16[256,1024]{1,0:T(8,128)(2,1)S(1)}, u32[]{:S(2)}) copy-start(bf16[256,1024]{1,0:T(8,128)(2,1)S(1)} %collective-permute-done.4.refs_1_) | copy-start | bytes 1572868
  73.2 31.4 %collective-permute-start.10 = (bf16[832,1024]{1,0:T(8,128)(2,1)}, bf16[832,1024]{1,0:T(8,128)(2,1)}, u32[]{:S(2)}, u32[]{:S(2)}) collective-permute-start(bf16[832,1024]{1,0:T(8,128)(2,1)} %collective-permute-done.8.refs_7_.refs_4_.refs_5_), channel_id=1, source_target_pairs={{0,4},{4,0},{8,12},{12,8},{16,20},{20,16},{24,28},{28,24},{1,5},{5... | collective-permute-start | bytes 5111816 | tf_op jit(solution)/shard_map/ppermute | solution.py:303
  82.6 19.3 %collective-permute-start.11 = (bf16[384,1024]{1,0:T(8,128)(2,1)S(1)}, bf16[384,1024]{1,0:T(8,128)(2,1)}, u32[]{:S(2)}, u32[]{:S(2)}) collective-permute-start(bf16[384,1024]{1,0:T(8,128)(2,1)S(1)} %slice.6), channel_id=1, source_target_pairs={{0,8},{4,12},{8,0},{12,4},{16,24},{20,28},{24,16},{28,20},{1,9},{5... | collective-permute-start | bytes 2359304 | tf_op jit(solution)/shard_map/ppermute | solution.py:303
  84.1 20.5 %collective-permute-start.14 = (bf16[448,1024]{1,0:T(8,128)(2,1)}, bf16[448,1024]{1,0:T(8,128)(2,1)}, u32[]{:S(2)}, u32[]{:S(2)}) collective-permute-start(bf16[448,1024]{1,0:T(8,128)(2,1)} %collective-permute-done.12.refs_10_.refs_6_.refs_8_), channel_id=1, source_target_pairs={{0,4},{4,0},{8,12},{12,8},{16,20},{20,16},{24,28},{28,24},{1,5},{5... | collective-permute-start | bytes 2752520 | tf_op jit(solution)/shard_map/ppermute | solution.py:303
  101.8 9.1 %collective-permute-start.13 = (bf16[384,1024]{1,0:T(8,128)(2,1)}, bf16[384,1024]{1,0:T(8,128)(2,1)}, u32[]{:S(2)}, u32[]{:S(2)}) collective-permute-start(bf16[384,1024]{1,0:T(8,128)(2,1)} %collective-permute-done.11.refs_9_.refs_7_), channel_id=1, source_target_pairs={{0,4},{4,0},{8,12},{12,8},{16,20},{20,16},{24,28},{28,24},{1,5},{5... | collective-permute-start | bytes 2359304 | tf_op jit(solution)/shard_map/ppermute | solution.py:303
  103.1 14.8 %collective-permute-start.5 = (bf16[256,1024]{1,0:T(8,128)(2,1)}, bf16[256,1024]{1,0:T(8,128)(2,1)}, u32[]{:S(2)}, u32[]{:S(2)}) collective-permute-start(bf16[256,1024]{1,0:T(8,128)(2,1)} %collective-permute-done.3.refs_2_), channel_id=1, source_target_pairs={{0,1},{1,0},{2,3},{3,2},{4,5},{5,4},{6,7},{7,6},{8,9},{9,8},{10,11... | collective-permute-start | bytes 1572872 | tf_op jit(solution)/shard_map/ppermute | solution.py:303
  124.9 10.8 %collective-permute-start.15 = (bf16[64,1536]{1,0:T(8,128)(2,1)S(1)}, bf16[64,1536]{1,0:T(8,128)(2,1)S(1)}, u32[]{:S(2)}, u32[]{:S(2)}) collective-permute-start(bf16[64,1536]{1,0:T(8,128)(2,1)S(1)} %get-tuple-element.36), channel_id=1, source_target_pairs={{0,1},{1,0},{2,3},{3,2},{4,5},{5,4},{6,7},{7,6},{8,9},{9,8},{10,11... | collective-permute-start | bytes 589832 | tf_op jit(solution)/shard_map/ppermute | solution.py:303
  126.9 17.1 %collective-permute-start.16 = (bf16[64,1536]{1,0:T(8,128)(2,1)S(1)}, bf16[64,1536]{1,0:T(8,128)(2,1)S(1)}, u32[]{:S(2)}, u32[]{:S(2)}) collective-permute-start(bf16[64,1536]{1,0:T(8,128)(2,1)S(1)} %get-tuple-element.37), channel_id=1, source_target_pairs={{0,2},{1,3},{2,0},{3,1},{4,6},{5,7},{6,4},{7,5},{8,10},{9,11},{10,... | collective-permute-start | bytes 589832 | tf_op jit(solution)/shard_map/ppermute | solution.py:303
  127.6 16.4 %collective-permute-start.17 = (bf16[64,1536]{1,0:T(8,128)(2,1)S(1)}, bf16[64,1536]{1,0:T(8,128)(2,1)S(1)}, u32[]{:S(2)}, u32[]{:S(2)}) collective-permute-start(bf16[64,1536]{1,0:T(8,128)(2,1)S(1)} %get-tuple-element.38), channel_id=1, source_target_pairs={{0,3},{1,2},{2,1},{3,0},{4,7},{5,6},{6,5},{7,4},{8,11},{9,10},{10,... | collective-permute-start | bytes 589832 | tf_op jit(solution)/shard_map/ppermute | solution.py:303
  (10 other events, 54.6 us)

commit v5 on v4

--- a/solution.py
+++ b/solution.py
@@ -55,98 +55,8 @@
     )(proj, table, qkv)
 
 
-def assemble_kernel(groups, sizes, place_ref, tokens_ref, *refs):
-    parts = refs[:groups]
-    looked_ref, qkv_ref, table, sems = refs[groups:]
-    table_rows, qkv_rows, firsts = sizes
-    half = qkv_rows // 2
-    depth = table.shape[1]
-    extra = qkv_ref.shape[1] - depth
-    place = place_ref[1]
-    table_copies, qkv_copies = [], []
-
-    def copy(source, target, number, into):
-        made = pltpu.make_async_copy(source, target, sems.at[number])
-        made.start()
-        into.append(made)
-
-    for n in range(groups):
-        g = jnp.bitwise_xor(place, n)
-        start = pl.multiple_of(g * table_rows, table_rows)
-        copy(
-            parts[n].at[pl.ds(firsts[n], table_rows)],
-            table.at[pl.ds(start, table_rows)],
-            4 * n,
-            table_copies,
-        )
-    for n in range(groups):
-        g = jnp.bitwise_xor(place, n)
-        at_qkv = firsts[n] + table_rows
-        start = pl.multiple_of(g * qkv_rows, qkv_rows)
-        copy(
-            parts[n].at[pl.ds(at_qkv, qkv_rows)],
-            qkv_ref.at[pl.ds(start, qkv_rows), pl.ds(0, depth)],
-            4 * n + 1,
-            qkv_copies,
-        )
-        for side in range(2):
-            start = pl.multiple_of(g * qkv_rows + side * half, half)
-            copy(
-                parts[n].at[pl.ds(at_qkv + qkv_rows, half), pl.ds(side * extra, extra)],
-                qkv_ref.at[pl.ds(start, half), pl.ds(depth, extra)],
-                4 * n + 2 + side,
-                qkv_copies,
-            )
-    columns = lax.broadcasted_iota(jnp.int32, (tokens_ref.shape[0], table.shape[0]), 1)
-    matches = (tokens_ref[...] == columns).astype(f32).astype(bf16)
-    for made in table_copies:
-        made.wait()
-    looked_ref[...] = jnp.dot(matches, table[...], preferred_element_type=f32).astype(bf16)
-    for made in qkv_copies:
-        made.wait()
-
-
-def assemble(place, tokens, parts, firsts, table_rows, qkv_rows, wide):
-    groups = len(parts)
-    frames_here = tokens.shape[0]
-    depth = parts[0].shape[1]
-    vmem = pl.BlockSpec(memory_space=pltpu.VMEM)
-    return pl.pallas_call(
-        functools.partial(assemble_kernel, groups, (table_rows, qkv_rows, firsts)),
-        out_shape=[
-            jax.ShapeDtypeStruct((frames_here, depth), bf16),
-            jax.ShapeDtypeStruct((groups * qkv_rows, wide), bf16),
-        ],
-        in_specs=[pl.BlockSpec(memory_space=pltpu.SMEM)] + [vmem] * (1 + groups),
-        out_specs=[vmem] * 2,
-        scratch_shapes=[
-            pltpu.VMEM((groups * table_rows, depth), bf16),
-            pltpu.SemaphoreType.DMA((4 * groups,)),
-        ],
-        compiler_params=pltpu.CompilerParams(vmem_limit_bytes=24 * 2**20),
-        name="lookup_and_qkv_rows",
-    )(place, tokens, *parts)
-
-
 def is_late(m):
     return (m % 2 == 1) & (m != 1)
-
-
-def add_products(late, books, pieces, where, refs, held, projected_ref):
-    here, group = where
-    rows_each = held.shape[2] * books // (1 + max(n for n, _, _ in pieces))
-    per_book = held.shape[2] // rows_each
-    for (n, row, count), ref in zip(pieces, refs):
-        owner = jnp.bitwise_xor(group, n)
-        book = owner // per_book
-        start = (owner % per_book) * rows_each + row
-
-        @pl.when(is_late(jnp.bitwise_xor(here, book)) == late)
-        def _():
-            columns = pl.ds(pl.multiple_of(start, 128), count)
-            projected_ref[...] += jnp.dot(
-                held[book, :, columns], ref[:count, :], preferred_element_type=f32
-            )
 
 
 def hold_blocks(blocks, here, gain_ref, held):
@@ -161,87 +71,164 @@
     return square
 
 
-def early_kernel(books, early, pieces, place_ref, gain_ref, *refs):
+def early_kernel(books, early, pieces, sizes, place_ref, tokens_ref, gain_ref, *refs):
     blocks = dict(zip(early, refs))
-    proj = refs[len(early) : len(early) + len(pieces)]
-    projected_ref, square_ref, held = refs[len(early) + len(pieces) :]
-    where = place_ref[0], place_ref[1]
-    square_ref[...] = hold_blocks(blocks, where[0], gain_ref, held)
+    parts = refs[len(early) : len(early) + len(pieces)]
+    outs = refs[len(early) + len(pieces) :]
+    projected_ref, square_ref, later_ref, looked_ref, qkv_ref, held, table, sems = outs
+    proj_rows, table_rows, qkv_rows = sizes
+    here, group = place_ref[0], place_ref[1]
+    width = held.shape[2]
+    per_book = width // proj_rows
+    half = qkv_rows // 2
+    depth = table.shape[1]
+    extra = qkv_ref.shape[1] - depth
+
+    moves = []
+    for (n, first), ref in zip(pieces, parts):
+        if first + ref.shape[0] <= proj_rows:
+            continue
+        g = jnp.bitwise_xor(group, n)
+        at_table = proj_rows - first
+        at_qkv = at_table + table_rows
+        at_extra = at_qkv + qkv_rows
+        start = pl.multiple_of(g * table_rows, table_rows)
+        moves.append(
+            (0, ref.at[pl.ds(at_table, table_rows)], table.at[pl.ds(start, table_rows)])
+        )
+        start = pl.multiple_of(g * qkv_rows, qkv_rows)
+        moves.append(
+            (
+                1,
+                ref.at[pl.ds(at_qkv, qkv_rows)],
+                qkv_ref.at[pl.ds(start, qkv_rows), pl.ds(0, depth)],
+            )
+        )
+        for side in range(2):
+            start = pl.multiple_of(g * qkv_rows + side * half, half)
+            moves.append(
+                (
+                    1,
+                    ref.at[pl.ds(at_extra, half), pl.ds(side * extra, extra)],
+                    qkv_ref.at[pl.ds(start, half), pl.ds(depth, extra)],
+                )
+            )
+    copies = [
+        (kind, pltpu.make_async_copy(source, target, sems.at[number]))
+        for number, (kind, source, target) in enumerate(moves)
+    ]
+    for _, made in copies:
+        made.start()
+
+    square_ref[...] = hold_blocks(blocks, here, gain_ref, held)
     projected_ref[...] = jnp.zeros_like(projected_ref)
-    add_products(False, books, pieces, where, proj, held, projected_ref)
-
-
-def project_early(place, gain, blocks, early, pieces, proj):
+    for (n, first), ref in zip(pieces, parts):
+        count = min(ref.shape[0], proj_rows - first)
+        owner = jnp.bitwise_xor(group, n)
+        book = owner // per_book
+        start = pl.multiple_of((owner % per_book) * proj_rows + first, 128)
+        late = is_late(jnp.bitwise_xor(here, book))
+
+        @pl.when(jnp.logical_not(late))
+        def _():
+            projected_ref[...] += jnp.dot(
+                held[book, :, pl.ds(start, count)], ref[:count, :], preferred_element_type=f32
+            )
+
+        @pl.when(late)
+        def _():
+            slot = jnp.bitwise_xor(here, book) // 2 - 1
+            later_ref[slot, pl.ds(start, count), :] = ref[:count, :]
+
+    columns = lax.broadcasted_iota(jnp.int32, (tokens_ref.shape[0], table.shape[0]), 1)
+    matches = (tokens_ref[...] == columns).astype(f32).astype(bf16)
+    for kind, made in copies:
+        if kind == 0:
+            made.wait()
+    looked_ref[...] = jnp.dot(matches, table[...], preferred_element_type=f32).astype(bf16)
+    for kind, made in copies:
+        if kind == 1:
+            made.wait()
+
+
+def project_early(place, tokens, gain, blocks, early, pieces, parts, sizes, wide):
     books = len(blocks)
     frames_here, width = blocks[0].shape
-    depth = proj[0].shape[1]
+    depth = parts[0].shape[1]
+    proj_rows, table_rows, qkv_rows = sizes
+    groups = books * width // proj_rows
     vmem = pl.BlockSpec(memory_space=pltpu.VMEM)
     return pl.pallas_call(
-        functools.partial(early_kernel, books, early, pieces),
+        functools.partial(early_kernel, books, early, pieces, sizes),
         out_shape=[
             jax.ShapeDtypeStruct((frames_here, depth), f32),
             jax.ShapeDtypeStruct((frames_here, 1), f32),
+            jax.ShapeDtypeStruct((books - len(early), width, depth), bf16),
+            jax.ShapeDtypeStruct((frames_here, depth), bf16),
+            jax.ShapeDtypeStruct((groups * qkv_rows, wide), bf16),
         ],
         in_specs=[pl.BlockSpec(memory_space=pltpu.SMEM)]
-        + [vmem] * (1 + len(early) + len(pieces)),
-        out_specs=[vmem] * 2,
-        scratch_shapes=[pltpu.VMEM((books, frames_here, width), bf16)],
-        compiler_params=pltpu.CompilerParams(vmem_limit_bytes=24 * 2**20),
-        name="project_early_blocks",
-    )(place, gain, *[blocks[m] for m in early], *proj)
-
-
-def late_kernel(books, late, pieces, place_ref, gain_ref, *refs):
+        + [vmem] * (2 + len(early) + len(parts)),
+        out_specs=[vmem] * 5,
+        scratch_shapes=[
+            pltpu.VMEM((books, frames_here, width), bf16),
+            pltpu.VMEM((groups * table_rows, depth), bf16),
+            pltpu.SemaphoreType.DMA((4 * groups,)),
+        ],
+        compiler_params=pltpu.CompilerParams(vmem_limit_bytes=36 * 2**20),
+        cost_estimate=pl.CostEstimate(flops=0, bytes_accessed=0, transcendentals=0),
+        name="early_products_and_lookup",
+    )(place, tokens, gain, *[blocks[m] for m in early], *parts)
+
+
+def late_kernel(books, late, place_ref, gain_ref, *refs):
     blocks = dict(zip(late, refs))
-    refs = refs[len(late) :]
-    proj = refs[: len(pieces)]
-    early_ref, square_ref, looked_ref, depth_gain_ref, qkv_ref = refs[
-        len(pieces) : len(pieces) + 5
+    later_ref, early_ref, square_ref, looked_ref, depth_gain_ref, qkv_ref = refs[
+        len(late) : len(late) + 6
     ]
-    refs = refs[len(pieces) + 5 :]
+    refs = refs[len(late) + 6 :]
     outs = refs[:books]
-    held, projected_ref, packed = refs[books:]
-    where = place_ref[0], place_ref[1]
+    held, packed = refs[books:]
+    here = place_ref[0]
     frames_here, width = held.shape[1:]
-    square = square_ref[...] + hold_blocks(blocks, where[0], gain_ref, held)
-    projected_ref[...] = early_ref[...]
-    add_products(True, books, pieces, where, proj, held, projected_ref)
-    projected = projected_ref[...] * lax.rsqrt(square / (books * width) + 1e-05)
+    square = square_ref[...] + hold_blocks(blocks, here, gain_ref, held)
+    projected = early_ref[...]
+    for slot, m in enumerate(late):
+        projected = projected + jnp.dot(
+            held[jnp.bitwise_xor(here, m)], later_ref[slot], preferred_element_type=f32
+        )
+    projected = projected * lax.rsqrt(square / (books * width) + 1e-05)
     depth_in = (projected + looked_ref[...].astype(f32)).astype(bf16).astype(f32)
     moment = jnp.mean(depth_in * depth_in, axis=-1, keepdims=True)
     depth_normed = (depth_in * lax.rsqrt(moment + 1e-05) * depth_gain_ref[...]).astype(bf16)
     packed[...] = jnp.dot(depth_normed, qkv_ref[...], preferred_element_type=f32).astype(bf16)
     rows = frames_here // books
     for m in range(books):
-        start = pl.multiple_of(jnp.bitwise_xor(where[0], m) * rows, rows)
+        start = pl.multiple_of(jnp.bitwise_xor(here, m) * rows, rows)
         outs[m][...] = packed[pl.ds(start, rows), :]
 
 
-def project_late(
-    place, gain, blocks, late, pieces, proj, projected, square, looked, depth_gain, qkv
-):
+def project_late(place, gain, blocks, late, later, projected, square, looked, depth_gain, qkv):
     books = len(blocks)
     frames_here, width = blocks[0].shape
-    depth, wide = qkv.shape
+    wide = qkv.shape[1]
     vmem = pl.BlockSpec(memory_space=pltpu.VMEM)
     return pl.pallas_call(
-        functools.partial(late_kernel, books, late, pieces),
+        functools.partial(late_kernel, books, late),
         out_shape=[jax.ShapeDtypeStruct((frames_here // books, wide), bf16)] * books,
-        in_specs=[pl.BlockSpec(memory_space=pltpu.SMEM)]
-        + [vmem] * (1 + len(late) + len(pieces) + 5),
+        in_specs=[pl.BlockSpec(memory_space=pltpu.SMEM)] + [vmem] * (len(late) + 7),
         out_specs=[vmem] * books,
         scratch_shapes=[
             pltpu.VMEM((books, frames_here, width), bf16),
-            pltpu.VMEM((frames_here, depth), f32),
             pltpu.VMEM((frames_here, wide), bf16),
         ],
-        compiler_params=pltpu.CompilerParams(vmem_limit_bytes=28 * 2**20),
-        name="project_late_blocks_and_qkv",
+        compiler_params=pltpu.CompilerParams(vmem_limit_bytes=24 * 2**20),
+        name="late_products_and_qkv",
     )(
         place,
         gain,
         *[blocks[m] for m in late],
-        *proj,
+        later,
         projected,
         square,
         looked,
@@ -352,7 +339,10 @@
     for n in near:
         parts[n] = [(0, swap(rows, "frames", n))]
 
+    parts[1] = [(0, swap(rows, "frames", 1))]
     sums[books - 2] = lax.optimization_barrier(share(books - 2, rows))
+    for m in range(books - 3, 0, -1):
+        sums[m] = lax.optimization_barrier(share(m, parts[1][0][1]))
     distance = 1
     while distance < books:
         came = None
@@ -361,20 +351,13 @@
             if came is not None:
                 going = after(going, came, sums[m + distance])
             came = swap(going, "book", distance)
+            sums[m ^ distance] = sums[m ^ distance] + came.astype(f32)
             if m == books - 1:
-                for n in range(books - 3, -1, -1):
-                    sums[n] = lax.optimization_barrier(share(n, came))
+                sums[0] = lax.optimization_barrier(share(0, came))
                 sums[0] = sums[0] + residual.astype(f32)
-            sums[m ^ distance] = sums[m ^ distance] + came.astype(f32)
         distance *= 2
 
     blocks = {0: sums[0].astype(bf16)}
-    distance = books // 2
-    while distance:
-        for m in sorted(blocks):
-            going = blocks[m] if m == 0 else after(blocks[m], blocks[distance])
-            blocks[m ^ distance] = swap(going, "book", distance)
-        distance //= 2
 
     arrived = after([parts[n][0][1] for n in near], blocks[0])
     for n, value in zip(near, arrived):
@@ -390,33 +373,41 @@
             parts[n] = [(0, upper), (cut, lower)]
         else:
             parts[n] = [(0, swap(rows, "frames", n))]
-    for n in range(0, groups, 2):
+    for n in range(2, groups, 2):
         parts[n + 1] = [(first, swap(value, "frames", 1)) for first, value in parts[n]]
-    looked, qkv = assemble(
+
+    near_there = [parts[n + 1][0][1] for n in near]
+    distance = books // 2
+    while distance:
+        for m in sorted(blocks):
+            going = blocks[m]
+            if m:
+                going = after(going, blocks[distance])
+            elif distance == 1:
+                going = after(going, *near_there)
+            blocks[m ^ distance] = swap(going, "book", distance)
+        distance //= 2
+
+    pieces = [(n, first) for n in range(groups) for first, _ in parts[n]]
+    early = [m for m in range(books) if not is_late(m)]
+    late = [m for m in range(books) if is_late(m)]
+    projected, square, later, looked, qkv = project_early(
         place,
         token_ids,
-        [parts[n][-1][1] for n in range(groups)],
-        [proj_rows - parts[n][-1][0] for n in range(groups)],
-        table_rows,
-        qkv_rows,
+        gain,
+        blocks,
+        early,
+        pieces,
+        [value for n in range(groups) for _, value in parts[n]],
+        (proj_rows, table_rows, qkv_rows),
         wide,
     )
-
-    pieces, proj = [], []
-    for n in range(groups):
-        for first, value in parts[n]:
-            pieces.append((n, first, min(value.shape[0], proj_rows - first)))
-            proj.append(value)
-    early = [m for m in range(books) if not is_late(m)]
-    late = [m for m in range(books) if is_late(m)]
-    projected, square = project_early(place, gain, blocks, early, pieces, proj)
     packed = project_late(
         place,
         gain,
         blocks,
         late,
-        pieces,
-        proj,
+        later,
         projected,
         square,
         looked,

time: 148 us -> 136 us (0.919)
  waiting for transfers between devices: 77.5 us -> 60.6 us
  local copies, waits for them, and re-layouts: 4.97 us -> 13.7 us
  Pallas kernels: 21.7 us -> 16.7 us
  starting transfers between devices: 21.1 us -> 22.7 us
    ppermute x18, waiting for transfers between devices: 77.5 us -> 60.6 us  [swap(): lax.ppermute(value, axis, [(i, i ^ distance) for i in range(lax.axis_size...]
    unnamed x33, local copies, waits for them, and re-layouts: 3.54 us -> 12.5 us
    pallas_call x3 -> x2, Pallas kernels: 18.7 us -> 13.7 us  [the longest x1 10.7 us: project_early(): pl.pallas_call(functools.partial(early_kernel, books, early, pieces, size...]
    ppermute x18, starting transfers between devices: 21.1 us -> 22.7 us  [swap(): lax.ppermute(value, axis, [(i, i ^ distance) for i in range(lax.axis_size...]
  transfers between devices with their start and end apart: 18 -> 18, of which waited for: 8 -> 8; matrix products, arithmetic and copies ran while one was open for 12% -> 13% of each run, Pallas kernels for 8% -> 8%
where the time goes in v5:
time: 136 us
  waiting for transfers between devices  60.6 us (45%)
  starting transfers between devices  22.7 us (17%)
  Pallas kernels  16.7 us (12%)
  matrix products  15.1 us (11%)
  local copies, waits for them, and re-layouts  13.7 us (10%)
  other arithmetic  6.47 us (5%)
    ppermute x18, waiting for transfers between devices, swap(): lax.ppermute(value, axis, [(i, i ^ distance) for i in range(lax.axis_size...  60.6 us
    ppermute x18, starting transfers between devices, swap(): lax.ppermute(value, axis, [(i, i ^ distance) for i in range(lax.axis_size...  22.7 us
    dot_general x4, matrix products, share(): return jnp.dot(factor, block, preferred_element_type=f32)  15.1 us
    unnamed x33, local copies, waits for them, and re-layouts  12.5 us
    pallas_call x1, Pallas kernels, project_early(): pl.pallas_call(functools.partial(early_kernel, books, early, pieces, size...  10.7 us
    pallas_call x1, Pallas kernels, project_late(): pl.pallas_call(functools.partial(late_kernel, books, late), out_shape=[ja...  3 us
    pallas_call x1, Pallas kernels, attend(): pl.pallas_call(functools.partial(attend_kernel, books), out_shape=jax.Sha...  2.79 us
  transfers between devices with their start and end apart: 18, of which 8 were waited for; matrix products, arithmetic and copies ran while one was open for 13% of the time, Pallas kernels for 8%

profile of v5, /device:TPU:0, one launch (start us, length us, event | category | flops | bytes accessed | tf_op | source)
XLA Modules:
  0.0 135.6 jit_solution(11014399090140199783)
XLA Ops:
  0.0 1.9 %fusion.12 = bf16[256,1536]{1,0:T(8,128)(2,1)S(1)} fusion(bf16[256,1536]{1,0:T(8,128)(2,1)} %param.11, bf16[256,1536]{1,0:T(8,128)(2,1)} %param.10), kind=kLoop, calls=%fused_computation.14 | loop fusion | flops 3145728 | bytes 2359296 | tf_op jit(solution)/shard_map/convert_element_type | solution.py:325
  1.9 4.0 %fusion.13 = bf16[256,1024]{1,0:T(8,128)(2,1)} fusion(bf16[256,1536]{1,0:T(8,128)(2,1)S(1)} %fusion.12, bf16[1536,4096]{1,0:T(8,128)(2,1)} %param.12, s32[]{:T(128)S(6)} %select_n.12), kind=kOutput, calls=%fused_computation.15 | convolution fusion | flops 805568512 | bytes 4456452 | tf_op jit(solution)/shard_map/dot_general | solution.py:331
  6.6 2.6 %collective-permute-start = (bf16[256,1024]{1,0:T(8,128)(2,1)}, bf16[256,1024]{1,0:T(8,128)(2,1)}, u32[]{:S(2)}, u32[]{:S(2)}) collective-permute-start(bf16[256,1024]{1,0:T(8,128)(2,1)} %fusion.13), channel_id=1, source_target_pairs={{0,1},{1,0},{2,3},{3,2},{4,5},{5,4},{6,7},{7,6},{8,9},{9,8},{10,11... | collective-permute-start | bytes 1572872 | tf_op jit(solution)/shard_map/ppermute | solution.py:290
  12.3 4.1 %fusion = f32[256,1024]{1,0:T(8,128)} fusion(bf16[256,1536]{1,0:T(8,128)(2,1)} %copy-done.13, bf16[1536,4096]{1,0:T(8,128)(2,1)} %param.12, s32[]{:T(128)S(6)} %select_n.15), kind=kOutput, calls=%fused_computation | convolution fusion | flops 805306368 | bytes 4980740 | tf_op jit(solution)/shard_map/dot_general | solution.py:331
  16.4 5.7 %collective-permute-done = bf16[256,1024]{1,0:T(8,128)(2,1)} collective-permute-done((bf16[256,1024]{1,0:T(8,128)(2,1)}, bf16[256,1024]{1,0:T(8,128)(2,1)}, u32[]{:S(2)}, u32[]{:S(2)}) %collective-permute-start) | collective-permute-done | bytes 524320 | tf_op jit(solution)/shard_map/ppermute | solution.py:290
  22.1 2.3 %convert_add_fusion = bf16[256,1024]{1,0:T(8,128)(2,1)} fusion(f32[256,1024]{1,0:T(8,128)} %fusion, bf16[256,1024]{1,0:T(8,128)(2,1)} %collective-permute-done), kind=kLoop, calls=%fused_computation.17 | loop fusion | flops 786432 | bytes 2097152 | tf_op jit(solution)/shard_map/add | solution.py:354
  24.4 2.8 %collective-permute-start.3 = (bf16[256,1024]{1,0:T(8,128)(2,1)}, bf16[256,1024]{1,0:T(8,128)(2,1)}, u32[]{:S(2)}, u32[]{:S(2)}) collective-permute-start(bf16[256,1024]{1,0:T(8,128)(2,1)} %convert_add_fusion), channel_id=1, source_target_pairs={{0,2},{1,3},{2,0},{3,1},{4,6},{5,7},{6,4},{7,5},{8,10},{9,11},{10,... | collective-permute-start | bytes 1572872 | tf_op jit(solution)/shard_map/ppermute | solution.py:290
  27.2 3.9 %fusion.2 = bf16[256,1024]{1,0:T(8,128)(2,1)} fusion(bf16[256,1536]{1,0:T(8,128)(2,1)} %copy-done.13, bf16[1536,4096]{1,0:T(8,128)(2,1)} %param.12, s32[]{:T(128)S(6)} %select_n.14), kind=kOutput, calls=%fused_computation.2 | convolution fusion | flops 805306368 | bytes 4456452 | tf_op jit(solution)/shard_map/dot_general | solution.py:331
  32.7 3.2 %fusion.4 = f32[256,1024]{1,0:T(8,128)S(1)} fusion(bf16[256,1536]{1,0:T(8,128)(2,1)} %copy-done.13, bf16[1536,4096]{1,0:T(8,128)(2,1)} %param.12, s32[]{:T(128)S(6)} %select_n.13), kind=kOutput, calls=%fused_computation.4 | convolution fusion | flops 805306368 | bytes 4980740 | tf_op jit(solution)/shard_map/dot_general | solution.py:331
  35.8 14.8 %collective-permute-done.3 = bf16[256,1024]{1,0:T(8,128)(2,1)} collective-permute-done((bf16[256,1024]{1,0:T(8,128)(2,1)}, bf16[256,1024]{1,0:T(8,128)(2,1)}, u32[]{:S(2)}, u32[]{:S(2)}) %collective-permute-start.3) | collective-permute-done | bytes 524320 | tf_op jit(solution)/shard_map/ppermute | solution.py:290
  50.6 4.1 %collective-permute-done.2 = bf16[256,1024]{1,0:T(8,128)(2,1)} collective-permute-done((bf16[256,1024]{1,0:T(8,128)(2,1)}, bf16[256,1024]{1,0:T(8,128)(2,1)}, u32[]{:S(2)}, u32[]{:S(2)}) %collective-permute-start.2) | collective-permute-done | bytes 524320 | tf_op jit(solution)/shard_map/ppermute | solution.py:290
  57.0 1.6 %collective-permute-start.12 = (bf16[448,1024]{1,0:T(8,128)(2,1)S(1)}, bf16[448,1024]{1,0:T(8,128)(2,1)}, u32[]{:S(2)}, u32[]{:S(2)}) collective-permute-start(bf16[448,1024]{1,0:T(8,128)(2,1)S(1)} %slice.7), channel_id=1, source_target_pairs={{0,16},{4,20},{8,24},{12,28},{16,0},{20,4},{24,8},{28,12},{1,17},{... | collective-permute-start | bytes 2752520 | tf_op jit(solution)/shard_map/ppermute | solution.py:290
  64.1 2.5 %collective-permute-start.9 = (bf16[256,1024]{1,0:T(8,128)(2,1)S(1)}, bf16[256,1024]{1,0:T(8,128)(2,1)S(1)}, u32[]{:S(2)}, u32[]{:S(2)}) collective-permute-start(bf16[256,1024]{1,0:T(8,128)(2,1)S(1)} %add_convert_fusion.refs_0_), channel_id=1, source_target_pairs={{0,1},{1,0},{2,3},{3,2},{4,5},{5,4},{6,7},{7,6},{8,9},{9,8},{10,11... | collective-permute-start | bytes 1572872 | tf_op jit(solution)/shard_map/ppermute | solution.py:290
  66.6 12.8 %collective-permute-done.12.refs_10_ = bf16[448,1024]{1,0:T(8,128)(2,1)} collective-permute-done((bf16[448,1024]{1,0:T(8,128)(2,1)S(1)}, bf16[448,1024]{1,0:T(8,128)(2,1)}, u32[]{:S(2)}, u32[]{:S(2)}) %collective-permute-start.12) | collective-permute-done | bytes 917536 | tf_op jit(solution)/shard_map/ppermute | solution.py:290
  80.0 6.7 %collective-permute-done.4.refs_2_ = bf16[256,1024]{1,0:T(8,128)(2,1)} collective-permute-done((bf16[256,1024]{1,0:T(8,128)(2,1)S(1)}, bf16[256,1024]{1,0:T(8,128)(2,1)}, u32[]{:S(2)}, u32[]{:S(2)}) %collective-permute-start.4) | collective-permute-done | bytes 524320 | tf_op jit(solution)/shard_map/ppermute | solution.py:290
  86.7 2.4 %collective-permute-done.9.refs_1_ = bf16[256,1024]{1,0:T(8,128)(2,1)S(1)} collective-permute-done((bf16[256,1024]{1,0:T(8,128)(2,1)S(1)}, bf16[256,1024]{1,0:T(8,128)(2,1)S(1)}, u32[]{:S(2)}, u32[]{:S(2)}) %collective-permute-start.9) | collective-permute-done | bytes 524320 | tf_op jit(solution)/shard_map/ppermute | solution.py:290
  96.5 10.7 %early_products_and_lookup.1 = (f32[256,1024]{1,0:T(8,128)S(1)}, f32[256,1]{1,0:T(8,128)S(1)}, bf16[1,1024,1024]{2,1,0:T(8,128)(2,1)}, bf16[256,1024]{1,0:T(8,128)(2,1)S(1)}, bf16[1024,1536]{1,0:T(8,128)(2,1)}) custom-call(s32[2]{0:T(128)S(1)} %pad_add_fusion.place_ref, s32[256,1]{1,0:T(8,128)S(1)} %copy.11.tokens_ref, f32[1,4096]{1,0:T(1,128)S(1)} %bitcast.13, ...), custom_call_target="tpu_custom_call" | custom-call | tf_op jit(solution)/shard_map/early_products_and_lookup/pallas_call | solution.py:161
  107.3 1.9 %copy-done = bf16[1024,1536]{1,0:T(8,128)(2,1)S(1)} copy-done((bf16[1024,1536]{1,0:T(8,128)(2,1)S(1)}, bf16[1024,1536]{1,0:T(8,128)(2,1)}, u32[]{:S(2)}) %copy-start) | copy-done | bytes 3145752
  109.2 1.6 %copy-done.1 = bf16[1,1024,1024]{2,1,0:T(8,128)(2,1)S(1)} copy-done((bf16[1,1024,1024]{2,1,0:T(8,128)(2,1)S(1)}, bf16[1,1024,1024]{2,1,0:T(8,128)(2,1)}, u32[]{:S(2)}) %copy-start.1) | copy-done | bytes 2097176
  110.8 3.0 %late_products_and_qkv.1 = (bf16[64,1536]{1,0:T(8,128)(2,1)S(1)}, bf16[64,1536]{1,0:T(8,128)(2,1)S(1)}, bf16[64,1536]{1,0:T(8,128)(2,1)S(1)}, bf16[64,1536]{1,0:T(8,128)(2,1)S(1)}) custom-call(s32[2]{0:T(128)S(1)} %pad_add_fusion.place_ref, f32[1,4096]{1,0:T(1,128)S(1)} %bitcast.14, bf16[256,1024]{1,0:T(8,128)(2,1)} %collective-permute-done.10.refs_0_, ...), custom_call_target="tpu_custom_call" | custom-call | tf_op jit(solution)/shard_map/late_products_and_qkv/pallas_call | solution.py:216
  113.8 2.6 %collective-permute-start.15 = (bf16[64,1536]{1,0:T(8,128)(2,1)S(1)}, bf16[64,1536]{1,0:T(8,128)(2,1)S(1)}, u32[]{:S(2)}, u32[]{:S(2)}) collective-permute-start(bf16[64,1536]{1,0:T(8,128)(2,1)S(1)} %get-tuple-element.42), channel_id=1, source_target_pairs={{0,1},{1,0},{2,3},{3,2},{4,5},{5,4},{6,7},{7,6},{8,9},{9,8},{10,11... | collective-permute-start | bytes 589832 | tf_op jit(solution)/shard_map/ppermute | solution.py:290
  118.8 3.7 %collective-permute-done.15.refs_1_ = bf16[64,1536]{1,0:T(8,128)(2,1)S(1)} collective-permute-done((bf16[64,1536]{1,0:T(8,128)(2,1)S(1)}, bf16[64,1536]{1,0:T(8,128)(2,1)S(1)}, u32[]{:S(2)}, u32[]{:S(2)}) %collective-permute-start.15) | collective-permute-done | bytes 196640 | tf_op jit(solution)/shard_map/ppermute | solution.py:290
  122.5 10.2 %collective-permute-done.16.refs_2_ = bf16[64,1536]{1,0:T(8,128)(2,1)S(1)} collective-permute-done((bf16[64,1536]{1,0:T(8,128)(2,1)S(1)}, bf16[64,1536]{1,0:T(8,128)(2,1)S(1)}, u32[]{:S(2)}, u32[]{:S(2)}) %collective-permute-start.16) | collective-permute-done | bytes 196640 | tf_op jit(solution)/shard_map/ppermute | solution.py:290
  132.8 2.8 %attend_books.1 = bf16[64,4,512]{2,1,0:T(4,128)(2,1)} custom-call(s32[2]{0:T(128)S(1)} %pad_add_fusion.place_ref, bf16[64,1536]{1,0:T(8,128)(2,1)S(1)} %get-tuple-element.41.refs_0_, bf16[64,1536]{1,0:T(8,128)(2,1)S(1)} %collective-permute-done.15.refs_1_, bf16[64,1536]{1,0:T(8,128)(2,1)S(1)} %collective-permute-done.16.refs_2_, ...), custom_call_target="tpu_custom_call" | custom-call | tf_op jit(solution)/shard_map/attend_books/pallas_call | solution.py:278
  (61 shorter events, 23.4 us)
Async XLA Ops:
  1.9 4.0 %copy-start.13 = (bf16[256,1536]{1,0:T(8,128)(2,1)}, bf16[256,1536]{1,0:T(8,128)(2,1)S(1)}, u32[]{:S(2)}) copy-start(bf16[256,1536]{1,0:T(8,128)(2,1)S(1)} %fusion.12) | copy-start | bytes 2359300
  1.9 4.0 %copy-start.8 = (bf16[1,512,1024]{2,1,0:T(8,128)(2,1)S(1)}, bf16[1,512,1024]{2,1,0:T(8,128)(2,1)}, u32[]{:S(2)}) copy-start(bf16[1,512,1024]{2,1,0:T(8,128)(2,1)} %param.15) | copy-start | bytes 3145732
  1.9 4.0 %copy-start.11 = (bf16[1,128,1536]{2,1,0:T(8,128)(2,1)S(1)}, bf16[1,128,1536]{2,1,0:T(8,128)(2,1)}, u32[]{:S(2)}) copy-start(bf16[1,128,1536]{2,1,0:T(8,128)(2,1)} %param.19) | copy-start | bytes 1179652
  6.1 21.1 %collective-permute-start.1 = (bf16[832,1024]{1,0:T(8,128)(2,1)S(1)}, bf16[832,1024]{1,0:T(8,128)(2,1)}, u32[]{:S(2)}, u32[]{:S(2)}) collective-permute-start(bf16[832,1024]{1,0:T(8,128)(2,1)S(1)} %pack_weight_rows.1.refs_3_), channel_id=1, source_target_pairs={{0,4},{4,0},{8,12},{12,8},{16,20},{20,16},{24,28},{28,24},{1,5},{5... | collective-permute-start | bytes 5111816 | tf_op jit(solution)/shard_map/ppermute | solution.py:290
  6.6 15.5 %collective-permute-start = (bf16[256,1024]{1,0:T(8,128)(2,1)}, bf16[256,1024]{1,0:T(8,128)(2,1)}, u32[]{:S(2)}, u32[]{:S(2)}) collective-permute-start(bf16[256,1024]{1,0:T(8,128)(2,1)} %fusion.13), channel_id=1, source_target_pairs={{0,1},{1,0},{2,3},{3,2},{4,5},{5,4},{6,7},{7,6},{8,9},{9,8},{10,11... | collective-permute-start | bytes 1572872 | tf_op jit(solution)/shard_map/ppermute | solution.py:290
  9.3 47.0 %collective-permute-start.5 = (bf16[832,1024]{1,0:T(8,128)(2,1)S(1)}, bf16[832,1024]{1,0:T(8,128)(2,1)S(1)}, u32[]{:S(2)}, u32[]{:S(2)}) collective-permute-start(bf16[832,1024]{1,0:T(8,128)(2,1)S(1)} %pack_weight_rows.1.refs_3_), channel_id=1, source_target_pairs={{0,8},{4,12},{8,0},{12,4},{16,24},{20,28},{24,16},{28,20},{1,9},{5... | collective-permute-start | bytes 5111816 | tf_op jit(solution)/shard_map/ppermute | solution.py:290
  10.8 45.5 %collective-permute-start.6 = (bf16[832,1024]{1,0:T(8,128)(2,1)S(1)}, bf16[832,1024]{1,0:T(8,128)(2,1)}, u32[]{:S(2)}, u32[]{:S(2)}) collective-permute-start(bf16[832,1024]{1,0:T(8,128)(2,1)S(1)} %pack_weight_rows.1.refs_3_), channel_id=1, source_target_pairs={{0,16},{4,20},{8,24},{12,28},{16,0},{20,4},{24,8},{28,12},{1,17},{... | collective-permute-start | bytes 5111816 | tf_op jit(solution)/shard_map/ppermute | solution.py:290
  24.4 26.2 %collective-permute-start.3 = (bf16[256,1024]{1,0:T(8,128)(2,1)}, bf16[256,1024]{1,0:T(8,128)(2,1)}, u32[]{:S(2)}, u32[]{:S(2)}) collective-permute-start(bf16[256,1024]{1,0:T(8,128)(2,1)} %convert_add_fusion), channel_id=1, source_target_pairs={{0,2},{1,3},{2,0},{3,1},{4,6},{5,7},{6,4},{7,5},{8,10},{9,11},{10,... | collective-permute-start | bytes 1572872 | tf_op jit(solution)/shard_map/ppermute | solution.py:290
  31.1 23.7 %collective-permute-start.2 = (bf16[256,1024]{1,0:T(8,128)(2,1)}, bf16[256,1024]{1,0:T(8,128)(2,1)}, u32[]{:S(2)}, u32[]{:S(2)}) collective-permute-start(bf16[256,1024]{1,0:T(8,128)(2,1)} %fusion.2), channel_id=1, source_target_pairs={{0,1},{1,0},{2,3},{3,2},{4,5},{5,4},{6,7},{7,6},{8,9},{9,8},{10,11... | collective-permute-start | bytes 1572872 | tf_op jit(solution)/shard_map/ppermute | solution.py:290
  32.7 22.1 %copy-start.14 = (bf16[256,1024]{1,0:T(8,128)(2,1)S(1)}, bf16[256,1024]{1,0:T(8,128)(2,1)}, u32[]{:S(2)}) copy-start(bf16[256,1024]{1,0:T(8,128)(2,1)} %param.13) | copy-start | bytes 1572868
  35.8 54.1 %copy-start.15 = (bf16[4096]{0:T(1024)(128)(2,1)S(1)}, bf16[4096]{0:T(1024)(128)(2,1)}, u32[]{:S(2)}) copy-start(bf16[4096]{0:T(1024)(128)(2,1)} %param.14) | copy-start | bytes 24580
  56.3 6.7 %copy-start.2 = (bf16[256,1024]{1,0:T(8,128)(2,1)}, bf16[256,1024]{1,0:T(8,128)(2,1)S(1)}, u32[]{:S(2)}) copy-start(bf16[256,1024]{1,0:T(8,128)(2,1)S(1)} %add_convert_fusion.refs_0_) | copy-start | bytes 1572868
  56.3 5.4 %collective-permute-start.7 = (bf16[832,1024]{1,0:T(8,128)(2,1)S(1)}, bf16[832,1024]{1,0:T(8,128)(2,1)S(1)}, u32[]{:S(2)}, u32[]{:S(2)}) collective-permute-start(bf16[832,1024]{1,0:T(8,128)(2,1)S(1)} %collective-permute-done.5.refs_5_), channel_id=1, source_target_pairs={{0,4},{4,0},{8,12},{12,8},{16,20},{20,16},{24,28},{28,24},{1,5},{5... | collective-permute-start | bytes 5111816 | tf_op jit(solution)/shard_map/ppermute | solution.py:290
  56.4 6.5 %collective-permute-start.8 = (bf16[832,1024]{1,0:T(8,128)(2,1)}, bf16[832,1024]{1,0:T(8,128)(2,1)S(1)}, u32[]{:S(2)}, u32[]{:S(2)}) collective-permute-start(bf16[832,1024]{1,0:T(8,128)(2,1)} %collective-permute-done.6.refs_7_), channel_id=1, source_target_pairs={{0,4},{4,0},{8,12},{12,8},{16,20},{20,16},{24,28},{28,24},{1,5},{5... | collective-permute-start | bytes 5111816 | tf_op jit(solution)/shard_map/ppermute | solution.py:290
  57.0 22.5 %collective-permute-start.12 = (bf16[448,1024]{1,0:T(8,128)(2,1)S(1)}, bf16[448,1024]{1,0:T(8,128)(2,1)}, u32[]{:S(2)}, u32[]{:S(2)}) collective-permute-start(bf16[448,1024]{1,0:T(8,128)(2,1)S(1)} %slice.7), channel_id=1, source_target_pairs={{0,16},{4,20},{8,24},{12,28},{16,0},{20,4},{24,8},{28,12},{1,17},{... | collective-permute-start | bytes 2752520 | tf_op jit(solution)/shard_map/ppermute | solution.py:290
  59.7 19.7 %collective-permute-start.11 = (bf16[384,1024]{1,0:T(8,128)(2,1)S(1)}, bf16[384,1024]{1,0:T(8,128)(2,1)}, u32[]{:S(2)}, u32[]{:S(2)}) collective-permute-start(bf16[384,1024]{1,0:T(8,128)(2,1)S(1)} %slice.6), channel_id=1, source_target_pairs={{0,8},{4,12},{8,0},{12,4},{16,24},{20,28},{24,16},{28,20},{1,9},{5... | collective-permute-start | bytes 2359304 | tf_op jit(solution)/shard_map/ppermute | solution.py:290
  61.3 25.4 %collective-permute-start.4 = (bf16[256,1024]{1,0:T(8,128)(2,1)S(1)}, bf16[256,1024]{1,0:T(8,128)(2,1)}, u32[]{:S(2)}, u32[]{:S(2)}) collective-permute-start(bf16[256,1024]{1,0:T(8,128)(2,1)S(1)} %add_convert_fusion.refs_0_), channel_id=1, source_target_pairs={{0,2},{1,3},{2,0},{3,1},{4,6},{5,7},{6,4},{7,5},{8,10},{9,11},{10,... | collective-permute-start | bytes 1572872 | tf_op jit(solution)/shard_map/ppermute | solution.py:290
  64.1 25.0 %collective-permute-start.9 = (bf16[256,1024]{1,0:T(8,128)(2,1)S(1)}, bf16[256,1024]{1,0:T(8,128)(2,1)S(1)}, u32[]{:S(2)}, u32[]{:S(2)}) collective-permute-start(bf16[256,1024]{1,0:T(8,128)(2,1)S(1)} %add_convert_fusion.refs_0_), channel_id=1, source_target_pairs={{0,1},{1,0},{2,3},{3,2},{4,5},{5,4},{6,7},{7,6},{8,9},{9,8},{10,11... | collective-permute-start | bytes 1572872 | tf_op jit(solution)/shard_map/ppermute | solution.py:290
  79.5 12.1 %collective-permute-start.14 = (bf16[448,1024]{1,0:T(8,128)(2,1)}, bf16[448,1024]{1,0:T(8,128)(2,1)}, u32[]{:S(2)}, u32[]{:S(2)}) collective-permute-start(bf16[448,1024]{1,0:T(8,128)(2,1)} %collective-permute-done.12.refs_10_), channel_id=1, source_target_pairs={{0,4},{4,0},{8,12},{12,8},{16,20},{20,16},{24,28},{28,24},{1,5},{5... | collective-permute-start | bytes 2752520 | tf_op jit(solution)/shard_map/ppermute | solution.py:290
  79.5 12.1 %collective-permute-start.13 = (bf16[384,1024]{1,0:T(8,128)(2,1)}, bf16[384,1024]{1,0:T(8,128)(2,1)}, u32[]{:S(2)}, u32[]{:S(2)}) collective-permute-start(bf16[384,1024]{1,0:T(8,128)(2,1)} %collective-permute-done.11.refs_9_), channel_id=1, source_target_pairs={{0,4},{4,0},{8,12},{12,8},{16,20},{20,16},{24,28},{28,24},{1,5},{5... | collective-permute-start | bytes 2359304 | tf_op jit(solution)/shard_map/ppermute | solution.py:290
  89.9 17.3 %collective-permute-start.10 = (bf16[256,1024]{1,0:T(8,128)(2,1)}, bf16[256,1024]{1,0:T(8,128)(2,1)}, u32[]{:S(2)}, u32[]{:S(2)}) collective-permute-start(bf16[256,1024]{1,0:T(8,128)(2,1)} %collective-permute-done.4.refs_2_), channel_id=1, source_target_pairs={{0,1},{1,0},{2,3},{3,2},{4,5},{5,4},{6,7},{7,6},{8,9},{9,8},{10,11... | collective-permute-start | bytes 1572872 | tf_op jit(solution)/shard_map/ppermute | solution.py:290
  113.8 8.8 %collective-permute-start.15 = (bf16[64,1536]{1,0:T(8,128)(2,1)S(1)}, bf16[64,1536]{1,0:T(8,128)(2,1)S(1)}, u32[]{:S(2)}, u32[]{:S(2)}) collective-permute-start(bf16[64,1536]{1,0:T(8,128)(2,1)S(1)} %get-tuple-element.42), channel_id=1, source_target_pairs={{0,1},{1,0},{2,3},{3,2},{4,5},{5,4},{6,7},{7,6},{8,9},{9,8},{10,11... | collective-permute-start | bytes 589832 | tf_op jit(solution)/shard_map/ppermute | solution.py:290
  116.4 16.4 %collective-permute-start.16 = (bf16[64,1536]{1,0:T(8,128)(2,1)S(1)}, bf16[64,1536]{1,0:T(8,128)(2,1)S(1)}, u32[]{:S(2)}, u32[]{:S(2)}) collective-permute-start(bf16[64,1536]{1,0:T(8,128)(2,1)S(1)} %get-tuple-element.43), channel_id=1, source_target_pairs={{0,2},{1,3},{2,0},{3,1},{4,6},{5,7},{6,4},{7,5},{8,10},{9,11},{10,... | collective-permute-start | bytes 589832 | tf_op jit(solution)/shard_map/ppermute | solution.py:290
  117.4 15.4 %collective-permute-start.17 = (bf16[64,1536]{1,0:T(8,128)(2,1)S(1)}, bf16[64,1536]{1,0:T(8,128)(2,1)S(1)}, u32[]{:S(2)}, u32[]{:S(2)}) collective-permute-start(bf16[64,1536]{1,0:T(8,128)(2,1)S(1)} %get-tuple-element.44), channel_id=1, source_target_pairs={{0,3},{1,2},{2,1},{3,0},{4,7},{5,6},{6,5},{7,4},{8,11},{9,10},{10,... | collective-permute-start | bytes 589832 | tf_op jit(solution)/shard_map/ppermute | solution.py:290
  (10 other events, 15.7 us)

commit v6 on v5

--- a/solution.py
+++ b/solution.py
@@ -10,6 +10,55 @@
 H = 8
 HD = 64
 f32, bf16 = jnp.float32, jnp.bfloat16
+
+
+def first_kernel(place_ref, gate_ref, up_ref, down_ref, hidden_ref, first_ref, held, sems):
+    steps, each, width = held.shape
+    books = down_ref.shape[1] // width
+    start = pl.multiple_of(jnp.bitwise_xor(place_ref[0], books - 1) * width, width)
+    copies = []
+    for step in range(steps):
+        copies.append(
+            pltpu.make_async_copy(
+                down_ref.at[pl.ds(step * each, each), pl.ds(start, width)],
+                held.at[step],
+                sems.at[step],
+            )
+        )
+        copies[-1].start()
+    total = 0.0
+    for step in range(steps):
+        columns = pl.ds(step * each, each)
+        gate = gate_ref[:, columns].astype(f32)
+        hidden = gate / (1.0 + jnp.exp(-gate)) * up_ref[:, columns].astype(f32)
+        hidden = hidden.astype(bf16)
+        hidden_ref[:, columns] = hidden
+        copies[step].wait()
+        total = total + jnp.dot(hidden, held[step], preferred_element_type=f32)
+    first_ref[...] = total.astype(bf16)
+
+
+def first_products(place, gate, up, down, width):
+    frames_here, hidden_width = gate.shape
+    steps = max(hidden_width // 512, 1)
+    vmem = pl.BlockSpec(memory_space=pltpu.VMEM)
+    return pl.pallas_call(
+        first_kernel,
+        out_shape=[
+            jax.ShapeDtypeStruct((frames_here, hidden_width), bf16),
+            jax.ShapeDtypeStruct((frames_here, width), bf16),
+        ],
+        in_specs=[pl.BlockSpec(memory_space=pltpu.SMEM)]
+        + [vmem] * 2
+        + [pl.BlockSpec(memory_space=pl.ANY)],
+        out_specs=[vmem] * 2,
+        scratch_shapes=[
+            pltpu.VMEM((steps, hidden_width // steps, width), bf16),
+            pltpu.SemaphoreType.DMA((steps,)),
+        ],
+        compiler_params=pltpu.CompilerParams(vmem_limit_bytes=56 * 2**20),
+        name="hidden_and_first_products",
+    )(place, gate, up, down)
 
 
 def pack_kernel(proj_ref, table_ref, qkv_ref, packed_ref, sems):
@@ -50,7 +99,7 @@
         in_specs=[pl.BlockSpec(memory_space=pl.ANY)] * 3,
         out_specs=pl.BlockSpec(memory_space=pltpu.VMEM),
         scratch_shapes=[pltpu.SemaphoreType.DMA((5,))],
-        compiler_params=pltpu.CompilerParams(vmem_limit_bytes=4 * 2**20),
+        compiler_params=pltpu.CompilerParams(vmem_limit_bytes=56 * 2**20),
         name="pack_weight_rows",
     )(proj, table, qkv)
 
@@ -67,95 +116,73 @@
         square = square + jnp.sum(part * part, axis=-1, keepdims=True)
         width = part.shape[1]
         columns = pl.ds(pl.multiple_of(book * width, width), width)
-        held[book] = (part * gain_ref[:, columns]).astype(bf16)
+        held[book] = (part * gain_ref[:, columns].astype(f32)).astype(bf16)
     return square
 
 
 def early_kernel(books, early, pieces, sizes, place_ref, tokens_ref, gain_ref, *refs):
     blocks = dict(zip(early, refs))
     parts = refs[len(early) : len(early) + len(pieces)]
-    outs = refs[len(early) + len(pieces) :]
-    projected_ref, square_ref, later_ref, looked_ref, qkv_ref, held, table, sems = outs
-    proj_rows, table_rows, qkv_rows = sizes
+    projected_ref, square_ref, looked_ref, held, proj, table, sems = refs[
+        len(early) + len(pieces) :
+    ]
+    proj_rows, table_rows, _ = sizes
     here, group = place_ref[0], place_ref[1]
-    width = held.shape[2]
-    per_book = width // proj_rows
-    half = qkv_rows // 2
-    depth = table.shape[1]
-    extra = qkv_ref.shape[1] - depth
-
-    moves = []
-    for (n, first), ref in zip(pieces, parts):
-        if first + ref.shape[0] <= proj_rows:
-            continue
-        g = jnp.bitwise_xor(group, n)
-        at_table = proj_rows - first
-        at_qkv = at_table + table_rows
-        at_extra = at_qkv + qkv_rows
-        start = pl.multiple_of(g * table_rows, table_rows)
-        moves.append(
-            (0, ref.at[pl.ds(at_table, table_rows)], table.at[pl.ds(start, table_rows)])
+    per_book = held.shape[2] // proj_rows
+
+    table_copies, proj_copies = [], []
+    for number, ((n, first), ref) in enumerate(zip(pieces, parts)):
+        if first + ref.shape[0] > proj_rows:
+            g = jnp.bitwise_xor(group, n)
+            start = pl.multiple_of(g * table_rows, table_rows)
+            made = pltpu.make_async_copy(
+                ref.at[pl.ds(proj_rows - first, table_rows)],
+                table.at[pl.ds(start, table_rows)],
+                sems.at[number],
+            )
+            made.start()
+            table_copies.append(made)
+    for number, ((n, first), ref) in enumerate(zip(pieces, parts)):
+        count = min(ref.shape[0], proj_rows - first)
+        made = pltpu.make_async_copy(
+            ref.at[pl.ds(0, count)],
+            proj.at[pl.ds(n * proj_rows + first, count)],
+            sems.at[len(pieces) + number],
         )
-        start = pl.multiple_of(g * qkv_rows, qkv_rows)
-        moves.append(
-            (
-                1,
-                ref.at[pl.ds(at_qkv, qkv_rows)],
-                qkv_ref.at[pl.ds(start, qkv_rows), pl.ds(0, depth)],
-            )
-        )
-        for side in range(2):
-            start = pl.multiple_of(g * qkv_rows + side * half, half)
-            moves.append(
-                (
-                    1,
-                    ref.at[pl.ds(at_extra, half), pl.ds(side * extra, extra)],
-                    qkv_ref.at[pl.ds(start, half), pl.ds(depth, extra)],
-                )
-            )
-    copies = [
-        (kind, pltpu.make_async_copy(source, target, sems.at[number]))
-        for number, (kind, source, target) in enumerate(moves)
-    ]
-    for _, made in copies:
         made.start()
+        proj_copies.append(made)
 
     square_ref[...] = hold_blocks(blocks, here, gain_ref, held)
+    codes = lax.broadcasted_iota(jnp.int32, (table.shape[0], tokens_ref.shape[1]), 0)
+    matches = (tokens_ref[...] == codes).astype(f32).astype(bf16)
+    for made in table_copies:
+        made.wait()
+    looked = lax.dot_general(
+        matches, table[...], (((0,), (0,)), ((), ())), preferred_element_type=f32
+    )
+    looked_ref[...] = looked.astype(bf16)
     projected_ref[...] = jnp.zeros_like(projected_ref)
-    for (n, first), ref in zip(pieces, parts):
+    for (n, first), made, ref in zip(pieces, proj_copies, parts):
         count = min(ref.shape[0], proj_rows - first)
         owner = jnp.bitwise_xor(group, n)
         book = owner // per_book
         start = pl.multiple_of((owner % per_book) * proj_rows + first, 128)
-        late = is_late(jnp.bitwise_xor(here, book))
-
-        @pl.when(jnp.logical_not(late))
+        made.wait()
+
+        @pl.when(jnp.logical_not(is_late(jnp.bitwise_xor(here, book))))
         def _():
             projected_ref[...] += jnp.dot(
-                held[book, :, pl.ds(start, count)], ref[:count, :], preferred_element_type=f32
+                held[book, :, pl.ds(start, count)],
+                proj[pl.ds(n * proj_rows + first, count), :],
+                preferred_element_type=f32,
             )
 
-        @pl.when(late)
-        def _():
-            slot = jnp.bitwise_xor(here, book) // 2 - 1
-            later_ref[slot, pl.ds(start, count), :] = ref[:count, :]
-
-    columns = lax.broadcasted_iota(jnp.int32, (tokens_ref.shape[0], table.shape[0]), 1)
-    matches = (tokens_ref[...] == columns).astype(f32).astype(bf16)
-    for kind, made in copies:
-        if kind == 0:
-            made.wait()
-    looked_ref[...] = jnp.dot(matches, table[...], preferred_element_type=f32).astype(bf16)
-    for kind, made in copies:
-        if kind == 1:
-            made.wait()
-
-
-def project_early(place, tokens, gain, blocks, early, pieces, parts, sizes, wide):
+
+def project_early(place, tokens, gain, blocks, early, pieces, parts, sizes):
     books = len(blocks)
     frames_here, width = blocks[0].shape
     depth = parts[0].shape[1]
-    proj_rows, table_rows, qkv_rows = sizes
+    proj_rows, table_rows, _ = sizes
     groups = books * width // proj_rows
     vmem = pl.BlockSpec(memory_space=pltpu.VMEM)
     return pl.pallas_call(
@@ -163,77 +190,130 @@
         out_shape=[
             jax.ShapeDtypeStruct((frames_here, depth), f32),
             jax.ShapeDtypeStruct((frames_here, 1), f32),
-            jax.ShapeDtypeStruct((books - len(early), width, depth), bf16),
             jax.ShapeDtypeStruct((frames_here, depth), bf16),
-            jax.ShapeDtypeStruct((groups * qkv_rows, wide), bf16),
         ],
         in_specs=[pl.BlockSpec(memory_space=pltpu.SMEM)]
-        + [vmem] * (2 + len(early) + len(parts)),
-        out_specs=[vmem] * 5,
+        + [vmem] * (2 + len(early))
+        + [pl.BlockSpec(memory_space=pl.ANY)] * len(parts),
+        out_specs=[vmem] * 3,
         scratch_shapes=[
             pltpu.VMEM((books, frames_here, width), bf16),
+            pltpu.VMEM((books * width, depth), bf16),
             pltpu.VMEM((groups * table_rows, depth), bf16),
-            pltpu.SemaphoreType.DMA((4 * groups,)),
+            pltpu.SemaphoreType.DMA((2 * len(pieces),)),
         ],
-        compiler_params=pltpu.CompilerParams(vmem_limit_bytes=36 * 2**20),
+        compiler_params=pltpu.CompilerParams(vmem_limit_bytes=50 * 2**20),
         cost_estimate=pl.CostEstimate(flops=0, bytes_accessed=0, transcendentals=0),
         name="early_products_and_lookup",
     )(place, tokens, gain, *[blocks[m] for m in early], *parts)
 
 
-def late_kernel(books, late, place_ref, gain_ref, *refs):
+def late_kernel(books, late, pieces, sizes, place_ref, gain_ref, *refs):
     blocks = dict(zip(late, refs))
-    later_ref, early_ref, square_ref, looked_ref, depth_gain_ref, qkv_ref = refs[
-        len(late) : len(late) + 6
-    ]
-    refs = refs[len(late) + 6 :]
-    outs = refs[:books]
-    held, packed = refs[books:]
-    here = place_ref[0]
+    early_ref, square_ref, looked_ref, depth_gain_ref = refs[len(late) : len(late) + 4]
+    refs = refs[len(late) + 4 :]
+    parts = refs[: len(pieces)]
+    outs = refs[len(pieces) : len(pieces) + books]
+    held, proj, qkv, packed, sems = refs[len(pieces) + books :]
+    proj_rows, table_rows, qkv_rows = sizes
+    here, group = place_ref[0], place_ref[1]
     frames_here, width = held.shape[1:]
+    per_book = width // proj_rows
+    half = qkv_rows // 2
+    depth = proj.shape[2]
+    extra = qkv.shape[1] - depth
+
+    proj_copies = []
+    for number, ((n, first), ref) in enumerate(zip(pieces, parts)):
+        count = min(ref.shape[0], proj_rows - first)
+        owner = jnp.bitwise_xor(group, n)
+        m = jnp.bitwise_xor(here, owner // per_book)
+        start = pl.multiple_of((owner % per_book) * proj_rows + first, 128)
+        slot = jnp.maximum(m // 2 - 1, 0)
+        made = pltpu.make_async_copy(
+            ref.at[pl.ds(0, count)], proj.at[slot, pl.ds(start, count)], sems.at[number]
+        )
+        pl.when(is_late(m))(made.start)
+        proj_copies.append((is_late(m), made))
+    qkv_copies = []
+
+    def copy(source, target):
+        made = pltpu.make_async_copy(source, target, sems.at[len(pieces) + len(qkv_copies)])
+        made.start()
+        qkv_copies.append(made)
+
+    for (n, first), ref in zip(pieces, parts):
+        if first + ref.shape[0] > proj_rows:
+            g = jnp.bitwise_xor(group, n)
+            at_qkv = proj_rows - first + table_rows
+            start = pl.multiple_of(g * qkv_rows, qkv_rows)
+            copy(
+                ref.at[pl.ds(at_qkv, qkv_rows)], qkv.at[pl.ds(start, qkv_rows), pl.ds(0, depth)]
+            )
+            for side in range(2):
+                start = pl.multiple_of(g * qkv_rows + side * half, half)
+                copy(
+                    ref.at[pl.ds(at_qkv + qkv_rows, half), pl.ds(side * extra, extra)],
+                    qkv.at[pl.ds(start, half), pl.ds(depth, extra)],
+                )
+
     square = square_ref[...] + hold_blocks(blocks, here, gain_ref, held)
     projected = early_ref[...]
+    for late_here, made in proj_copies:
+        pl.when(late_here)(made.wait)
     for slot, m in enumerate(late):
         projected = projected + jnp.dot(
-            held[jnp.bitwise_xor(here, m)], later_ref[slot], preferred_element_type=f32
+            held[jnp.bitwise_xor(here, m)], proj[slot], preferred_element_type=f32
         )
     projected = projected * lax.rsqrt(square / (books * width) + 1e-05)
     depth_in = (projected + looked_ref[...].astype(f32)).astype(bf16).astype(f32)
     moment = jnp.mean(depth_in * depth_in, axis=-1, keepdims=True)
-    depth_normed = (depth_in * lax.rsqrt(moment + 1e-05) * depth_gain_ref[...]).astype(bf16)
-    packed[...] = jnp.dot(depth_normed, qkv_ref[...], preferred_element_type=f32).astype(bf16)
+    depth_normed = depth_in * lax.rsqrt(moment + 1e-05) * depth_gain_ref[...].astype(f32)
+    for made in qkv_copies:
+        made.wait()
+    packed[...] = jnp.dot(
+        depth_normed.astype(bf16), qkv[...], preferred_element_type=f32
+    ).astype(bf16)
     rows = frames_here // books
     for m in range(books):
         start = pl.multiple_of(jnp.bitwise_xor(here, m) * rows, rows)
         outs[m][...] = packed[pl.ds(start, rows), :]
 
 
-def project_late(place, gain, blocks, late, later, projected, square, looked, depth_gain, qkv):
+def project_late(
+    place, gain, blocks, late, projected, square, looked, depth_gain, pieces, parts, sizes, wide
+):
     books = len(blocks)
     frames_here, width = blocks[0].shape
-    wide = qkv.shape[1]
+    depth = projected.shape[1]
+    proj_rows, _, qkv_rows = sizes
+    groups = books * width // proj_rows
     vmem = pl.BlockSpec(memory_space=pltpu.VMEM)
     return pl.pallas_call(
-        functools.partial(late_kernel, books, late),
+        functools.partial(late_kernel, books, late, pieces, sizes),
         out_shape=[jax.ShapeDtypeStruct((frames_here // books, wide), bf16)] * books,
-        in_specs=[pl.BlockSpec(memory_space=pltpu.SMEM)] + [vmem] * (len(late) + 7),
+        in_specs=[pl.BlockSpec(memory_space=pltpu.SMEM)]
+        + [vmem] * (len(late) + 5)
+        + [pl.BlockSpec(memory_space=pl.ANY)] * len(parts),
         out_specs=[vmem] * books,
         scratch_shapes=[
             pltpu.VMEM((books, frames_here, width), bf16),
+            pltpu.VMEM((len(late), width, depth), bf16),
+            pltpu.VMEM((groups * qkv_rows, wide), bf16),
             pltpu.VMEM((frames_here, wide), bf16),
+            pltpu.SemaphoreType.DMA((len(pieces) + 3 * groups,)),
         ],
-        compiler_params=pltpu.CompilerParams(vmem_limit_bytes=24 * 2**20),
+        compiler_params=pltpu.CompilerParams(vmem_limit_bytes=50 * 2**20),
         name="late_products_and_qkv",
     )(
         place,
         gain,
         *[blocks[m] for m in late],
-        later,
         projected,
         square,
         looked,
         depth_gain,
-        qkv,
+        *parts,
     )
 
 
@@ -315,14 +395,10 @@
     here = lax.axis_index("book").astype(jnp.int32)
     place = jnp.stack([here, lax.axis_index("frames").astype(jnp.int32)])
     width = residual.shape[1]
-    depth = in_proj.shape[2]
-    wide = qkv_weight.shape[2]
     proj_rows = in_proj.shape[1]
-    table_rows = embedding.shape[1]
-    qkv_rows = qkv_weight.shape[1]
-    gain = out_gain.astype(f32)[None]
-
-    hidden = (jax.nn.silu(gate_pre.astype(f32)) * up_pre.astype(f32)).astype(bf16)
+    gain = out_gain[None]
+
+    hidden, first = first_products(place, gate_pre, up_pre, down_weight, width)
 
     def share(m, *others):
         start = jnp.bitwise_xor(here, m) * width
@@ -330,19 +406,17 @@
         factor = after(hidden, *others) if others else hidden
         return jnp.dot(factor, block, preferred_element_type=f32)
 
-    sums = {books - 1: share(books - 1)}
-    first = sums[books - 1].astype(bf16)
-
     rows = pack(*after((in_proj[0], embedding[0], qkv_weight[0]), first))
     parts = {0: [(0, rows)]}
     near = [n for n in range(2, groups, 2) if len(bits_of(n)) == 1]
     for n in near:
         parts[n] = [(0, swap(rows, "frames", n))]
 
+    sums = {books - 1: first}
     parts[1] = [(0, swap(rows, "frames", 1))]
     sums[books - 2] = lax.optimization_barrier(share(books - 2, rows))
-    for m in range(books - 3, 0, -1):
-        sums[m] = lax.optimization_barrier(share(m, parts[1][0][1]))
+    for n in range(books - 3, 0, -1):
+        sums[n] = lax.optimization_barrier(share(n, parts[1][0][1]))
     distance = 1
     while distance < books:
         came = None
@@ -389,30 +463,26 @@
         distance //= 2
 
     pieces = [(n, first) for n in range(groups) for first, _ in parts[n]]
+    arrived = [value for n in range(groups) for _, value in parts[n]]
+    sizes = proj_rows, embedding.shape[1], qkv_weight.shape[1]
     early = [m for m in range(books) if not is_late(m)]
     late = [m for m in range(books) if is_late(m)]
-    projected, square, later, looked, qkv = project_early(
-        place,
-        token_ids,
-        gain,
-        blocks,
-        early,
-        pieces,
-        [value for n in range(groups) for _, value in parts[n]],
-        (proj_rows, table_rows, qkv_rows),
-        wide,
+    projected, square, looked = project_early(
+        place, token_ids.reshape(1, -1), gain, blocks, early, pieces, arrived, sizes
     )
     packed = project_late(
         place,
         gain,
         blocks,
         late,
-        later,
         projected,
         square,
         looked,
-        depth_gain.astype(f32),
-        qkv,
+        depth_gain,
+        pieces,
+        arrived,
+        sizes,
+        qkv_weight.shape[2],
     )
     far = {m: swap(packed[m], "book", m) for m in range(books - 1, 0, -1)}
     return attend(place, [packed[0]] + [far[m] for m in range(1, books)])

time: 136 us -> 128 us (0.941)
  local copies, waits for them, and re-layouts: 13.7 us -> 1.11 us
  waiting for transfers between devices: 60.6 us -> 68.4 us
  Pallas kernels: 16.7 us -> 22.1 us
  matrix products: 15.1 us -> 11.2 us
  starting transfers between devices: 22.7 us -> 20.4 us
  other arithmetic: 6.47 us -> 4.44 us
    unnamed x33 -> x22, local copies, waits for them, and re-layouts: 12.5 us -> 0.98 us
    ppermute x18, waiting for transfers between devices: 60.6 us -> 68.4 us  [swap(): lax.ppermute(value, axis, [(i, i ^ distance) for i in range(lax.axis_size...]
    pallas_call x1 -> x2, Pallas kernels: 3 us -> 9.93 us  [the longest x1 4.98 us: first_products(): pl.pallas_call(first_kernel, out_shape=[jax.ShapeDtypeStruct((frames_here...]
    dot_general x4 -> x3, matrix products: 15.1 us -> 11.2 us  [share(): return jnp.dot(factor, block, preferred_element_type=f32)]
    pallas_call x1, Pallas kernels: 10.7 us -> 6.79 us  [project_early(): pl.pallas_call(functools.partial(early_kernel, books, early, pieces, size...]
    convert_element_type x2 -> x0, other arithmetic: 2.55 us -> none  [the longest x1 1.85 us: per_device(): (jax.nn.silu(gate_pre.astype(f32)) * up_pre.astype(f32)).astype(bf16)]
    pallas_call x1, Pallas kernels: 0.18 us -> 2.62 us  [pack(): pl.pallas_call(pack_kernel, out_shape=jax.ShapeDtypeStruct((rows, depth),...]
    ppermute x18, starting transfers between devices: 22.7 us -> 20.4 us  [swap(): lax.ppermute(value, axis, [(i, i ^ distance) for i in range(lax.axis_size...]
  transfers between devices with their start and end apart: 18 -> 18, of which waited for: 8 -> 10; matrix products, arithmetic and copies ran while one was open for 13% -> 12% of each run, Pallas kernels for 8% -> 5%
where the time goes in v6:
time: 128 us
  waiting for transfers between devices  68.4 us (53%)
  Pallas kernels  22.1 us (17%)
  starting transfers between devices  20.4 us (16%)
  matrix products  11.2 us (9%)
  other arithmetic  4.44 us (3%)
    ppermute x18, waiting for transfers between devices, swap(): lax.ppermute(value, axis, [(i, i ^ distance) for i in range(lax.axis_size...  68.4 us
    ppermute x18, starting transfers between devices, swap(): lax.ppermute(value, axis, [(i, i ^ distance) for i in range(lax.axis_size...  20.4 us
    dot_general x3, matrix products, share(): return jnp.dot(factor, block, preferred_element_type=f32)  11.2 us
    pallas_call x1, Pallas kernels, project_early(): pl.pallas_call(functools.partial(early_kernel, books, early, pieces, size...  6.79 us
    pallas_call x1, Pallas kernels, first_products(): pl.pallas_call(first_kernel, out_shape=[jax.ShapeDtypeStruct((frames_here...  4.98 us
    pallas_call x1, Pallas kernels, project_late(): pl.pallas_call(functools.partial(late_kernel, books, late, pieces, sizes)...  4.95 us
    pallas_call x1, Pallas kernels, attend(): pl.pallas_call(functools.partial(attend_kernel, books), out_shape=jax.Sha...  2.79 us
    pallas_call x1, Pallas kernels, pack(): pl.pallas_call(pack_kernel, out_shape=jax.ShapeDtypeStruct((rows, depth),...  2.62 us
  transfers between devices with their start and end apart: 18, of which 10 were waited for; matrix products, arithmetic and copies ran while one was open for 12% of the time, Pallas kernels for 5%

profile of v6, /device:TPU:0, one launch (start us, length us, event | category | flops | bytes accessed | tf_op | source)
XLA Modules:
  0.0 127.8 jit_solution(14015569041119142993)
XLA Ops:
  0.6 5.0 %hidden_and_first_products.1 = (bf16[256,1536]{1,0:T(8,128)(2,1)}, bf16[256,1024]{1,0:T(8,128)(2,1)}) custom-call(s32[2]{0:T(128)} %pad_add_fusion.place_ref, bf16[256,1536]{1,0:T(8,128)(2,1)} %gate_ref.1, bf16[256,1536]{1,0:T(8,128)(2,1)} %up_ref.1, bf16[1536,4096]{1,0:T(8,128)(2,1)} %down_ref.1), custom_call_target="tpu_custom_call" | custom-call | tf_op jit(solution)/shard_map/hidden_and_first_products/pallas_call | solution.py:45
  5.6 2.6 %pack_weight_rows.1.refs_3_.refs_5_ = bf16[832,1024]{1,0:T(8,128)(2,1)} custom-call(bf16[512,1024]{1,0:T(8,128)(2,1)} %bitcast.10, bf16[128,1024]{1,0:T(8,128)(2,1)} %bitcast.12, bf16[128,1536]{1,0:T(8,128)(2,1)} %bitcast.11), custom_call_target="tpu_custom_call" | custom-call | tf_op jit(solution)/shard_map/pack_weight_rows/pallas_call | solution.py:96
  8.8 2.6 %collective-permute-start = (bf16[256,1024]{1,0:T(8,128)(2,1)}, bf16[256,1024]{1,0:T(8,128)(2,1)}, u32[]{:S(2)}, u32[]{:S(2)}) collective-permute-start(bf16[256,1024]{1,0:T(8,128)(2,1)} %get-tuple-element.26), channel_id=1, source_target_pairs={{0,1},{1,0},{2,3},{3,2},{4,5},{5,4},{6,7},{7,6},{8,9},{9,8},{10,11... | collective-permute-start | bytes 1572872 | tf_op jit(solution)/shard_map/ppermute | solution.py:370
  14.4 4.1 %fusion = f32[256,1024]{1,0:T(8,128)} fusion(bf16[256,1536]{1,0:T(8,128)(2,1)} %get-tuple-element.27, bf16[1536,4096]{1,0:T(8,128)(2,1)} %down_ref.1, s32[]{:T(128)S(6)} %select_n.11), kind=kOutput, calls=%fused_computation | convolution fusion | flops 805306368 | bytes 4980740 | tf_op jit(solution)/shard_map/dot_general | solution.py:407
  18.5 5.7 %collective-permute-done = bf16[256,1024]{1,0:T(8,128)(2,1)} collective-permute-done((bf16[256,1024]{1,0:T(8,128)(2,1)}, bf16[256,1024]{1,0:T(8,128)(2,1)}, u32[]{:S(2)}, u32[]{:S(2)}) %collective-permute-start) | collective-permute-done | bytes 524320 | tf_op jit(solution)/shard_map/ppermute | solution.py:370
  24.2 2.3 %convert_add_fusion = bf16[256,1024]{1,0:T(8,128)(2,1)} fusion(f32[256,1024]{1,0:T(8,128)} %fusion, bf16[256,1024]{1,0:T(8,128)(2,1)} %collective-permute-done), kind=kLoop, calls=%fused_computation.7 | loop fusion | flops 786432 | bytes 2097152 | tf_op jit(solution)/shard_map/add | solution.py:428
  26.5 2.8 %collective-permute-start.3 = (bf16[256,1024]{1,0:T(8,128)(2,1)}, bf16[256,1024]{1,0:T(8,128)(2,1)}, u32[]{:S(2)}, u32[]{:S(2)}) collective-permute-start(bf16[256,1024]{1,0:T(8,128)(2,1)} %convert_add_fusion), channel_id=1, source_target_pairs={{0,2},{1,3},{2,0},{3,1},{4,6},{5,7},{6,4},{7,5},{8,10},{9,11},{10,... | collective-permute-start | bytes 1572872 | tf_op jit(solution)/shard_map/ppermute | solution.py:370
  29.3 3.9 %fusion.2 = bf16[256,1024]{1,0:T(8,128)(2,1)} fusion(bf16[256,1536]{1,0:T(8,128)(2,1)} %get-tuple-element.27, bf16[1536,4096]{1,0:T(8,128)(2,1)} %down_ref.1, s32[]{:T(128)S(6)} %select_n.10), kind=kOutput, calls=%fused_computation.2 | convolution fusion | flops 805306368 | bytes 4456452 | tf_op jit(solution)/shard_map/dot_general | solution.py:407
  33.2 1.6 %collective-permute-start.2 = (bf16[256,1024]{1,0:T(8,128)(2,1)}, bf16[256,1024]{1,0:T(8,128)(2,1)}, u32[]{:S(2)}, u32[]{:S(2)}) collective-permute-start(bf16[256,1024]{1,0:T(8,128)(2,1)} %fusion.2), channel_id=1, source_target_pairs={{0,1},{1,0},{2,3},{3,2},{4,5},{5,4},{6,7},{7,6},{8,9},{9,8},{10,11... | collective-permute-start | bytes 1572872 | tf_op jit(solution)/shard_map/ppermute | solution.py:370
  34.8 3.2 %fusion.4 = f32[256,1024]{1,0:T(8,128)S(1)} fusion(bf16[256,1536]{1,0:T(8,128)(2,1)} %get-tuple-element.27, bf16[1536,4096]{1,0:T(8,128)(2,1)} %down_ref.1, s32[]{:T(128)S(6)} %select_n.9), kind=kOutput, calls=%fused_computation.4 | convolution fusion | flops 805306368 | bytes 4980740 | tf_op jit(solution)/shard_map/dot_general | solution.py:407
  38.0 14.8 %collective-permute-done.3 = bf16[256,1024]{1,0:T(8,128)(2,1)} collective-permute-done((bf16[256,1024]{1,0:T(8,128)(2,1)}, bf16[256,1024]{1,0:T(8,128)(2,1)}, u32[]{:S(2)}, u32[]{:S(2)}) %collective-permute-start.3) | collective-permute-done | bytes 524320 | tf_op jit(solution)/shard_map/ppermute | solution.py:370
  52.8 4.1 %collective-permute-done.2 = bf16[256,1024]{1,0:T(8,128)(2,1)} collective-permute-done((bf16[256,1024]{1,0:T(8,128)(2,1)}, bf16[256,1024]{1,0:T(8,128)(2,1)}, u32[]{:S(2)}, u32[]{:S(2)}) %collective-permute-start.2) | collective-permute-done | bytes 524320 | tf_op jit(solution)/shard_map/ppermute | solution.py:370
  59.1 1.6 %collective-permute-start.12 = (bf16[448,1024]{1,0:T(8,128)(2,1)S(1)}, bf16[448,1024]{1,0:T(8,128)(2,1)S(1)}, u32[]{:S(2)}, u32[]{:S(2)}) collective-permute-start(bf16[448,1024]{1,0:T(8,128)(2,1)S(1)} %slice.7), channel_id=1, source_target_pairs={{0,16},{4,20},{8,24},{12,28},{16,0},{20,4},{24,8},{28,12},{1,17},{... | collective-permute-start | bytes 2752520 | tf_op jit(solution)/shard_map/ppermute | solution.py:370
  62.7 1.8 %collective-permute-done.8.refs_8_.refs_10_ = bf16[832,1024]{1,0:T(8,128)(2,1)S(1)} collective-permute-done((bf16[832,1024]{1,0:T(8,128)(2,1)S(1)}, bf16[832,1024]{1,0:T(8,128)(2,1)S(1)}, u32[]{:S(2)}, u32[]{:S(2)}) %collective-permute-start.8) | collective-permute-done | bytes 1703968 | tf_op jit(solution)/shard_map/ppermute | solution.py:370
  65.3 16.2 %collective-permute-done.12.refs_10_.refs_12_ = bf16[448,1024]{1,0:T(8,128)(2,1)S(1)} collective-permute-done((bf16[448,1024]{1,0:T(8,128)(2,1)S(1)}, bf16[448,1024]{1,0:T(8,128)(2,1)S(1)}, u32[]{:S(2)}, u32[]{:S(2)}) %collective-permute-start.12) | collective-permute-done | bytes 917536 | tf_op jit(solution)/shard_map/ppermute | solution.py:370
  82.0 5.6 %collective-permute-done.4.refs_2_ = bf16[256,1024]{1,0:T(8,128)(2,1)S(1)} collective-permute-done((bf16[256,1024]{1,0:T(8,128)(2,1)S(1)}, bf16[256,1024]{1,0:T(8,128)(2,1)S(1)}, u32[]{:S(2)}, u32[]{:S(2)}) %collective-permute-start.4) | collective-permute-done | bytes 524320 | tf_op jit(solution)/shard_map/ppermute | solution.py:370
  87.6 2.1 %collective-permute-done.9.refs_1_ = bf16[256,1024]{1,0:T(8,128)(2,1)S(1)} collective-permute-done((bf16[256,1024]{1,0:T(8,128)(2,1)S(1)}, bf16[256,1024]{1,0:T(8,128)(2,1)S(1)}, u32[]{:S(2)}, u32[]{:S(2)}) %collective-permute-start.9) | collective-permute-done | bytes 524320 | tf_op jit(solution)/shard_map/ppermute | solution.py:370
  90.7 6.8 %early_products_and_lookup.1 = (f32[256,1024]{1,0:T(8,128)}, f32[256,1]{1,0:T(8,128)S(1)}, bf16[256,1024]{1,0:T(8,128)(2,1)S(1)}) custom-call(s32[2]{0:T(128)S(1)} %copy-done, s32[1,256]{1,0:T(1,128)S(1)} %bitcast.9, bf16[1,4096]{1,0:T(2,128)(2,1)S(1)} %broadcast_in_dim.3.gain_ref, bf16[256,1024]{1,0:T(8,128)(2,1)S(1)} %add_convert_fusion.refs_0_, ...), custom_call_target="tpu_custom_call" | custom-call | tf_op jit(solution)/shard_map/early_products_and_lookup/pallas_call | solution.py:188
  97.5 5.3 %collective-permute-done.10.refs_0_ = bf16[256,1024]{1,0:T(8,128)(2,1)S(1)} collective-permute-done((bf16[256,1024]{1,0:T(8,128)(2,1)S(1)}, bf16[256,1024]{1,0:T(8,128)(2,1)S(1)}, u32[]{:S(2)}, u32[]{:S(2)}) %collective-permute-start.10) | collective-permute-done | bytes 524320 | tf_op jit(solution)/shard_map/ppermute | solution.py:370
  102.8 5.0 %late_products_and_qkv.1 = (bf16[64,1536]{1,0:T(8,128)(2,1)S(1)}, bf16[64,1536]{1,0:T(8,128)(2,1)S(1)}, bf16[64,1536]{1,0:T(8,128)(2,1)S(1)}, bf16[64,1536]{1,0:T(8,128)(2,1)S(1)}) custom-call(s32[2]{0:T(128)S(1)} %copy-done, bf16[1,4096]{1,0:T(2,128)(2,1)S(1)} %broadcast_in_dim.3.gain_ref, bf16[256,1024]{1,0:T(8,128)(2,1)S(1)} %collective-permute-done.10.refs_0_, ...), custom_call_target="tpu_custom_call" | custom-call | tf_op jit(solution)/shard_map/late_products_and_qkv/pallas_call | solution.py:292
  108.4 2.6 %collective-permute-start.16 = (bf16[64,1536]{1,0:T(8,128)(2,1)S(1)}, bf16[64,1536]{1,0:T(8,128)(2,1)S(1)}, u32[]{:S(2)}, u32[]{:S(2)}) collective-permute-start(bf16[64,1536]{1,0:T(8,128)(2,1)S(1)} %get-tuple-element.43), channel_id=1, source_target_pairs={{0,2},{1,3},{2,0},{3,1},{4,6},{5,7},{6,4},{7,5},{8,10},{9,11},{10,... | collective-permute-start | bytes 589832 | tf_op jit(solution)/shard_map/ppermute | solution.py:370
  112.2 3.6 %collective-permute-done.15.refs_1_ = bf16[64,1536]{1,0:T(8,128)(2,1)S(1)} collective-permute-done((bf16[64,1536]{1,0:T(8,128)(2,1)S(1)}, bf16[64,1536]{1,0:T(8,128)(2,1)S(1)}, u32[]{:S(2)}, u32[]{:S(2)}) %collective-permute-start.15) | collective-permute-done | bytes 196640 | tf_op jit(solution)/shard_map/ppermute | solution.py:370
  115.9 9.2 %collective-permute-done.16.refs_2_ = bf16[64,1536]{1,0:T(8,128)(2,1)S(1)} collective-permute-done((bf16[64,1536]{1,0:T(8,128)(2,1)S(1)}, bf16[64,1536]{1,0:T(8,128)(2,1)S(1)}, u32[]{:S(2)}, u32[]{:S(2)}) %collective-permute-start.16) | collective-permute-done | bytes 196640 | tf_op jit(solution)/shard_map/ppermute | solution.py:370
  125.0 2.8 %attend_books.1 = bf16[64,4,512]{2,1,0:T(4,128)(2,1)} custom-call(s32[2]{0:T(128)S(1)} %copy-done, bf16[64,1536]{1,0:T(8,128)(2,1)S(1)} %get-tuple-element.41.refs_0_, bf16[64,1536]{1,0:T(8,128)(2,1)S(1)} %collective-permute-done.15.refs_1_, bf16[64,1536]{1,0:T(8,128)(2,1)S(1)} %collective-permute-done.16.refs_2_, ...), custom_call_target="tpu_custom_call" | custom-call | tf_op jit(solution)/shard_map/attend_books/pallas_call | solution.py:358
  (48 shorter events, 12.5 us)
Async XLA Ops:
  8.2 21.1 %collective-permute-start.1 = (bf16[832,1024]{1,0:T(8,128)(2,1)}, bf16[832,1024]{1,0:T(8,128)(2,1)}, u32[]{:S(2)}, u32[]{:S(2)}) collective-permute-start(bf16[832,1024]{1,0:T(8,128)(2,1)} %pack_weight_rows.1.refs_3_.refs_5_), channel_id=1, source_target_pairs={{0,4},{4,0},{8,12},{12,8},{16,20},{20,16},{24,28},{28,24},{1,5},{5... | collective-permute-start | bytes 5111816 | tf_op jit(solution)/shard_map/ppermute | solution.py:370
  8.8 15.5 %collective-permute-start = (bf16[256,1024]{1,0:T(8,128)(2,1)}, bf16[256,1024]{1,0:T(8,128)(2,1)}, u32[]{:S(2)}, u32[]{:S(2)}) collective-permute-start(bf16[256,1024]{1,0:T(8,128)(2,1)} %get-tuple-element.26), channel_id=1, source_target_pairs={{0,1},{1,0},{2,3},{3,2},{4,5},{5,4},{6,7},{7,6},{8,9},{9,8},{10,11... | collective-permute-start | bytes 1572872 | tf_op jit(solution)/shard_map/ppermute | solution.py:370
  11.4 47.0 %collective-permute-start.5 = (bf16[832,1024]{1,0:T(8,128)(2,1)}, bf16[832,1024]{1,0:T(8,128)(2,1)S(1)}, u32[]{:S(2)}, u32[]{:S(2)}) collective-permute-start(bf16[832,1024]{1,0:T(8,128)(2,1)} %pack_weight_rows.1.refs_3_.refs_5_), channel_id=1, source_target_pairs={{0,8},{4,12},{8,0},{12,4},{16,24},{20,28},{24,16},{28,20},{1,9},{5... | collective-permute-start | bytes 5111816 | tf_op jit(solution)/shard_map/ppermute | solution.py:370
  12.9 45.5 %collective-permute-start.6 = (bf16[832,1024]{1,0:T(8,128)(2,1)}, bf16[832,1024]{1,0:T(8,128)(2,1)S(1)}, u32[]{:S(2)}, u32[]{:S(2)}) collective-permute-start(bf16[832,1024]{1,0:T(8,128)(2,1)} %pack_weight_rows.1.refs_3_.refs_5_), channel_id=1, source_target_pairs={{0,16},{4,20},{8,24},{12,28},{16,0},{20,4},{24,8},{28,12},{1,17},{... | collective-permute-start | bytes 5111816 | tf_op jit(solution)/shard_map/ppermute | solution.py:370
  26.5 26.2 %collective-permute-start.3 = (bf16[256,1024]{1,0:T(8,128)(2,1)}, bf16[256,1024]{1,0:T(8,128)(2,1)}, u32[]{:S(2)}, u32[]{:S(2)}) collective-permute-start(bf16[256,1024]{1,0:T(8,128)(2,1)} %convert_add_fusion), channel_id=1, source_target_pairs={{0,2},{1,3},{2,0},{3,1},{4,6},{5,7},{6,4},{7,5},{8,10},{9,11},{10,... | collective-permute-start | bytes 1572872 | tf_op jit(solution)/shard_map/ppermute | solution.py:370
  33.2 23.7 %collective-permute-start.2 = (bf16[256,1024]{1,0:T(8,128)(2,1)}, bf16[256,1024]{1,0:T(8,128)(2,1)}, u32[]{:S(2)}, u32[]{:S(2)}) collective-permute-start(bf16[256,1024]{1,0:T(8,128)(2,1)} %fusion.2), channel_id=1, source_target_pairs={{0,1},{1,0},{2,3},{3,2},{4,5},{5,4},{6,7},{7,6},{8,9},{9,8},{10,11... | collective-permute-start | bytes 1572872 | tf_op jit(solution)/shard_map/ppermute | solution.py:370
  38.0 51.7 %copy-start.10 = (bf16[4096]{0:T(1024)(128)(2,1)S(1)}, bf16[4096]{0:T(1024)(128)(2,1)}, u32[]{:S(2)}) copy-start(bf16[4096]{0:T(1024)(128)(2,1)} %param.14) | copy-start | bytes 24580
  38.0 52.7 %copy-start = (s32[2]{0:T(128)S(1)}, s32[2]{0:T(128)}, u32[]{:S(2)}) copy-start(s32[2]{0:T(128)} %pad_add_fusion.place_ref) | copy-start | bytes 28
  38.0 52.7 %copy-start.2 = (s32[256,1]{0,1:T(1,128)S(1)}, s32[256,1]{0,1:T(1,128)}, u32[]{:S(2)}) copy-start(s32[256,1]{0,1:T(1,128)} %param.17) | copy-start | bytes 3076
  58.4 31.3 %copy-start.3 = (bf16[832,1024]{1,0:T(8,128)(2,1)}, bf16[832,1024]{1,0:T(8,128)(2,1)S(1)}, u32[]{:S(2)}) copy-start(bf16[832,1024]{1,0:T(8,128)(2,1)S(1)} %collective-permute-done.5.refs_5_.refs_7_) | copy-start | bytes 5111812
  58.4 31.3 %copy-start.4 = (bf16[832,1024]{1,0:T(8,128)(2,1)}, bf16[832,1024]{1,0:T(8,128)(2,1)S(1)}, u32[]{:S(2)}) copy-start(bf16[832,1024]{1,0:T(8,128)(2,1)S(1)} %collective-permute-done.6.refs_7_.refs_9_) | copy-start | bytes 5111812
  58.5 4.3 %collective-permute-start.7 = (bf16[832,1024]{1,0:T(8,128)(2,1)S(1)}, bf16[832,1024]{1,0:T(8,128)(2,1)S(1)}, u32[]{:S(2)}, u32[]{:S(2)}) collective-permute-start(bf16[832,1024]{1,0:T(8,128)(2,1)S(1)} %collective-permute-done.5.refs_5_.refs_7_), channel_id=1, source_target_pairs={{0,4},{4,0},{8,12},{12,8},{16,20},{20,16},{24,28},{28,24},{1,5},{5... | collective-permute-start | bytes 5111816 | tf_op jit(solution)/shard_map/ppermute | solution.py:370
  58.5 6.0 %collective-permute-start.8 = (bf16[832,1024]{1,0:T(8,128)(2,1)S(1)}, bf16[832,1024]{1,0:T(8,128)(2,1)S(1)}, u32[]{:S(2)}, u32[]{:S(2)}) collective-permute-start(bf16[832,1024]{1,0:T(8,128)(2,1)S(1)} %collective-permute-done.6.refs_7_.refs_9_), channel_id=1, source_target_pairs={{0,4},{4,0},{8,12},{12,8},{16,20},{20,16},{24,28},{28,24},{1,5},{5... | collective-permute-start | bytes 5111816 | tf_op jit(solution)/shard_map/ppermute | solution.py:370
  59.1 22.4 %collective-permute-start.12 = (bf16[448,1024]{1,0:T(8,128)(2,1)S(1)}, bf16[448,1024]{1,0:T(8,128)(2,1)S(1)}, u32[]{:S(2)}, u32[]{:S(2)}) collective-permute-start(bf16[448,1024]{1,0:T(8,128)(2,1)S(1)} %slice.7), channel_id=1, source_target_pairs={{0,16},{4,20},{8,24},{12,28},{16,0},{20,4},{24,8},{28,12},{1,17},{... | collective-permute-start | bytes 2752520 | tf_op jit(solution)/shard_map/ppermute | solution.py:370
  60.7 20.8 %collective-permute-start.11 = (bf16[384,1024]{1,0:T(8,128)(2,1)S(1)}, bf16[384,1024]{1,0:T(8,128)(2,1)S(1)}, u32[]{:S(2)}, u32[]{:S(2)}) collective-permute-start(bf16[384,1024]{1,0:T(8,128)(2,1)S(1)} %slice.6), channel_id=1, source_target_pairs={{0,8},{4,12},{8,0},{12,4},{16,24},{20,28},{24,16},{28,20},{1,9},{5... | collective-permute-start | bytes 2359304 | tf_op jit(solution)/shard_map/ppermute | solution.py:370
  62.3 25.3 %collective-permute-start.4 = (bf16[256,1024]{1,0:T(8,128)(2,1)S(1)}, bf16[256,1024]{1,0:T(8,128)(2,1)S(1)}, u32[]{:S(2)}, u32[]{:S(2)}) collective-permute-start(bf16[256,1024]{1,0:T(8,128)(2,1)S(1)} %add_convert_fusion.refs_0_), channel_id=1, source_target_pairs={{0,2},{1,3},{2,0},{3,1},{4,6},{5,7},{6,4},{7,5},{8,10},{9,11},{10,... | collective-permute-start | bytes 1572872 | tf_op jit(solution)/shard_map/ppermute | solution.py:370
  62.7 27.0 %copy-start.5 = (bf16[832,1024]{1,0:T(8,128)(2,1)}, bf16[832,1024]{1,0:T(8,128)(2,1)S(1)}, u32[]{:S(2)}) copy-start(bf16[832,1024]{1,0:T(8,128)(2,1)S(1)} %collective-permute-done.7.refs_6_.refs_8_) | copy-start | bytes 5111812
  64.6 25.1 %collective-permute-start.9 = (bf16[256,1024]{1,0:T(8,128)(2,1)S(1)}, bf16[256,1024]{1,0:T(8,128)(2,1)S(1)}, u32[]{:S(2)}, u32[]{:S(2)}) collective-permute-start(bf16[256,1024]{1,0:T(8,128)(2,1)S(1)} %add_convert_fusion.refs_0_), channel_id=1, source_target_pairs={{0,1},{1,0},{2,3},{3,2},{4,5},{5,4},{6,7},{7,6},{8,9},{9,8},{10,11... | collective-permute-start | bytes 1572872 | tf_op jit(solution)/shard_map/ppermute | solution.py:370
  81.5 8.2 %collective-permute-start.14 = (bf16[448,1024]{1,0:T(8,128)(2,1)S(1)}, bf16[448,1024]{1,0:T(8,128)(2,1)S(1)}, u32[]{:S(2)}, u32[]{:S(2)}) collective-permute-start(bf16[448,1024]{1,0:T(8,128)(2,1)S(1)} %collective-permute-done.12.refs_10_.refs_12_), channel_id=1, source_target_pairs={{0,4},{4,0},{8,12},{12,8},{16,20},{20,16},{24,28},{28,24},{1,5},{5... | collective-permute-start | bytes 2752520 | tf_op jit(solution)/shard_map/ppermute | solution.py:370
  81.5 8.2 %collective-permute-start.13 = (bf16[384,1024]{1,0:T(8,128)(2,1)S(1)}, bf16[384,1024]{1,0:T(8,128)(2,1)S(1)}, u32[]{:S(2)}, u32[]{:S(2)}) collective-permute-start(bf16[384,1024]{1,0:T(8,128)(2,1)S(1)} %collective-permute-done.11.refs_9_.refs_11_), channel_id=1, source_target_pairs={{0,4},{4,0},{8,12},{12,8},{16,20},{20,16},{24,28},{28,24},{1,5},{5... | collective-permute-start | bytes 2359304 | tf_op jit(solution)/shard_map/ppermute | solution.py:370
  89.7 13.1 %collective-permute-start.10 = (bf16[256,1024]{1,0:T(8,128)(2,1)S(1)}, bf16[256,1024]{1,0:T(8,128)(2,1)S(1)}, u32[]{:S(2)}, u32[]{:S(2)}) collective-permute-start(bf16[256,1024]{1,0:T(8,128)(2,1)S(1)} %collective-permute-done.4.refs_2_), channel_id=1, source_target_pairs={{0,1},{1,0},{2,3},{3,2},{4,5},{5,4},{6,7},{7,6},{8,9},{9,8},{10,11... | collective-permute-start | bytes 1572872 | tf_op jit(solution)/shard_map/ppermute | solution.py:370
  107.8 8.1 %collective-permute-start.15 = (bf16[64,1536]{1,0:T(8,128)(2,1)S(1)}, bf16[64,1536]{1,0:T(8,128)(2,1)S(1)}, u32[]{:S(2)}, u32[]{:S(2)}) collective-permute-start(bf16[64,1536]{1,0:T(8,128)(2,1)S(1)} %get-tuple-element.42), channel_id=1, source_target_pairs={{0,1},{1,0},{2,3},{3,2},{4,5},{5,4},{6,7},{7,6},{8,9},{9,8},{10,11... | collective-permute-start | bytes 589832 | tf_op jit(solution)/shard_map/ppermute | solution.py:370
  108.4 16.7 %collective-permute-start.16 = (bf16[64,1536]{1,0:T(8,128)(2,1)S(1)}, bf16[64,1536]{1,0:T(8,128)(2,1)S(1)}, u32[]{:S(2)}, u32[]{:S(2)}) collective-permute-start(bf16[64,1536]{1,0:T(8,128)(2,1)S(1)} %get-tuple-element.43), channel_id=1, source_target_pairs={{0,2},{1,3},{2,0},{3,1},{4,6},{5,7},{6,4},{7,5},{8,10},{9,11},{10,... | collective-permute-start | bytes 589832 | tf_op jit(solution)/shard_map/ppermute | solution.py:370
  110.9 14.1 %collective-permute-start.17 = (bf16[64,1536]{1,0:T(8,128)(2,1)S(1)}, bf16[64,1536]{1,0:T(8,128)(2,1)S(1)}, u32[]{:S(2)}, u32[]{:S(2)}) collective-permute-start(bf16[64,1536]{1,0:T(8,128)(2,1)S(1)} %get-tuple-element.44), channel_id=1, source_target_pairs={{0,3},{1,2},{2,1},{3,0},{4,7},{5,6},{6,5},{7,4},{8,11},{9,10},{10,... | collective-permute-start | bytes 589832 | tf_op jit(solution)/shard_map/ppermute | solution.py:370
  (5 other events, 68.6 us)

commit v7 on v6

--- a/solution.py
+++ b/solution.py
@@ -12,33 +12,35 @@
 f32, bf16 = jnp.float32, jnp.bfloat16
 
 
-def first_kernel(place_ref, gate_ref, up_ref, down_ref, hidden_ref, first_ref, held, sems):
+def first_kernel(gate_ref, up_ref, down_ref, hidden_ref, first_ref, gates, ups, held, sems):
     steps, each, width = held.shape
     books = down_ref.shape[1] // width
-    start = pl.multiple_of(jnp.bitwise_xor(place_ref[0], books - 1) * width, width)
+    start = pl.multiple_of(jnp.bitwise_xor(lax.axis_index("book"), books - 1) * width, width)
     copies = []
     for step in range(steps):
-        copies.append(
-            pltpu.make_async_copy(
-                down_ref.at[pl.ds(step * each, each), pl.ds(start, width)],
-                held.at[step],
-                sems.at[step],
-            )
-        )
-        copies[-1].start()
+        rows = pl.ds(step * each, each)
+        moves = [
+            (gate_ref.at[:, rows], gates.at[step]),
+            (up_ref.at[:, rows], ups.at[step]),
+            (down_ref.at[rows, pl.ds(start, width)], held.at[step]),
+        ]
+        for kind, (source, target) in enumerate(moves):
+            copies.append(pltpu.make_async_copy(source, target, sems.at[3 * step + kind]))
+            copies[-1].start()
     total = 0.0
     for step in range(steps):
-        columns = pl.ds(step * each, each)
-        gate = gate_ref[:, columns].astype(f32)
-        hidden = gate / (1.0 + jnp.exp(-gate)) * up_ref[:, columns].astype(f32)
+        copies[3 * step].wait()
+        copies[3 * step + 1].wait()
+        gate = gates[step].astype(f32)
+        hidden = gate / (1.0 + jnp.exp(-gate)) * ups[step].astype(f32)
         hidden = hidden.astype(bf16)
-        hidden_ref[:, columns] = hidden
-        copies[step].wait()
+        hidden_ref[:, pl.ds(step * each, each)] = hidden
+        copies[3 * step + 2].wait()
         total = total + jnp.dot(hidden, held[step], preferred_element_type=f32)
     first_ref[...] = total.astype(bf16)
 
 
-def first_products(place, gate, up, down, width):
+def first_products(gate, up, down, width):
     frames_here, hidden_width = gate.shape
     steps = max(hidden_width // 512, 1)
     vmem = pl.BlockSpec(memory_space=pltpu.VMEM)
@@ -48,17 +50,17 @@
             jax.ShapeDtypeStruct((frames_here, hidden_width), bf16),
             jax.ShapeDtypeStruct((frames_here, width), bf16),
         ],
-        in_specs=[pl.BlockSpec(memory_space=pltpu.SMEM)]
-        + [vmem] * 2
-        + [pl.BlockSpec(memory_space=pl.ANY)],
+        in_specs=[pl.BlockSpec(memory_space=pl.ANY)] * 3,
         out_specs=[vmem] * 2,
         scratch_shapes=[
+            pltpu.VMEM((steps, frames_here, hidden_width // steps), bf16),
+            pltpu.VMEM((steps, frames_here, hidden_width // steps), bf16),
             pltpu.VMEM((steps, hidden_width // steps, width), bf16),
-            pltpu.SemaphoreType.DMA((steps,)),
+            pltpu.SemaphoreType.DMA((3 * steps,)),
         ],
-        compiler_params=pltpu.CompilerParams(vmem_limit_bytes=56 * 2**20),
+        compiler_params=pltpu.CompilerParams(vmem_limit_bytes=53 * 2**20),
         name="hidden_and_first_products",
-    )(place, gate, up, down)
+    )(gate, up, down)
 
 
 def pack_kernel(proj_ref, table_ref, qkv_ref, packed_ref, sems):
@@ -99,7 +101,7 @@
         in_specs=[pl.BlockSpec(memory_space=pl.ANY)] * 3,
         out_specs=pl.BlockSpec(memory_space=pltpu.VMEM),
         scratch_shapes=[pltpu.SemaphoreType.DMA((5,))],
-        compiler_params=pltpu.CompilerParams(vmem_limit_bytes=56 * 2**20),
+        compiler_params=pltpu.CompilerParams(vmem_limit_bytes=4 * 2**20),
         name="pack_weight_rows",
     )(proj, table, qkv)
 
@@ -120,14 +122,14 @@
     return square
 
 
-def early_kernel(books, early, pieces, sizes, place_ref, tokens_ref, gain_ref, *refs):
+def early_kernel(books, early, pieces, sizes, tokens_ref, gain_ref, *refs):
     blocks = dict(zip(early, refs))
     parts = refs[len(early) : len(early) + len(pieces)]
     projected_ref, square_ref, looked_ref, held, proj, table, sems = refs[
         len(early) + len(pieces) :
     ]
     proj_rows, table_rows, _ = sizes
-    here, group = place_ref[0], place_ref[1]
+    here, group = lax.axis_index("book"), lax.axis_index("frames")
     per_book = held.shape[2] // proj_rows
 
     table_copies, proj_copies = [], []
@@ -178,7 +180,7 @@
             )
 
 
-def project_early(place, tokens, gain, blocks, early, pieces, parts, sizes):
+def project_early(tokens, gain, blocks, early, pieces, parts, sizes):
     books = len(blocks)
     frames_here, width = blocks[0].shape
     depth = parts[0].shape[1]
@@ -192,8 +194,7 @@
             jax.ShapeDtypeStruct((frames_here, 1), f32),
             jax.ShapeDtypeStruct((frames_here, depth), bf16),
         ],
-        in_specs=[pl.BlockSpec(memory_space=pltpu.SMEM)]
-        + [vmem] * (2 + len(early))
+        in_specs=[vmem] * (2 + len(early))
         + [pl.BlockSpec(memory_space=pl.ANY)] * len(parts),
         out_specs=[vmem] * 3,
         scratch_shapes=[
@@ -205,10 +206,10 @@
         compiler_params=pltpu.CompilerParams(vmem_limit_bytes=50 * 2**20),
         cost_estimate=pl.CostEstimate(flops=0, bytes_accessed=0, transcendentals=0),
         name="early_products_and_lookup",
-    )(place, tokens, gain, *[blocks[m] for m in early], *parts)
-
-
-def late_kernel(books, late, pieces, sizes, place_ref, gain_ref, *refs):
+    )(tokens, gain, *[blocks[m] for m in early], *parts)
+
+
+def late_kernel(books, late, pieces, sizes, gain_ref, *refs):
     blocks = dict(zip(late, refs))
     early_ref, square_ref, looked_ref, depth_gain_ref = refs[len(late) : len(late) + 4]
     refs = refs[len(late) + 4 :]
@@ -216,7 +217,7 @@
     outs = refs[len(pieces) : len(pieces) + books]
     held, proj, qkv, packed, sems = refs[len(pieces) + books :]
     proj_rows, table_rows, qkv_rows = sizes
-    here, group = place_ref[0], place_ref[1]
+    here, group = lax.axis_index("book"), lax.axis_index("frames")
     frames_here, width = held.shape[1:]
     per_book = width // proj_rows
     half = qkv_rows // 2
@@ -281,7 +282,7 @@
 
 
 def project_late(
-    place, gain, blocks, late, projected, square, looked, depth_gain, pieces, parts, sizes, wide
+    gain, blocks, late, projected, square, looked, depth_gain, pieces, parts, sizes, wide
 ):
     books = len(blocks)
     frames_here, width = blocks[0].shape
@@ -292,8 +293,7 @@
     return pl.pallas_call(
         functools.partial(late_kernel, books, late, pieces, sizes),
         out_shape=[jax.ShapeDtypeStruct((frames_here // books, wide), bf16)] * books,
-        in_specs=[pl.BlockSpec(memory_space=pltpu.SMEM)]
-        + [vmem] * (len(late) + 5)
+        in_specs=[vmem] * (len(late) + 5)
         + [pl.BlockSpec(memory_space=pl.ANY)] * len(parts),
         out_specs=[vmem] * books,
         scratch_shapes=[
@@ -306,7 +306,6 @@
         compiler_params=pltpu.CompilerParams(vmem_limit_bytes=50 * 2**20),
         name="late_products_and_qkv",
     )(
-        place,
         gain,
         *[blocks[m] for m in late],
         projected,
@@ -317,10 +316,10 @@
     )
 
 
-def attend_kernel(books, place_ref, *refs):
+def attend_kernel(books, *refs):
     arrived = refs[:books]
     out_ref, inner = refs[books:]
-    place = place_ref[0]
+    place = lax.axis_index("book")
     rows, wide = arrived[0].shape
     width = wide // 3
     for m in range(books):
@@ -351,19 +350,19 @@
     out_ref[...] = jnp.stack(contexts, axis=1).astype(bf16)
 
 
-def attend(place, arrived):
+def attend(arrived):
     books = len(arrived)
     rows, wide = arrived[0].shape
     vmem = pl.BlockSpec(memory_space=pltpu.VMEM)
     return pl.pallas_call(
         functools.partial(attend_kernel, books),
         out_shape=jax.ShapeDtypeStruct((rows, books, wide // 3), bf16),
-        in_specs=[pl.BlockSpec(memory_space=pltpu.SMEM)] + [vmem] * books,
+        in_specs=[vmem] * books,
         out_specs=vmem,
         scratch_shapes=[pltpu.VMEM((books, rows, wide), bf16)],
         compiler_params=pltpu.CompilerParams(vmem_limit_bytes=16 * 2**20),
         name="attend_books",
-    )(place, *arrived)
+    )(*arrived)
 
 
 def swap(value, axis, distance):
@@ -393,12 +392,11 @@
     books = lax.axis_size("book")
     groups = lax.axis_size("frames")
     here = lax.axis_index("book").astype(jnp.int32)
-    place = jnp.stack([here, lax.axis_index("frames").astype(jnp.int32)])
     width = residual.shape[1]
     proj_rows = in_proj.shape[1]
     gain = out_gain[None]
 
-    hidden, first = first_products(place, gate_pre, up_pre, down_weight, width)
+    hidden, first = first_products(gate_pre, up_pre, down_weight, width)
 
     def share(m, *others):
         start = jnp.bitwise_xor(here, m) * width
@@ -425,6 +423,8 @@
             if came is not None:
                 going = after(going, came, sums[m + distance])
             came = swap(going, "book", distance)
+            if m == books - 1:
+                came = after(came, *[sums[n] for n in range(1, books - 1)])
             sums[m ^ distance] = sums[m ^ distance] + came.astype(f32)
             if m == books - 1:
                 sums[0] = lax.optimization_barrier(share(0, came))
@@ -468,10 +468,9 @@
     early = [m for m in range(books) if not is_late(m)]
     late = [m for m in range(books) if is_late(m)]
     projected, square, looked = project_early(
-        place, token_ids.reshape(1, -1), gain, blocks, early, pieces, arrived, sizes
+        token_ids.reshape(1, -1), gain, blocks, early, pieces, arrived, sizes
     )
     packed = project_late(
-        place,
         gain,
         blocks,
         late,
@@ -485,7 +484,7 @@
         qkv_weight.shape[2],
     )
     far = {m: swap(packed[m], "book", m) for m in range(books - 1, 0, -1)}
-    return attend(place, [packed[0]] + [far[m] for m in range(1, books)])
+    return attend([packed[0]] + [far[m] for m in range(1, books)])
 
 
 def solution(mesh):

time: 128 us -> 121 us (0.945)
  Pallas kernels: 22.1 us -> 17.3 us
  local copies, waits for them, and re-layouts: 1.11 us -> 3.44 us
  other arithmetic: 4.44 us -> 2.39 us
  starting transfers between devices: 20.4 us -> 18.4 us
    pallas_call x1, Pallas kernels: 2.62 us -> 0.18 us  [pack(): pl.pallas_call(pack_kernel, out_shape=jax.ShapeDtypeStruct((rows, depth),...]
    ppermute x18, starting transfers between devices: 20.4 us -> 18.4 us  [swap(): lax.ppermute(value, axis, [(i, i ^ distance) for i in range(lax.axis_size...]
where the time goes in v7:
time: 121 us; the launch traced here: 120 us
  waiting for transfers between devices  68.5 us (57%)
  starting transfers between devices  18.4 us (15%)
  Pallas kernels  17.3 us (14%)
  matrix products  10.2 us (8%)
  local copies, waits for them, and re-layouts  3.44 us (3%)
  other arithmetic  2.39 us (2%)
    ppermute x18, waiting for transfers between devices, swap(): lax.ppermute(value, axis, [(i, i ^ distance) for i in range(lax.axis_size...  68.5 us
    ppermute x18, starting transfers between devices, swap(): lax.ppermute(value, axis, [(i, i ^ distance) for i in range(lax.axis_size...  18.4 us
    dot_general x3, matrix products, share(): return jnp.dot(factor, block, preferred_element_type=f32)  10.2 us
    pallas_call x1, Pallas kernels, project_early(): pl.pallas_call(functools.partial(early_kernel, books, early, pieces, size...  6.25 us
    pallas_call x1, Pallas kernels, project_late(): pl.pallas_call(functools.partial(late_kernel, books, late, pieces, sizes)...  4.85 us
    pallas_call x1, Pallas kernels, first_products(): pl.pallas_call(first_kernel, out_shape=[jax.ShapeDtypeStruct((frames_here...  3.73 us
  transfers between devices with their start and end apart: 18, of which 10 were waited for; matrix products, arithmetic and copies ran while one was open for 12% of the time, Pallas kernels for 5%

profile of v7, /device:TPU:0, one launch (start us, length us, event | category | flops | bytes accessed | tf_op | source)
XLA Modules:
  0.0 120.3 jit_solution(1405949474107362693)
XLA Ops:
  0.0 3.7 %hidden_and_first_products.1 = (bf16[256,1536]{1,0:T(8,128)(2,1)}, bf16[256,1024]{1,0:T(8,128)(2,1)S(1)}) custom-call(bf16[256,1536]{1,0:T(8,128)(2,1)} %gate_ref.1, bf16[256,1536]{1,0:T(8,128)(2,1)} %up_ref.1, bf16[1536,4096]{1,0:T(8,128)(2,1)} %down_ref.1), custom_call_target="tpu_custom_call" | custom-call | tf_op jit(solution)/shard_map/hidden_and_first_products/pallas_call | solution.py:47
  4.5 2.6 %collective-permute-start.5 = (bf16[832,1024]{1,0:T(8,128)(2,1)S(1)}, bf16[832,1024]{1,0:T(8,128)(2,1)}, u32[]{:S(2)}, u32[]{:S(2)}) collective-permute-start(bf16[832,1024]{1,0:T(8,128)(2,1)S(1)} %pack_weight_rows.1.refs_3_.refs_5_), channel_id=1, source_target_pairs={{0,8},{4,12},{8,0},{12,4},{16,24},{20,28},{24,16},{28,20},{1,9},{5... | collective-permute-start | bytes 5111816 | tf_op jit(solution)/shard_map/ppermute | solution.py:369
  7.1 1.5 %collective-permute-start.6 = (bf16[832,1024]{1,0:T(8,128)(2,1)S(1)}, bf16[832,1024]{1,0:T(8,128)(2,1)}, u32[]{:S(2)}, u32[]{:S(2)}) collective-permute-start(bf16[832,1024]{1,0:T(8,128)(2,1)S(1)} %pack_weight_rows.1.refs_3_.refs_5_), channel_id=1, source_target_pairs={{0,16},{4,20},{8,24},{12,28},{16,0},{20,4},{24,8},{28,12},{1,17},{... | collective-permute-start | bytes 5111816 | tf_op jit(solution)/shard_map/ppermute | solution.py:369
  8.6 1.6 %collective-permute-start = (bf16[256,1024]{1,0:T(8,128)(2,1)S(1)}, bf16[256,1024]{1,0:T(8,128)(2,1)}, u32[]{:S(2)}, u32[]{:S(2)}) collective-permute-start(bf16[256,1024]{1,0:T(8,128)(2,1)S(1)} %get-tuple-element.27), channel_id=1, source_target_pairs={{0,1},{1,0},{2,3},{3,2},{4,5},{5,4},{6,7},{7,6},{8,9},{9,8},{10,11... | collective-permute-start | bytes 1572872 | tf_op jit(solution)/shard_map/ppermute | solution.py:369
  10.2 3.1 %fusion.2 = f32[256,1024]{1,0:T(8,128)S(1)} fusion(bf16[256,1536]{1,0:T(8,128)(2,1)} %get-tuple-element.34, bf16[1536,4096]{1,0:T(8,128)(2,1)} %down_ref.1, s32[]{:T(128)S(6)} %select_n.10), kind=kOutput, calls=%fused_computation.2 | convolution fusion | flops 805306368 | bytes 4980740 | tf_op jit(solution)/shard_map/dot_general | solution.py:405
  13.3 4.0 %fusion.4 = bf16[256,1024]{1,0:T(8,128)(2,1)} fusion(bf16[256,1536]{1,0:T(8,128)(2,1)} %get-tuple-element.34, bf16[1536,4096]{1,0:T(8,128)(2,1)} %down_ref.1, s32[]{:T(128)S(6)} %select_n.9), kind=kOutput, calls=%fused_computation.4 | convolution fusion | flops 805306368 | bytes 4456452 | tf_op jit(solution)/shard_map/dot_general | solution.py:405
  17.2 5.2 %collective-permute-done = bf16[256,1024]{1,0:T(8,128)(2,1)} collective-permute-done((bf16[256,1024]{1,0:T(8,128)(2,1)S(1)}, bf16[256,1024]{1,0:T(8,128)(2,1)}, u32[]{:S(2)}, u32[]{:S(2)}) %collective-permute-start) | collective-permute-done | bytes 524320 | tf_op jit(solution)/shard_map/ppermute | solution.py:369
  22.4 2.0 %convert_add_fusion = bf16[256,1024]{1,0:T(8,128)(2,1)} fusion(f32[256,1024]{1,0:T(8,128)S(1)} %fusion.2, bf16[256,1024]{1,0:T(8,128)(2,1)} %collective-permute-done), kind=kLoop, calls=%fused_computation.7 | loop fusion | flops 786432 | bytes 2097152 | tf_op jit(solution)/shard_map/add | solution.py:428
  24.4 1.6 %collective-permute-start.2 = (bf16[256,1024]{1,0:T(8,128)(2,1)}, bf16[256,1024]{1,0:T(8,128)(2,1)S(1)}, u32[]{:S(2)}, u32[]{:S(2)}) collective-permute-start(bf16[256,1024]{1,0:T(8,128)(2,1)} %fusion.4), channel_id=1, source_target_pairs={{0,1},{1,0},{2,3},{3,2},{4,5},{5,4},{6,7},{7,6},{8,9},{9,8},{10,11... | collective-permute-start | bytes 1572872 | tf_op jit(solution)/shard_map/ppermute | solution.py:369
  26.0 2.6 %collective-permute-start.3 = (bf16[256,1024]{1,0:T(8,128)(2,1)}, bf16[256,1024]{1,0:T(8,128)(2,1)S(1)}, u32[]{:S(2)}, u32[]{:S(2)}) collective-permute-start(bf16[256,1024]{1,0:T(8,128)(2,1)} %convert_add_fusion), channel_id=1, source_target_pairs={{0,2},{1,3},{2,0},{3,1},{4,6},{5,7},{6,4},{7,5},{8,10},{9,11},{10,... | collective-permute-start | bytes 1572872 | tf_op jit(solution)/shard_map/ppermute | solution.py:369
  28.6 3.1 %fusion = f32[256,1024]{1,0:T(8,128)S(1)} fusion(bf16[256,1536]{1,0:T(8,128)(2,1)} %get-tuple-element.34, bf16[1536,4096]{1,0:T(8,128)(2,1)} %down_ref.1, s32[]{:T(128)S(6)} %select_n.11), kind=kOutput, calls=%fused_computation | convolution fusion | flops 805306368 | bytes 4980740 | tf_op jit(solution)/shard_map/dot_general | solution.py:405
  31.8 16.9 %collective-permute-done.2 = bf16[256,1024]{1,0:T(8,128)(2,1)S(1)} collective-permute-done((bf16[256,1024]{1,0:T(8,128)(2,1)}, bf16[256,1024]{1,0:T(8,128)(2,1)S(1)}, u32[]{:S(2)}, u32[]{:S(2)}) %collective-permute-start.2) | collective-permute-done | bytes 524320 | tf_op jit(solution)/shard_map/ppermute | solution.py:369
  48.6 2.4 %collective-permute-done.3 = bf16[256,1024]{1,0:T(8,128)(2,1)S(1)} collective-permute-done((bf16[256,1024]{1,0:T(8,128)(2,1)}, bf16[256,1024]{1,0:T(8,128)(2,1)S(1)}, u32[]{:S(2)}, u32[]{:S(2)}) %collective-permute-start.3) | collective-permute-done | bytes 524320 | tf_op jit(solution)/shard_map/ppermute | solution.py:369
  55.9 1.8 %collective-permute-done.8.refs_8_.refs_10_ = bf16[832,1024]{1,0:T(8,128)(2,1)S(1)} collective-permute-done((bf16[832,1024]{1,0:T(8,128)(2,1)}, bf16[832,1024]{1,0:T(8,128)(2,1)S(1)}, u32[]{:S(2)}, u32[]{:S(2)}) %collective-permute-start.8) | collective-permute-done | bytes 1703968 | tf_op jit(solution)/shard_map/ppermute | solution.py:369
  58.7 16.9 %collective-permute-done.12.refs_10_.refs_12_ = bf16[448,1024]{1,0:T(8,128)(2,1)S(1)} collective-permute-done((bf16[448,1024]{1,0:T(8,128)(2,1)S(1)}, bf16[448,1024]{1,0:T(8,128)(2,1)S(1)}, u32[]{:S(2)}, u32[]{:S(2)}) %collective-permute-start.12) | collective-permute-done | bytes 917536 | tf_op jit(solution)/shard_map/ppermute | solution.py:369
  76.1 4.9 %collective-permute-done.4.refs_2_ = bf16[256,1024]{1,0:T(8,128)(2,1)S(1)} collective-permute-done((bf16[256,1024]{1,0:T(8,128)(2,1)S(1)}, bf16[256,1024]{1,0:T(8,128)(2,1)S(1)}, u32[]{:S(2)}, u32[]{:S(2)}) %collective-permute-start.4) | collective-permute-done | bytes 524320 | tf_op jit(solution)/shard_map/ppermute | solution.py:369
  81.0 1.8 %collective-permute-done.9.refs_1_ = bf16[256,1024]{1,0:T(8,128)(2,1)S(1)} collective-permute-done((bf16[256,1024]{1,0:T(8,128)(2,1)S(1)}, bf16[256,1024]{1,0:T(8,128)(2,1)S(1)}, u32[]{:S(2)}, u32[]{:S(2)}) %collective-permute-start.9) | collective-permute-done | bytes 524320 | tf_op jit(solution)/shard_map/ppermute | solution.py:369
  83.8 6.2 %early_products_and_lookup.1 = (f32[256,1024]{1,0:T(8,128)}, f32[256,1]{1,0:T(8,128)S(1)}, bf16[256,1024]{1,0:T(8,128)(2,1)S(1)}) custom-call(s32[1,256]{1,0:T(1,128)S(1)} %bitcast.10, bf16[1,4096]{1,0:T(2,128)(2,1)S(1)} %broadcast_in_dim.3.gain_ref, bf16[256,1024]{1,0:T(8,128)(2,1)S(1)} %add_convert_fusion.refs_0_, ...), custom_call_target="tpu_custom_call" | custom-call | tf_op jit(solution)/shard_map/early_products_and_lookup/pallas_call | solution.py:190
  90.1 5.8 %collective-permute-done.10.refs_0_ = bf16[256,1024]{1,0:T(8,128)(2,1)S(1)} collective-permute-done((bf16[256,1024]{1,0:T(8,128)(2,1)S(1)}, bf16[256,1024]{1,0:T(8,128)(2,1)S(1)}, u32[]{:S(2)}, u32[]{:S(2)}) %collective-permute-start.10) | collective-permute-done | bytes 524320 | tf_op jit(solution)/shard_map/ppermute | solution.py:369
  95.9 4.8 %late_products_and_qkv.1 = (bf16[64,1536]{1,0:T(8,128)(2,1)S(1)}, bf16[64,1536]{1,0:T(8,128)(2,1)S(1)}, bf16[64,1536]{1,0:T(8,128)(2,1)S(1)}, bf16[64,1536]{1,0:T(8,128)(2,1)S(1)}) custom-call(bf16[1,4096]{1,0:T(2,128)(2,1)S(1)} %broadcast_in_dim.3.gain_ref, bf16[256,1024]{1,0:T(8,128)(2,1)S(1)} %collective-permute-done.10.refs_0_, ...), custom_call_target="tpu_custom_call" | custom-call | tf_op jit(solution)/shard_map/late_products_and_qkv/pallas_call | solution.py:293
  101.4 2.8 %collective-permute-start.16 = (bf16[64,1536]{1,0:T(8,128)(2,1)S(1)}, bf16[64,1536]{1,0:T(8,128)(2,1)S(1)}, u32[]{:S(2)}, u32[]{:S(2)}) collective-permute-start(bf16[64,1536]{1,0:T(8,128)(2,1)S(1)} %get-tuple-element.45), channel_id=1, source_target_pairs={{0,2},{1,3},{2,0},{3,1},{4,6},{5,7},{6,4},{7,5},{8,10},{9,11},{10,... | collective-permute-start | bytes 589832 | tf_op jit(solution)/shard_map/ppermute | solution.py:369
  105.2 3.6 %collective-permute-done.15.refs_1_ = bf16[64,1536]{1,0:T(8,128)(2,1)S(1)} collective-permute-done((bf16[64,1536]{1,0:T(8,128)(2,1)S(1)}, bf16[64,1536]{1,0:T(8,128)(2,1)S(1)}, u32[]{:S(2)}, u32[]{:S(2)}) %collective-permute-start.15) | collective-permute-done | bytes 196640 | tf_op jit(solution)/shard_map/ppermute | solution.py:369
  108.8 9.2 %collective-permute-done.16.refs_2_ = bf16[64,1536]{1,0:T(8,128)(2,1)S(1)} collective-permute-done((bf16[64,1536]{1,0:T(8,128)(2,1)S(1)}, bf16[64,1536]{1,0:T(8,128)(2,1)S(1)}, u32[]{:S(2)}, u32[]{:S(2)}) %collective-permute-start.16) | collective-permute-done | bytes 196640 | tf_op jit(solution)/shard_map/ppermute | solution.py:369
  118.1 2.3 %attend_books.1 = bf16[64,4,512]{2,1,0:T(4,128)(2,1)} custom-call(bf16[64,1536]{1,0:T(8,128)(2,1)S(1)} %get-tuple-element.43.refs_0_, bf16[64,1536]{1,0:T(8,128)(2,1)S(1)} %collective-permute-done.15.refs_1_, bf16[64,1536]{1,0:T(8,128)(2,1)S(1)} %collective-permute-done.16.refs_2_, bf16[64,1536]{1,0:T(8,128)(2,1)S(1)} %collective-permute-done.17.refs_3_), custom_call_target="tpu_custom_call" | custom-call | tf_op jit(solution)/shard_map/attend_books/pallas_call | solution.py:357
  (49 shorter events, 9.8 us)
Async XLA Ops:
  4.0 13.3 %copy-start = (bf16[832,1024]{1,0:T(8,128)(2,1)}, bf16[832,1024]{1,0:T(8,128)(2,1)S(1)}, u32[]{:S(2)}) copy-start(bf16[832,1024]{1,0:T(8,128)(2,1)S(1)} %pack_weight_rows.1.refs_3_.refs_5_) | copy-start | bytes 5111812
  4.0 9.3 %collective-permute-start.1 = (bf16[832,1024]{1,0:T(8,128)(2,1)S(1)}, bf16[832,1024]{1,0:T(8,128)(2,1)}, u32[]{:S(2)}, u32[]{:S(2)}) collective-permute-start(bf16[832,1024]{1,0:T(8,128)(2,1)S(1)} %pack_weight_rows.1.refs_3_.refs_5_), channel_id=1, source_target_pairs={{0,4},{4,0},{8,12},{12,8},{16,20},{20,16},{24,28},{28,24},{1,5},{5... | collective-permute-start | bytes 5111816 | tf_op jit(solution)/shard_map/ppermute | solution.py:369
  4.5 46.8 %collective-permute-start.5 = (bf16[832,1024]{1,0:T(8,128)(2,1)S(1)}, bf16[832,1024]{1,0:T(8,128)(2,1)}, u32[]{:S(2)}, u32[]{:S(2)}) collective-permute-start(bf16[832,1024]{1,0:T(8,128)(2,1)S(1)} %pack_weight_rows.1.refs_3_.refs_5_), channel_id=1, source_target_pairs={{0,8},{4,12},{8,0},{12,4},{16,24},{20,28},{24,16},{28,20},{1,9},{5... | collective-permute-start | bytes 5111816 | tf_op jit(solution)/shard_map/ppermute | solution.py:369
  7.1 44.3 %collective-permute-start.6 = (bf16[832,1024]{1,0:T(8,128)(2,1)S(1)}, bf16[832,1024]{1,0:T(8,128)(2,1)}, u32[]{:S(2)}, u32[]{:S(2)}) collective-permute-start(bf16[832,1024]{1,0:T(8,128)(2,1)S(1)} %pack_weight_rows.1.refs_3_.refs_5_), channel_id=1, source_target_pairs={{0,16},{4,20},{8,24},{12,28},{16,0},{20,4},{24,8},{28,12},{1,17},{... | collective-permute-start | bytes 5111816 | tf_op jit(solution)/shard_map/ppermute | solution.py:369
  8.6 13.8 %collective-permute-start = (bf16[256,1024]{1,0:T(8,128)(2,1)S(1)}, bf16[256,1024]{1,0:T(8,128)(2,1)}, u32[]{:S(2)}, u32[]{:S(2)}) collective-permute-start(bf16[256,1024]{1,0:T(8,128)(2,1)S(1)} %get-tuple-element.27), channel_id=1, source_target_pairs={{0,1},{1,0},{2,3},{3,2},{4,5},{5,4},{6,7},{7,6},{8,9},{9,8},{10,11... | collective-permute-start | bytes 1572872 | tf_op jit(solution)/shard_map/ppermute | solution.py:369
  24.4 26.5 %copy-start.10 = (bf16[256,1024]{1,0:T(8,128)(2,1)S(1)}, bf16[256,1024]{1,0:T(8,128)(2,1)}, u32[]{:S(2)}) copy-start(bf16[256,1024]{1,0:T(8,128)(2,1)} %param.13) | copy-start | bytes 1572868
  24.4 24.2 %collective-permute-start.2 = (bf16[256,1024]{1,0:T(8,128)(2,1)}, bf16[256,1024]{1,0:T(8,128)(2,1)S(1)}, u32[]{:S(2)}, u32[]{:S(2)}) collective-permute-start(bf16[256,1024]{1,0:T(8,128)(2,1)} %fusion.4), channel_id=1, source_target_pairs={{0,1},{1,0},{2,3},{3,2},{4,5},{5,4},{6,7},{7,6},{8,9},{9,8},{10,11... | collective-permute-start | bytes 1572872 | tf_op jit(solution)/shard_map/ppermute | solution.py:369
  26.0 25.0 %collective-permute-start.3 = (bf16[256,1024]{1,0:T(8,128)(2,1)}, bf16[256,1024]{1,0:T(8,128)(2,1)S(1)}, u32[]{:S(2)}, u32[]{:S(2)}) collective-permute-start(bf16[256,1024]{1,0:T(8,128)(2,1)} %convert_add_fusion), channel_id=1, source_target_pairs={{0,2},{1,3},{2,0},{3,1},{4,6},{5,7},{6,4},{7,5},{8,10},{9,11},{10,... | collective-permute-start | bytes 1572872 | tf_op jit(solution)/shard_map/ppermute | solution.py:369
  31.7 51.0 %copy-start.11 = (bf16[4096]{0:T(1024)(128)(2,1)S(1)}, bf16[4096]{0:T(1024)(128)(2,1)}, u32[]{:S(2)}) copy-start(bf16[4096]{0:T(1024)(128)(2,1)} %param.14) | copy-start | bytes 24580
  31.7 52.1 %copy-start.5 = (s32[256,1]{0,1:T(1,128)S(1)}, s32[256,1]{0,1:T(1,128)}, u32[]{:S(2)}) copy-start(s32[256,1]{0,1:T(1,128)} %param.17) | copy-start | bytes 3076
  51.4 4.5 %collective-permute-start.7 = (bf16[832,1024]{1,0:T(8,128)(2,1)}, bf16[832,1024]{1,0:T(8,128)(2,1)S(1)}, u32[]{:S(2)}, u32[]{:S(2)}) collective-permute-start(bf16[832,1024]{1,0:T(8,128)(2,1)} %collective-permute-done.5.refs_5_.refs_7_), channel_id=1, source_target_pairs={{0,4},{4,0},{8,12},{12,8},{16,20},{20,16},{24,28},{28,24},{1,5},{5... | collective-permute-start | bytes 5111816 | tf_op jit(solution)/shard_map/ppermute | solution.py:369
  51.4 6.2 %collective-permute-start.8 = (bf16[832,1024]{1,0:T(8,128)(2,1)}, bf16[832,1024]{1,0:T(8,128)(2,1)S(1)}, u32[]{:S(2)}, u32[]{:S(2)}) collective-permute-start(bf16[832,1024]{1,0:T(8,128)(2,1)} %collective-permute-done.6.refs_7_.refs_9_), channel_id=1, source_target_pairs={{0,4},{4,0},{8,12},{12,8},{16,20},{20,16},{24,28},{28,24},{1,5},{5... | collective-permute-start | bytes 5111816 | tf_op jit(solution)/shard_map/ppermute | solution.py:369
  53.2 22.4 %collective-permute-start.12 = (bf16[448,1024]{1,0:T(8,128)(2,1)S(1)}, bf16[448,1024]{1,0:T(8,128)(2,1)S(1)}, u32[]{:S(2)}, u32[]{:S(2)}) collective-permute-start(bf16[448,1024]{1,0:T(8,128)(2,1)S(1)} %slice.7), channel_id=1, source_target_pairs={{0,16},{4,20},{8,24},{12,28},{16,0},{20,4},{24,8},{28,12},{1,17},{... | collective-permute-start | bytes 2752520 | tf_op jit(solution)/shard_map/ppermute | solution.py:369
  54.9 20.6 %collective-permute-start.11 = (bf16[384,1024]{1,0:T(8,128)(2,1)S(1)}, bf16[384,1024]{1,0:T(8,128)(2,1)S(1)}, u32[]{:S(2)}, u32[]{:S(2)}) collective-permute-start(bf16[384,1024]{1,0:T(8,128)(2,1)S(1)} %slice.6), channel_id=1, source_target_pairs={{0,8},{4,12},{8,0},{12,4},{16,24},{20,28},{24,16},{28,20},{1,9},{5... | collective-permute-start | bytes 2359304 | tf_op jit(solution)/shard_map/ppermute | solution.py:369
  55.5 25.5 %collective-permute-start.4 = (bf16[256,1024]{1,0:T(8,128)(2,1)S(1)}, bf16[256,1024]{1,0:T(8,128)(2,1)S(1)}, u32[]{:S(2)}, u32[]{:S(2)}) collective-permute-start(bf16[256,1024]{1,0:T(8,128)(2,1)S(1)} %add_convert_fusion.refs_0_), channel_id=1, source_target_pairs={{0,2},{1,3},{2,0},{3,1},{4,6},{5,7},{6,4},{7,5},{8,10},{9,11},{10,... | collective-permute-start | bytes 1572872 | tf_op jit(solution)/shard_map/ppermute | solution.py:369
  55.9 27.0 %copy-start.6 = (bf16[832,1024]{1,0:T(8,128)(2,1)}, bf16[832,1024]{1,0:T(8,128)(2,1)S(1)}, u32[]{:S(2)}) copy-start(bf16[832,1024]{1,0:T(8,128)(2,1)S(1)} %collective-permute-done.7.refs_6_.refs_8_) | copy-start | bytes 5111812
  57.7 25.2 %copy-start.7 = (bf16[832,1024]{1,0:T(8,128)(2,1)}, bf16[832,1024]{1,0:T(8,128)(2,1)S(1)}, u32[]{:S(2)}) copy-start(bf16[832,1024]{1,0:T(8,128)(2,1)S(1)} %collective-permute-done.8.refs_8_.refs_10_) | copy-start | bytes 5111812
  57.7 25.1 %collective-permute-start.9 = (bf16[256,1024]{1,0:T(8,128)(2,1)S(1)}, bf16[256,1024]{1,0:T(8,128)(2,1)S(1)}, u32[]{:S(2)}, u32[]{:S(2)}) collective-permute-start(bf16[256,1024]{1,0:T(8,128)(2,1)S(1)} %add_convert_fusion.refs_0_), channel_id=1, source_target_pairs={{0,1},{1,0},{2,3},{3,2},{4,5},{5,4},{6,7},{7,6},{8,9},{9,8},{10,11... | collective-permute-start | bytes 1572872 | tf_op jit(solution)/shard_map/ppermute | solution.py:369
  75.6 7.2 %collective-permute-start.14 = (bf16[448,1024]{1,0:T(8,128)(2,1)S(1)}, bf16[448,1024]{1,0:T(8,128)(2,1)S(1)}, u32[]{:S(2)}, u32[]{:S(2)}) collective-permute-start(bf16[448,1024]{1,0:T(8,128)(2,1)S(1)} %collective-permute-done.12.refs_10_.refs_12_), channel_id=1, source_target_pairs={{0,4},{4,0},{8,12},{12,8},{16,20},{20,16},{24,28},{28,24},{1,5},{5... | collective-permute-start | bytes 2752520 | tf_op jit(solution)/shard_map/ppermute | solution.py:369
  75.6 7.2 %collective-permute-start.13 = (bf16[384,1024]{1,0:T(8,128)(2,1)S(1)}, bf16[384,1024]{1,0:T(8,128)(2,1)S(1)}, u32[]{:S(2)}, u32[]{:S(2)}) collective-permute-start(bf16[384,1024]{1,0:T(8,128)(2,1)S(1)} %collective-permute-done.11.refs_9_.refs_11_), channel_id=1, source_target_pairs={{0,4},{4,0},{8,12},{12,8},{16,20},{20,16},{24,28},{28,24},{1,5},{5... | collective-permute-start | bytes 2359304 | tf_op jit(solution)/shard_map/ppermute | solution.py:369
  82.8 13.1 %collective-permute-start.10 = (bf16[256,1024]{1,0:T(8,128)(2,1)S(1)}, bf16[256,1024]{1,0:T(8,128)(2,1)S(1)}, u32[]{:S(2)}, u32[]{:S(2)}) collective-permute-start(bf16[256,1024]{1,0:T(8,128)(2,1)S(1)} %collective-permute-done.4.refs_2_), channel_id=1, source_target_pairs={{0,1},{1,0},{2,3},{3,2},{4,5},{5,4},{6,7},{7,6},{8,9},{9,8},{10,11... | collective-permute-start | bytes 1572872 | tf_op jit(solution)/shard_map/ppermute | solution.py:369
  100.8 8.1 %collective-permute-start.15 = (bf16[64,1536]{1,0:T(8,128)(2,1)S(1)}, bf16[64,1536]{1,0:T(8,128)(2,1)S(1)}, u32[]{:S(2)}, u32[]{:S(2)}) collective-permute-start(bf16[64,1536]{1,0:T(8,128)(2,1)S(1)} %get-tuple-element.44), channel_id=1, source_target_pairs={{0,1},{1,0},{2,3},{3,2},{4,5},{5,4},{6,7},{7,6},{8,9},{9,8},{10,11... | collective-permute-start | bytes 589832 | tf_op jit(solution)/shard_map/ppermute | solution.py:369
  101.4 16.7 %collective-permute-start.16 = (bf16[64,1536]{1,0:T(8,128)(2,1)S(1)}, bf16[64,1536]{1,0:T(8,128)(2,1)S(1)}, u32[]{:S(2)}, u32[]{:S(2)}) collective-permute-start(bf16[64,1536]{1,0:T(8,128)(2,1)S(1)} %get-tuple-element.45), channel_id=1, source_target_pairs={{0,2},{1,3},{2,0},{3,1},{4,6},{5,7},{6,4},{7,5},{8,10},{9,11},{10,... | collective-permute-start | bytes 589832 | tf_op jit(solution)/shard_map/ppermute | solution.py:369
  104.1 13.9 %collective-permute-start.17 = (bf16[64,1536]{1,0:T(8,128)(2,1)S(1)}, bf16[64,1536]{1,0:T(8,128)(2,1)S(1)}, u32[]{:S(2)}, u32[]{:S(2)}) collective-permute-start(bf16[64,1536]{1,0:T(8,128)(2,1)S(1)} %get-tuple-element.46), channel_id=1, source_target_pairs={{0,3},{1,2},{2,1},{3,0},{4,7},{5,6},{6,5},{7,4},{8,11},{9,10},{10,... | collective-permute-start | bytes 589832 | tf_op jit(solution)/shard_map/ppermute | solution.py:369
  (6 other events, 31.6 us)

commit v8 on v7

--- a/solution.py
+++ b/solution.py
@@ -59,6 +59,7 @@
             pltpu.SemaphoreType.DMA((3 * steps,)),
         ],
         compiler_params=pltpu.CompilerParams(vmem_limit_bytes=53 * 2**20),
+        cost_estimate=pl.CostEstimate(flops=0, bytes_accessed=0, transcendentals=0),
         name="hidden_and_first_products",
     )(gate, up, down)
 
@@ -106,28 +107,63 @@
     )(proj, table, qkv)
 
 
+def cut_kernel(cut, upper_from, lower_from, upper_ref, lower_ref, sems):
+    upper = pltpu.make_async_copy(upper_from.at[pl.ds(0, cut)], upper_ref, sems.at[0])
+    lower = pltpu.make_async_copy(
+        lower_from.at[pl.ds(cut, lower_ref.shape[0])], lower_ref, sems.at[1]
+    )
+    upper.start()
+    lower.start()
+    upper.wait()
+    lower.wait()
+
+
+def cut_rows(upper_from, lower_from, cut):
+    rows, depth = upper_from.shape
+    return pl.pallas_call(
+        functools.partial(cut_kernel, cut),
+        out_shape=[
+            jax.ShapeDtypeStruct((cut, depth), bf16),
+            jax.ShapeDtypeStruct((rows - cut, depth), bf16),
+        ],
+        in_specs=[pl.BlockSpec(memory_space=pl.ANY)] * 2,
+        out_specs=[pl.BlockSpec(memory_space=pl.ANY)] * 2,
+        scratch_shapes=[pltpu.SemaphoreType.DMA((2,))],
+        name="cut_rows",
+    )(upper_from, lower_from)
+
+
 def is_late(m):
     return (m % 2 == 1) & (m != 1)
 
 
-def hold_blocks(blocks, here, gain_ref, held):
-    square = 0.0
-    for m, ref in blocks.items():
+def hold_blocks(blocks, here, gain_ref, held, square_ref):
+    for m, pieces in blocks.items():
         book = jnp.bitwise_xor(here, m)
-        part = ref[...].astype(f32)
-        square = square + jnp.sum(part * part, axis=-1, keepdims=True)
-        width = part.shape[1]
+        width = held.shape[2]
         columns = pl.ds(pl.multiple_of(book * width, width), width)
-        held[book] = (part * gain_ref[:, columns].astype(f32)).astype(bf16)
-    return square
-
-
-def early_kernel(books, early, pieces, sizes, tokens_ref, gain_ref, *refs):
-    blocks = dict(zip(early, refs))
-    parts = refs[len(early) : len(early) + len(pieces)]
-    projected_ref, square_ref, looked_ref, held, proj, table, sems = refs[
-        len(early) + len(pieces) :
-    ]
+        gain = gain_ref[:, columns].astype(f32)
+        row = 0
+        for ref in pieces:
+            rows = pl.ds(row, ref.shape[0])
+            row += ref.shape[0]
+            part = ref[...].astype(f32)
+            square_ref[rows, :] += jnp.sum(part * part, axis=-1, keepdims=True)
+            held[book, rows, :] = (part * gain).astype(bf16)
+
+
+def with_refs(counts, refs):
+    blocks, at = {}, 0
+    for m, count in counts:
+        blocks[m] = refs[at : at + count]
+        at += count
+    return blocks, refs[at:]
+
+
+def early_kernel(books, counts, pieces, sizes, tokens_ref, gain_ref, *refs):
+    blocks, refs = with_refs(counts, refs)
+    parts = refs[: len(pieces)]
+    projected_ref, square_ref, looked_ref, held, proj, table, sems = refs[len(pieces) :]
     proj_rows, table_rows, _ = sizes
     here, group = lax.axis_index("book"), lax.axis_index("frames")
     per_book = held.shape[2] // proj_rows
@@ -154,7 +190,8 @@
         made.start()
         proj_copies.append(made)
 
-    square_ref[...] = hold_blocks(blocks, here, gain_ref, held)
+    square_ref[...] = jnp.zeros_like(square_ref)
+    hold_blocks(blocks, here, gain_ref, held, square_ref)
     codes = lax.broadcasted_iota(jnp.int32, (table.shape[0], tokens_ref.shape[1]), 0)
     matches = (tokens_ref[...] == codes).astype(f32).astype(bf16)
     for made in table_copies:
@@ -182,19 +219,21 @@
 
 def project_early(tokens, gain, blocks, early, pieces, parts, sizes):
     books = len(blocks)
-    frames_here, width = blocks[0].shape
+    frames_here, width = blocks[0][0].shape
+    counts = [(m, len(blocks[m])) for m in early]
+    given = [piece for m in early for piece in blocks[m]]
     depth = parts[0].shape[1]
     proj_rows, table_rows, _ = sizes
     groups = books * width // proj_rows
     vmem = pl.BlockSpec(memory_space=pltpu.VMEM)
     return pl.pallas_call(
-        functools.partial(early_kernel, books, early, pieces, sizes),
+        functools.partial(early_kernel, books, counts, pieces, sizes),
         out_shape=[
             jax.ShapeDtypeStruct((frames_here, depth), f32),
             jax.ShapeDtypeStruct((frames_here, 1), f32),
             jax.ShapeDtypeStruct((frames_here, depth), bf16),
         ],
-        in_specs=[vmem] * (2 + len(early))
+        in_specs=[vmem] * (2 + len(given))
         + [pl.BlockSpec(memory_space=pl.ANY)] * len(parts),
         out_specs=[vmem] * 3,
         scratch_shapes=[
@@ -206,16 +245,16 @@
         compiler_params=pltpu.CompilerParams(vmem_limit_bytes=50 * 2**20),
         cost_estimate=pl.CostEstimate(flops=0, bytes_accessed=0, transcendentals=0),
         name="early_products_and_lookup",
-    )(tokens, gain, *[blocks[m] for m in early], *parts)
-
-
-def late_kernel(books, late, pieces, sizes, gain_ref, *refs):
-    blocks = dict(zip(late, refs))
-    early_ref, square_ref, looked_ref, depth_gain_ref = refs[len(late) : len(late) + 4]
-    refs = refs[len(late) + 4 :]
-    parts = refs[: len(pieces)]
-    outs = refs[len(pieces) : len(pieces) + books]
-    held, proj, qkv, packed, sems = refs[len(pieces) + books :]
+    )(tokens, gain, *given, *parts)
+
+
+def late_kernel(books, counts, pieces, sizes, gain_ref, *refs):
+    blocks, refs = with_refs(counts, refs)
+    early_ref, square_ref, looked_ref, depth_gain_ref = refs[:4]
+    parts = refs[4 : len(pieces) + 4]
+    refs = refs[len(pieces) + 4 :]
+    outs = refs[:books]
+    held, proj, qkv, packed, squares, sems = refs[books:]
     proj_rows, table_rows, qkv_rows = sizes
     here, group = lax.axis_index("book"), lax.axis_index("frames")
     frames_here, width = held.shape[1:]
@@ -258,11 +297,13 @@
                     qkv.at[pl.ds(start, half), pl.ds(depth, extra)],
                 )
 
-    square = square_ref[...] + hold_blocks(blocks, here, gain_ref, held)
+    squares[...] = square_ref[...]
+    hold_blocks(blocks, here, gain_ref, held, squares)
+    square = squares[...]
     projected = early_ref[...]
     for late_here, made in proj_copies:
         pl.when(late_here)(made.wait)
-    for slot, m in enumerate(late):
+    for slot, (m, _) in enumerate(counts):
         projected = projected + jnp.dot(
             held[jnp.bitwise_xor(here, m)], proj[slot], preferred_element_type=f32
         )
@@ -285,15 +326,17 @@
     gain, blocks, late, projected, square, looked, depth_gain, pieces, parts, sizes, wide
 ):
     books = len(blocks)
-    frames_here, width = blocks[0].shape
+    frames_here, width = blocks[0][0].shape
+    counts = [(m, len(blocks[m])) for m in late]
+    given = [piece for m in late for piece in blocks[m]]
     depth = projected.shape[1]
     proj_rows, _, qkv_rows = sizes
     groups = books * width // proj_rows
     vmem = pl.BlockSpec(memory_space=pltpu.VMEM)
     return pl.pallas_call(
-        functools.partial(late_kernel, books, late, pieces, sizes),
+        functools.partial(late_kernel, books, counts, pieces, sizes),
         out_shape=[jax.ShapeDtypeStruct((frames_here // books, wide), bf16)] * books,
-        in_specs=[vmem] * (len(late) + 5)
+        in_specs=[vmem] * (len(given) + 5)
         + [pl.BlockSpec(memory_space=pl.ANY)] * len(parts),
         out_specs=[vmem] * books,
         scratch_shapes=[
@@ -301,13 +344,14 @@
             pltpu.VMEM((len(late), width, depth), bf16),
             pltpu.VMEM((groups * qkv_rows, wide), bf16),
             pltpu.VMEM((frames_here, wide), bf16),
+            pltpu.VMEM((frames_here, 1), f32),
             pltpu.SemaphoreType.DMA((len(pieces) + 3 * groups,)),
         ],
         compiler_params=pltpu.CompilerParams(vmem_limit_bytes=50 * 2**20),
         name="late_products_and_qkv",
     )(
         gain,
-        *[blocks[m] for m in late],
+        *given,
         projected,
         square,
         looked,
@@ -373,6 +417,11 @@
     return lax.optimization_barrier((value, *others))[0]
 
 
+def halves(value):
+    rows = value.shape[0] * 3 // 8 // 16 * 16
+    return [value[:rows], value[rows:]]
+
+
 def bits_of(number):
     return [1 << place for place in range(number.bit_length()) if number >> place & 1]
 
@@ -396,7 +445,14 @@
     proj_rows = in_proj.shape[1]
     gain = out_gain[None]
 
-    hidden, first = first_products(gate_pre, up_pre, down_weight, width)
+    rows = pack(in_proj[0], embedding[0], qkv_weight[0])
+    parts = {0: [(0, rows)]}
+    near = [n for n in range(2, groups, 2) if len(bits_of(n)) == 1]
+    for n in near:
+        parts[n] = [(0, swap(rows, "frames", n))]
+    parts[1] = [(0, swap(rows, "frames", 1))]
+
+    hidden, first = first_products(after(gate_pre, rows), up_pre, down_weight, width)
 
     def share(m, *others):
         start = jnp.bitwise_xor(here, m) * width
@@ -404,36 +460,35 @@
         factor = after(hidden, *others) if others else hidden
         return jnp.dot(factor, block, preferred_element_type=f32)
 
-    rows = pack(*after((in_proj[0], embedding[0], qkv_weight[0]), first))
-    parts = {0: [(0, rows)]}
-    near = [n for n in range(2, groups, 2) if len(bits_of(n)) == 1]
-    for n in near:
-        parts[n] = [(0, swap(rows, "frames", n))]
-
-    sums = {books - 1: first}
-    parts[1] = [(0, swap(rows, "frames", 1))]
-    sums[books - 2] = lax.optimization_barrier(share(books - 2, rows))
+    sums = {books - 1: first, books - 2: lax.optimization_barrier(share(books - 2))}
     for n in range(books - 3, 0, -1):
         sums[n] = lax.optimization_barrier(share(n, parts[1][0][1]))
+    sums = {m: halves(value) for m, value in sums.items()}
     distance = 1
     while distance < books:
         came = None
         for m in range(books - distance, 0, -2 * distance):
-            going = sums.pop(m).astype(bf16)
-            if came is not None:
-                going = after(going, came, sums[m + distance])
-            came = swap(going, "book", distance)
+            going = [half.astype(bf16) for half in sums.pop(m)]
+            if came is None:
+                came = [swap(half, "book", distance) for half in going]
+                midway = [came[0], going[1]] + sums.get(0, [])
+            else:
+                whole = after(jnp.concatenate(going, axis=0), came[0], sums[m + distance][0])
+                came = halves(swap(whole, "book", distance))
             if m == books - 1:
-                came = after(came, *[sums[n] for n in range(1, books - 1)])
-            sums[m ^ distance] = sums[m ^ distance] + came.astype(f32)
+                first_came = came[0]
+                came[0] = after(came[0], *[sums[n][0] for n in range(1, books - 1)])
+            sums[m ^ distance] = [
+                kept + half.astype(f32) for kept, half in zip(sums[m ^ distance], came)
+            ]
             if m == books - 1:
-                sums[0] = lax.optimization_barrier(share(0, came))
-                sums[0] = sums[0] + residual.astype(f32)
+                sums[0] = halves(
+                    lax.optimization_barrier(share(0, first_came)) + residual.astype(f32)
+                )
         distance *= 2
-
-    blocks = {0: sums[0].astype(bf16)}
-
-    arrived = after([parts[n][0][1] for n in near], blocks[0])
+    own = jnp.concatenate([half.astype(bf16) for half in sums[0]], axis=0)
+
+    arrived = after([parts[n][0][1] for n in near], *midway)
     for n, value in zip(near, arrived):
         parts[n] = [(0, value)]
     cut = rows.shape[0] // 2 // 128 * 128
@@ -442,25 +497,33 @@
         if n in near:
             continue
         if len(sides) == 2 and 0 < cut < proj_rows:
-            upper = swap(parts[n ^ sides[0]][0][1][:cut], "frames", sides[0])
-            lower = swap(parts[n ^ sides[1]][0][1][cut:], "frames", sides[1])
+            upper, lower = cut_rows(parts[n ^ sides[0]][0][1], parts[n ^ sides[1]][0][1], cut)
+            upper = swap(upper, "frames", sides[0])
+            lower = swap(lower, "frames", sides[1])
             parts[n] = [(0, upper), (cut, lower)]
         else:
             parts[n] = [(0, swap(rows, "frames", n))]
-    for n in range(2, groups, 2):
-        parts[n + 1] = [(first, swap(value, "frames", 1)) for first, value in parts[n]]
+    for n in near:
+        parts[n + 1] = [(0, swap(parts[n][0][1], "frames", 1))]
 
     near_there = [parts[n + 1][0][1] for n in near]
+    blocks = {0: [own]}
     distance = books // 2
     while distance:
         for m in sorted(blocks):
             going = blocks[m]
-            if m:
-                going = after(going, blocks[distance])
-            elif distance == 1:
-                going = after(going, *near_there)
-            blocks[m ^ distance] = swap(going, "book", distance)
+            if m == 0:
+                going = [after(own, *near_there)] if distance == 1 else halves(own)
+            blocks[m ^ distance] = [swap(piece, "book", distance) for piece in going]
         distance //= 2
+
+    through = blocks[1] + blocks[books // 2] + blocks[books - 1][:1]
+    for n in range(2, groups, 2):
+        if n not in near:
+            parts[n + 1] = [
+                (first, swap(after(value, *through), "frames", 1))
+                for first, value in parts[n]
+            ]
 
     pieces = [(n, first) for n in range(groups) for first, _ in parts[n]]
     arrived = [value for n in range(groups) for _, value in parts[n]]

time: 121 us -> 176 us (1.45)
  Pallas kernels: 17.3 us -> 69.9 us
  waiting for transfers between devices: 68.5 us -> 56.1 us
  starting transfers between devices: 18.4 us -> 26.7 us
  local copies, waits for them, and re-layouts: 3.44 us -> 6.31 us
  other arithmetic: 2.39 us -> 4.91 us
    pallas_call x2 -> x3, Pallas kernels: 11.1 us -> 63.9 us  [the longest x1 52.7 us: cut_rows(): pl.pallas_call(functools.partial(cut_kernel, cut), out_shape=[jax.ShapeDt...]
    ppermute x18 -> x22, waiting for transfers between devices: 68.5 us -> 56.1 us  [swap(): lax.ppermute(value, axis, [(i, i ^ distance) for i in range(lax.axis_size...]
    ppermute x18 -> x22, starting transfers between devices: 18.4 us -> 26.7 us  [swap(): lax.ppermute(value, axis, [(i, i ^ distance) for i in range(lax.axis_size...]
    unnamed x24 -> x26, local copies, waits for them, and re-layouts: 1 us -> 4.83 us
    convert_element_type x1 -> x3, other arithmetic: 0.35 us -> 2.67 us  [the longest x2 1.62 us: per_device(): own = jnp.concatenate([half.astype(bf16) for half in sums[0]], axis=0)]
  transfers between devices with their start and end apart: 18 -> 22, of which waited for: 10 -> 9; matrix products, arithmetic and copies ran while one was open for 12% -> 9% of each run, Pallas kernels for 5% -> 36%
where the time goes in v8:
time: 176 us; the launch traced here: 174 us
  Pallas kernels  69.9 us (40%)
  waiting for transfers between devices  56.1 us (32%)
  starting transfers between devices  26.7 us (15%)
  matrix products  10.1 us (6%)
  local copies, waits for them, and re-layouts  6.31 us (4%)
  other arithmetic  4.91 us (3%)
    ppermute x22, waiting for transfers between devices, swap(): lax.ppermute(value, axis, [(i, i ^ distance) for i in range(lax.axis_size...  56.1 us
    pallas_call x1, Pallas kernels, cut_rows(): pl.pallas_call(functools.partial(cut_kernel, cut), out_shape=[jax.ShapeDt...  52.7 us
    ppermute x22, starting transfers between devices, swap(): lax.ppermute(value, axis, [(i, i ^ distance) for i in range(lax.axis_size...  26.7 us
    dot_general x3, matrix products, share(): return jnp.dot(factor, block, preferred_element_type=f32)  10.1 us
    pallas_call x1, Pallas kernels, project_early(): pl.pallas_call(functools.partial(early_kernel, books, counts, pieces, siz...  6.26 us
    pallas_call x1, Pallas kernels, project_late(): pl.pallas_call(functools.partial(late_kernel, books, counts, pieces, size...  4.89 us
    unnamed x26, local copies, waits for them, and re-layouts  4.83 us
    pallas_call x1, Pallas kernels, first_products(): pl.pallas_call(first_kernel, out_shape=[jax.ShapeDtypeStruct((frames_here...  3.61 us
  transfers between devices with their start and end apart: 22, of which 9 were waited for; matrix products, arithmetic and copies ran while one was open for 9% of the time, Pallas kernels for 36%

profile of v8, /device:TPU:0, one launch (start us, length us, event | category | flops | bytes accessed | tf_op | source)
XLA Modules:
  0.0 174.2 jit_solution(7301920420018467124)
XLA Ops:
  3.9 2.6 %collective-permute-start.10 = (bf16[832,1024]{1,0:T(8,128)(2,1)S(1)}, bf16[832,1024]{1,0:T(8,128)(2,1)S(1)}, u32[]{:S(2)}, u32[]{:S(2)}) collective-permute-start(bf16[832,1024]{1,0:T(8,128)(2,1)S(1)} %pack_weight_rows.1.refs_4_.refs_6_), channel_id=1, source_target_pairs={{0,8},{4,12},{8,0},{12,4},{16,24},{20,28},{24,16},{28,20},{1,9},{5... | collective-permute-start | bytes 5111816 | tf_op jit(solution)/shard_map/ppermute | solution.py:413
  6.5 1.5 collective-permute-start.11
  8.0 3.6 %hidden_and_first_products.1 = (bf16[256,1536]{1,0:T(8,128)(2,1)}, bf16[256,1024]{1,0:T(8,128)(2,1)S(1)}) custom-call(bf16[256,1536]{1,0:T(8,128)(2,1)} %gate_ref, bf16[256,1536]{1,0:T(8,128)(2,1)} %up_ref.1, bf16[1536,4096]{1,0:T(8,128)(2,1)} %down_ref.1), custom_call_target="tpu_custom_call" | custom-call | tf_op jit(solution)/shard_map/hidden_and_first_products/pallas_call | solution.py:47
  12.3 1.6 collective-permute-start
  15.1 4.1 %fusion = f32[256,1024]{1,0:T(8,128)} fusion(bf16[256,1536]{1,0:T(8,128)(2,1)} %get-tuple-element.29, bf16[1536,4096]{1,0:T(8,128)(2,1)} %down_ref.1, s32[]{:T(128)S(6)} %select_n.11), kind=kOutput, calls=%fused_computation | convolution fusion | flops 805306368 | bytes 4980740 | tf_op jit(solution)/shard_map/dot_general | solution.py:461
  20.4 3.1 %fusion.4 = f32[256,1024]{1,0:T(8,128)S(1)} fusion(bf16[256,1536]{1,0:T(8,128)(2,1)} %get-tuple-element.29, bf16[1536,4096]{1,0:T(8,128)(2,1)} %down_ref.1, s32[]{:T(128)S(6)} %select_n.9), kind=kOutput, calls=%fused_computation.4 | convolution fusion | flops 805306368 | bytes 4980740 | tf_op jit(solution)/shard_map/dot_general | solution.py:461
  24.5 2.7 %collective-permute-start.3 = (bf16[96,1024]{1,0:T(8,128)(2,1)S(1)}, bf16[96,1024]{1,0:T(8,128)(2,1)S(1)}, u32[]{:S(2)}, u32[]{:S(2)}) collective-permute-start(bf16[96,1024]{1,0:T(8,128)(2,1)S(1)} %convert_add_fusion.1), channel_id=1, source_target_pairs={{0,2},{1,3},{2,0},{3,1},{4,6},{5,7},{6,4},{7,5},{8,10},{9,11},{10,... | collective-permute-start | bytes 589832 | tf_op jit(solution)/shard_map/ppermute | solution.py:413
  27.2 2.9 %fusion.2 = bf16[256,1024]{1,0:T(8,128)(2,1)S(1)} fusion(bf16[256,1536]{1,0:T(8,128)(2,1)S(1)} %copy-done.12, bf16[1536,4096]{1,0:T(8,128)(2,1)} %down_ref.1, s32[]{:T(128)S(6)} %select_n.10), kind=kOutput, calls=%fused_computation.2 | convolution fusion | flops 805306368 | bytes 4456452 | tf_op jit(solution)/shard_map/dot_general | solution.py:461
  30.2 1.6 collective-permute-start.2
  33.5 1.7 collective-permute-done.3
  35.2 16.0 %collective-permute-done.2 = bf16[256,1024]{1,0:T(8,128)(2,1)S(1)} collective-permute-done((bf16[256,1024]{1,0:T(8,128)(2,1)S(1)}, bf16[256,1024]{1,0:T(8,128)(2,1)S(1)}, u32[]{:S(2)}, u32[]{:S(2)}) %collective-permute-start.2) | collective-permute-done | bytes 524320 | tf_op jit(solution)/shard_map/ppermute | solution.py:413
  54.0 52.7 %cut_rows.1 = (bf16[384,1024]{1,0:T(8,128)(2,1)}, bf16[448,1024]{1,0:T(8,128)(2,1)}) custom-call(bf16[832,1024]{1,0:T(8,128)(2,1)} %collective-permute-done.11.upper_from.refs_8_.refs_10_, bf16[832,1024]{1,0:T(8,128)(2,1)} %copy-done.6), custom_call_target="tpu_custom_call" | custom-call | tf_op jit(solution)/shard_map/cut_rows/pallas_call | solution.py:123
  109.0 3.8 %collective-permute-start.4 = (bf16[96,1024]{1,0:T(8,128)(2,1)}, bf16[96,1024]{1,0:T(8,128)(2,1)S(1)}, u32[]{:S(2)}, u32[]{:S(2)}) collective-permute-start(bf16[96,1024]{1,0:T(8,128)(2,1)} %add_convert_fusion.1), channel_id=1, source_target_pairs={{0,2},{1,3},{2,0},{3,1},{4,6},{5,7},{6,4},{7,5},{8,10},{9,11},{10,... | collective-permute-start | bytes 589832 | tf_op jit(solution)/shard_map/ppermute | solution.py:413
  112.8 12.9 %collective-permute-done.4.refs_2_ = bf16[96,1024]{1,0:T(8,128)(2,1)S(1)} collective-permute-done((bf16[96,1024]{1,0:T(8,128)(2,1)}, bf16[96,1024]{1,0:T(8,128)(2,1)S(1)}, u32[]{:S(2)}, u32[]{:S(2)}) %collective-permute-start.4) | collective-permute-done | bytes 196640 | tf_op jit(solution)/shard_map/ppermute | solution.py:413
  125.8 4.2 %collective-permute-start.5 = (bf16[96,1024]{1,0:T(8,128)(2,1)S(1)}, bf16[96,1024]{1,0:T(8,128)(2,1)S(1)}, u32[]{:S(2)}, u32[]{:S(2)}) collective-permute-start(bf16[96,1024]{1,0:T(8,128)(2,1)S(1)} %collective-permute-done.4.refs_2_), channel_id=1, source_target_pairs={{0,1},{1,0},{2,3},{3,2},{4,5},{5,4},{6,7},{7,6},{8,9},{9,8},{10,11... | collective-permute-start | bytes 589832 | tf_op jit(solution)/shard_map/ppermute | solution.py:413
  129.9 3.7 %collective-permute-done.8.refs_3_ = bf16[160,1024]{1,0:T(8,128)(2,1)S(1)} collective-permute-done((bf16[160,1024]{1,0:T(8,128)(2,1)}, bf16[160,1024]{1,0:T(8,128)(2,1)S(1)}, u32[]{:S(2)}, u32[]{:S(2)}) %collective-permute-start.8) | collective-permute-done | bytes 327712 | tf_op jit(solution)/shard_map/ppermute | solution.py:413
  133.6 3.6 %collective-permute-done.5.refs_0_ = bf16[96,1024]{1,0:T(8,128)(2,1)S(1)} collective-permute-done((bf16[96,1024]{1,0:T(8,128)(2,1)S(1)}, bf16[96,1024]{1,0:T(8,128)(2,1)S(1)}, u32[]{:S(2)}, u32[]{:S(2)}) %collective-permute-start.5) | collective-permute-done | bytes 196640 | tf_op jit(solution)/shard_map/ppermute | solution.py:413
  138.1 2.7 %collective-permute-done.17.refs_12_.refs_14_ = bf16[384,1024]{1,0:T(8,128)(2,1)S(1)} collective-permute-done((bf16[384,1024]{1,0:T(8,128)(2,1)S(1)}, bf16[384,1024]{1,0:T(8,128)(2,1)S(1)}, u32[]{:S(2)}, u32[]{:S(2)}) %collective-permute-start.17) | collective-permute-done | bytes 786464 | tf_op jit(solution)/shard_map/ppermute | solution.py:413
  141.8 6.3 %early_products_and_lookup.1 = (f32[256,1024]{1,0:T(8,128)}, f32[256,1]{1,0:T(8,128)S(1)}, bf16[256,1024]{1,0:T(8,128)(2,1)S(1)}) custom-call(s32[1,256]{1,0:T(1,128)S(1)} %bitcast.10, bf16[1,4096]{1,0:T(2,128)(2,1)S(1)} %broadcast_in_dim.3.gain_ref, bf16[256,1024]{1,0:T(8,128)(2,1)S(1)} %pad_maximum_fusion.1.refs_0_, ...), custom_call_target="tpu_custom_call" | custom-call | tf_op jit(solution)/shard_map/early_products_and_lookup/pallas_call | solution.py:229
  148.1 4.9 %late_products_and_qkv.1 = (bf16[64,1536]{1,0:T(8,128)(2,1)S(1)}, bf16[64,1536]{1,0:T(8,128)(2,1)S(1)}, bf16[64,1536]{1,0:T(8,128)(2,1)S(1)}, bf16[64,1536]{1,0:T(8,128)(2,1)S(1)}) custom-call(bf16[1,4096]{1,0:T(2,128)(2,1)S(1)} %broadcast_in_dim.3.gain_ref, bf16[96,1024]{1,0:T(8,128)(2,1)S(1)} %collective-permute-done.5.refs_0_, ...), custom_call_target="tpu_custom_call" | custom-call | tf_op jit(solution)/shard_map/late_products_and_qkv/pallas_call | solution.py:336
  154.2 3.6 %collective-permute-start.20 = (bf16[64,1536]{1,0:T(8,128)(2,1)S(1)}, bf16[64,1536]{1,0:T(8,128)(2,1)S(1)}, u32[]{:S(2)}, u32[]{:S(2)}) collective-permute-start(bf16[64,1536]{1,0:T(8,128)(2,1)S(1)} %get-tuple-element.45), channel_id=1, source_target_pairs={{0,2},{1,3},{2,0},{3,1},{4,6},{5,7},{6,4},{7,5},{8,10},{9,11},{10,... | collective-permute-start | bytes 589832 | tf_op jit(solution)/shard_map/ppermute | solution.py:413
  157.8 5.9 %collective-permute-done.19.refs_1_ = bf16[64,1536]{1,0:T(8,128)(2,1)S(1)} collective-permute-done((bf16[64,1536]{1,0:T(8,128)(2,1)S(1)}, bf16[64,1536]{1,0:T(8,128)(2,1)S(1)}, u32[]{:S(2)}, u32[]{:S(2)}) %collective-permute-start.19) | collective-permute-done | bytes 196640 | tf_op jit(solution)/shard_map/ppermute | solution.py:413
  163.7 8.2 %collective-permute-done.20.refs_2_ = bf16[64,1536]{1,0:T(8,128)(2,1)S(1)} collective-permute-done((bf16[64,1536]{1,0:T(8,128)(2,1)S(1)}, bf16[64,1536]{1,0:T(8,128)(2,1)S(1)}, u32[]{:S(2)}, u32[]{:S(2)}) %collective-permute-start.20) | collective-permute-done | bytes 196640 | tf_op jit(solution)/shard_map/ppermute | solution.py:413
  172.0 2.3 %attend_books.1 = bf16[64,4,512]{2,1,0:T(4,128)(2,1)} custom-call(bf16[64,1536]{1,0:T(8,128)(2,1)S(1)} %get-tuple-element.43.refs_0_, bf16[64,1536]{1,0:T(8,128)(2,1)S(1)} %collective-permute-done.19.refs_1_, bf16[64,1536]{1,0:T(8,128)(2,1)S(1)} %collective-permute-done.20.refs_2_, bf16[64,1536]{1,0:T(8,128)(2,1)S(1)} %collective-permute-done.21.refs_3_), custom_call_target="tpu_custom_call" | custom-call | tf_op jit(solution)/shard_map/attend_books/pallas_call | solution.py:401
  (67 shorter events, 17.8 us)
Async XLA Ops:
  3.4 23.8 %collective-permute-start.1 = (bf16[832,1024]{1,0:T(8,128)(2,1)S(1)}, bf16[832,1024]{1,0:T(8,128)(2,1)}, u32[]{:S(2)}, u32[]{:S(2)}) collective-permute-start(bf16[832,1024]{1,0:T(8,128)(2,1)S(1)} %pack_weight_rows.1.refs_4_.refs_6_), channel_id=1, source_target_pairs={{0,4},{4,0},{8,12},{12,8},{16,20},{20,16},{24,28},{28,24},{1,5},{5... | collective-permute-start | bytes 5111816 | tf_op jit(solution)/shard_map/ppermute | solution.py:413
  3.9 48.9 %collective-permute-start.10 = (bf16[832,1024]{1,0:T(8,128)(2,1)S(1)}, bf16[832,1024]{1,0:T(8,128)(2,1)S(1)}, u32[]{:S(2)}, u32[]{:S(2)}) collective-permute-start(bf16[832,1024]{1,0:T(8,128)(2,1)S(1)} %pack_weight_rows.1.refs_4_.refs_6_), channel_id=1, source_target_pairs={{0,8},{4,12},{8,0},{12,4},{16,24},{20,28},{24,16},{28,20},{1,9},{5... | collective-permute-start | bytes 5111816 | tf_op jit(solution)/shard_map/ppermute | solution.py:413
  6.5 46.4 %collective-permute-start.11 = (bf16[832,1024]{1,0:T(8,128)(2,1)S(1)}, bf16[832,1024]{1,0:T(8,128)(2,1)}, u32[]{:S(2)}, u32[]{:S(2)}) collective-permute-start(bf16[832,1024]{1,0:T(8,128)(2,1)S(1)} %pack_weight_rows.1.refs_4_.refs_6_), channel_id=1, source_target_pairs={{0,16},{4,20},{8,24},{12,28},{16,0},{20,4},{24,8},{28,12},{1,17},{... | collective-permute-start | bytes 5111816 | tf_op jit(solution)/shard_map/ppermute | solution.py:413
  12.3 8.1 %collective-permute-start = (bf16[96,1024]{1,0:T(8,128)(2,1)}, bf16[96,1024]{1,0:T(8,128)(2,1)}, u32[]{:S(2)}, u32[]{:S(2)}) collective-permute-start(bf16[96,1024]{1,0:T(8,128)(2,1)} %slice.31), channel_id=1, source_target_pairs={{0,1},{1,0},{2,3},{3,2},{4,5},{5,4},{6,7},{7,6},{8,9},{9,8},{10,11... | collective-permute-start | bytes 589832 | tf_op jit(solution)/shard_map/ppermute | solution.py:413
  14.6 17.2 %collective-permute-start.6 = (bf16[160,1024]{1,0:T(8,128)(2,1)}, bf16[160,1024]{1,0:T(8,128)(2,1)}, u32[]{:S(2)}, u32[]{:S(2)}) collective-permute-start(bf16[160,1024]{1,0:T(8,128)(2,1)} %slice.40), channel_id=1, source_target_pairs={{0,1},{1,0},{2,3},{3,2},{4,5},{5,4},{6,7},{7,6},{8,9},{9,8},{10,11... | collective-permute-start | bytes 983048 | tf_op jit(solution)/shard_map/ppermute | solution.py:413
  24.5 10.7 %collective-permute-start.3 = (bf16[96,1024]{1,0:T(8,128)(2,1)S(1)}, bf16[96,1024]{1,0:T(8,128)(2,1)S(1)}, u32[]{:S(2)}, u32[]{:S(2)}) collective-permute-start(bf16[96,1024]{1,0:T(8,128)(2,1)S(1)} %convert_add_fusion.1), channel_id=1, source_target_pairs={{0,2},{1,3},{2,0},{3,1},{4,6},{5,7},{6,4},{7,5},{8,10},{9,11},{10,... | collective-permute-start | bytes 589832 | tf_op jit(solution)/shard_map/ppermute | solution.py:413
  30.2 21.0 %collective-permute-start.2 = (bf16[256,1024]{1,0:T(8,128)(2,1)S(1)}, bf16[256,1024]{1,0:T(8,128)(2,1)S(1)}, u32[]{:S(2)}, u32[]{:S(2)}) collective-permute-start(bf16[256,1024]{1,0:T(8,128)(2,1)S(1)} %pad_maximum_fusion), channel_id=1, source_target_pairs={{0,1},{1,0},{2,3},{3,2},{4,5},{5,4},{6,7},{7,6},{8,9},{9,8},{10,11... | collective-permute-start | bytes 1572872 | tf_op jit(solution)/shard_map/ppermute | solution.py:413
  32.9 19.0 %collective-permute-start.7 = (bf16[160,1024]{1,0:T(8,128)(2,1)S(1)}, bf16[160,1024]{1,0:T(8,128)(2,1)S(1)}, u32[]{:S(2)}, u32[]{:S(2)}) collective-permute-start(bf16[160,1024]{1,0:T(8,128)(2,1)S(1)} %fusion.6), channel_id=1, source_target_pairs={{0,2},{1,3},{2,0},{3,1},{4,6},{5,7},{6,4},{7,5},{8,10},{9,11},{10,... | collective-permute-start | bytes 983048 | tf_op jit(solution)/shard_map/ppermute | solution.py:413
  52.0 86.1 %copy-start.11 = (bf16[4096]{0:T(1024)(128)(2,1)S(1)}, bf16[4096]{0:T(1024)(128)(2,1)}, u32[]{:S(2)}) copy-start(bf16[4096]{0:T(1024)(128)(2,1)} %param.14) | copy-start | bytes 24580
  52.0 89.9 %copy-start.5 = (s32[256,1]{0,1:T(1,128)S(1)}, s32[256,1]{0,1:T(1,128)}, u32[]{:S(2)}) copy-start(s32[256,1]{0,1:T(1,128)} %param.17) | copy-start | bytes 3076
  52.8 56.1 %collective-permute-start.12 = (bf16[832,1024]{1,0:T(8,128)(2,1)S(1)}, bf16[832,1024]{1,0:T(8,128)(2,1)}, u32[]{:S(2)}, u32[]{:S(2)}) collective-permute-start(bf16[832,1024]{1,0:T(8,128)(2,1)S(1)} %collective-permute-done.10.lower_from.refs_6_.refs_8_), channel_id=1, source_target_pairs={{0,4},{4,0},{8,12},{12,8},{16,20},{20,16},{24,28},{28,24},{1,5},{5... | collective-permute-start | bytes 5111816 | tf_op jit(solution)/shard_map/ppermute | solution.py:413
  52.9 56.0 %collective-permute-start.13 = (bf16[832,1024]{1,0:T(8,128)(2,1)}, bf16[832,1024]{1,0:T(8,128)(2,1)}, u32[]{:S(2)}, u32[]{:S(2)}) collective-permute-start(bf16[832,1024]{1,0:T(8,128)(2,1)} %collective-permute-done.11.upper_from.refs_8_.refs_10_), channel_id=1, source_target_pairs={{0,4},{4,0},{8,12},{12,8},{16,20},{20,16},{24,28},{28,24},{1,5},{5... | collective-permute-start | bytes 5111816 | tf_op jit(solution)/shard_map/ppermute | solution.py:413
  106.8 30.4 %collective-permute-start.16 = (bf16[448,1024]{1,0:T(8,128)(2,1)}, bf16[448,1024]{1,0:T(8,128)(2,1)S(1)}, u32[]{:S(2)}, u32[]{:S(2)}) collective-permute-start(bf16[448,1024]{1,0:T(8,128)(2,1)} %get-tuple-element.37), channel_id=1, source_target_pairs={{0,16},{4,20},{8,24},{12,28},{16,0},{20,4},{24,8},{28,12},{1,17},{... | collective-permute-start | bytes 2752520 | tf_op jit(solution)/shard_map/ppermute | solution.py:413
  107.4 29.9 %collective-permute-start.15 = (bf16[384,1024]{1,0:T(8,128)(2,1)}, bf16[384,1024]{1,0:T(8,128)(2,1)S(1)}, u32[]{:S(2)}, u32[]{:S(2)}) collective-permute-start(bf16[384,1024]{1,0:T(8,128)(2,1)} %get-tuple-element.36), channel_id=1, source_target_pairs={{0,8},{4,12},{8,0},{12,4},{16,24},{20,28},{24,16},{28,20},{1,9},{5... | collective-permute-start | bytes 2359304 | tf_op jit(solution)/shard_map/ppermute | solution.py:413
  108.9 28.2 %collective-permute-start.14 = (bf16[256,1024]{1,0:T(8,128)(2,1)S(1)}, bf16[256,1024]{1,0:T(8,128)(2,1)S(1)}, u32[]{:S(2)}, u32[]{:S(2)}) collective-permute-start(bf16[256,1024]{1,0:T(8,128)(2,1)S(1)} %pad_maximum_fusion.1.refs_0_), channel_id=1, source_target_pairs={{0,1},{1,0},{2,3},{3,2},{4,5},{5,4},{6,7},{7,6},{8,9},{9,8},{10,11... | collective-permute-start | bytes 1572872 | tf_op jit(solution)/shard_map/ppermute | solution.py:413
  109.0 16.7 %collective-permute-start.4 = (bf16[96,1024]{1,0:T(8,128)(2,1)}, bf16[96,1024]{1,0:T(8,128)(2,1)S(1)}, u32[]{:S(2)}, u32[]{:S(2)}) collective-permute-start(bf16[96,1024]{1,0:T(8,128)(2,1)} %add_convert_fusion.1), channel_id=1, source_target_pairs={{0,2},{1,3},{2,0},{3,1},{4,6},{5,7},{6,4},{7,5},{8,10},{9,11},{10,... | collective-permute-start | bytes 589832 | tf_op jit(solution)/shard_map/ppermute | solution.py:413
  112.8 20.8 %collective-permute-start.8 = (bf16[160,1024]{1,0:T(8,128)(2,1)}, bf16[160,1024]{1,0:T(8,128)(2,1)S(1)}, u32[]{:S(2)}, u32[]{:S(2)}) collective-permute-start(bf16[160,1024]{1,0:T(8,128)(2,1)} %add_convert_fusion), channel_id=1, source_target_pairs={{0,2},{1,3},{2,0},{3,1},{4,6},{5,7},{6,4},{7,5},{8,10},{9,11},{10,... | collective-permute-start | bytes 983048 | tf_op jit(solution)/shard_map/ppermute | solution.py:413
  125.8 11.4 %collective-permute-start.5 = (bf16[96,1024]{1,0:T(8,128)(2,1)S(1)}, bf16[96,1024]{1,0:T(8,128)(2,1)S(1)}, u32[]{:S(2)}, u32[]{:S(2)}) collective-permute-start(bf16[96,1024]{1,0:T(8,128)(2,1)S(1)} %collective-permute-done.4.refs_2_), channel_id=1, source_target_pairs={{0,1},{1,0},{2,3},{3,2},{4,5},{5,4},{6,7},{7,6},{8,9},{9,8},{10,11... | collective-permute-start | bytes 589832 | tf_op jit(solution)/shard_map/ppermute | solution.py:413
  137.2 3.7 %collective-permute-start.18 = (bf16[448,1024]{1,0:T(8,128)(2,1)S(1)}, bf16[448,1024]{1,0:T(8,128)(2,1)S(1)}, u32[]{:S(2)}, u32[]{:S(2)}) collective-permute-start(bf16[448,1024]{1,0:T(8,128)(2,1)S(1)} %collective-permute-done.16.refs_11_.refs_13_), channel_id=1, source_target_pairs={{0,4},{4,0},{8,12},{12,8},{16,20},{20,16},{24,28},{28,24},{1,5},{5... | collective-permute-start | bytes 2752520 | tf_op jit(solution)/shard_map/ppermute | solution.py:413
  137.3 3.6 %collective-permute-start.17 = (bf16[384,1024]{1,0:T(8,128)(2,1)S(1)}, bf16[384,1024]{1,0:T(8,128)(2,1)S(1)}, u32[]{:S(2)}, u32[]{:S(2)}) collective-permute-start(bf16[384,1024]{1,0:T(8,128)(2,1)S(1)} %collective-permute-done.15.refs_10_.refs_12_), channel_id=1, source_target_pairs={{0,4},{4,0},{8,12},{12,8},{16,20},{20,16},{24,28},{28,24},{1,5},{5... | collective-permute-start | bytes 2359304 | tf_op jit(solution)/shard_map/ppermute | solution.py:413
  137.8 10.4 %collective-permute-start.9 = (bf16[160,1024]{1,0:T(8,128)(2,1)S(1)}, bf16[160,1024]{1,0:T(8,128)(2,1)S(1)}, u32[]{:S(2)}, u32[]{:S(2)}) collective-permute-start(bf16[160,1024]{1,0:T(8,128)(2,1)S(1)} %collective-permute-done.8.refs_3_), channel_id=1, source_target_pairs={{0,1},{1,0},{2,3},{3,2},{4,5},{5,4},{6,7},{7,6},{8,9},{9,8},{10,11... | collective-permute-start | bytes 983048 | tf_op jit(solution)/shard_map/ppermute | solution.py:413
  153.0 10.7 %collective-permute-start.19 = (bf16[64,1536]{1,0:T(8,128)(2,1)S(1)}, bf16[64,1536]{1,0:T(8,128)(2,1)S(1)}, u32[]{:S(2)}, u32[]{:S(2)}) collective-permute-start(bf16[64,1536]{1,0:T(8,128)(2,1)S(1)} %get-tuple-element.44), channel_id=1, source_target_pairs={{0,1},{1,0},{2,3},{3,2},{4,5},{5,4},{6,7},{7,6},{8,9},{9,8},{10,11... | collective-permute-start | bytes 589832 | tf_op jit(solution)/shard_map/ppermute | solution.py:413
  154.2 17.8 %collective-permute-start.20 = (bf16[64,1536]{1,0:T(8,128)(2,1)S(1)}, bf16[64,1536]{1,0:T(8,128)(2,1)S(1)}, u32[]{:S(2)}, u32[]{:S(2)}) collective-permute-start(bf16[64,1536]{1,0:T(8,128)(2,1)S(1)} %get-tuple-element.45), channel_id=1, source_target_pairs={{0,2},{1,3},{2,0},{3,1},{4,6},{5,7},{6,4},{7,5},{8,10},{9,11},{10,... | collective-permute-start | bytes 589832 | tf_op jit(solution)/shard_map/ppermute | solution.py:413
  157.8 14.2 %collective-permute-start.21 = (bf16[64,1536]{1,0:T(8,128)(2,1)S(1)}, bf16[64,1536]{1,0:T(8,128)(2,1)S(1)}, u32[]{:S(2)}, u32[]{:S(2)}) collective-permute-start(bf16[64,1536]{1,0:T(8,128)(2,1)S(1)} %get-tuple-element.46), channel_id=1, source_target_pairs={{0,3},{1,2},{2,1},{3,0},{4,7},{5,6},{6,5},{7,4},{8,11},{9,10},{10,... | collective-permute-start | bytes 589832 | tf_op jit(solution)/shard_map/ppermute | solution.py:413
  (11 other events, 44.8 us)

commit v9 on v7

--- a/solution.py
+++ b/solution.py
@@ -63,6 +63,45 @@
     )(gate, up, down)
 
 
+def share_kernel(partner, hidden_ref, down_ref, out_ref, held, sems):
+    steps, each, width = held.shape
+    start = pl.multiple_of(jnp.bitwise_xor(lax.axis_index("book"), partner) * width, width)
+    copies = []
+    for step in range(steps):
+        rows = pl.ds(step * each, each)
+        copies.append(
+            pltpu.make_async_copy(
+                down_ref.at[rows, pl.ds(start, width)], held.at[step], sems.at[step]
+            )
+        )
+        copies[-1].start()
+    total = 0.0
+    for step in range(steps):
+        copies[step].wait()
+        total = total + jnp.dot(
+            hidden_ref[:, pl.ds(step * each, each)], held[step], preferred_element_type=f32
+        )
+    out_ref[...] = total
+
+
+def share_products(hidden, down, width, partner):
+    frames_here, hidden_width = hidden.shape
+    steps = max(hidden_width // 512, 1)
+    vmem = pl.BlockSpec(memory_space=pltpu.VMEM)
+    return pl.pallas_call(
+        functools.partial(share_kernel, partner),
+        out_shape=jax.ShapeDtypeStruct((frames_here, width), f32),
+        in_specs=[vmem, pl.BlockSpec(memory_space=pl.ANY)],
+        out_specs=vmem,
+        scratch_shapes=[
+            pltpu.VMEM((steps, hidden_width // steps, width), bf16),
+            pltpu.SemaphoreType.DMA((steps,)),
+        ],
+        compiler_params=pltpu.CompilerParams(vmem_limit_bytes=53 * 2**20),
+        name="share_products",
+    )(hidden, down)
+
+
 def pack_kernel(proj_ref, table_ref, qkv_ref, packed_ref, sems):
     proj_rows, depth = proj_ref.shape
     table_rows = table_ref.shape[0]
@@ -106,6 +145,32 @@
     )(proj, table, qkv)
 
 
+def cut_kernel(cut, upper_from, lower_from, upper_ref, lower_ref, sems):
+    upper = pltpu.make_async_copy(upper_from.at[pl.ds(0, cut)], upper_ref, sems.at[0])
+    lower = pltpu.make_async_copy(
+        lower_from.at[pl.ds(cut, lower_ref.shape[0])], lower_ref, sems.at[1]
+    )
+    upper.start()
+    lower.start()
+    upper.wait()
+    lower.wait()
+
+
+def cut_rows(upper_from, lower_from, cut):
+    rows, depth = upper_from.shape
+    return pl.pallas_call(
+        functools.partial(cut_kernel, cut),
+        out_shape=[
+            jax.ShapeDtypeStruct((cut, depth), bf16),
+            jax.ShapeDtypeStruct((rows - cut, depth), bf16),
+        ],
+        in_specs=[pl.BlockSpec(memory_space=pl.ANY)] * 2,
+        out_specs=[pl.BlockSpec(memory_space=pltpu.VMEM)] * 2,
+        scratch_shapes=[pltpu.SemaphoreType.DMA((2,))],
+        name="cut_rows",
+    )(upper_from, lower_from)
+
+
 def is_late(m):
     return (m % 2 == 1) & (m != 1)
 
@@ -204,7 +269,6 @@
             pltpu.SemaphoreType.DMA((2 * len(pieces),)),
         ],
         compiler_params=pltpu.CompilerParams(vmem_limit_bytes=50 * 2**20),
-        cost_estimate=pl.CostEstimate(flops=0, bytes_accessed=0, transcendentals=0),
         name="early_products_and_lookup",
     )(tokens, gain, *[blocks[m] for m in early], *parts)
 
@@ -399,10 +463,8 @@
     hidden, first = first_products(gate_pre, up_pre, down_weight, width)
 
     def share(m, *others):
-        start = jnp.bitwise_xor(here, m) * width
-        block = lax.dynamic_slice_in_dim(down_weight, start, width, 1)
         factor = after(hidden, *others) if others else hidden
-        return jnp.dot(factor, block, preferred_element_type=f32)
+        return share_products(factor, down_weight, width, m)
 
     rows = pack(*after((in_proj[0], embedding[0], qkv_weight[0]), first))
     parts = {0: [(0, rows)]}
@@ -414,7 +476,7 @@
     parts[1] = [(0, swap(rows, "frames", 1))]
     sums[books - 2] = lax.optimization_barrier(share(books - 2, rows))
     for n in range(books - 3, 0, -1):
-        sums[n] = lax.optimization_barrier(share(n, parts[1][0][1]))
+        sums[n] = lax.optimization_barrier(share(n, rows))
     distance = 1
     while distance < books:
         came = None
@@ -427,7 +489,7 @@
                 came = after(came, *[sums[n] for n in range(1, books - 1)])
             sums[m ^ distance] = sums[m ^ distance] + came.astype(f32)
             if m == books - 1:
-                sums[0] = lax.optimization_barrier(share(0, came))
+                sums[0] = lax.optimization_barrier(share(0, came, parts[1][0][1]))
                 sums[0] = sums[0] + residual.astype(f32)
         distance *= 2
 
@@ -442,8 +504,9 @@
         if n in near:
             continue
         if len(sides) == 2 and 0 < cut < proj_rows:
-            upper = swap(parts[n ^ sides[0]][0][1][:cut], "frames", sides[0])
-            lower = swap(parts[n ^ sides[1]][0][1][cut:], "frames", sides[1])
+            upper, lower = cut_rows(parts[n ^ sides[0]][0][1], parts[n ^ sides[1]][0][1], cut)
+            upper = swap(upper, "frames", sides[0])
+            lower = swap(lower, "frames", sides[1])
             parts[n] = [(0, upper), (cut, lower)]
         else:
             parts[n] = [(0, swap(rows, "frames", n))]

time: 121 us -> 120 us (level)
  Pallas kernels: 17.3 us -> 31.4 us
  matrix products: 10.2 us -> 0 us
  local copies, waits for them, and re-layouts: 3.44 us -> 1.03 us
  waiting for transfers between devices: 68.5 us -> 66.8 us
    pallas_call x0 -> x4, Pallas kernels: none -> 14.1 us  [the longest x3 11.5 us: share_products(): pl.pallas_call(functools.partial(share_kernel, partner), out_shape=jax.Sh...]
    dot_general x3 -> x0, matrix products: 10.2 us -> none  [share(): return jnp.dot(factor, block, preferred_element_type=f32)]
    slice x2 -> x0, local copies, waits for them, and re-layouts: 2.42 us -> none  [the longest x1 1.24 us: per_device(): lower = swap(parts[n ^ sides[1]][0][1][cut:], 'frames', sides[1])]
    add x1, other arithmetic: 2.04 us -> 0.14 us  [per_device(): sums[m ^ distance] = sums[m ^ distance] + came.astype(f32)]
    ppermute x18, waiting for transfers between devices: 68.5 us -> 66.8 us  [swap(): lax.ppermute(value, axis, [(i, i ^ distance) for i in range(lax.axis_size...]
  transfers between devices with their start and end apart: 18 -> 18, of which waited for: 10 -> 11; matrix products, arithmetic and copies ran while one was open for 12% -> 1% of each run, Pallas kernels for 5% -> 17%
where the time goes in v9:
time: 120 us
  waiting for transfers between devices  66.8 us (56%)
  Pallas kernels  31.4 us (26%)
  starting transfers between devices  18.4 us (15%)
  other arithmetic  1.74 us (1%)
    ppermute x18, waiting for transfers between devices, swap(): lax.ppermute(value, axis, [(i, i ^ distance) for i in range(lax.axis_size...  66.8 us
    ppermute x18, starting transfers between devices, swap(): lax.ppermute(value, axis, [(i, i ^ distance) for i in range(lax.axis_size...  18.4 us
    pallas_call x3, Pallas kernels, share_products(): pl.pallas_call(functools.partial(share_kernel, partner), out_shape=jax.Sh...  11.5 us
    pallas_call x1, Pallas kernels, project_early(): pl.pallas_call(functools.partial(early_kernel, books, early, pieces, size...  6.26 us
    pallas_call x1, Pallas kernels, project_late(): pl.pallas_call(functools.partial(late_kernel, books, late, pieces, sizes)...  4.83 us
    pallas_call x1, Pallas kernels, first_products(): pl.pallas_call(first_kernel, out_shape=[jax.ShapeDtypeStruct((frames_here...  3.73 us
    pallas_call x1, Pallas kernels, cut_rows(): pl.pallas_call(functools.partial(cut_kernel, cut), out_shape=[jax.ShapeDt...  2.68 us
  transfers between devices with their start and end apart: 18, of which 11 were waited for; matrix products, arithmetic and copies ran while one was open for 1% of the time, Pallas kernels for 17%

profile of v9, /device:TPU:0, one launch (start us, length us, event | category | flops | bytes accessed | tf_op | source)
XLA Modules:
  0.0 119.6 jit_solution(15287740421132914830)
XLA Ops:
  0.0 3.7 %hidden_and_first_products.1 = (bf16[256,1536]{1,0:T(8,128)(2,1)}, bf16[256,1024]{1,0:T(8,128)(2,1)S(1)}) custom-call(bf16[256,1536]{1,0:T(8,128)(2,1)} %gate_ref.1, bf16[256,1536]{1,0:T(8,128)(2,1)} %up_ref.1, bf16[1536,4096]{1,0:T(8,128)(2,1)} %down_ref.7), custom_call_target="tpu_custom_call" | custom-call | tf_op jit(solution)/shard_map/hidden_and_first_products/pallas_call | solution.py:47
  4.5 2.6 %collective-permute-start.5 = (bf16[832,1024]{1,0:T(8,128)(2,1)S(1)}, bf16[832,1024]{1,0:T(8,128)(2,1)}, u32[]{:S(2)}, u32[]{:S(2)}) collective-permute-start(bf16[832,1024]{1,0:T(8,128)(2,1)S(1)} %pack_weight_rows.1.refs_3_.refs_5_), channel_id=1, source_target_pairs={{0,8},{4,12},{8,0},{12,4},{16,24},{20,28},{24,16},{28,20},{1,9},{5... | collective-permute-start | bytes 5111816 | tf_op jit(solution)/shard_map/ppermute | solution.py:433
  7.1 1.5 %collective-permute-start.6 = (bf16[832,1024]{1,0:T(8,128)(2,1)S(1)}, bf16[832,1024]{1,0:T(8,128)(2,1)}, u32[]{:S(2)}, u32[]{:S(2)}) collective-permute-start(bf16[832,1024]{1,0:T(8,128)(2,1)S(1)} %pack_weight_rows.1.refs_3_.refs_5_), channel_id=1, source_target_pairs={{0,16},{4,20},{8,24},{12,28},{16,0},{20,4},{24,8},{28,12},{1,17},{... | collective-permute-start | bytes 5111816 | tf_op jit(solution)/shard_map/ppermute | solution.py:433
  8.6 1.6 %collective-permute-start = (bf16[256,1024]{1,0:T(8,128)(2,1)S(1)}, bf16[256,1024]{1,0:T(8,128)(2,1)S(1)}, u32[]{:S(2)}, u32[]{:S(2)}) collective-permute-start(bf16[256,1024]{1,0:T(8,128)(2,1)S(1)} %get-tuple-element.28), channel_id=1, source_target_pairs={{0,1},{1,0},{2,3},{3,2},{4,5},{5,4},{6,7},{7,6},{8,9},{9,8},{10,11... | collective-permute-start | bytes 1572872 | tf_op jit(solution)/shard_map/ppermute | solution.py:433
  10.2 3.6 %share_products.3 = f32[256,1024]{1,0:T(8,128)} custom-call(bf16[256,1536]{1,0:T(8,128)(2,1)S(1)} %copy-done.1, bf16[1536,4096]{1,0:T(8,128)(2,1)} %down_ref.7), custom_call_target="tpu_custom_call" | custom-call | tf_op jit(solution)/shard_map/share_products/pallas_call | solution.py:91
  13.8 3.7 %share_products.4 = f32[256,1024]{1,0:T(8,128)} custom-call(bf16[256,1536]{1,0:T(8,128)(2,1)S(1)} %copy-done.1, bf16[1536,4096]{1,0:T(8,128)(2,1)} %down_ref.7), custom_call_target="tpu_custom_call" | custom-call | tf_op jit(solution)/shard_map/share_products/pallas_call | solution.py:91
  17.5 4.8 %collective-permute-done = bf16[256,1024]{1,0:T(8,128)(2,1)S(1)} collective-permute-done((bf16[256,1024]{1,0:T(8,128)(2,1)S(1)}, bf16[256,1024]{1,0:T(8,128)(2,1)S(1)}, u32[]{:S(2)}, u32[]{:S(2)}) %collective-permute-start) | collective-permute-done | bytes 524320 | tf_op jit(solution)/shard_map/ppermute | solution.py:433
  22.5 1.6 %collective-permute-start.2 = (bf16[256,1024]{1,0:T(8,128)(2,1)S(1)}, bf16[256,1024]{1,0:T(8,128)(2,1)S(1)}, u32[]{:S(2)}, u32[]{:S(2)}) collective-permute-start(bf16[256,1024]{1,0:T(8,128)(2,1)S(1)} %convert_element_type.22), channel_id=1, source_target_pairs={{0,1},{1,0},{2,3},{3,2},{4,5},{5,4},{6,7},{7,6},{8,9},{9,8},{10,11... | collective-permute-start | bytes 1572872 | tf_op jit(solution)/shard_map/ppermute | solution.py:433
  24.1 2.6 %collective-permute-start.3 = (bf16[256,1024]{1,0:T(8,128)(2,1)S(1)}, bf16[256,1024]{1,0:T(8,128)(2,1)S(1)}, u32[]{:S(2)}, u32[]{:S(2)}) collective-permute-start(bf16[256,1024]{1,0:T(8,128)(2,1)S(1)} %convert_add_fusion), channel_id=1, source_target_pairs={{0,2},{1,3},{2,0},{3,1},{4,6},{5,7},{6,4},{7,5},{8,10},{9,11},{10,... | collective-permute-start | bytes 1572872 | tf_op jit(solution)/shard_map/ppermute | solution.py:433
  26.7 4.2 %share_products.5 = f32[256,1024]{1,0:T(8,128)} custom-call(bf16[256,1536]{1,0:T(8,128)(2,1)S(1)} %copy-done.1, bf16[1536,4096]{1,0:T(8,128)(2,1)} %down_ref.7), custom_call_target="tpu_custom_call" | custom-call | tf_op jit(solution)/shard_map/share_products/pallas_call | solution.py:91
  30.9 15.7 %collective-permute-done.2 = bf16[256,1024]{1,0:T(8,128)(2,1)S(1)} collective-permute-done((bf16[256,1024]{1,0:T(8,128)(2,1)S(1)}, bf16[256,1024]{1,0:T(8,128)(2,1)S(1)}, u32[]{:S(2)}, u32[]{:S(2)}) %collective-permute-start.2) | collective-permute-done | bytes 524320 | tf_op jit(solution)/shard_map/ppermute | solution.py:433
  46.6 2.4 %collective-permute-done.3 = bf16[256,1024]{1,0:T(8,128)(2,1)S(1)} collective-permute-done((bf16[256,1024]{1,0:T(8,128)(2,1)S(1)}, bf16[256,1024]{1,0:T(8,128)(2,1)S(1)}, u32[]{:S(2)}, u32[]{:S(2)}) %collective-permute-start.3) | collective-permute-done | bytes 524320 | tf_op jit(solution)/shard_map/ppermute | solution.py:433
  49.0 1.5 %add_convert_fusion.refs_0_ = bf16[256,1024]{1,0:T(8,128)(2,1)S(1)} fusion(bf16[256,1024]{1,0:T(8,128)(2,1)S(1)} %collective-permute-done.3, bf16[256,1024]{1,0:T(8,128)(2,1)S(1)} %collective-permute-done.2, f32[256,1024]{1,0:T(8,128)} %share_products.5, bf16[256,1024]{1,0:T(8,128)(2,1)S(1)} %copy-done.13), kind=kLoop, calls=%fused_computation | loop fusion | flops 1835008 | bytes 3145728 | tf_op jit(solution)/shard_map/convert_element_type | solution.py:496
  51.1 2.7 %cut_rows.1 = (bf16[384,1024]{1,0:T(8,128)(2,1)}, bf16[448,1024]{1,0:T(8,128)(2,1)}) custom-call(bf16[832,1024]{1,0:T(8,128)(2,1)} %collective-permute-done.6.upper_from.refs_7_.refs_9_, bf16[832,1024]{1,0:T(8,128)(2,1)} %collective-permute-done.5.lower_from.refs_5_.refs_7_), custom_call_target="tpu_custom_call" | custom-call | tf_op jit(solution)/shard_map/cut_rows/pallas_call | solution.py:161
  58.0 18.4 %collective-permute-done.12.refs_10_.refs_12_ = bf16[448,1024]{1,0:T(8,128)(2,1)S(1)} collective-permute-done((bf16[448,1024]{1,0:T(8,128)(2,1)}, bf16[448,1024]{1,0:T(8,128)(2,1)S(1)}, u32[]{:S(2)}, u32[]{:S(2)}) %collective-permute-start.12) | collective-permute-done | bytes 917536 | tf_op jit(solution)/shard_map/ppermute | solution.py:433
  76.9 3.5 %collective-permute-done.4.refs_2_ = bf16[256,1024]{1,0:T(8,128)(2,1)S(1)} collective-permute-done((bf16[256,1024]{1,0:T(8,128)(2,1)S(1)}, bf16[256,1024]{1,0:T(8,128)(2,1)S(1)}, u32[]{:S(2)}, u32[]{:S(2)}) %collective-permute-start.4) | collective-permute-done | bytes 524320 | tf_op jit(solution)/shard_map/ppermute | solution.py:433
  80.4 1.7 %collective-permute-done.9.refs_1_ = bf16[256,1024]{1,0:T(8,128)(2,1)S(1)} collective-permute-done((bf16[256,1024]{1,0:T(8,128)(2,1)S(1)}, bf16[256,1024]{1,0:T(8,128)(2,1)S(1)}, u32[]{:S(2)}, u32[]{:S(2)}) %collective-permute-start.9) | collective-permute-done | bytes 524320 | tf_op jit(solution)/shard_map/ppermute | solution.py:433
  83.1 6.3 %early_products_and_lookup.1 = (f32[256,1024]{1,0:T(8,128)}, f32[256,1]{1,0:T(8,128)S(1)}, bf16[256,1024]{1,0:T(8,128)(2,1)S(1)}) custom-call(s32[1,256]{1,0:T(1,128)S(1)} %bitcast.7, bf16[1,4096]{1,0:T(2,128)(2,1)S(1)} %broadcast_in_dim.3.gain_ref, bf16[256,1024]{1,0:T(8,128)(2,1)S(1)} %add_convert_fusion.refs_0_, ...), custom_call_target="tpu_custom_call" | custom-call | tf_op jit(solution)/shard_map/early_products_and_lookup/pallas_call | solution.py:255
  89.4 5.8 %collective-permute-done.10.refs_0_ = bf16[256,1024]{1,0:T(8,128)(2,1)S(1)} collective-permute-done((bf16[256,1024]{1,0:T(8,128)(2,1)S(1)}, bf16[256,1024]{1,0:T(8,128)(2,1)S(1)}, u32[]{:S(2)}, u32[]{:S(2)}) %collective-permute-start.10) | collective-permute-done | bytes 524320 | tf_op jit(solution)/shard_map/ppermute | solution.py:433
  95.2 4.8 %late_products_and_qkv.1 = (bf16[64,1536]{1,0:T(8,128)(2,1)S(1)}, bf16[64,1536]{1,0:T(8,128)(2,1)S(1)}, bf16[64,1536]{1,0:T(8,128)(2,1)S(1)}, bf16[64,1536]{1,0:T(8,128)(2,1)S(1)}) custom-call(bf16[1,4096]{1,0:T(2,128)(2,1)S(1)} %broadcast_in_dim.3.gain_ref, bf16[256,1024]{1,0:T(8,128)(2,1)S(1)} %collective-permute-done.10.refs_0_, ...), custom_call_target="tpu_custom_call" | custom-call | tf_op jit(solution)/shard_map/late_products_and_qkv/pallas_call | solution.py:357
  100.7 2.8 %collective-permute-start.16 = (bf16[64,1536]{1,0:T(8,128)(2,1)S(1)}, bf16[64,1536]{1,0:T(8,128)(2,1)S(1)}, u32[]{:S(2)}, u32[]{:S(2)}) collective-permute-start(bf16[64,1536]{1,0:T(8,128)(2,1)S(1)} %get-tuple-element.47), channel_id=1, source_target_pairs={{0,2},{1,3},{2,0},{3,1},{4,6},{5,7},{6,4},{7,5},{8,10},{9,11},{10,... | collective-permute-start | bytes 589832 | tf_op jit(solution)/shard_map/ppermute | solution.py:433
  104.5 3.6 %collective-permute-done.15.refs_1_ = bf16[64,1536]{1,0:T(8,128)(2,1)S(1)} collective-permute-done((bf16[64,1536]{1,0:T(8,128)(2,1)S(1)}, bf16[64,1536]{1,0:T(8,128)(2,1)S(1)}, u32[]{:S(2)}, u32[]{:S(2)}) %collective-permute-start.15) | collective-permute-done | bytes 196640 | tf_op jit(solution)/shard_map/ppermute | solution.py:433
  108.2 9.2 %collective-permute-done.16.refs_2_ = bf16[64,1536]{1,0:T(8,128)(2,1)S(1)} collective-permute-done((bf16[64,1536]{1,0:T(8,128)(2,1)S(1)}, bf16[64,1536]{1,0:T(8,128)(2,1)S(1)}, u32[]{:S(2)}, u32[]{:S(2)}) %collective-permute-start.16) | collective-permute-done | bytes 196640 | tf_op jit(solution)/shard_map/ppermute | solution.py:433
  117.4 2.3 %attend_books.1 = bf16[64,4,512]{2,1,0:T(4,128)(2,1)} custom-call(bf16[64,1536]{1,0:T(8,128)(2,1)S(1)} %get-tuple-element.45.refs_0_, bf16[64,1536]{1,0:T(8,128)(2,1)S(1)} %collective-permute-done.15.refs_1_, bf16[64,1536]{1,0:T(8,128)(2,1)S(1)} %collective-permute-done.16.refs_2_, bf16[64,1536]{1,0:T(8,128)(2,1)S(1)} %collective-permute-done.17.refs_3_), custom_call_target="tpu_custom_call" | custom-call | tf_op jit(solution)/shard_map/attend_books/pallas_call | solution.py:421
  (55 shorter events, 8.9 us)
Async XLA Ops:
  4.0 9.8 %copy-start = (bf16[832,1024]{1,0:T(8,128)(2,1)}, bf16[832,1024]{1,0:T(8,128)(2,1)S(1)}, u32[]{:S(2)}) copy-start(bf16[832,1024]{1,0:T(8,128)(2,1)S(1)} %pack_weight_rows.1.refs_3_.refs_5_) | copy-start | bytes 5111812
  4.0 22.7 %collective-permute-start.1 = (bf16[832,1024]{1,0:T(8,128)(2,1)S(1)}, bf16[832,1024]{1,0:T(8,128)(2,1)S(1)}, u32[]{:S(2)}, u32[]{:S(2)}) collective-permute-start(bf16[832,1024]{1,0:T(8,128)(2,1)S(1)} %pack_weight_rows.1.refs_3_.refs_5_), channel_id=1, source_target_pairs={{0,4},{4,0},{8,12},{12,8},{16,20},{20,16},{24,28},{28,24},{1,5},{5... | collective-permute-start | bytes 5111816 | tf_op jit(solution)/shard_map/ppermute | solution.py:433
  4.5 46.0 %collective-permute-start.5 = (bf16[832,1024]{1,0:T(8,128)(2,1)S(1)}, bf16[832,1024]{1,0:T(8,128)(2,1)}, u32[]{:S(2)}, u32[]{:S(2)}) collective-permute-start(bf16[832,1024]{1,0:T(8,128)(2,1)S(1)} %pack_weight_rows.1.refs_3_.refs_5_), channel_id=1, source_target_pairs={{0,8},{4,12},{8,0},{12,4},{16,24},{20,28},{24,16},{28,20},{1,9},{5... | collective-permute-start | bytes 5111816 | tf_op jit(solution)/shard_map/ppermute | solution.py:433
  7.1 43.5 %collective-permute-start.6 = (bf16[832,1024]{1,0:T(8,128)(2,1)S(1)}, bf16[832,1024]{1,0:T(8,128)(2,1)}, u32[]{:S(2)}, u32[]{:S(2)}) collective-permute-start(bf16[832,1024]{1,0:T(8,128)(2,1)S(1)} %pack_weight_rows.1.refs_3_.refs_5_), channel_id=1, source_target_pairs={{0,16},{4,20},{8,24},{12,28},{16,0},{20,4},{24,8},{28,12},{1,17},{... | collective-permute-start | bytes 5111816 | tf_op jit(solution)/shard_map/ppermute | solution.py:433
  8.6 13.7 %collective-permute-start = (bf16[256,1024]{1,0:T(8,128)(2,1)S(1)}, bf16[256,1024]{1,0:T(8,128)(2,1)S(1)}, u32[]{:S(2)}, u32[]{:S(2)}) collective-permute-start(bf16[256,1024]{1,0:T(8,128)(2,1)S(1)} %get-tuple-element.28), channel_id=1, source_target_pairs={{0,1},{1,0},{2,3},{3,2},{4,5},{5,4},{6,7},{7,6},{8,9},{9,8},{10,11... | collective-permute-start | bytes 1572872 | tf_op jit(solution)/shard_map/ppermute | solution.py:433
  22.5 26.5 %copy-start.13 = (bf16[256,1024]{1,0:T(8,128)(2,1)S(1)}, bf16[256,1024]{1,0:T(8,128)(2,1)}, u32[]{:S(2)}) copy-start(bf16[256,1024]{1,0:T(8,128)(2,1)} %param.13) | copy-start | bytes 1572868
  22.5 24.1 %collective-permute-start.2 = (bf16[256,1024]{1,0:T(8,128)(2,1)S(1)}, bf16[256,1024]{1,0:T(8,128)(2,1)S(1)}, u32[]{:S(2)}, u32[]{:S(2)}) collective-permute-start(bf16[256,1024]{1,0:T(8,128)(2,1)S(1)} %convert_element_type.22), channel_id=1, source_target_pairs={{0,1},{1,0},{2,3},{3,2},{4,5},{5,4},{6,7},{7,6},{8,9},{9,8},{10,11... | collective-permute-start | bytes 1572872 | tf_op jit(solution)/shard_map/ppermute | solution.py:433
  24.1 24.9 %collective-permute-start.3 = (bf16[256,1024]{1,0:T(8,128)(2,1)S(1)}, bf16[256,1024]{1,0:T(8,128)(2,1)S(1)}, u32[]{:S(2)}, u32[]{:S(2)}) collective-permute-start(bf16[256,1024]{1,0:T(8,128)(2,1)S(1)} %convert_add_fusion), channel_id=1, source_target_pairs={{0,2},{1,3},{2,0},{3,1},{4,6},{5,7},{6,4},{7,5},{8,10},{9,11},{10,... | collective-permute-start | bytes 1572872 | tf_op jit(solution)/shard_map/ppermute | solution.py:433
  50.5 31.6 %copy-start.14 = (bf16[4096]{0:T(1024)(128)(2,1)S(1)}, bf16[4096]{0:T(1024)(128)(2,1)}, u32[]{:S(2)}) copy-start(bf16[4096]{0:T(1024)(128)(2,1)} %param.14) | copy-start | bytes 24580
  50.5 32.6 %copy-start.6 = (s32[256,1]{0,1:T(1,128)S(1)}, s32[256,1]{0,1:T(1,128)}, u32[]{:S(2)}) copy-start(s32[256,1]{0,1:T(1,128)} %param.17) | copy-start | bytes 3076
  50.6 5.5 %collective-permute-start.7 = (bf16[832,1024]{1,0:T(8,128)(2,1)}, bf16[832,1024]{1,0:T(8,128)(2,1)S(1)}, u32[]{:S(2)}, u32[]{:S(2)}) collective-permute-start(bf16[832,1024]{1,0:T(8,128)(2,1)} %collective-permute-done.5.lower_from.refs_5_.refs_7_), channel_id=1, source_target_pairs={{0,4},{4,0},{8,12},{12,8},{16,20},{20,16},{24,28},{28,24},{1,5},{5... | collective-permute-start | bytes 5111816 | tf_op jit(solution)/shard_map/ppermute | solution.py:433
  50.6 6.4 %collective-permute-start.8 = (bf16[832,1024]{1,0:T(8,128)(2,1)}, bf16[832,1024]{1,0:T(8,128)(2,1)}, u32[]{:S(2)}, u32[]{:S(2)}) collective-permute-start(bf16[832,1024]{1,0:T(8,128)(2,1)} %collective-permute-done.6.upper_from.refs_7_.refs_9_), channel_id=1, source_target_pairs={{0,4},{4,0},{8,12},{12,8},{16,20},{20,16},{24,28},{28,24},{1,5},{5... | collective-permute-start | bytes 5111816 | tf_op jit(solution)/shard_map/ppermute | solution.py:433
  53.8 22.6 %collective-permute-start.12 = (bf16[448,1024]{1,0:T(8,128)(2,1)}, bf16[448,1024]{1,0:T(8,128)(2,1)S(1)}, u32[]{:S(2)}, u32[]{:S(2)}) collective-permute-start(bf16[448,1024]{1,0:T(8,128)(2,1)} %get-tuple-element.41), channel_id=1, source_target_pairs={{0,16},{4,20},{8,24},{12,28},{16,0},{20,4},{24,8},{28,12},{1,17},{... | collective-permute-start | bytes 2752520 | tf_op jit(solution)/shard_map/ppermute | solution.py:433
  54.4 22.0 %collective-permute-start.11 = (bf16[384,1024]{1,0:T(8,128)(2,1)}, bf16[384,1024]{1,0:T(8,128)(2,1)S(1)}, u32[]{:S(2)}, u32[]{:S(2)}) collective-permute-start(bf16[384,1024]{1,0:T(8,128)(2,1)} %get-tuple-element.40), channel_id=1, source_target_pairs={{0,8},{4,12},{8,0},{12,4},{16,24},{20,28},{24,16},{28,20},{1,9},{5... | collective-permute-start | bytes 2359304 | tf_op jit(solution)/shard_map/ppermute | solution.py:433
  54.9 25.5 %collective-permute-start.4 = (bf16[256,1024]{1,0:T(8,128)(2,1)S(1)}, bf16[256,1024]{1,0:T(8,128)(2,1)S(1)}, u32[]{:S(2)}, u32[]{:S(2)}) collective-permute-start(bf16[256,1024]{1,0:T(8,128)(2,1)S(1)} %add_convert_fusion.refs_0_), channel_id=1, source_target_pairs={{0,2},{1,3},{2,0},{3,1},{4,6},{5,7},{6,4},{7,5},{8,10},{9,11},{10,... | collective-permute-start | bytes 1572872 | tf_op jit(solution)/shard_map/ppermute | solution.py:433
  56.1 26.1 %copy-start.8 = (bf16[832,1024]{1,0:T(8,128)(2,1)}, bf16[832,1024]{1,0:T(8,128)(2,1)S(1)}, u32[]{:S(2)}) copy-start(bf16[832,1024]{1,0:T(8,128)(2,1)S(1)} %collective-permute-done.7.refs_6_.refs_8_) | copy-start | bytes 5111812
  57.0 25.1 %collective-permute-start.9 = (bf16[256,1024]{1,0:T(8,128)(2,1)S(1)}, bf16[256,1024]{1,0:T(8,128)(2,1)S(1)}, u32[]{:S(2)}, u32[]{:S(2)}) collective-permute-start(bf16[256,1024]{1,0:T(8,128)(2,1)S(1)} %add_convert_fusion.refs_0_), channel_id=1, source_target_pairs={{0,1},{1,0},{2,3},{3,2},{4,5},{5,4},{6,7},{7,6},{8,9},{9,8},{10,11... | collective-permute-start | bytes 1572872 | tf_op jit(solution)/shard_map/ppermute | solution.py:433
  76.4 5.7 %collective-permute-start.14 = (bf16[448,1024]{1,0:T(8,128)(2,1)S(1)}, bf16[448,1024]{1,0:T(8,128)(2,1)S(1)}, u32[]{:S(2)}, u32[]{:S(2)}) collective-permute-start(bf16[448,1024]{1,0:T(8,128)(2,1)S(1)} %collective-permute-done.12.refs_10_.refs_12_), channel_id=1, source_target_pairs={{0,4},{4,0},{8,12},{12,8},{16,20},{20,16},{24,28},{28,24},{1,5},{5... | collective-permute-start | bytes 2752520 | tf_op jit(solution)/shard_map/ppermute | solution.py:433
  76.4 5.7 %collective-permute-start.13 = (bf16[384,1024]{1,0:T(8,128)(2,1)S(1)}, bf16[384,1024]{1,0:T(8,128)(2,1)S(1)}, u32[]{:S(2)}, u32[]{:S(2)}) collective-permute-start(bf16[384,1024]{1,0:T(8,128)(2,1)S(1)} %collective-permute-done.11.refs_9_.refs_11_), channel_id=1, source_target_pairs={{0,4},{4,0},{8,12},{12,8},{16,20},{20,16},{24,28},{28,24},{1,5},{5... | collective-permute-start | bytes 2359304 | tf_op jit(solution)/shard_map/ppermute | solution.py:433
  82.1 13.1 %collective-permute-start.10 = (bf16[256,1024]{1,0:T(8,128)(2,1)S(1)}, bf16[256,1024]{1,0:T(8,128)(2,1)S(1)}, u32[]{:S(2)}, u32[]{:S(2)}) collective-permute-start(bf16[256,1024]{1,0:T(8,128)(2,1)S(1)} %collective-permute-done.4.refs_2_), channel_id=1, source_target_pairs={{0,1},{1,0},{2,3},{3,2},{4,5},{5,4},{6,7},{7,6},{8,9},{9,8},{10,11... | collective-permute-start | bytes 1572872 | tf_op jit(solution)/shard_map/ppermute | solution.py:433
  83.1 12.1 %copy-start.5 = (bf16[1,1024]{1,0:T(2,128)(2,1)S(1)}, bf16[1,1024]{1,0:T(2,128)(2,1)}, u32[]{:S(2)}) copy-start(bf16[1,1024]{1,0:T(2,128)(2,1)} %refs_4_.1) | copy-start | bytes 6148
  100.1 8.1 %collective-permute-start.15 = (bf16[64,1536]{1,0:T(8,128)(2,1)S(1)}, bf16[64,1536]{1,0:T(8,128)(2,1)S(1)}, u32[]{:S(2)}, u32[]{:S(2)}) collective-permute-start(bf16[64,1536]{1,0:T(8,128)(2,1)S(1)} %get-tuple-element.46), channel_id=1, source_target_pairs={{0,1},{1,0},{2,3},{3,2},{4,5},{5,4},{6,7},{7,6},{8,9},{9,8},{10,11... | collective-permute-start | bytes 589832 | tf_op jit(solution)/shard_map/ppermute | solution.py:433
  100.7 16.7 %collective-permute-start.16 = (bf16[64,1536]{1,0:T(8,128)(2,1)S(1)}, bf16[64,1536]{1,0:T(8,128)(2,1)S(1)}, u32[]{:S(2)}, u32[]{:S(2)}) collective-permute-start(bf16[64,1536]{1,0:T(8,128)(2,1)S(1)} %get-tuple-element.47), channel_id=1, source_target_pairs={{0,2},{1,3},{2,0},{3,1},{4,6},{5,7},{6,4},{7,5},{8,10},{9,11},{10,... | collective-permute-start | bytes 589832 | tf_op jit(solution)/shard_map/ppermute | solution.py:433
  103.4 13.9 %collective-permute-start.17 = (bf16[64,1536]{1,0:T(8,128)(2,1)S(1)}, bf16[64,1536]{1,0:T(8,128)(2,1)S(1)}, u32[]{:S(2)}, u32[]{:S(2)}) collective-permute-start(bf16[64,1536]{1,0:T(8,128)(2,1)S(1)} %get-tuple-element.48), channel_id=1, source_target_pairs={{0,3},{1,2},{2,1},{3,0},{4,7},{5,6},{6,5},{7,4},{8,11},{9,10},{10,... | collective-permute-start | bytes 589832 | tf_op jit(solution)/shard_map/ppermute | solution.py:433
  (9 other events, 37.2 us)

commit v10 on v8

--- a/solution.py
+++ b/solution.py
@@ -12,7 +12,12 @@
 f32, bf16 = jnp.float32, jnp.bfloat16
 
 
-def first_kernel(gate_ref, up_ref, down_ref, hidden_ref, first_ref, gates, ups, held, sems):
+def split_frames(frames):
+    first = frames * 11 // 16 // 16 * 16
+    return [first, frames - first]
+
+
+def first_kernel(gate_ref, up_ref, down_ref, hidden_ref, one_ref, two_ref, gates, ups, held, sems):
     steps, each, width = held.shape
     books = down_ref.shape[1] // width
     start = pl.multiple_of(jnp.bitwise_xor(lax.axis_index("book"), books - 1) * width, width)
@@ -37,7 +42,8 @@
         hidden_ref[:, pl.ds(step * each, each)] = hidden
         copies[3 * step + 2].wait()
         total = total + jnp.dot(hidden, held[step], preferred_element_type=f32)
-    first_ref[...] = total.astype(bf16)
+    one_ref[...] = total[: one_ref.shape[0]].astype(bf16)
+    two_ref[...] = total[one_ref.shape[0] :].astype(bf16)
 
 
 def first_products(gate, up, down, width):
@@ -48,10 +54,10 @@
         first_kernel,
         out_shape=[
             jax.ShapeDtypeStruct((frames_here, hidden_width), bf16),
-            jax.ShapeDtypeStruct((frames_here, width), bf16),
+            *[jax.ShapeDtypeStruct((rows, width), bf16) for rows in split_frames(frames_here)],
         ],
         in_specs=[pl.BlockSpec(memory_space=pl.ANY)] * 3,
-        out_specs=[vmem] * 2,
+        out_specs=[vmem] * 3,
         scratch_shapes=[
             pltpu.VMEM((steps, frames_here, hidden_width // steps), bf16),
             pltpu.VMEM((steps, frames_here, hidden_width // steps), bf16),
@@ -59,9 +65,83 @@
             pltpu.SemaphoreType.DMA((3 * steps,)),
         ],
         compiler_params=pltpu.CompilerParams(vmem_limit_bytes=53 * 2**20),
-        cost_estimate=pl.CostEstimate(flops=0, bytes_accessed=0, transcendentals=0),
         name="hidden_and_first_products",
     )(gate, up, down)
+
+
+def share_kernel(partner, counts, hidden_ref, down_ref, *refs):
+    outs = refs[: len(counts)]
+    held, sems = refs[len(counts) :]
+    steps, each, width = held.shape
+    start = pl.multiple_of(jnp.bitwise_xor(lax.axis_index("book"), partner) * width, width)
+    copies = []
+    for step in range(steps):
+        rows = pl.ds(step * each, each)
+        copies.append(
+            pltpu.make_async_copy(
+                down_ref.at[rows, pl.ds(start, width)], held.at[step], sems.at[step]
+            )
+        )
+        copies[-1].start()
+    total = 0.0
+    for step in range(steps):
+        copies[step].wait()
+        total = total + jnp.dot(
+            hidden_ref[:, pl.ds(step * each, each)], held[step], preferred_element_type=f32
+        )
+    row = 0
+    for ref, count in zip(outs, counts):
+        ref[...] = total[row : row + count].astype(ref.dtype)
+        row += count
+
+
+def share_products(hidden, down, width, partner):
+    frames_here, hidden_width = hidden.shape
+    steps = max(hidden_width // 512, 1)
+    vmem = pl.BlockSpec(memory_space=pltpu.VMEM)
+    counts = [frames_here]
+    held_as = bf16 if partner % 2 else f32
+    return pl.pallas_call(
+        functools.partial(share_kernel, partner, counts),
+        out_shape=[jax.ShapeDtypeStruct((rows, width), held_as) for rows in counts],
+        in_specs=[vmem, pl.BlockSpec(memory_space=pl.ANY)],
+        out_specs=[vmem] * len(counts),
+        scratch_shapes=[
+            pltpu.VMEM((steps, hidden_width // steps, width), bf16),
+            pltpu.SemaphoreType.DMA((steps,)),
+        ],
+        compiler_params=pltpu.CompilerParams(vmem_limit_bytes=53 * 2**20),
+        name="share_products",
+    )(hidden, down)
+
+
+def total_kernel(starts, *refs):
+    terms = refs[: len(starts)]
+    whole_ref, two_ref, total = refs[len(starts) :]
+    total[...] = terms[0][...].astype(f32)
+    for start, ref in zip(starts[1:], terms[1:]):
+        rows = pl.ds(start, ref.shape[0])
+        total[rows, :] += ref[...].astype(f32)
+    whole_ref[...] = total[...].astype(bf16)
+    at = total.shape[0] - two_ref.shape[0]
+    two_ref[...] = total[pl.ds(at, two_ref.shape[0]), :].astype(bf16)
+
+
+def total_up(terms):
+    frames_here, width = terms[0][1].shape
+    vmem = pl.BlockSpec(memory_space=pltpu.VMEM)
+    return pl.pallas_call(
+        functools.partial(total_kernel, [start for start, _ in terms]),
+        out_shape=[
+            jax.ShapeDtypeStruct((frames_here, width), bf16),
+            jax.ShapeDtypeStruct((split_frames(frames_here)[1], width), bf16),
+        ],
+        in_specs=[vmem] * len(terms),
+        out_specs=[vmem] * 2,
+        scratch_shapes=[pltpu.VMEM((frames_here, width), f32)],
+        compiler_params=pltpu.CompilerParams(vmem_limit_bytes=16 * 2**20),
+        name="total_of_sums",
+    )(*[value for _, value in terms])
 
 
 def pack_kernel(proj_ref, table_ref, qkv_ref, packed_ref, sems):
@@ -127,7 +207,7 @@
             jax.ShapeDtypeStruct((rows - cut, depth), bf16),
         ],
         in_specs=[pl.BlockSpec(memory_space=pl.ANY)] * 2,
-        out_specs=[pl.BlockSpec(memory_space=pl.ANY)] * 2,
+        out_specs=[pl.BlockSpec(memory_space=pltpu.VMEM)] * 2,
         scratch_shapes=[pltpu.SemaphoreType.DMA((2,))],
         name="cut_rows",
     )(upper_from, lower_from)
@@ -219,7 +299,8 @@
 
 def project_early(tokens, gain, blocks, early, pieces, parts, sizes):
     books = len(blocks)
-    frames_here, width = blocks[0][0].shape
+    frames_here = sum(piece.shape[0] for piece in blocks[0])
+    width = blocks[0][0].shape[1]
     counts = [(m, len(blocks[m])) for m in early]
     given = [piece for m in early for piece in blocks[m]]
     depth = parts[0].shape[1]
@@ -243,7 +324,6 @@
             pltpu.SemaphoreType.DMA((2 * len(pieces),)),
         ],
         compiler_params=pltpu.CompilerParams(vmem_limit_bytes=50 * 2**20),
-        cost_estimate=pl.CostEstimate(flops=0, bytes_accessed=0, transcendentals=0),
         name="early_products_and_lookup",
     )(tokens, gain, *given, *parts)
 
@@ -326,7 +406,8 @@
     gain, blocks, late, projected, square, looked, depth_gain, pieces, parts, sizes, wide
 ):
     books = len(blocks)
-    frames_here, width = blocks[0][0].shape
+    frames_here = sum(piece.shape[0] for piece in blocks[0])
+    width = blocks[0][0].shape[1]
     counts = [(m, len(blocks[m])) for m in late]
     given = [piece for m in late for piece in blocks[m]]
     depth = projected.shape[1]
@@ -417,11 +498,6 @@
     return lax.optimization_barrier((value, *others))[0]
 
 
-def halves(value):
-    rows = value.shape[0] * 3 // 8 // 16 * 16
-    return [value[:rows], value[rows:]]
-
-
 def bits_of(number):
     return [1 << place for place in range(number.bit_length()) if number >> place & 1]
 
@@ -445,50 +521,43 @@
     proj_rows = in_proj.shape[1]
     gain = out_gain[None]
 
-    rows = pack(in_proj[0], embedding[0], qkv_weight[0])
+    hidden, *first = first_products(gate_pre, up_pre, down_weight, width)
+
+    def share(m, *others):
+        factor = after(hidden, *others) if others else hidden
+        return share_products(factor, down_weight, width, m)
+
+    rows = pack(*after((in_proj[0], embedding[0], qkv_weight[0]), *first))
     parts = {0: [(0, rows)]}
     near = [n for n in range(2, groups, 2) if len(bits_of(n)) == 1]
     for n in near:
         parts[n] = [(0, swap(rows, "frames", n))]
+
+    sums = {books - 1: first}
     parts[1] = [(0, swap(rows, "frames", 1))]
-
-    hidden, first = first_products(after(gate_pre, rows), up_pre, down_weight, width)
-
-    def share(m, *others):
-        start = jnp.bitwise_xor(here, m) * width
-        block = lax.dynamic_slice_in_dim(down_weight, start, width, 1)
-        factor = after(hidden, *others) if others else hidden
-        return jnp.dot(factor, block, preferred_element_type=f32)
-
-    sums = {books - 1: first, books - 2: lax.optimization_barrier(share(books - 2))}
+    sums[books - 2] = lax.optimization_barrier(share(books - 2, rows))
     for n in range(books - 3, 0, -1):
         sums[n] = lax.optimization_barrier(share(n, parts[1][0][1]))
-    sums = {m: halves(value) for m, value in sums.items()}
-    distance = 1
+    near_came = swap(first[0], "book", 1)
+    far_came = swap(first[1], "book", books - 1)
+    del sums[books - 1]
+    one = first[0].shape[0]
+    sums[0] = lax.optimization_barrier(share(0, near_came))
+    terms = {m: [(0, sums[m][0])] for m in range(0, books, 2)}
+    terms[0] += [(0, residual), (one, far_came)]
+    terms[books - 2].append((0, near_came))
+    for m in range(books - 3, 0, -2):
+        came = swap(after(sums[m][0], near_came, far_came), "book", 1)
+        terms[m ^ 1].append((0, came))
+    distance = 2
     while distance < books:
-        came = None
         for m in range(books - distance, 0, -2 * distance):
-            going = [half.astype(bf16) for half in sums.pop(m)]
-            if came is None:
-                came = [swap(half, "book", distance) for half in going]
-                midway = [came[0], going[1]] + sums.get(0, [])
-            else:
-                whole = after(jnp.concatenate(going, axis=0), came[0], sums[m + distance][0])
-                came = halves(swap(whole, "book", distance))
-            if m == books - 1:
-                first_came = came[0]
-                came[0] = after(came[0], *[sums[n][0] for n in range(1, books - 1)])
-            sums[m ^ distance] = [
-                kept + half.astype(f32) for kept, half in zip(sums[m ^ distance], came)
-            ]
-            if m == books - 1:
-                sums[0] = halves(
-                    lax.optimization_barrier(share(0, first_came)) + residual.astype(f32)
-                )
+            came = swap(total_up(terms.pop(m))[0], "book", distance)
+            terms[m ^ distance].append((0, came))
         distance *= 2
-    own = jnp.concatenate([half.astype(bf16) for half in sums[0]], axis=0)
-
-    arrived = after([parts[n][0][1] for n in near], *midway)
+    own, own_two = total_up(terms[0])
+
+    arrived = after([parts[n][0][1] for n in near], own)
     for n, value in zip(near, arrived):
         parts[n] = [(0, value)]
     cut = rows.shape[0] // 2 // 128 * 128
@@ -507,23 +576,25 @@
         parts[n + 1] = [(0, swap(parts[n][0][1], "frames", 1))]
 
     near_there = [parts[n + 1][0][1] for n in near]
-    blocks = {0: [own]}
+    blocks = {0: own}
     distance = books // 2
-    while distance:
+    while distance > 1:
         for m in sorted(blocks):
-            going = blocks[m]
-            if m == 0:
-                going = [after(own, *near_there)] if distance == 1 else halves(own)
-            blocks[m ^ distance] = [swap(piece, "book", distance) for piece in going]
+            blocks[m ^ distance] = swap(blocks[m], "book", distance)
         distance //= 2
-
-    through = blocks[1] + blocks[books // 2] + blocks[books - 1][:1]
+    blocks = {m: [block] for m, block in blocks.items()}
+    blocks[1] = [swap(after(own, *near_there), "book", 1)]
     for n in range(2, groups, 2):
         if n not in near:
             parts[n + 1] = [
-                (first, swap(after(value, *through), "frames", 1))
+                (first, swap(after(value, *blocks[books // 2], *blocks[1]), "frames", 1))
                 for first, value in parts[n]
             ]
+    for m in range(2, books, 2):
+        blocks[m + 1] = [
+            swap(after(blocks[m][0][:one], *blocks[1]), "book", 1),
+            swap(after(own_two, *blocks[m]), "book", m + 1),
+        ]
 
     pieces = [(n, first) for n in range(groups) for first, _ in parts[n]]
     arrived = [value for n in range(groups) for _, value in parts[n]]

time: 176 us -> 124 us (0.70)
  Pallas kernels: 69.9 us -> 32.5 us
  matrix products: 10.1 us -> 0 us
  waiting for transfers between devices: 56.1 us -> 62.4 us
  other arithmetic: 4.91 us -> 0 us
  local copies, waits for them, and re-layouts: 6.31 us -> 3.52 us
  starting transfers between devices: 26.7 us -> 24.8 us
    pallas_call x1, Pallas kernels: 52.7 us -> 2.66 us  [cut_rows(): pl.pallas_call(functools.partial(cut_kernel, cut), out_shape=[jax.ShapeDt...]
    pallas_call x0 -> x5, Pallas kernels: none -> 12.5 us  [the longest x3 11.5 us: share_products(): pl.pallas_call(functools.partial(share_kernel, partner, counts), out_shap...]
    dot_general x3 -> x0, matrix products: 10.1 us -> none  [share(): return jnp.dot(factor, block, preferred_element_type=f32)]
    ppermute x22 -> x20, waiting for transfers between devices: 56.1 us -> 62.4 us  [swap(): lax.ppermute(value, axis, [(i, i ^ distance) for i in range(lax.axis_size...]
    convert_element_type x3 -> x0, other arithmetic: 2.67 us -> none  [the longest x2 1.62 us: per_device(): own = jnp.concatenate([half.astype(bf16) for half in sums[0]], axis=0)]
    ppermute x22 -> x20, starting transfers between devices: 26.7 us -> 24.8 us  [swap(): lax.ppermute(value, axis, [(i, i ^ distance) for i in range(lax.axis_size...]
    unnamed x26 -> x30, local copies, waits for them, and re-layouts: 4.83 us -> 3.48 us
  transfers between devices with their start and end apart: 22 -> 20, of which waited for: 9 -> 10; matrix products, arithmetic and copies ran while one was open for 9% -> 0% of each run, Pallas kernels for 36% -> 17%
where the time goes in v10:
time: 124 us
  waiting for transfers between devices  62.4 us (50%)
  Pallas kernels  32.5 us (26%)
  starting transfers between devices  24.8 us (20%)
  local copies, waits for them, and re-layouts  3.52 us (3%)
    ppermute x20, waiting for transfers between devices, swap(): lax.ppermute(value, axis, [(i, i ^ distance) for i in range(lax.axis_size...  62.4 us
    ppermute x20, starting transfers between devices, swap(): lax.ppermute(value, axis, [(i, i ^ distance) for i in range(lax.axis_size...  24.8 us
    pallas_call x3, Pallas kernels, share_products(): pl.pallas_call(functools.partial(share_kernel, partner, counts), out_shap...  11.5 us
    pallas_call x1, Pallas kernels, project_early(): pl.pallas_call(functools.partial(early_kernel, books, counts, pieces, siz...  6.26 us
    pallas_call x1, Pallas kernels, project_late(): pl.pallas_call(functools.partial(late_kernel, books, counts, pieces, size...  4.94 us
    pallas_call x1, Pallas kernels, first_products(): pl.pallas_call(first_kernel, out_shape=[jax.ShapeDtypeStruct((frames_here...  3.73 us
    unnamed x30, local copies, waits for them, and re-layouts  3.48 us
    pallas_call x1, Pallas kernels, cut_rows(): pl.pallas_call(functools.partial(cut_kernel, cut), out_shape=[jax.ShapeDt...  2.66 us
  transfers between devices with their start and end apart: 20, of which 10 were waited for; matrix products, arithmetic and copies ran while one was open for 0% of the time, Pallas kernels for 17%

profile of v10, /device:TPU:0, one launch (start us, length us, event | category | flops | bytes accessed | tf_op | source)
XLA Modules:
  0.0 123.5 jit_solution(5886158176808695689)
XLA Ops:
  0.0 3.7 %hidden_and_first_products.1 = (bf16[256,1536]{1,0:T(8,128)(2,1)}, bf16[176,1024]{1,0:T(8,128)(2,1)S(1)}, bf16[80,1024]{1,0:T(8,128)(2,1)S(1)}) custom-call(bf16[256,1536]{1,0:T(8,128)(2,1)} %gate_ref.1, bf16[256,1536]{1,0:T(8,128)(2,1)} %up_ref.1, bf16[1536,4096]{1,0:T(8,128)(2,1)} %down_ref.7), custom_call_target="tpu_custom_call" | custom-call | tf_op jit(solution)/shard_map/hidden_and_first_products/pallas_call | solution.py:53
  4.5 2.6 %collective-permute-start.6 = (bf16[832,1024]{1,0:T(8,128)(2,1)S(1)}, bf16[832,1024]{1,0:T(8,128)(2,1)}, u32[]{:S(2)}, u32[]{:S(2)}) collective-permute-start(bf16[832,1024]{1,0:T(8,128)(2,1)S(1)} %pack_weight_rows.1.refs_3_.refs_6_), channel_id=1, source_target_pairs={{0,8},{4,12},{8,0},{12,4},{16,24},{20,28},{24,16},{28,20},{1,9},{5... | collective-permute-start | bytes 5111816 | tf_op jit(solution)/shard_map/ppermute | solution.py:494
  8.6 1.6 %collective-permute-start = (bf16[176,1024]{1,0:T(8,128)(2,1)S(1)}, bf16[176,1024]{1,0:T(8,128)(2,1)S(1)}, u32[]{:S(2)}, u32[]{:S(2)}) collective-permute-start(bf16[176,1024]{1,0:T(8,128)(2,1)S(1)} %get-tuple-element.35), channel_id=1, source_target_pairs={{0,1},{1,0},{2,3},{3,2},{4,5},{5,4},{6,7},{7,6},{8,9},{9,8},{10,11... | collective-permute-start | bytes 1081352 | tf_op jit(solution)/shard_map/ppermute | solution.py:494
  10.2 2.5 %collective-permute-start.1 = (bf16[80,1024]{1,0:T(8,128)(2,1)S(1)}, bf16[80,1024]{1,0:T(8,128)(2,1)S(1)}, u32[]{:S(2)}, u32[]{:S(2)}) collective-permute-start(bf16[80,1024]{1,0:T(8,128)(2,1)S(1)} %get-tuple-element.37), channel_id=1, source_target_pairs={{0,3},{1,2},{2,1},{3,0},{4,7},{5,6},{6,5},{7,4},{8,11},{9,10},{10,... | collective-permute-start | bytes 491528 | tf_op jit(solution)/shard_map/ppermute | solution.py:494
  12.7 3.6 %share_products.5.refs_0_ = f32[256,1024]{1,0:T(8,128)} custom-call(bf16[256,1536]{1,0:T(8,128)(2,1)S(1)} %copy-done.1, bf16[1536,4096]{1,0:T(8,128)(2,1)} %down_ref.7), custom_call_target="tpu_custom_call" | custom-call | tf_op jit(solution)/shard_map/share_products/pallas_call | solution.py:104
  16.3 2.7 %collective-permute-done.refs_1_ = bf16[176,1024]{1,0:T(8,128)(2,1)S(1)} collective-permute-done((bf16[176,1024]{1,0:T(8,128)(2,1)S(1)}, bf16[176,1024]{1,0:T(8,128)(2,1)S(1)}, u32[]{:S(2)}, u32[]{:S(2)}) %collective-permute-start) | collective-permute-done | bytes 360480 | tf_op jit(solution)/shard_map/ppermute | solution.py:494
  20.9 3.5 %collective-permute-start.4 = (bf16[256,1024]{1,0:T(8,128)(2,1)S(1)}, bf16[256,1024]{1,0:T(8,128)(2,1)S(1)}, u32[]{:S(2)}, u32[]{:S(2)}) collective-permute-start(bf16[256,1024]{1,0:T(8,128)(2,1)S(1)} %get-tuple-element.44), channel_id=1, source_target_pairs={{0,2},{1,3},{2,0},{3,1},{4,6},{5,7},{6,4},{7,5},{8,10},{9,11},{10,... | collective-permute-start | bytes 1572872 | tf_op jit(solution)/shard_map/ppermute | solution.py:494
  24.4 4.3 %share_products.4 = bf16[256,1024]{1,0:T(8,128)(2,1)S(1)} custom-call(bf16[256,1536]{1,0:T(8,128)(2,1)} %get-tuple-element.43.hidden_ref, bf16[1536,4096]{1,0:T(8,128)(2,1)} %down_ref.7), custom_call_target="tpu_custom_call" | custom-call | tf_op jit(solution)/shard_map/share_products/pallas_call | solution.py:104
  28.8 4.1 %collective-permute-start.3 = (bf16[256,1024]{1,0:T(8,128)(2,1)S(1)}, bf16[256,1024]{1,0:T(8,128)(2,1)S(1)}, u32[]{:S(2)}, u32[]{:S(2)}) collective-permute-start(bf16[256,1024]{1,0:T(8,128)(2,1)S(1)} %share_products.4), channel_id=1, source_target_pairs={{0,1},{1,0},{2,3},{3,2},{4,5},{5,4},{6,7},{7,6},{8,9},{9,8},{10,11... | collective-permute-start | bytes 1572872 | tf_op jit(solution)/shard_map/ppermute | solution.py:494
  32.8 3.6 %share_products.3.refs_0_ = f32[256,1024]{1,0:T(8,128)} custom-call(bf16[256,1536]{1,0:T(8,128)(2,1)S(1)} %copy-done.2, bf16[1536,4096]{1,0:T(8,128)(2,1)} %down_ref.7), custom_call_target="tpu_custom_call" | custom-call | tf_op jit(solution)/shard_map/share_products/pallas_call | solution.py:104
  36.5 10.5 %collective-permute-done.4.refs_4_ = bf16[256,1024]{1,0:T(8,128)(2,1)S(1)} collective-permute-done((bf16[256,1024]{1,0:T(8,128)(2,1)S(1)}, bf16[256,1024]{1,0:T(8,128)(2,1)S(1)}, u32[]{:S(2)}, u32[]{:S(2)}) %collective-permute-start.4) | collective-permute-done | bytes 524320 | tf_op jit(solution)/shard_map/ppermute | solution.py:494
  46.9 4.6 %collective-permute-done.3.refs_3_ = bf16[256,1024]{1,0:T(8,128)(2,1)S(1)} collective-permute-done((bf16[256,1024]{1,0:T(8,128)(2,1)S(1)}, bf16[256,1024]{1,0:T(8,128)(2,1)S(1)}, u32[]{:S(2)}, u32[]{:S(2)}) %collective-permute-start.3) | collective-permute-done | bytes 524320 | tf_op jit(solution)/shard_map/ppermute | solution.py:494
  53.6 2.7 %cut_rows.1 = (bf16[384,1024]{1,0:T(8,128)(2,1)}, bf16[448,1024]{1,0:T(8,128)(2,1)}) custom-call(bf16[832,1024]{1,0:T(8,128)(2,1)} %collective-permute-done.7.upper_from.refs_7_.refs_10_, bf16[832,1024]{1,0:T(8,128)(2,1)} %collective-permute-done.6.lower_from.refs_5_.refs_8_), custom_call_target="tpu_custom_call" | custom-call | tf_op jit(solution)/shard_map/cut_rows/pallas_call | solution.py:203
  57.4 2.1 %collective-permute-done.9.refs_8_.refs_11_ = bf16[832,1024]{1,0:T(8,128)(2,1)} collective-permute-done((bf16[832,1024]{1,0:T(8,128)(2,1)}, bf16[832,1024]{1,0:T(8,128)(2,1)}, u32[]{:S(2)}, u32[]{:S(2)}) %collective-permute-start.9) | collective-permute-done | bytes 1703968 | tf_op jit(solution)/shard_map/ppermute | solution.py:494
  59.6 22.4 %collective-permute-done.5.refs_2_ = bf16[256,1024]{1,0:T(8,128)(2,1)S(1)} collective-permute-done((bf16[256,1024]{1,0:T(8,128)(2,1)S(1)}, bf16[256,1024]{1,0:T(8,128)(2,1)S(1)}, u32[]{:S(2)}, u32[]{:S(2)}) %collective-permute-start.5) | collective-permute-done | bytes 524320 | tf_op jit(solution)/shard_map/ppermute | solution.py:494
  82.0 2.6 %collective-permute-done.10.refs_1_ = bf16[256,1024]{1,0:T(8,128)(2,1)S(1)} collective-permute-done((bf16[256,1024]{1,0:T(8,128)(2,1)S(1)}, bf16[256,1024]{1,0:T(8,128)(2,1)S(1)}, u32[]{:S(2)}, u32[]{:S(2)}) %collective-permute-start.10) | collective-permute-done | bytes 524320 | tf_op jit(solution)/shard_map/ppermute | solution.py:494
  85.2 1.8 %collective-permute-start.12 = (bf16[80,1024]{1,0:T(8,128)(2,1)S(1)}, bf16[80,1024]{1,0:T(8,128)(2,1)S(1)}, u32[]{:S(2)}, u32[]{:S(2)}) collective-permute-start(bf16[80,1024]{1,0:T(8,128)(2,1)S(1)} %get-tuple-element.51), channel_id=1, source_target_pairs={{0,3},{1,2},{2,1},{3,0},{4,7},{5,6},{6,5},{7,4},{8,11},{9,10},{10,... | collective-permute-start | bytes 491528 | tf_op jit(solution)/shard_map/ppermute | solution.py:494
  89.1 6.3 %early_products_and_lookup.1 = (f32[256,1024]{1,0:T(8,128)}, f32[256,1]{1,0:T(8,128)S(1)}, bf16[256,1024]{1,0:T(8,128)(2,1)S(1)}) custom-call(s32[1,256]{1,0:T(1,128)S(1)} %bitcast.7, bf16[1,4096]{1,0:T(2,128)(2,1)S(1)} %broadcast_in_dim.3.gain_ref, bf16[256,1024]{1,0:T(8,128)(2,1)S(1)} %get-tuple-element.48.refs_0_, ...), custom_call_target="tpu_custom_call" | custom-call | tf_op jit(solution)/shard_map/early_products_and_lookup/pallas_call | solution.py:310
  95.4 3.6 %collective-permute-done.12.refs_1_ = bf16[80,1024]{1,0:T(8,128)(2,1)S(1)} collective-permute-done((bf16[80,1024]{1,0:T(8,128)(2,1)S(1)}, bf16[80,1024]{1,0:T(8,128)(2,1)S(1)}, u32[]{:S(2)}, u32[]{:S(2)}) %collective-permute-start.12) | collective-permute-done | bytes 163872 | tf_op jit(solution)/shard_map/ppermute | solution.py:494
  99.0 4.9 %late_products_and_qkv.1 = (bf16[64,1536]{1,0:T(8,128)(2,1)S(1)}, bf16[64,1536]{1,0:T(8,128)(2,1)S(1)}, bf16[64,1536]{1,0:T(8,128)(2,1)S(1)}, bf16[64,1536]{1,0:T(8,128)(2,1)S(1)}) custom-call(bf16[1,4096]{1,0:T(2,128)(2,1)S(1)} %broadcast_in_dim.3.gain_ref, bf16[176,1024]{1,0:T(8,128)(2,1)S(1)} %collective-permute-done.11.refs_0_, ...), custom_call_target="tpu_custom_call" | custom-call | tf_op jit(solution)/shard_map/late_products_and_qkv/pallas_call | solution.py:417
  104.0 2.8 %collective-permute-start.18 = (bf16[64,1536]{1,0:T(8,128)(2,1)S(1)}, bf16[64,1536]{1,0:T(8,128)(2,1)S(1)}, u32[]{:S(2)}, u32[]{:S(2)}) collective-permute-start(bf16[64,1536]{1,0:T(8,128)(2,1)S(1)} %get-tuple-element.61), channel_id=1, source_target_pairs={{0,2},{1,3},{2,0},{3,1},{4,6},{5,7},{6,4},{7,5},{8,10},{9,11},{10,... | collective-permute-start | bytes 589832 | tf_op jit(solution)/shard_map/ppermute | solution.py:494
  108.4 5.1 %collective-permute-done.17.refs_1_ = bf16[64,1536]{1,0:T(8,128)(2,1)S(1)} collective-permute-done((bf16[64,1536]{1,0:T(8,128)(2,1)S(1)}, bf16[64,1536]{1,0:T(8,128)(2,1)S(1)}, u32[]{:S(2)}, u32[]{:S(2)}) %collective-permute-start.17) | collective-permute-done | bytes 196640 | tf_op jit(solution)/shard_map/ppermute | solution.py:494
  113.5 7.8 %collective-permute-done.18.refs_2_ = bf16[64,1536]{1,0:T(8,128)(2,1)S(1)} collective-permute-done((bf16[64,1536]{1,0:T(8,128)(2,1)S(1)}, bf16[64,1536]{1,0:T(8,128)(2,1)S(1)}, u32[]{:S(2)}, u32[]{:S(2)}) %collective-permute-start.18) | collective-permute-done | bytes 196640 | tf_op jit(solution)/shard_map/ppermute | solution.py:494
  121.3 2.3 %attend_books.1 = bf16[64,4,512]{2,1,0:T(4,128)(2,1)} custom-call(bf16[64,1536]{1,0:T(8,128)(2,1)S(1)} %get-tuple-element.59.refs_0_, bf16[64,1536]{1,0:T(8,128)(2,1)S(1)} %collective-permute-done.17.refs_1_, bf16[64,1536]{1,0:T(8,128)(2,1)S(1)} %collective-permute-done.18.refs_2_, bf16[64,1536]{1,0:T(8,128)(2,1)S(1)} %collective-permute-done.19.refs_3_), custom_call_target="tpu_custom_call" | custom-call | tf_op jit(solution)/shard_map/attend_books/pallas_call | solution.py:482
  (59 shorter events, 12.0 us)
Async XLA Ops:
  4.0 12.3 %copy-start = (bf16[832,1024]{1,0:T(8,128)(2,1)}, bf16[832,1024]{1,0:T(8,128)(2,1)S(1)}, u32[]{:S(2)}) copy-start(bf16[832,1024]{1,0:T(8,128)(2,1)S(1)} %pack_weight_rows.1.refs_3_.refs_6_) | copy-start | bytes 5111812
  4.0 20.5 %collective-permute-start.2 = (bf16[832,1024]{1,0:T(8,128)(2,1)S(1)}, bf16[832,1024]{1,0:T(8,128)(2,1)S(1)}, u32[]{:S(2)}, u32[]{:S(2)}) collective-permute-start(bf16[832,1024]{1,0:T(8,128)(2,1)S(1)} %pack_weight_rows.1.refs_3_.refs_6_), channel_id=1, source_target_pairs={{0,4},{4,0},{8,12},{12,8},{16,20},{20,16},{24,28},{28,24},{1,5},{5... | collective-permute-start | bytes 5111816 | tf_op jit(solution)/shard_map/ppermute | solution.py:494
  4.5 48.5 %collective-permute-start.6 = (bf16[832,1024]{1,0:T(8,128)(2,1)S(1)}, bf16[832,1024]{1,0:T(8,128)(2,1)}, u32[]{:S(2)}, u32[]{:S(2)}) collective-permute-start(bf16[832,1024]{1,0:T(8,128)(2,1)S(1)} %pack_weight_rows.1.refs_3_.refs_6_), channel_id=1, source_target_pairs={{0,8},{4,12},{8,0},{12,4},{16,24},{20,28},{24,16},{28,20},{1,9},{5... | collective-permute-start | bytes 5111816 | tf_op jit(solution)/shard_map/ppermute | solution.py:494
  7.1 45.9 %collective-permute-start.7 = (bf16[832,1024]{1,0:T(8,128)(2,1)S(1)}, bf16[832,1024]{1,0:T(8,128)(2,1)}, u32[]{:S(2)}, u32[]{:S(2)}) collective-permute-start(bf16[832,1024]{1,0:T(8,128)(2,1)S(1)} %pack_weight_rows.1.refs_3_.refs_6_), channel_id=1, source_target_pairs={{0,16},{4,20},{8,24},{12,28},{16,0},{20,4},{24,8},{28,12},{1,17},{... | collective-permute-start | bytes 5111816 | tf_op jit(solution)/shard_map/ppermute | solution.py:494
  8.6 10.4 %collective-permute-start = (bf16[176,1024]{1,0:T(8,128)(2,1)S(1)}, bf16[176,1024]{1,0:T(8,128)(2,1)S(1)}, u32[]{:S(2)}, u32[]{:S(2)}) collective-permute-start(bf16[176,1024]{1,0:T(8,128)(2,1)S(1)} %get-tuple-element.35), channel_id=1, source_target_pairs={{0,1},{1,0},{2,3},{3,2},{4,5},{5,4},{6,7},{7,6},{8,9},{9,8},{10,11... | collective-permute-start | bytes 1081352 | tf_op jit(solution)/shard_map/ppermute | solution.py:494
  10.2 18.6 %collective-permute-start.1 = (bf16[80,1024]{1,0:T(8,128)(2,1)S(1)}, bf16[80,1024]{1,0:T(8,128)(2,1)S(1)}, u32[]{:S(2)}, u32[]{:S(2)}) collective-permute-start(bf16[80,1024]{1,0:T(8,128)(2,1)S(1)} %get-tuple-element.37), channel_id=1, source_target_pairs={{0,3},{1,2},{2,1},{3,0},{4,7},{5,6},{6,5},{7,4},{8,11},{9,10},{10,... | collective-permute-start | bytes 491528 | tf_op jit(solution)/shard_map/ppermute | solution.py:494
  20.9 26.0 %collective-permute-start.4 = (bf16[256,1024]{1,0:T(8,128)(2,1)S(1)}, bf16[256,1024]{1,0:T(8,128)(2,1)S(1)}, u32[]{:S(2)}, u32[]{:S(2)}) collective-permute-start(bf16[256,1024]{1,0:T(8,128)(2,1)S(1)} %get-tuple-element.44), channel_id=1, source_target_pairs={{0,2},{1,3},{2,0},{3,1},{4,6},{5,7},{6,4},{7,5},{8,10},{9,11},{10,... | collective-permute-start | bytes 1572872 | tf_op jit(solution)/shard_map/ppermute | solution.py:494
  28.7 22.7 %copy-start.6 = (bf16[256,1024]{1,0:T(8,128)(2,1)S(1)}, bf16[256,1024]{1,0:T(8,128)(2,1)}, u32[]{:S(2)}) copy-start(bf16[256,1024]{1,0:T(8,128)(2,1)} %refs_1_.1) | copy-start | bytes 1572868
  28.8 22.7 %collective-permute-start.3 = (bf16[256,1024]{1,0:T(8,128)(2,1)S(1)}, bf16[256,1024]{1,0:T(8,128)(2,1)S(1)}, u32[]{:S(2)}, u32[]{:S(2)}) collective-permute-start(bf16[256,1024]{1,0:T(8,128)(2,1)S(1)} %share_products.4), channel_id=1, source_target_pairs={{0,1},{1,0},{2,3},{3,2},{4,5},{5,4},{6,7},{7,6},{8,9},{9,8},{10,11... | collective-permute-start | bytes 1572872 | tf_op jit(solution)/shard_map/ppermute | solution.py:494
  53.0 33.9 %copy-start.14 = (bf16[4096]{0:T(1024)(128)(2,1)S(1)}, bf16[4096]{0:T(1024)(128)(2,1)}, u32[]{:S(2)}) copy-start(bf16[4096]{0:T(1024)(128)(2,1)} %param.14) | copy-start | bytes 24580
  53.0 36.1 %copy-start.10 = (s32[256,1]{0,1:T(1,128)S(1)}, s32[256,1]{0,1:T(1,128)}, u32[]{:S(2)}) copy-start(s32[256,1]{0,1:T(1,128)} %param.17) | copy-start | bytes 3076
  53.0 4.4 %collective-permute-start.8 = (bf16[832,1024]{1,0:T(8,128)(2,1)}, bf16[832,1024]{1,0:T(8,128)(2,1)}, u32[]{:S(2)}, u32[]{:S(2)}) collective-permute-start(bf16[832,1024]{1,0:T(8,128)(2,1)} %collective-permute-done.6.lower_from.refs_5_.refs_8_), channel_id=1, source_target_pairs={{0,4},{4,0},{8,12},{12,8},{16,20},{20,16},{24,28},{28,24},{1,5},{5... | collective-permute-start | bytes 5111816 | tf_op jit(solution)/shard_map/ppermute | solution.py:494
  53.1 6.4 %collective-permute-start.9 = (bf16[832,1024]{1,0:T(8,128)(2,1)}, bf16[832,1024]{1,0:T(8,128)(2,1)}, u32[]{:S(2)}, u32[]{:S(2)}) collective-permute-start(bf16[832,1024]{1,0:T(8,128)(2,1)} %collective-permute-done.7.upper_from.refs_7_.refs_10_), channel_id=1, source_target_pairs={{0,4},{4,0},{8,12},{12,8},{16,20},{20,16},{24,28},{28,24},{1,5},{5... | collective-permute-start | bytes 5111816 | tf_op jit(solution)/shard_map/ppermute | solution.py:494
  56.2 25.7 %collective-permute-start.14 = (bf16[448,1024]{1,0:T(8,128)(2,1)}, bf16[448,1024]{1,0:T(8,128)(2,1)S(1)}, u32[]{:S(2)}, u32[]{:S(2)}) collective-permute-start(bf16[448,1024]{1,0:T(8,128)(2,1)} %get-tuple-element.53), channel_id=1, source_target_pairs={{0,16},{4,20},{8,24},{12,28},{16,0},{20,4},{24,8},{28,12},{1,17},{... | collective-permute-start | bytes 2752520 | tf_op jit(solution)/shard_map/ppermute | solution.py:494
  56.8 27.7 %collective-permute-start.13 = (bf16[384,1024]{1,0:T(8,128)(2,1)}, bf16[384,1024]{1,0:T(8,128)(2,1)S(1)}, u32[]{:S(2)}, u32[]{:S(2)}) collective-permute-start(bf16[384,1024]{1,0:T(8,128)(2,1)} %get-tuple-element.52), channel_id=1, source_target_pairs={{0,8},{4,12},{8,0},{12,4},{16,24},{20,28},{24,16},{28,20},{1,9},{5... | collective-permute-start | bytes 2359304 | tf_op jit(solution)/shard_map/ppermute | solution.py:494
  57.4 24.6 %collective-permute-start.5 = (bf16[256,1024]{1,0:T(8,128)(2,1)S(1)}, bf16[256,1024]{1,0:T(8,128)(2,1)S(1)}, u32[]{:S(2)}, u32[]{:S(2)}) collective-permute-start(bf16[256,1024]{1,0:T(8,128)(2,1)S(1)} %get-tuple-element.48.refs_0_), channel_id=1, source_target_pairs={{0,2},{1,3},{2,0},{3,1},{4,6},{5,7},{6,4},{7,5},{8,10},{9,11},{10,... | collective-permute-start | bytes 1572872 | tf_op jit(solution)/shard_map/ppermute | solution.py:494
  59.4 25.1 %collective-permute-start.10 = (bf16[256,1024]{1,0:T(8,128)(2,1)S(1)}, bf16[256,1024]{1,0:T(8,128)(2,1)S(1)}, u32[]{:S(2)}, u32[]{:S(2)}) collective-permute-start(bf16[256,1024]{1,0:T(8,128)(2,1)S(1)} %get-tuple-element.48.refs_0_), channel_id=1, source_target_pairs={{0,1},{1,0},{2,3},{3,2},{4,5},{5,4},{6,7},{7,6},{8,9},{9,8},{10,11... | collective-permute-start | bytes 1572872 | tf_op jit(solution)/shard_map/ppermute | solution.py:494
  84.6 3.6 %collective-permute-start.16 = (bf16[448,1024]{1,0:T(8,128)(2,1)S(1)}, bf16[448,1024]{1,0:T(8,128)(2,1)S(1)}, u32[]{:S(2)}, u32[]{:S(2)}) collective-permute-start(bf16[448,1024]{1,0:T(8,128)(2,1)S(1)} %collective-permute-done.14.refs_10_.refs_13_), channel_id=1, source_target_pairs={{0,4},{4,0},{8,12},{12,8},{16,20},{20,16},{24,28},{28,24},{1,5},{5... | collective-permute-start | bytes 2752520 | tf_op jit(solution)/shard_map/ppermute | solution.py:494
  84.6 3.6 %collective-permute-start.15 = (bf16[384,1024]{1,0:T(8,128)(2,1)S(1)}, bf16[384,1024]{1,0:T(8,128)(2,1)S(1)}, u32[]{:S(2)}, u32[]{:S(2)}) collective-permute-start(bf16[384,1024]{1,0:T(8,128)(2,1)S(1)} %collective-permute-done.13.refs_9_.refs_12_), channel_id=1, source_target_pairs={{0,4},{4,0},{8,12},{12,8},{16,20},{20,16},{24,28},{28,24},{1,5},{5... | collective-permute-start | bytes 2359304 | tf_op jit(solution)/shard_map/ppermute | solution.py:494
  85.1 13.9 %collective-permute-start.11 = (bf16[176,1024]{1,0:T(8,128)(2,1)S(1)}, bf16[176,1024]{1,0:T(8,128)(2,1)S(1)}, u32[]{:S(2)}, u32[]{:S(2)}) collective-permute-start(bf16[176,1024]{1,0:T(8,128)(2,1)S(1)} %slice.4), channel_id=1, source_target_pairs={{0,1},{1,0},{2,3},{3,2},{4,5},{5,4},{6,7},{7,6},{8,9},{9,8},{10,11... | collective-permute-start | bytes 1081352 | tf_op jit(solution)/shard_map/ppermute | solution.py:494
  85.2 13.8 %collective-permute-start.12 = (bf16[80,1024]{1,0:T(8,128)(2,1)S(1)}, bf16[80,1024]{1,0:T(8,128)(2,1)S(1)}, u32[]{:S(2)}, u32[]{:S(2)}) collective-permute-start(bf16[80,1024]{1,0:T(8,128)(2,1)S(1)} %get-tuple-element.51), channel_id=1, source_target_pairs={{0,3},{1,2},{2,1},{3,0},{4,7},{5,6},{6,5},{7,4},{8,11},{9,10},{10,... | collective-permute-start | bytes 491528 | tf_op jit(solution)/shard_map/ppermute | solution.py:494
  103.9 9.5 %collective-permute-start.17 = (bf16[64,1536]{1,0:T(8,128)(2,1)S(1)}, bf16[64,1536]{1,0:T(8,128)(2,1)S(1)}, u32[]{:S(2)}, u32[]{:S(2)}) collective-permute-start(bf16[64,1536]{1,0:T(8,128)(2,1)S(1)} %get-tuple-element.60), channel_id=1, source_target_pairs={{0,1},{1,0},{2,3},{3,2},{4,5},{5,4},{6,7},{7,6},{8,9},{9,8},{10,11... | collective-permute-start | bytes 589832 | tf_op jit(solution)/shard_map/ppermute | solution.py:494
  104.0 17.2 %collective-permute-start.18 = (bf16[64,1536]{1,0:T(8,128)(2,1)S(1)}, bf16[64,1536]{1,0:T(8,128)(2,1)S(1)}, u32[]{:S(2)}, u32[]{:S(2)}) collective-permute-start(bf16[64,1536]{1,0:T(8,128)(2,1)S(1)} %get-tuple-element.61), channel_id=1, source_target_pairs={{0,2},{1,3},{2,0},{3,1},{4,6},{5,7},{6,4},{7,5},{8,10},{9,11},{10,... | collective-permute-start | bytes 589832 | tf_op jit(solution)/shard_map/ppermute | solution.py:494
  106.8 14.4 %collective-permute-start.19 = (bf16[64,1536]{1,0:T(8,128)(2,1)S(1)}, bf16[64,1536]{1,0:T(8,128)(2,1)S(1)}, u32[]{:S(2)}, u32[]{:S(2)}) collective-permute-start(bf16[64,1536]{1,0:T(8,128)(2,1)S(1)} %get-tuple-element.62), channel_id=1, source_target_pairs={{0,3},{1,2},{2,1},{3,0},{4,7},{5,6},{6,5},{7,4},{8,11},{9,10},{10,... | collective-permute-start | bytes 589832 | tf_op jit(solution)/shard_map/ppermute | solution.py:494
  (11 other events, 55.8 us)

commit v11 on v9

--- a/solution.py
+++ b/solution.py
@@ -42,7 +42,7 @@
 
 def first_products(gate, up, down, width):
     frames_here, hidden_width = gate.shape
-    steps = max(hidden_width // 512, 1)
+    steps = max(hidden_width // 256, 1)
     vmem = pl.BlockSpec(memory_space=pltpu.VMEM)
     return pl.pallas_call(
         first_kernel,
@@ -190,34 +190,59 @@
 def early_kernel(books, early, pieces, sizes, tokens_ref, gain_ref, *refs):
     blocks = dict(zip(early, refs))
     parts = refs[len(early) : len(early) + len(pieces)]
-    projected_ref, square_ref, looked_ref, held, proj, table, sems = refs[
-        len(early) + len(pieces) :
-    ]
-    proj_rows, table_rows, _ = sizes
+    outs = refs[len(early) + len(pieces) :]
+    projected_ref, square_ref, later_ref, looked_ref, qkv_ref, held, proj, table, sems = outs
+    proj_rows, table_rows, qkv_rows = sizes
     here, group = lax.axis_index("book"), lax.axis_index("frames")
-    per_book = held.shape[2] // proj_rows
-
-    table_copies, proj_copies = [], []
-    for number, ((n, first), ref) in enumerate(zip(pieces, parts)):
+    width = held.shape[2]
+    per_book = width // proj_rows
+    half = qkv_rows // 2
+    depth = table.shape[1]
+    extra = qkv_ref.shape[1] - depth
+
+    started = []
+
+    def copy(source, target):
+        made = pltpu.make_async_copy(source, target, sems.at[len(started)])
+        made.start()
+        started.append(made)
+        return made
+
+    table_copies, proj_copies, qkv_copies = [], [], []
+    for (n, first), ref in zip(pieces, parts):
         if first + ref.shape[0] > proj_rows:
             g = jnp.bitwise_xor(group, n)
             start = pl.multiple_of(g * table_rows, table_rows)
-            made = pltpu.make_async_copy(
-                ref.at[pl.ds(proj_rows - first, table_rows)],
-                table.at[pl.ds(start, table_rows)],
-                sems.at[number],
+            table_copies.append(
+                copy(
+                    ref.at[pl.ds(proj_rows - first, table_rows)], table.at[pl.ds(start, table_rows)]
+                )
             )
-            made.start()
-            table_copies.append(made)
-    for number, ((n, first), ref) in enumerate(zip(pieces, parts)):
+    for (n, first), ref in zip(pieces, parts):
         count = min(ref.shape[0], proj_rows - first)
-        made = pltpu.make_async_copy(
-            ref.at[pl.ds(0, count)],
-            proj.at[pl.ds(n * proj_rows + first, count)],
-            sems.at[len(pieces) + number],
+        proj_copies.append(
+            copy(ref.at[pl.ds(0, count)], proj.at[pl.ds(n * proj_rows + first, count)])
         )
-        made.start()
-        proj_copies.append(made)
+    for (n, first), ref in zip(pieces, parts):
+        if first + ref.shape[0] > proj_rows:
+            g = jnp.bitwise_xor(group, n)
+            at_qkv = proj_rows - first + table_rows
+            at_extra = at_qkv + qkv_rows
+            start = pl.multiple_of(g * qkv_rows, qkv_rows)
+            qkv_copies.append(
+                copy(
+                    ref.at[pl.ds(at_qkv, qkv_rows)],
+                    qkv_ref.at[pl.ds(start, qkv_rows), pl.ds(0, depth)],
+                )
+            )
+            for side in range(2):
+                start = pl.multiple_of(g * qkv_rows + side * half, half)
+                qkv_copies.append(
+                    copy(
+                        ref.at[pl.ds(at_extra, half), pl.ds(side * extra, extra)],
+                        qkv_ref.at[pl.ds(start, half), pl.ds(depth, extra)],
+                    )
+                )
 
     square_ref[...] = hold_blocks(blocks, here, gain_ref, held)
     codes = lax.broadcasted_iota(jnp.int32, (table.shape[0], tokens_ref.shape[1]), 0)
@@ -231,25 +256,33 @@
     projected_ref[...] = jnp.zeros_like(projected_ref)
     for (n, first), made, ref in zip(pieces, proj_copies, parts):
         count = min(ref.shape[0], proj_rows - first)
+        rows = pl.ds(n * proj_rows + first, count)
         owner = jnp.bitwise_xor(group, n)
         book = owner // per_book
         start = pl.multiple_of((owner % per_book) * proj_rows + first, 128)
+        late = is_late(jnp.bitwise_xor(here, book))
         made.wait()
 
-        @pl.when(jnp.logical_not(is_late(jnp.bitwise_xor(here, book))))
+        @pl.when(jnp.logical_not(late))
         def _():
             projected_ref[...] += jnp.dot(
-                held[book, :, pl.ds(start, count)],
-                proj[pl.ds(n * proj_rows + first, count), :],
-                preferred_element_type=f32,
+                held[book, :, pl.ds(start, count)], proj[rows, :], preferred_element_type=f32
             )
 
-
-def project_early(tokens, gain, blocks, early, pieces, parts, sizes):
+        @pl.when(late)
+        def _():
+            slot = jnp.bitwise_xor(here, book) // 2 - 1
+            later_ref[slot, pl.ds(start, count), :] = proj[rows, :]
+
+    for made in qkv_copies:
+        made.wait()
+
+
+def project_early(tokens, gain, blocks, early, pieces, parts, sizes, wide):
     books = len(blocks)
     frames_here, width = blocks[0].shape
     depth = parts[0].shape[1]
-    proj_rows, table_rows, _ = sizes
+    proj_rows, table_rows, qkv_rows = sizes
     groups = books * width // proj_rows
     vmem = pl.BlockSpec(memory_space=pltpu.VMEM)
     return pl.pallas_call(
@@ -257,126 +290,88 @@
         out_shape=[
             jax.ShapeDtypeStruct((frames_here, depth), f32),
             jax.ShapeDtypeStruct((frames_here, 1), f32),
+            jax.ShapeDtypeStruct((books - len(early), width, depth), bf16),
             jax.ShapeDtypeStruct((frames_here, depth), bf16),
+            jax.ShapeDtypeStruct((groups * qkv_rows, wide), bf16),
         ],
         in_specs=[vmem] * (2 + len(early))
         + [pl.BlockSpec(memory_space=pl.ANY)] * len(parts),
-        out_specs=[vmem] * 3,
+        out_specs=[vmem] * 5,
         scratch_shapes=[
             pltpu.VMEM((books, frames_here, width), bf16),
             pltpu.VMEM((books * width, depth), bf16),
             pltpu.VMEM((groups * table_rows, depth), bf16),
-            pltpu.SemaphoreType.DMA((2 * len(pieces),)),
-        ],
-        compiler_params=pltpu.CompilerParams(vmem_limit_bytes=50 * 2**20),
+            pltpu.SemaphoreType.DMA((len(pieces) + 4 * groups,)),
+        ],
+        compiler_params=pltpu.CompilerParams(vmem_limit_bytes=45 * 2**20),
         name="early_products_and_lookup",
     )(tokens, gain, *[blocks[m] for m in early], *parts)
 
 
-def late_kernel(books, late, pieces, sizes, gain_ref, *refs):
+def late_kernel(books, late, gain_ref, *refs):
     blocks = dict(zip(late, refs))
-    early_ref, square_ref, looked_ref, depth_gain_ref = refs[len(late) : len(late) + 4]
-    refs = refs[len(late) + 4 :]
-    parts = refs[: len(pieces)]
-    outs = refs[len(pieces) : len(pieces) + books]
-    held, proj, qkv, packed, sems = refs[len(pieces) + books :]
-    proj_rows, table_rows, qkv_rows = sizes
-    here, group = lax.axis_index("book"), lax.axis_index("frames")
+    later_from, early_ref, square_ref, looked_ref, depth_gain_ref, qkv_from = refs[
+        len(late) : len(late) + 6
+    ]
+    refs = refs[len(late) + 6 :]
+    outs = refs[:books]
+    held, packed, later_ref, qkv_ref, sems = refs[books:]
+    later_copy = pltpu.make_async_copy(later_from, later_ref, sems.at[0])
+    later_copy.start()
+    qkv_copy = pltpu.make_async_copy(qkv_from, qkv_ref, sems.at[1])
+    qkv_copy.start()
+    here = lax.axis_index("book")
     frames_here, width = held.shape[1:]
-    per_book = width // proj_rows
-    half = qkv_rows // 2
-    depth = proj.shape[2]
-    extra = qkv.shape[1] - depth
-
-    proj_copies = []
-    for number, ((n, first), ref) in enumerate(zip(pieces, parts)):
-        count = min(ref.shape[0], proj_rows - first)
-        owner = jnp.bitwise_xor(group, n)
-        m = jnp.bitwise_xor(here, owner // per_book)
-        start = pl.multiple_of((owner % per_book) * proj_rows + first, 128)
-        slot = jnp.maximum(m // 2 - 1, 0)
-        made = pltpu.make_async_copy(
-            ref.at[pl.ds(0, count)], proj.at[slot, pl.ds(start, count)], sems.at[number]
-        )
-        pl.when(is_late(m))(made.start)
-        proj_copies.append((is_late(m), made))
-    qkv_copies = []
-
-    def copy(source, target):
-        made = pltpu.make_async_copy(source, target, sems.at[len(pieces) + len(qkv_copies)])
-        made.start()
-        qkv_copies.append(made)
-
-    for (n, first), ref in zip(pieces, parts):
-        if first + ref.shape[0] > proj_rows:
-            g = jnp.bitwise_xor(group, n)
-            at_qkv = proj_rows - first + table_rows
-            start = pl.multiple_of(g * qkv_rows, qkv_rows)
-            copy(
-                ref.at[pl.ds(at_qkv, qkv_rows)], qkv.at[pl.ds(start, qkv_rows), pl.ds(0, depth)]
-            )
-            for side in range(2):
-                start = pl.multiple_of(g * qkv_rows + side * half, half)
-                copy(
-                    ref.at[pl.ds(at_qkv + qkv_rows, half), pl.ds(side * extra, extra)],
-                    qkv.at[pl.ds(start, half), pl.ds(depth, extra)],
-                )
-
     square = square_ref[...] + hold_blocks(blocks, here, gain_ref, held)
     projected = early_ref[...]
-    for late_here, made in proj_copies:
-        pl.when(late_here)(made.wait)
+    later_copy.wait()
     for slot, m in enumerate(late):
         projected = projected + jnp.dot(
-            held[jnp.bitwise_xor(here, m)], proj[slot], preferred_element_type=f32
+            held[jnp.bitwise_xor(here, m)], later_ref[slot], preferred_element_type=f32
         )
     projected = projected * lax.rsqrt(square / (books * width) + 1e-05)
     depth_in = (projected + looked_ref[...].astype(f32)).astype(bf16).astype(f32)
     moment = jnp.mean(depth_in * depth_in, axis=-1, keepdims=True)
-    depth_normed = depth_in * lax.rsqrt(moment + 1e-05) * depth_gain_ref[...].astype(f32)
-    for made in qkv_copies:
-        made.wait()
-    packed[...] = jnp.dot(
-        depth_normed.astype(bf16), qkv[...], preferred_element_type=f32
-    ).astype(bf16)
+    depth_normed = (depth_in * lax.rsqrt(moment + 1e-05) * depth_gain_ref[...].astype(f32)).astype(bf16)
+    qkv_copy.wait()
+    packed[...] = jnp.dot(depth_normed, qkv_ref[...], preferred_element_type=f32).astype(bf16)
     rows = frames_here // books
     for m in range(books):
         start = pl.multiple_of(jnp.bitwise_xor(here, m) * rows, rows)
         outs[m][...] = packed[pl.ds(start, rows), :]
 
 
-def project_late(
-    gain, blocks, late, projected, square, looked, depth_gain, pieces, parts, sizes, wide
-):
+def project_late(gain, blocks, late, later, projected, square, looked, depth_gain, qkv):
     books = len(blocks)
     frames_here, width = blocks[0].shape
-    depth = projected.shape[1]
-    proj_rows, _, qkv_rows = sizes
-    groups = books * width // proj_rows
+    wide = qkv.shape[1]
     vmem = pl.BlockSpec(memory_space=pltpu.VMEM)
     return pl.pallas_call(
-        functools.partial(late_kernel, books, late, pieces, sizes),
+        functools.partial(late_kernel, books, late),
         out_shape=[jax.ShapeDtypeStruct((frames_here // books, wide), bf16)] * books,
-        in_specs=[vmem] * (len(late) + 5)
-        + [pl.BlockSpec(memory_space=pl.ANY)] * len(parts),
+        in_specs=[vmem] * (len(late) + 1)
+        + [pl.BlockSpec(memory_space=pl.ANY)]
+        + [vmem] * 4
+        + [pl.BlockSpec(memory_space=pl.ANY)],
         out_specs=[vmem] * books,
         scratch_shapes=[
             pltpu.VMEM((books, frames_here, width), bf16),
-            pltpu.VMEM((len(late), width, depth), bf16),
-            pltpu.VMEM((groups * qkv_rows, wide), bf16),
             pltpu.VMEM((frames_here, wide), bf16),
-            pltpu.SemaphoreType.DMA((len(pieces) + 3 * groups,)),
+            pltpu.VMEM(later.shape, bf16),
+            pltpu.VMEM(qkv.shape, bf16),
+            pltpu.SemaphoreType.DMA((2,)),
         ],
         compiler_params=pltpu.CompilerParams(vmem_limit_bytes=50 * 2**20),
         name="late_products_and_qkv",
     )(
         gain,
         *[blocks[m] for m in late],
+        later,
         projected,
         square,
         looked,
         depth_gain,
-        *parts,
+        qkv,
     )
 
 
@@ -464,6 +459,11 @@
 
     def share(m, *others):
         factor = after(hidden, *others) if others else hidden
+        if m == 0:
+            block = lax.dynamic_slice_in_dim(
+                down_weight, lax.axis_index("book") * width, width, 1
+            )
+            return jnp.dot(factor, block, preferred_element_type=f32)
         return share_products(factor, down_weight, width, m)
 
     rows = pack(*after((in_proj[0], embedding[0], qkv_weight[0]), first))
@@ -530,21 +530,11 @@
     sizes = proj_rows, embedding.shape[1], qkv_weight.shape[1]
     early = [m for m in range(books) if not is_late(m)]
     late = [m for m in range(books) if is_late(m)]
-    projected, square, looked = project_early(
-        token_ids.reshape(1, -1), gain, blocks, early, pieces, arrived, sizes
+    projected, square, later, looked, qkv = project_early(
+        token_ids.reshape(1, -1), gain, blocks, early, pieces, arrived, sizes, qkv_weight.shape[2]
     )
     packed = project_late(
-        gain,
-        blocks,
-        late,
-        projected,
-        square,
-        looked,
-        depth_gain,
-        pieces,
-        arrived,
-        sizes,
-        qkv_weight.shape[2],
+        gain, blocks, late, later, projected, square, looked, depth_gain, qkv
     )
     far = {m: swap(packed[m], "book", m) for m in range(books - 1, 0, -1)}
     return attend([packed[0]] + [far[m] for m in range(1, books)])

time: 120 us -> 119 us (level)
  Pallas kernels: 31.4 us -> 27.7 us
  matrix products: 0 us -> 2.92 us
  other arithmetic: 1.74 us -> 3.06 us
    pallas_call x3 -> x2, Pallas kernels: 11.5 us -> 7.17 us  [share_products(): pl.pallas_call(functools.partial(share_kernel, partner), out_shape=jax.Sh...]
    dot_general x0 -> x1, matrix products: none -> 2.92 us  [share(): return jnp.dot(factor, block, preferred_element_type=f32)]
    pallas_call x1, Pallas kernels: 6.26 us -> 7.91 us  [project_early(): pl.pallas_call(functools.partial(early_kernel, books, early, pieces, size...]
    convert_element_type x1, other arithmetic: 0.07 us -> 1.38 us  [per_device(): going = sums.pop(m).astype(bf16)]
    pallas_call x1, Pallas kernels: 4.83 us -> 3.61 us  [project_late(): pl.pallas_call(functools.partial(late_kernel, books, late), out_shape=[ja...]
  transfers between devices with their start and end apart: 18 -> 18, of which waited for: 11 -> 10; matrix products, arithmetic and copies ran while one was open for 1% -> 5% of each run, Pallas kernels for 17% -> 15%
where the time goes in v11:
time: 119 us; the launch traced here: 118 us
  waiting for transfers between devices  66.1 us (56%)
  Pallas kernels  27.7 us (23%)
  starting transfers between devices  18.3 us (15%)
  other arithmetic  3.06 us (3%)
  matrix products  2.92 us (2%)
    ppermute x18, waiting for transfers between devices, swap(): lax.ppermute(value, axis, [(i, i ^ distance) for i in range(lax.axis_size...  66.1 us
    ppermute x18, starting transfers between devices, swap(): lax.ppermute(value, axis, [(i, i ^ distance) for i in range(lax.axis_size...  18.3 us
    pallas_call x1, Pallas kernels, project_early(): pl.pallas_call(functools.partial(early_kernel, books, early, pieces, size...  7.91 us
    pallas_call x2, Pallas kernels, share_products(): pl.pallas_call(functools.partial(share_kernel, partner), out_shape=jax.Sh...  7.17 us
    pallas_call x1, Pallas kernels, first_products(): pl.pallas_call(first_kernel, out_shape=[jax.ShapeDtypeStruct((frames_here...  3.88 us
    pallas_call x1, Pallas kernels, project_late(): pl.pallas_call(functools.partial(late_kernel, books, late), out_shape=[ja...  3.61 us
    dot_general x1, matrix products, share(): return jnp.dot(factor, block, preferred_element_type=f32)  2.92 us
    pallas_call x1, Pallas kernels, cut_rows(): pl.pallas_call(functools.partial(cut_kernel, cut), out_shape=[jax.ShapeDt...  2.66 us
  transfers between devices with their start and end apart: 18, of which 10 were waited for; matrix products, arithmetic and copies ran while one was open for 5% of the time, Pallas kernels for 15%

profile of v11, /device:TPU:0, one launch (start us, length us, event | category | flops | bytes accessed | tf_op | source)
XLA Modules:
  0.0 118.4 jit_solution(344443287504395172)
XLA Ops:
  0.0 3.9 %hidden_and_first_products.1 = (bf16[256,1536]{1,0:T(8,128)(2,1)}, bf16[256,1024]{1,0:T(8,128)(2,1)S(1)}) custom-call(bf16[256,1536]{1,0:T(8,128)(2,1)} %gate_ref.1, bf16[256,1536]{1,0:T(8,128)(2,1)} %up_ref.1, bf16[1536,4096]{1,0:T(8,128)(2,1)} %down_ref.5), custom_call_target="tpu_custom_call" | custom-call | tf_op jit(solution)/shard_map/hidden_and_first_products/pallas_call | solution.py:47
  4.6 2.6 %collective-permute-start.6 = (bf16[832,1024]{1,0:T(8,128)(2,1)S(1)}, bf16[832,1024]{1,0:T(8,128)(2,1)}, u32[]{:S(2)}, u32[]{:S(2)}) collective-permute-start(bf16[832,1024]{1,0:T(8,128)(2,1)S(1)} %pack_weight_rows.1.refs_3_), channel_id=1, source_target_pairs={{0,16},{4,20},{8,24},{12,28},{16,0},{20,4},{24,8},{28,12},{1,17},{... | collective-permute-start | bytes 5111816 | tf_op jit(solution)/shard_map/ppermute | solution.py:428
  8.7 1.6 %collective-permute-start = (bf16[256,1024]{1,0:T(8,128)(2,1)S(1)}, bf16[256,1024]{1,0:T(8,128)(2,1)S(1)}, u32[]{:S(2)}, u32[]{:S(2)}) collective-permute-start(bf16[256,1024]{1,0:T(8,128)(2,1)S(1)} %get-tuple-element.30), channel_id=1, source_target_pairs={{0,1},{1,0},{2,3},{3,2},{4,5},{5,4},{6,7},{7,6},{8,9},{9,8},{10,11... | collective-permute-start | bytes 1572872 | tf_op jit(solution)/shard_map/ppermute | solution.py:428
  10.3 3.6 %share_products.3 = f32[256,1024]{1,0:T(8,128)} custom-call(bf16[256,1536]{1,0:T(8,128)(2,1)S(1)} %copy-done, bf16[1536,4096]{1,0:T(8,128)(2,1)} %down_ref.5), custom_call_target="tpu_custom_call" | custom-call | tf_op jit(solution)/shard_map/share_products/pallas_call | solution.py:91
  13.9 3.6 %share_products.2 = f32[256,1024]{1,0:T(8,128)} custom-call(bf16[256,1536]{1,0:T(8,128)(2,1)S(1)} %copy-done, bf16[1536,4096]{1,0:T(8,128)(2,1)} %down_ref.5), custom_call_target="tpu_custom_call" | custom-call | tf_op jit(solution)/shard_map/share_products/pallas_call | solution.py:91
  18.9 3.5 %collective-permute-done = bf16[256,1024]{1,0:T(8,128)(2,1)S(1)} collective-permute-done((bf16[256,1024]{1,0:T(8,128)(2,1)S(1)}, bf16[256,1024]{1,0:T(8,128)(2,1)S(1)}, u32[]{:S(2)}, u32[]{:S(2)}) %collective-permute-start) | collective-permute-done | bytes 524320 | tf_op jit(solution)/shard_map/ppermute | solution.py:428
  22.6 1.6 %collective-permute-start.2 = (bf16[256,1024]{1,0:T(8,128)(2,1)S(1)}, bf16[256,1024]{1,0:T(8,128)(2,1)}, u32[]{:S(2)}, u32[]{:S(2)}) collective-permute-start(bf16[256,1024]{1,0:T(8,128)(2,1)S(1)} %convert_element_type.22), channel_id=1, source_target_pairs={{0,1},{1,0},{2,3},{3,2},{4,5},{5,4},{6,7},{7,6},{8,9},{9,8},{10,11... | collective-permute-start | bytes 1572872 | tf_op jit(solution)/shard_map/ppermute | solution.py:428
  24.2 2.6 %collective-permute-start.3 = (bf16[256,1024]{1,0:T(8,128)(2,1)S(1)}, bf16[256,1024]{1,0:T(8,128)(2,1)}, u32[]{:S(2)}, u32[]{:S(2)}) collective-permute-start(bf16[256,1024]{1,0:T(8,128)(2,1)S(1)} %convert_add_fusion), channel_id=1, source_target_pairs={{0,2},{1,3},{2,0},{3,1},{4,6},{5,7},{6,4},{7,5},{8,10},{9,11},{10,... | collective-permute-start | bytes 1572872 | tf_op jit(solution)/shard_map/ppermute | solution.py:428
  26.8 2.9 %fusion = f32[256,1024]{1,0:T(8,128)S(1)} fusion(bf16[256,1536]{1,0:T(8,128)(2,1)S(1)} %copy-done, bf16[1536,4096]{1,0:T(8,128)(2,1)} %down_ref.5, s32[]{:T(128)S(6)} %select_n.3), kind=kOutput, calls=%fused_computation | convolution fusion | flops 805306368 | bytes 4980740 | tf_op jit(solution)/shard_map/dot_general | solution.py:466
  29.8 17.1 %collective-permute-done.2 = bf16[256,1024]{1,0:T(8,128)(2,1)} collective-permute-done((bf16[256,1024]{1,0:T(8,128)(2,1)S(1)}, bf16[256,1024]{1,0:T(8,128)(2,1)}, u32[]{:S(2)}, u32[]{:S(2)}) %collective-permute-start.2) | collective-permute-done | bytes 524320 | tf_op jit(solution)/shard_map/ppermute | solution.py:428
  46.8 2.4 %collective-permute-done.3 = bf16[256,1024]{1,0:T(8,128)(2,1)} collective-permute-done((bf16[256,1024]{1,0:T(8,128)(2,1)S(1)}, bf16[256,1024]{1,0:T(8,128)(2,1)}, u32[]{:S(2)}, u32[]{:S(2)}) %collective-permute-start.3) | collective-permute-done | bytes 524320 | tf_op jit(solution)/shard_map/ppermute | solution.py:428
  49.2 1.5 %add_convert_fusion.refs_0_ = bf16[256,1024]{1,0:T(8,128)(2,1)S(1)} fusion(bf16[256,1024]{1,0:T(8,128)(2,1)} %collective-permute-done.3, bf16[256,1024]{1,0:T(8,128)(2,1)} %collective-permute-done.2, f32[256,1024]{1,0:T(8,128)S(1)} %fusion, bf16[256,1024]{1,0:T(8,128)(2,1)S(1)} %copy-done.7), kind=kLoop, calls=%fused_computation.2 | loop fusion | flops 1835008 | bytes 3145728 | tf_op jit(solution)/shard_map/convert_element_type | solution.py:496
  51.4 2.7 %cut_rows.1 = (bf16[384,1024]{1,0:T(8,128)(2,1)}, bf16[448,1024]{1,0:T(8,128)(2,1)}) custom-call(bf16[832,1024]{1,0:T(8,128)(2,1)} %collective-permute-done.6.upper_from.refs_7_, bf16[832,1024]{1,0:T(8,128)(2,1)} %collective-permute-done.5.lower_from.refs_5_), custom_call_target="tpu_custom_call" | custom-call | tf_op jit(solution)/shard_map/cut_rows/pallas_call | solution.py:161
  55.5 1.8 %collective-permute-done.8.refs_8_ = bf16[832,1024]{1,0:T(8,128)(2,1)} collective-permute-done((bf16[832,1024]{1,0:T(8,128)(2,1)}, bf16[832,1024]{1,0:T(8,128)(2,1)}, u32[]{:S(2)}, u32[]{:S(2)}) %collective-permute-start.8) | collective-permute-done | bytes 1703968 | tf_op jit(solution)/shard_map/ppermute | solution.py:428
  58.2 18.5 %collective-permute-done.12.refs_10_ = bf16[448,1024]{1,0:T(8,128)(2,1)S(1)} collective-permute-done((bf16[448,1024]{1,0:T(8,128)(2,1)}, bf16[448,1024]{1,0:T(8,128)(2,1)S(1)}, u32[]{:S(2)}, u32[]{:S(2)}) %collective-permute-start.12) | collective-permute-done | bytes 917536 | tf_op jit(solution)/shard_map/ppermute | solution.py:428
  77.2 3.5 %collective-permute-done.4.refs_2_ = bf16[256,1024]{1,0:T(8,128)(2,1)S(1)} collective-permute-done((bf16[256,1024]{1,0:T(8,128)(2,1)S(1)}, bf16[256,1024]{1,0:T(8,128)(2,1)S(1)}, u32[]{:S(2)}, u32[]{:S(2)}) %collective-permute-start.4) | collective-permute-done | bytes 524320 | tf_op jit(solution)/shard_map/ppermute | solution.py:428
  80.6 1.7 %collective-permute-done.9.refs_1_ = bf16[256,1024]{1,0:T(8,128)(2,1)S(1)} collective-permute-done((bf16[256,1024]{1,0:T(8,128)(2,1)S(1)}, bf16[256,1024]{1,0:T(8,128)(2,1)S(1)}, u32[]{:S(2)}, u32[]{:S(2)}) %collective-permute-start.9) | collective-permute-done | bytes 524320 | tf_op jit(solution)/shard_map/ppermute | solution.py:428
  82.4 7.9 %early_products_and_lookup.1 = (f32[256,1024]{1,0:T(8,128)S(1)}, f32[256,1]{1,0:T(8,128)S(1)}, bf16[1,1024,1024]{2,1,0:T(8,128)(2,1)}, bf16[256,1024]{1,0:T(8,128)(2,1)S(1)}, bf16[1024,1536]{1,0:T(8,128)(2,1)}) custom-call(s32[1,256]{1,0:T(1,128)S(1)} %bitcast.8, bf16[1,4096]{1,0:T(2,128)(2,1)S(1)} %broadcast_in_dim.3.gain_ref, ...), custom_call_target="tpu_custom_call" | custom-call | tf_op jit(solution)/shard_map/early_products_and_lookup/pallas_call | solution.py:288
  90.3 5.2 %collective-permute-done.10.refs_0_ = bf16[256,1024]{1,0:T(8,128)(2,1)S(1)} collective-permute-done((bf16[256,1024]{1,0:T(8,128)(2,1)S(1)}, bf16[256,1024]{1,0:T(8,128)(2,1)S(1)}, u32[]{:S(2)}, u32[]{:S(2)}) %collective-permute-start.10) | collective-permute-done | bytes 524320 | tf_op jit(solution)/shard_map/ppermute | solution.py:428
  95.5 3.6 %late_products_and_qkv.1 = (bf16[64,1536]{1,0:T(8,128)(2,1)S(1)}, bf16[64,1536]{1,0:T(8,128)(2,1)S(1)}, bf16[64,1536]{1,0:T(8,128)(2,1)S(1)}, bf16[64,1536]{1,0:T(8,128)(2,1)S(1)}) custom-call(bf16[1,4096]{1,0:T(2,128)(2,1)S(1)} %broadcast_in_dim.3.gain_ref, bf16[256,1024]{1,0:T(8,128)(2,1)S(1)} %collective-permute-done.10.refs_0_, ...), custom_call_target="tpu_custom_call" | custom-call | tf_op jit(solution)/shard_map/late_products_and_qkv/pallas_call | solution.py:349
  99.4 2.8 %collective-permute-start.16 = (bf16[64,1536]{1,0:T(8,128)(2,1)S(1)}, bf16[64,1536]{1,0:T(8,128)(2,1)S(1)}, u32[]{:S(2)}, u32[]{:S(2)}) collective-permute-start(bf16[64,1536]{1,0:T(8,128)(2,1)S(1)} %get-tuple-element.51), channel_id=1, source_target_pairs={{0,2},{1,3},{2,0},{3,1},{4,6},{5,7},{6,4},{7,5},{8,10},{9,11},{10,... | collective-permute-start | bytes 589832 | tf_op jit(solution)/shard_map/ppermute | solution.py:428
  103.6 3.8 %collective-permute-done.15.refs_1_ = bf16[64,1536]{1,0:T(8,128)(2,1)S(1)} collective-permute-done((bf16[64,1536]{1,0:T(8,128)(2,1)S(1)}, bf16[64,1536]{1,0:T(8,128)(2,1)S(1)}, u32[]{:S(2)}, u32[]{:S(2)}) %collective-permute-start.15) | collective-permute-done | bytes 196640 | tf_op jit(solution)/shard_map/ppermute | solution.py:428
  107.3 8.8 %collective-permute-done.16.refs_2_ = bf16[64,1536]{1,0:T(8,128)(2,1)S(1)} collective-permute-done((bf16[64,1536]{1,0:T(8,128)(2,1)S(1)}, bf16[64,1536]{1,0:T(8,128)(2,1)S(1)}, u32[]{:S(2)}, u32[]{:S(2)}) %collective-permute-start.16) | collective-permute-done | bytes 196640 | tf_op jit(solution)/shard_map/ppermute | solution.py:428
  116.1 2.3 %attend_books.1 = bf16[64,4,512]{2,1,0:T(4,128)(2,1)} custom-call(bf16[64,1536]{1,0:T(8,128)(2,1)S(1)} %get-tuple-element.49.refs_0_, bf16[64,1536]{1,0:T(8,128)(2,1)S(1)} %collective-permute-done.15.refs_1_, bf16[64,1536]{1,0:T(8,128)(2,1)S(1)} %collective-permute-done.16.refs_2_, bf16[64,1536]{1,0:T(8,128)(2,1)S(1)} %collective-permute-done.17.refs_3_), custom_call_target="tpu_custom_call" | custom-call | tf_op jit(solution)/shard_map/attend_books/pallas_call | solution.py:416
  (43 shorter events, 9.0 us)
Async XLA Ops:
  3.9 6.4 %copy-start = (bf16[256,1536]{1,0:T(8,128)(2,1)S(1)}, bf16[256,1536]{1,0:T(8,128)(2,1)}, u32[]{:S(2)}) copy-start(bf16[256,1536]{1,0:T(8,128)(2,1)} %get-tuple-element.36.hidden_ref) | copy-start | bytes 2359300
  4.1 22.7 %collective-permute-start.1 = (bf16[832,1024]{1,0:T(8,128)(2,1)S(1)}, bf16[832,1024]{1,0:T(8,128)(2,1)}, u32[]{:S(2)}, u32[]{:S(2)}) collective-permute-start(bf16[832,1024]{1,0:T(8,128)(2,1)S(1)} %pack_weight_rows.1.refs_3_), channel_id=1, source_target_pairs={{0,4},{4,0},{8,12},{12,8},{16,20},{20,16},{24,28},{28,24},{1,5},{5... | collective-permute-start | bytes 5111816 | tf_op jit(solution)/shard_map/ppermute | solution.py:428
  4.6 46.1 %collective-permute-start.6 = (bf16[832,1024]{1,0:T(8,128)(2,1)S(1)}, bf16[832,1024]{1,0:T(8,128)(2,1)}, u32[]{:S(2)}, u32[]{:S(2)}) collective-permute-start(bf16[832,1024]{1,0:T(8,128)(2,1)S(1)} %pack_weight_rows.1.refs_3_), channel_id=1, source_target_pairs={{0,16},{4,20},{8,24},{12,28},{16,0},{20,4},{24,8},{28,12},{1,17},{... | collective-permute-start | bytes 5111816 | tf_op jit(solution)/shard_map/ppermute | solution.py:428
  7.2 43.5 %collective-permute-start.5 = (bf16[832,1024]{1,0:T(8,128)(2,1)S(1)}, bf16[832,1024]{1,0:T(8,128)(2,1)}, u32[]{:S(2)}, u32[]{:S(2)}) collective-permute-start(bf16[832,1024]{1,0:T(8,128)(2,1)S(1)} %pack_weight_rows.1.refs_3_), channel_id=1, source_target_pairs={{0,8},{4,12},{8,0},{12,4},{16,24},{20,28},{24,16},{28,20},{1,9},{5... | collective-permute-start | bytes 5111816 | tf_op jit(solution)/shard_map/ppermute | solution.py:428
  8.7 13.7 %collective-permute-start = (bf16[256,1024]{1,0:T(8,128)(2,1)S(1)}, bf16[256,1024]{1,0:T(8,128)(2,1)S(1)}, u32[]{:S(2)}, u32[]{:S(2)}) collective-permute-start(bf16[256,1024]{1,0:T(8,128)(2,1)S(1)} %get-tuple-element.30), channel_id=1, source_target_pairs={{0,1},{1,0},{2,3},{3,2},{4,5},{5,4},{6,7},{7,6},{8,9},{9,8},{10,11... | collective-permute-start | bytes 1572872 | tf_op jit(solution)/shard_map/ppermute | solution.py:428
  17.5 5.0 %copy-start.6 = (f32[256,1024]{1,0:T(8,128)S(1)}, f32[256,1024]{1,0:T(8,128)}, u32[]{:S(2)}) copy-start(f32[256,1024]{1,0:T(8,128)} %share_products.3) | copy-start | bytes 3145732
  22.6 24.2 %collective-permute-start.2 = (bf16[256,1024]{1,0:T(8,128)(2,1)S(1)}, bf16[256,1024]{1,0:T(8,128)(2,1)}, u32[]{:S(2)}, u32[]{:S(2)}) collective-permute-start(bf16[256,1024]{1,0:T(8,128)(2,1)S(1)} %convert_element_type.22), channel_id=1, source_target_pairs={{0,1},{1,0},{2,3},{3,2},{4,5},{5,4},{6,7},{7,6},{8,9},{9,8},{10,11... | collective-permute-start | bytes 1572872 | tf_op jit(solution)/shard_map/ppermute | solution.py:428
  24.2 25.0 %collective-permute-start.3 = (bf16[256,1024]{1,0:T(8,128)(2,1)S(1)}, bf16[256,1024]{1,0:T(8,128)(2,1)}, u32[]{:S(2)}, u32[]{:S(2)}) collective-permute-start(bf16[256,1024]{1,0:T(8,128)(2,1)S(1)} %convert_add_fusion), channel_id=1, source_target_pairs={{0,2},{1,3},{2,0},{3,1},{4,6},{5,7},{6,4},{7,5},{8,10},{9,11},{10,... | collective-permute-start | bytes 1572872 | tf_op jit(solution)/shard_map/ppermute | solution.py:428
  26.8 22.4 %copy-start.7 = (bf16[256,1024]{1,0:T(8,128)(2,1)S(1)}, bf16[256,1024]{1,0:T(8,128)(2,1)}, u32[]{:S(2)}) copy-start(bf16[256,1024]{1,0:T(8,128)(2,1)} %param.13) | copy-start | bytes 1572868
  50.7 31.6 %copy-start.8 = (bf16[4096]{0:T(1024)(128)(2,1)S(1)}, bf16[4096]{0:T(1024)(128)(2,1)}, u32[]{:S(2)}) copy-start(bf16[4096]{0:T(1024)(128)(2,1)} %param.14) | copy-start | bytes 24580
  50.8 31.6 %copy-start.5 = (s32[256,1]{0,1:T(1,128)S(1)}, s32[256,1]{0,1:T(1,128)}, u32[]{:S(2)}) copy-start(s32[256,1]{0,1:T(1,128)} %param.17) | copy-start | bytes 3076
  50.8 4.7 %collective-permute-start.7 = (bf16[832,1024]{1,0:T(8,128)(2,1)}, bf16[832,1024]{1,0:T(8,128)(2,1)}, u32[]{:S(2)}, u32[]{:S(2)}) collective-permute-start(bf16[832,1024]{1,0:T(8,128)(2,1)} %collective-permute-done.5.lower_from.refs_5_), channel_id=1, source_target_pairs={{0,4},{4,0},{8,12},{12,8},{16,20},{20,16},{24,28},{28,24},{1,5},{5... | collective-permute-start | bytes 5111816 | tf_op jit(solution)/shard_map/ppermute | solution.py:428
  50.9 6.4 %collective-permute-start.8 = (bf16[832,1024]{1,0:T(8,128)(2,1)}, bf16[832,1024]{1,0:T(8,128)(2,1)}, u32[]{:S(2)}, u32[]{:S(2)}) collective-permute-start(bf16[832,1024]{1,0:T(8,128)(2,1)} %collective-permute-done.6.upper_from.refs_7_), channel_id=1, source_target_pairs={{0,4},{4,0},{8,12},{12,8},{16,20},{20,16},{24,28},{28,24},{1,5},{5... | collective-permute-start | bytes 5111816 | tf_op jit(solution)/shard_map/ppermute | solution.py:428
  54.0 22.6 %collective-permute-start.12 = (bf16[448,1024]{1,0:T(8,128)(2,1)}, bf16[448,1024]{1,0:T(8,128)(2,1)S(1)}, u32[]{:S(2)}, u32[]{:S(2)}) collective-permute-start(bf16[448,1024]{1,0:T(8,128)(2,1)} %get-tuple-element.43), channel_id=1, source_target_pairs={{0,16},{4,20},{8,24},{12,28},{16,0},{20,4},{24,8},{28,12},{1,17},{... | collective-permute-start | bytes 2752520 | tf_op jit(solution)/shard_map/ppermute | solution.py:428
  54.6 22.0 %collective-permute-start.11 = (bf16[384,1024]{1,0:T(8,128)(2,1)}, bf16[384,1024]{1,0:T(8,128)(2,1)S(1)}, u32[]{:S(2)}, u32[]{:S(2)}) collective-permute-start(bf16[384,1024]{1,0:T(8,128)(2,1)} %get-tuple-element.42), channel_id=1, source_target_pairs={{0,8},{4,12},{8,0},{12,4},{16,24},{20,28},{24,16},{28,20},{1,9},{5... | collective-permute-start | bytes 2359304 | tf_op jit(solution)/shard_map/ppermute | solution.py:428
  55.1 25.5 %collective-permute-start.4 = (bf16[256,1024]{1,0:T(8,128)(2,1)S(1)}, bf16[256,1024]{1,0:T(8,128)(2,1)S(1)}, u32[]{:S(2)}, u32[]{:S(2)}) collective-permute-start(bf16[256,1024]{1,0:T(8,128)(2,1)S(1)} %add_convert_fusion.refs_0_), channel_id=1, source_target_pairs={{0,2},{1,3},{2,0},{3,1},{4,6},{5,7},{6,4},{7,5},{8,10},{9,11},{10,... | collective-permute-start | bytes 1572872 | tf_op jit(solution)/shard_map/ppermute | solution.py:428
  57.2 25.1 %collective-permute-start.9 = (bf16[256,1024]{1,0:T(8,128)(2,1)S(1)}, bf16[256,1024]{1,0:T(8,128)(2,1)S(1)}, u32[]{:S(2)}, u32[]{:S(2)}) collective-permute-start(bf16[256,1024]{1,0:T(8,128)(2,1)S(1)} %add_convert_fusion.refs_0_), channel_id=1, source_target_pairs={{0,1},{1,0},{2,3},{3,2},{4,5},{5,4},{6,7},{7,6},{8,9},{9,8},{10,11... | collective-permute-start | bytes 1572872 | tf_op jit(solution)/shard_map/ppermute | solution.py:428
  76.6 5.7 %collective-permute-start.14 = (bf16[448,1024]{1,0:T(8,128)(2,1)S(1)}, bf16[448,1024]{1,0:T(8,128)(2,1)S(1)}, u32[]{:S(2)}, u32[]{:S(2)}) collective-permute-start(bf16[448,1024]{1,0:T(8,128)(2,1)S(1)} %collective-permute-done.12.refs_10_), channel_id=1, source_target_pairs={{0,4},{4,0},{8,12},{12,8},{16,20},{20,16},{24,28},{28,24},{1,5},{5... | collective-permute-start | bytes 2752520 | tf_op jit(solution)/shard_map/ppermute | solution.py:428
  76.7 5.7 %collective-permute-start.13 = (bf16[384,1024]{1,0:T(8,128)(2,1)S(1)}, bf16[384,1024]{1,0:T(8,128)(2,1)S(1)}, u32[]{:S(2)}, u32[]{:S(2)}) collective-permute-start(bf16[384,1024]{1,0:T(8,128)(2,1)S(1)} %collective-permute-done.11.refs_9_), channel_id=1, source_target_pairs={{0,4},{4,0},{8,12},{12,8},{16,20},{20,16},{24,28},{28,24},{1,5},{5... | collective-permute-start | bytes 2359304 | tf_op jit(solution)/shard_map/ppermute | solution.py:428
  82.3 13.1 %collective-permute-start.10 = (bf16[256,1024]{1,0:T(8,128)(2,1)S(1)}, bf16[256,1024]{1,0:T(8,128)(2,1)S(1)}, u32[]{:S(2)}, u32[]{:S(2)}) collective-permute-start(bf16[256,1024]{1,0:T(8,128)(2,1)S(1)} %collective-permute-done.4.refs_2_), channel_id=1, source_target_pairs={{0,1},{1,0},{2,3},{3,2},{4,5},{5,4},{6,7},{7,6},{8,9},{9,8},{10,11... | collective-permute-start | bytes 1572872 | tf_op jit(solution)/shard_map/ppermute | solution.py:428
  82.4 13.1 %copy-start.4 = (bf16[1,1024]{1,0:T(2,128)(2,1)S(1)}, bf16[1,1024]{1,0:T(2,128)(2,1)}, u32[]{:S(2)}) copy-start(bf16[1,1024]{1,0:T(2,128)(2,1)} %refs_5_.1) | copy-start | bytes 6148
  99.1 8.2 %collective-permute-start.15 = (bf16[64,1536]{1,0:T(8,128)(2,1)S(1)}, bf16[64,1536]{1,0:T(8,128)(2,1)S(1)}, u32[]{:S(2)}, u32[]{:S(2)}) collective-permute-start(bf16[64,1536]{1,0:T(8,128)(2,1)S(1)} %get-tuple-element.50), channel_id=1, source_target_pairs={{0,1},{1,0},{2,3},{3,2},{4,5},{5,4},{6,7},{7,6},{8,9},{9,8},{10,11... | collective-permute-start | bytes 589832 | tf_op jit(solution)/shard_map/ppermute | solution.py:428
  99.4 16.7 %collective-permute-start.16 = (bf16[64,1536]{1,0:T(8,128)(2,1)S(1)}, bf16[64,1536]{1,0:T(8,128)(2,1)S(1)}, u32[]{:S(2)}, u32[]{:S(2)}) collective-permute-start(bf16[64,1536]{1,0:T(8,128)(2,1)S(1)} %get-tuple-element.51), channel_id=1, source_target_pairs={{0,2},{1,3},{2,0},{3,1},{4,6},{5,7},{6,4},{7,5},{8,10},{9,11},{10,... | collective-permute-start | bytes 589832 | tf_op jit(solution)/shard_map/ppermute | solution.py:428
  102.2 13.9 %collective-permute-start.17 = (bf16[64,1536]{1,0:T(8,128)(2,1)S(1)}, bf16[64,1536]{1,0:T(8,128)(2,1)S(1)}, u32[]{:S(2)}, u32[]{:S(2)}) collective-permute-start(bf16[64,1536]{1,0:T(8,128)(2,1)S(1)} %get-tuple-element.52), channel_id=1, source_target_pairs={{0,3},{1,2},{2,1},{3,0},{4,7},{5,6},{6,5},{7,4},{8,11},{9,10},{10,... | collective-permute-start | bytes 589832 | tf_op jit(solution)/shard_map/ppermute | solution.py:428
  (3 other events, 11.7 us)

commit v12 on v11

--- a/solution.py
+++ b/solution.py
@@ -42,7 +42,7 @@
 
 def first_products(gate, up, down, width):
     frames_here, hidden_width = gate.shape
-    steps = max(hidden_width // 256, 1)
+    steps = max(hidden_width // 512, 1)
     vmem = pl.BlockSpec(memory_space=pltpu.VMEM)
     return pl.pallas_call(
         first_kernel,
@@ -477,20 +477,22 @@
     sums[books - 2] = lax.optimization_barrier(share(books - 2, rows))
     for n in range(books - 3, 0, -1):
         sums[n] = lax.optimization_barrier(share(n, rows))
-    distance = 1
+    came = swap(sums.pop(books - 1).astype(bf16), "book", 1)
+    came = after(came, *[sums[n] for n in range(1, books - 1)])
+    onward = (sums.pop(books - 2) + came.astype(f32)).astype(bf16)
+    far_came = swap(onward, "book", 2)
+    last = lax.optimization_barrier(share(0, came, parts[1][0][1]))
+    sums[0] = last + residual.astype(f32)
+    for m in range(books - 3, 0, -2):
+        near_came = swap(after(sums.pop(m).astype(bf16), onward, last), "book", 1)
+        sums[m ^ 1] = sums[m ^ 1] + near_came.astype(f32)
+    sums[(books - 2) ^ 2] = sums[(books - 2) ^ 2] + far_came.astype(f32)
+    distance = 2
     while distance < books:
-        came = None
         for m in range(books - distance, 0, -2 * distance):
-            going = sums.pop(m).astype(bf16)
-            if came is not None:
-                going = after(going, came, sums[m + distance])
-            came = swap(going, "book", distance)
-            if m == books - 1:
-                came = after(came, *[sums[n] for n in range(1, books - 1)])
-            sums[m ^ distance] = sums[m ^ distance] + came.astype(f32)
-            if m == books - 1:
-                sums[0] = lax.optimization_barrier(share(0, came, parts[1][0][1]))
-                sums[0] = sums[0] + residual.astype(f32)
+            if m in sums:
+                came = swap(sums.pop(m).astype(bf16), "book", distance)
+                sums[m ^ distance] = sums[m ^ distance] + came.astype(f32)
         distance *= 2
 
     blocks = {0: sums[0].astype(bf16)}

time: 119 us -> 120 us (level)
  starting transfers between devices: 18.3 us -> 22.2 us
  waiting for transfers between devices: 66.1 us -> 63 us
    ppermute x18, starting transfers between devices: 18.3 us -> 22.2 us  [swap(): lax.ppermute(value, axis, [(i, i ^ distance) for i in range(lax.axis_size...]
    ppermute x18, waiting for transfers between devices: 66.1 us -> 63 us  [swap(): lax.ppermute(value, axis, [(i, i ^ distance) for i in range(lax.axis_size...]
    convert_element_type x1 -> x2, other arithmetic: 1.38 us -> 2.8 us  [the longest x1 1.5 us: per_device(): onward = (sums.pop(books - 2) + came.astype(f32)).astype(bf16)]
    convert_element_type x1, other arithmetic: 1.54 us -> 0.33 us  [per_device(): blocks = {0: sums[0].astype(bf16)}]
  transfers between devices with their start and end apart: 18 -> 18, of which waited for: 10 -> 9; matrix products, arithmetic and copies ran while one was open for 5% -> 5% of each run, Pallas kernels for 15% -> 15%
where the time goes in v12:
time: 120 us; the launch traced here: 119 us
  waiting for transfers between devices  63 us (52%)
  Pallas kernels  27.5 us (23%)
  starting transfers between devices  22.2 us (18%)
  other arithmetic  3.13 us (3%)
  matrix products  2.86 us (2%)
    ppermute x18, waiting for transfers between devices, swap(): lax.ppermute(value, axis, [(i, i ^ distance) for i in range(lax.axis_size...  63 us
    ppermute x18, starting transfers between devices, swap(): lax.ppermute(value, axis, [(i, i ^ distance) for i in range(lax.axis_size...  22.2 us
    pallas_call x1, Pallas kernels, project_early(): pl.pallas_call(functools.partial(early_kernel, books, early, pieces, size...  7.91 us
    pallas_call x2, Pallas kernels, share_products(): pl.pallas_call(functools.partial(share_kernel, partner), out_shape=jax.Sh...  7.16 us
    pallas_call x1, Pallas kernels, first_products(): pl.pallas_call(first_kernel, out_shape=[jax.ShapeDtypeStruct((frames_here...  3.74 us
    pallas_call x1, Pallas kernels, project_late(): pl.pallas_call(functools.partial(late_kernel, books, late), out_shape=[ja...  3.61 us
    dot_general x1, matrix products, share(): return jnp.dot(factor, block, preferred_element_type=f32)  2.86 us
    pallas_call x1, Pallas kernels, cut_rows(): pl.pallas_call(functools.partial(cut_kernel, cut), out_shape=[jax.ShapeDt...  2.63 us
  transfers between devices with their start and end apart: 18, of which 9 were waited for; matrix products, arithmetic and copies ran while one was open for 5% of the time, Pallas kernels for 15%

profile of v12, /device:TPU:0, one launch (start us, length us, event | category | flops | bytes accessed | tf_op | source)
XLA Modules:
  0.0 119.0 jit_solution(4780762279060186976)
XLA Ops:
  0.0 3.7 %hidden_and_first_products.1 = (bf16[256,1536]{1,0:T(8,128)(2,1)}, bf16[256,1024]{1,0:T(8,128)(2,1)S(1)}) custom-call(bf16[256,1536]{1,0:T(8,128)(2,1)} %gate_ref.1, bf16[256,1536]{1,0:T(8,128)(2,1)} %up_ref.1, bf16[1536,4096]{1,0:T(8,128)(2,1)} %down_ref.5), custom_call_target="tpu_custom_call" | custom-call | tf_op jit(solution)/shard_map/hidden_and_first_products/pallas_call | solution.py:47
  4.5 2.7 %collective-permute-start = (bf16[256,1024]{1,0:T(8,128)(2,1)S(1)}, bf16[256,1024]{1,0:T(8,128)(2,1)}, u32[]{:S(2)}, u32[]{:S(2)}) collective-permute-start(bf16[256,1024]{1,0:T(8,128)(2,1)S(1)} %get-tuple-element.30), channel_id=1, source_target_pairs={{0,1},{1,0},{2,3},{3,2},{4,5},{5,4},{6,7},{7,6},{8,9},{9,8},{10,11... | collective-permute-start | bytes 1572872 | tf_op jit(solution)/shard_map/ppermute | solution.py:428
  7.2 1.5 %collective-permute-start.6 = (bf16[832,1024]{1,0:T(8,128)(2,1)S(1)}, bf16[832,1024]{1,0:T(8,128)(2,1)}, u32[]{:S(2)}, u32[]{:S(2)}) collective-permute-start(bf16[832,1024]{1,0:T(8,128)(2,1)S(1)} %pack_weight_rows.1.refs_3_), channel_id=1, source_target_pairs={{0,16},{4,20},{8,24},{12,28},{16,0},{20,4},{24,8},{28,12},{1,17},{... | collective-permute-start | bytes 5111816 | tf_op jit(solution)/shard_map/ppermute | solution.py:428
  10.2 3.6 %share_products.3 = f32[256,1024]{1,0:T(8,128)} custom-call(bf16[256,1536]{1,0:T(8,128)(2,1)S(1)} %copy-done, bf16[1536,4096]{1,0:T(8,128)(2,1)} %down_ref.5), custom_call_target="tpu_custom_call" | custom-call | tf_op jit(solution)/shard_map/share_products/pallas_call | solution.py:91
  13.8 3.6 %share_products.2 = f32[256,1024]{1,0:T(8,128)} custom-call(bf16[256,1536]{1,0:T(8,128)(2,1)S(1)} %copy-done, bf16[1536,4096]{1,0:T(8,128)(2,1)} %down_ref.5), custom_call_target="tpu_custom_call" | custom-call | tf_op jit(solution)/shard_map/share_products/pallas_call | solution.py:91
  19.8 1.5 %add_convert_fusion.1 = bf16[256,1024]{1,0:T(8,128)(2,1)S(1)} fusion(f32[256,1024]{1,0:T(8,128)} %share_products.3, bf16[256,1024]{1,0:T(8,128)(2,1)} %collective-permute-done), kind=kLoop, calls=%fused_computation.3 | loop fusion | flops 786432 | bytes 2097152 | tf_op jit(solution)/shard_map/convert_element_type | solution.py:482
  21.3 2.8 %collective-permute-start.3 = (bf16[256,1024]{1,0:T(8,128)(2,1)S(1)}, bf16[256,1024]{1,0:T(8,128)(2,1)S(1)}, u32[]{:S(2)}, u32[]{:S(2)}) collective-permute-start(bf16[256,1024]{1,0:T(8,128)(2,1)S(1)} %add_convert_fusion.1), channel_id=1, source_target_pairs={{0,2},{1,3},{2,0},{3,1},{4,6},{5,7},{6,4},{7,5},{8,10},{9,11},{10,... | collective-permute-start | bytes 1572872 | tf_op jit(solution)/shard_map/ppermute | solution.py:428
  24.1 2.9 %fusion = f32[256,1024]{1,0:T(8,128)S(1)} fusion(bf16[256,1536]{1,0:T(8,128)(2,1)S(1)} %copy-done, bf16[1536,4096]{1,0:T(8,128)(2,1)} %down_ref.5, s32[]{:T(128)S(6)} %select_n.3), kind=kOutput, calls=%fused_computation | convolution fusion | flops 805306368 | bytes 4980740 | tf_op jit(solution)/shard_map/dot_general | solution.py:466
  27.0 1.6 %collective-permute-start.2 = (bf16[256,1024]{1,0:T(8,128)(2,1)S(1)}, bf16[256,1024]{1,0:T(8,128)(2,1)S(1)}, u32[]{:S(2)}, u32[]{:S(2)}) collective-permute-start(bf16[256,1024]{1,0:T(8,128)(2,1)S(1)} %convert_element_type.22), channel_id=1, source_target_pairs={{0,1},{1,0},{2,3},{3,2},{4,5},{5,4},{6,7},{7,6},{8,9},{9,8},{10,11... | collective-permute-start | bytes 1572872 | tf_op jit(solution)/shard_map/ppermute | solution.py:428
  28.7 18.6 %collective-permute-done.3 = bf16[256,1024]{1,0:T(8,128)(2,1)S(1)} collective-permute-done((bf16[256,1024]{1,0:T(8,128)(2,1)S(1)}, bf16[256,1024]{1,0:T(8,128)(2,1)S(1)}, u32[]{:S(2)}, u32[]{:S(2)}) %collective-permute-start.3) | collective-permute-done | bytes 524320 | tf_op jit(solution)/shard_map/ppermute | solution.py:428
  47.3 3.1 %collective-permute-done.2 = bf16[256,1024]{1,0:T(8,128)(2,1)S(1)} collective-permute-done((bf16[256,1024]{1,0:T(8,128)(2,1)S(1)}, bf16[256,1024]{1,0:T(8,128)(2,1)S(1)}, u32[]{:S(2)}, u32[]{:S(2)}) %collective-permute-start.2) | collective-permute-done | bytes 524320 | tf_op jit(solution)/shard_map/ppermute | solution.py:428
  51.4 2.6 %cut_rows.1 = (bf16[384,1024]{1,0:T(8,128)(2,1)}, bf16[448,1024]{1,0:T(8,128)(2,1)}) custom-call(bf16[832,1024]{1,0:T(8,128)(2,1)} %collective-permute-done.6.upper_from.refs_7_, bf16[832,1024]{1,0:T(8,128)(2,1)} %collective-permute-done.5.lower_from.refs_5_), custom_call_target="tpu_custom_call" | custom-call | tf_op jit(solution)/shard_map/cut_rows/pallas_call | solution.py:161
  54.0 1.6 %collective-permute-start.12 = (bf16[448,1024]{1,0:T(8,128)(2,1)}, bf16[448,1024]{1,0:T(8,128)(2,1)S(1)}, u32[]{:S(2)}, u32[]{:S(2)}) collective-permute-start(bf16[448,1024]{1,0:T(8,128)(2,1)} %get-tuple-element.43), channel_id=1, source_target_pairs={{0,16},{4,20},{8,24},{12,28},{16,0},{20,4},{24,8},{28,12},{1,17},{... | collective-permute-start | bytes 2752520 | tf_op jit(solution)/shard_map/ppermute | solution.py:428
  57.6 2.5 %collective-permute-start.9 = (bf16[256,1024]{1,0:T(8,128)(2,1)S(1)}, bf16[256,1024]{1,0:T(8,128)(2,1)S(1)}, u32[]{:S(2)}, u32[]{:S(2)}) collective-permute-start(bf16[256,1024]{1,0:T(8,128)(2,1)S(1)} %add_convert_fusion.refs_0_), channel_id=1, source_target_pairs={{0,1},{1,0},{2,3},{3,2},{4,5},{5,4},{6,7},{7,6},{8,9},{9,8},{10,11... | collective-permute-start | bytes 1572872 | tf_op jit(solution)/shard_map/ppermute | solution.py:428
  60.1 16.6 %collective-permute-done.12.refs_10_ = bf16[448,1024]{1,0:T(8,128)(2,1)S(1)} collective-permute-done((bf16[448,1024]{1,0:T(8,128)(2,1)}, bf16[448,1024]{1,0:T(8,128)(2,1)S(1)}, u32[]{:S(2)}, u32[]{:S(2)}) %collective-permute-start.12) | collective-permute-done | bytes 917536 | tf_op jit(solution)/shard_map/ppermute | solution.py:428
  77.1 5.3 %collective-permute-done.4.refs_2_ = bf16[256,1024]{1,0:T(8,128)(2,1)S(1)} collective-permute-done((bf16[256,1024]{1,0:T(8,128)(2,1)S(1)}, bf16[256,1024]{1,0:T(8,128)(2,1)S(1)}, u32[]{:S(2)}, u32[]{:S(2)}) %collective-permute-start.4) | collective-permute-done | bytes 524320 | tf_op jit(solution)/shard_map/ppermute | solution.py:428
  82.7 7.9 %early_products_and_lookup.1 = (f32[256,1024]{1,0:T(8,128)S(1)}, f32[256,1]{1,0:T(8,128)S(1)}, bf16[1,1024,1024]{2,1,0:T(8,128)(2,1)}, bf16[256,1024]{1,0:T(8,128)(2,1)S(1)}, bf16[1024,1536]{1,0:T(8,128)(2,1)}) custom-call(s32[1,256]{1,0:T(1,128)S(1)} %bitcast.8, bf16[1,4096]{1,0:T(2,128)(2,1)S(1)} %broadcast_in_dim.3.gain_ref, ...), custom_call_target="tpu_custom_call" | custom-call | tf_op jit(solution)/shard_map/early_products_and_lookup/pallas_call | solution.py:288
  90.6 5.6 %collective-permute-done.10.refs_0_ = bf16[256,1024]{1,0:T(8,128)(2,1)S(1)} collective-permute-done((bf16[256,1024]{1,0:T(8,128)(2,1)S(1)}, bf16[256,1024]{1,0:T(8,128)(2,1)S(1)}, u32[]{:S(2)}, u32[]{:S(2)}) %collective-permute-start.10) | collective-permute-done | bytes 524320 | tf_op jit(solution)/shard_map/ppermute | solution.py:428
  96.2 3.6 %late_products_and_qkv.1 = (bf16[64,1536]{1,0:T(8,128)(2,1)S(1)}, bf16[64,1536]{1,0:T(8,128)(2,1)S(1)}, bf16[64,1536]{1,0:T(8,128)(2,1)S(1)}, bf16[64,1536]{1,0:T(8,128)(2,1)S(1)}) custom-call(bf16[1,4096]{1,0:T(2,128)(2,1)S(1)} %broadcast_in_dim.3.gain_ref, bf16[256,1024]{1,0:T(8,128)(2,1)S(1)} %collective-permute-done.10.refs_0_, ...), custom_call_target="tpu_custom_call" | custom-call | tf_op jit(solution)/shard_map/late_products_and_qkv/pallas_call | solution.py:349
  100.2 2.1 %collective-permute-start.16 = (bf16[64,1536]{1,0:T(8,128)(2,1)S(1)}, bf16[64,1536]{1,0:T(8,128)(2,1)S(1)}, u32[]{:S(2)}, u32[]{:S(2)}) collective-permute-start(bf16[64,1536]{1,0:T(8,128)(2,1)S(1)} %get-tuple-element.51), channel_id=1, source_target_pairs={{0,2},{1,3},{2,0},{3,1},{4,6},{5,7},{6,4},{7,5},{8,10},{9,11},{10,... | collective-permute-start | bytes 589832 | tf_op jit(solution)/shard_map/ppermute | solution.py:428
  102.3 2.0 %collective-permute-start.17 = (bf16[64,1536]{1,0:T(8,128)(2,1)S(1)}, bf16[64,1536]{1,0:T(8,128)(2,1)S(1)}, u32[]{:S(2)}, u32[]{:S(2)}) collective-permute-start(bf16[64,1536]{1,0:T(8,128)(2,1)S(1)} %get-tuple-element.52), channel_id=1, source_target_pairs={{0,3},{1,2},{2,1},{3,0},{4,7},{5,6},{6,5},{7,4},{8,11},{9,10},{10,... | collective-permute-start | bytes 589832 | tf_op jit(solution)/shard_map/ppermute | solution.py:428
  104.3 5.0 %collective-permute-done.15.refs_1_ = bf16[64,1536]{1,0:T(8,128)(2,1)S(1)} collective-permute-done((bf16[64,1536]{1,0:T(8,128)(2,1)S(1)}, bf16[64,1536]{1,0:T(8,128)(2,1)S(1)}, u32[]{:S(2)}, u32[]{:S(2)}) %collective-permute-start.15) | collective-permute-done | bytes 196640 | tf_op jit(solution)/shard_map/ppermute | solution.py:428
  109.3 7.4 %collective-permute-done.16.refs_2_ = bf16[64,1536]{1,0:T(8,128)(2,1)S(1)} collective-permute-done((bf16[64,1536]{1,0:T(8,128)(2,1)S(1)}, bf16[64,1536]{1,0:T(8,128)(2,1)S(1)}, u32[]{:S(2)}, u32[]{:S(2)}) %collective-permute-start.16) | collective-permute-done | bytes 196640 | tf_op jit(solution)/shard_map/ppermute | solution.py:428
  116.7 2.3 %attend_books.1 = bf16[64,4,512]{2,1,0:T(4,128)(2,1)} custom-call(bf16[64,1536]{1,0:T(8,128)(2,1)S(1)} %get-tuple-element.49.refs_0_, bf16[64,1536]{1,0:T(8,128)(2,1)S(1)} %collective-permute-done.15.refs_1_, bf16[64,1536]{1,0:T(8,128)(2,1)S(1)} %collective-permute-done.16.refs_2_, bf16[64,1536]{1,0:T(8,128)(2,1)S(1)} %collective-permute-done.17.refs_3_), custom_call_target="tpu_custom_call" | custom-call | tf_op jit(solution)/shard_map/attend_books/pallas_call | solution.py:416
  (41 shorter events, 8.6 us)
Async XLA Ops:
  0.0 3.8 %copy-start.1 = (bf16[1,512,1024]{2,1,0:T(8,128)(2,1)S(1)}, bf16[1,512,1024]{2,1,0:T(8,128)(2,1)}, u32[]{:S(2)}) copy-start(bf16[1,512,1024]{2,1,0:T(8,128)(2,1)} %param.15) | copy-start | bytes 3145732
  3.8 6.4 %copy-start = (bf16[256,1536]{1,0:T(8,128)(2,1)S(1)}, bf16[256,1536]{1,0:T(8,128)(2,1)}, u32[]{:S(2)}) copy-start(bf16[256,1536]{1,0:T(8,128)(2,1)} %get-tuple-element.36.hidden_ref) | copy-start | bytes 2359300
  4.0 20.2 %collective-permute-start.1 = (bf16[832,1024]{1,0:T(8,128)(2,1)S(1)}, bf16[832,1024]{1,0:T(8,128)(2,1)}, u32[]{:S(2)}, u32[]{:S(2)}) collective-permute-start(bf16[832,1024]{1,0:T(8,128)(2,1)S(1)} %pack_weight_rows.1.refs_3_), channel_id=1, source_target_pairs={{0,4},{4,0},{8,12},{12,8},{16,20},{20,16},{24,28},{28,24},{1,5},{5... | collective-permute-start | bytes 5111816 | tf_op jit(solution)/shard_map/ppermute | solution.py:428
  4.5 15.3 %collective-permute-start = (bf16[256,1024]{1,0:T(8,128)(2,1)S(1)}, bf16[256,1024]{1,0:T(8,128)(2,1)}, u32[]{:S(2)}, u32[]{:S(2)}) collective-permute-start(bf16[256,1024]{1,0:T(8,128)(2,1)S(1)} %get-tuple-element.30), channel_id=1, source_target_pairs={{0,1},{1,0},{2,3},{3,2},{4,5},{5,4},{6,7},{7,6},{8,9},{9,8},{10,11... | collective-permute-start | bytes 1572872 | tf_op jit(solution)/shard_map/ppermute | solution.py:428
  7.2 43.6 %collective-permute-start.6 = (bf16[832,1024]{1,0:T(8,128)(2,1)S(1)}, bf16[832,1024]{1,0:T(8,128)(2,1)}, u32[]{:S(2)}, u32[]{:S(2)}) collective-permute-start(bf16[832,1024]{1,0:T(8,128)(2,1)S(1)} %pack_weight_rows.1.refs_3_), channel_id=1, source_target_pairs={{0,16},{4,20},{8,24},{12,28},{16,0},{20,4},{24,8},{28,12},{1,17},{... | collective-permute-start | bytes 5111816 | tf_op jit(solution)/shard_map/ppermute | solution.py:428
  8.7 42.1 %collective-permute-start.5 = (bf16[832,1024]{1,0:T(8,128)(2,1)S(1)}, bf16[832,1024]{1,0:T(8,128)(2,1)}, u32[]{:S(2)}, u32[]{:S(2)}) collective-permute-start(bf16[832,1024]{1,0:T(8,128)(2,1)S(1)} %pack_weight_rows.1.refs_3_), channel_id=1, source_target_pairs={{0,8},{4,12},{8,0},{12,4},{16,24},{20,28},{24,16},{28,20},{1,9},{5... | collective-permute-start | bytes 5111816 | tf_op jit(solution)/shard_map/ppermute | solution.py:428
  21.3 29.1 %copy-start.6 = (bf16[256,1024]{1,0:T(8,128)(2,1)S(1)}, bf16[256,1024]{1,0:T(8,128)(2,1)}, u32[]{:S(2)}) copy-start(bf16[256,1024]{1,0:T(8,128)(2,1)} %param.13) | copy-start | bytes 1572868
  21.3 26.0 %collective-permute-start.3 = (bf16[256,1024]{1,0:T(8,128)(2,1)S(1)}, bf16[256,1024]{1,0:T(8,128)(2,1)S(1)}, u32[]{:S(2)}, u32[]{:S(2)}) collective-permute-start(bf16[256,1024]{1,0:T(8,128)(2,1)S(1)} %add_convert_fusion.1), channel_id=1, source_target_pairs={{0,2},{1,3},{2,0},{3,1},{4,6},{5,7},{6,4},{7,5},{8,10},{9,11},{10,... | collective-permute-start | bytes 1572872 | tf_op jit(solution)/shard_map/ppermute | solution.py:428
  27.0 23.4 %collective-permute-start.2 = (bf16[256,1024]{1,0:T(8,128)(2,1)S(1)}, bf16[256,1024]{1,0:T(8,128)(2,1)S(1)}, u32[]{:S(2)}, u32[]{:S(2)}) collective-permute-start(bf16[256,1024]{1,0:T(8,128)(2,1)S(1)} %convert_element_type.22), channel_id=1, source_target_pairs={{0,1},{1,0},{2,3},{3,2},{4,5},{5,4},{6,7},{7,6},{8,9},{9,8},{10,11... | collective-permute-start | bytes 1572872 | tf_op jit(solution)/shard_map/ppermute | solution.py:428
  50.8 31.9 %copy-start.7 = (bf16[4096]{0:T(1024)(128)(2,1)S(1)}, bf16[4096]{0:T(1024)(128)(2,1)}, u32[]{:S(2)}) copy-start(bf16[4096]{0:T(1024)(128)(2,1)} %param.14) | copy-start | bytes 24580
  50.8 31.9 %copy-start.5 = (s32[256,1]{0,1:T(1,128)S(1)}, s32[256,1]{0,1:T(1,128)}, u32[]{:S(2)}) copy-start(s32[256,1]{0,1:T(1,128)} %param.17) | copy-start | bytes 3076
  50.8 6.8 %collective-permute-start.7 = (bf16[832,1024]{1,0:T(8,128)(2,1)}, bf16[832,1024]{1,0:T(8,128)(2,1)}, u32[]{:S(2)}, u32[]{:S(2)}) collective-permute-start(bf16[832,1024]{1,0:T(8,128)(2,1)} %collective-permute-done.5.lower_from.refs_5_), channel_id=1, source_target_pairs={{0,4},{4,0},{8,12},{12,8},{16,20},{20,16},{24,28},{28,24},{1,5},{5... | collective-permute-start | bytes 5111816 | tf_op jit(solution)/shard_map/ppermute | solution.py:428
  50.9 6.7 %collective-permute-start.8 = (bf16[832,1024]{1,0:T(8,128)(2,1)}, bf16[832,1024]{1,0:T(8,128)(2,1)}, u32[]{:S(2)}, u32[]{:S(2)}) collective-permute-start(bf16[832,1024]{1,0:T(8,128)(2,1)} %collective-permute-done.6.upper_from.refs_7_), channel_id=1, source_target_pairs={{0,4},{4,0},{8,12},{12,8},{16,20},{20,16},{24,28},{28,24},{1,5},{5... | collective-permute-start | bytes 5111816 | tf_op jit(solution)/shard_map/ppermute | solution.py:428
  54.0 22.6 %collective-permute-start.12 = (bf16[448,1024]{1,0:T(8,128)(2,1)}, bf16[448,1024]{1,0:T(8,128)(2,1)S(1)}, u32[]{:S(2)}, u32[]{:S(2)}) collective-permute-start(bf16[448,1024]{1,0:T(8,128)(2,1)} %get-tuple-element.43), channel_id=1, source_target_pairs={{0,16},{4,20},{8,24},{12,28},{16,0},{20,4},{24,8},{28,12},{1,17},{... | collective-permute-start | bytes 2752520 | tf_op jit(solution)/shard_map/ppermute | solution.py:428
  55.6 21.0 %collective-permute-start.11 = (bf16[384,1024]{1,0:T(8,128)(2,1)}, bf16[384,1024]{1,0:T(8,128)(2,1)S(1)}, u32[]{:S(2)}, u32[]{:S(2)}) collective-permute-start(bf16[384,1024]{1,0:T(8,128)(2,1)} %get-tuple-element.42), channel_id=1, source_target_pairs={{0,8},{4,12},{8,0},{12,4},{16,24},{20,28},{24,16},{28,20},{1,9},{5... | collective-permute-start | bytes 2359304 | tf_op jit(solution)/shard_map/ppermute | solution.py:428
  57.1 25.3 %collective-permute-start.4 = (bf16[256,1024]{1,0:T(8,128)(2,1)S(1)}, bf16[256,1024]{1,0:T(8,128)(2,1)S(1)}, u32[]{:S(2)}, u32[]{:S(2)}) collective-permute-start(bf16[256,1024]{1,0:T(8,128)(2,1)S(1)} %add_convert_fusion.refs_0_), channel_id=1, source_target_pairs={{0,2},{1,3},{2,0},{3,1},{4,6},{5,7},{6,4},{7,5},{8,10},{9,11},{10,... | collective-permute-start | bytes 1572872 | tf_op jit(solution)/shard_map/ppermute | solution.py:428
  57.6 25.0 %collective-permute-start.9 = (bf16[256,1024]{1,0:T(8,128)(2,1)S(1)}, bf16[256,1024]{1,0:T(8,128)(2,1)S(1)}, u32[]{:S(2)}, u32[]{:S(2)}) collective-permute-start(bf16[256,1024]{1,0:T(8,128)(2,1)S(1)} %add_convert_fusion.refs_0_), channel_id=1, source_target_pairs={{0,1},{1,0},{2,3},{3,2},{4,5},{5,4},{6,7},{7,6},{8,9},{9,8},{10,11... | collective-permute-start | bytes 1572872 | tf_op jit(solution)/shard_map/ppermute | solution.py:428
  76.6 6.0 %collective-permute-start.14 = (bf16[448,1024]{1,0:T(8,128)(2,1)S(1)}, bf16[448,1024]{1,0:T(8,128)(2,1)S(1)}, u32[]{:S(2)}, u32[]{:S(2)}) collective-permute-start(bf16[448,1024]{1,0:T(8,128)(2,1)S(1)} %collective-permute-done.12.refs_10_), channel_id=1, source_target_pairs={{0,4},{4,0},{8,12},{12,8},{16,20},{20,16},{24,28},{28,24},{1,5},{5... | collective-permute-start | bytes 2752520 | tf_op jit(solution)/shard_map/ppermute | solution.py:428
  76.6 6.0 %collective-permute-start.13 = (bf16[384,1024]{1,0:T(8,128)(2,1)S(1)}, bf16[384,1024]{1,0:T(8,128)(2,1)S(1)}, u32[]{:S(2)}, u32[]{:S(2)}) collective-permute-start(bf16[384,1024]{1,0:T(8,128)(2,1)S(1)} %collective-permute-done.11.refs_9_), channel_id=1, source_target_pairs={{0,4},{4,0},{8,12},{12,8},{16,20},{20,16},{24,28},{28,24},{1,5},{5... | collective-permute-start | bytes 2359304 | tf_op jit(solution)/shard_map/ppermute | solution.py:428
  82.6 13.6 %collective-permute-start.10 = (bf16[256,1024]{1,0:T(8,128)(2,1)S(1)}, bf16[256,1024]{1,0:T(8,128)(2,1)S(1)}, u32[]{:S(2)}, u32[]{:S(2)}) collective-permute-start(bf16[256,1024]{1,0:T(8,128)(2,1)S(1)} %collective-permute-done.4.refs_2_), channel_id=1, source_target_pairs={{0,1},{1,0},{2,3},{3,2},{4,5},{5,4},{6,7},{7,6},{8,9},{9,8},{10,11... | collective-permute-start | bytes 1572872 | tf_op jit(solution)/shard_map/ppermute | solution.py:428
  82.7 13.6 %copy-start.4 = (bf16[1,1024]{1,0:T(2,128)(2,1)S(1)}, bf16[1,1024]{1,0:T(2,128)(2,1)}, u32[]{:S(2)}) copy-start(bf16[1,1024]{1,0:T(2,128)(2,1)} %refs_5_.1) | copy-start | bytes 6148
  99.8 9.5 %collective-permute-start.15 = (bf16[64,1536]{1,0:T(8,128)(2,1)S(1)}, bf16[64,1536]{1,0:T(8,128)(2,1)S(1)}, u32[]{:S(2)}, u32[]{:S(2)}) collective-permute-start(bf16[64,1536]{1,0:T(8,128)(2,1)S(1)} %get-tuple-element.50), channel_id=1, source_target_pairs={{0,1},{1,0},{2,3},{3,2},{4,5},{5,4},{6,7},{7,6},{8,9},{9,8},{10,11... | collective-permute-start | bytes 589832 | tf_op jit(solution)/shard_map/ppermute | solution.py:428
  100.2 16.5 %collective-permute-start.16 = (bf16[64,1536]{1,0:T(8,128)(2,1)S(1)}, bf16[64,1536]{1,0:T(8,128)(2,1)S(1)}, u32[]{:S(2)}, u32[]{:S(2)}) collective-permute-start(bf16[64,1536]{1,0:T(8,128)(2,1)S(1)} %get-tuple-element.51), channel_id=1, source_target_pairs={{0,2},{1,3},{2,0},{3,1},{4,6},{5,7},{6,4},{7,5},{8,10},{9,11},{10,... | collective-permute-start | bytes 589832 | tf_op jit(solution)/shard_map/ppermute | solution.py:428
  102.3 14.4 %collective-permute-start.17 = (bf16[64,1536]{1,0:T(8,128)(2,1)S(1)}, bf16[64,1536]{1,0:T(8,128)(2,1)S(1)}, u32[]{:S(2)}, u32[]{:S(2)}) collective-permute-start(bf16[64,1536]{1,0:T(8,128)(2,1)S(1)} %get-tuple-element.52), channel_id=1, source_target_pairs={{0,3},{1,2},{2,1},{3,0},{4,7},{5,6},{6,5},{7,4},{8,11},{9,10},{10,... | collective-permute-start | bytes 589832 | tf_op jit(solution)/shard_map/ppermute | solution.py:428
  (2 other events, 7.5 us)

commit v13 on v12

--- a/solution.py
+++ b/solution.py
@@ -460,10 +460,16 @@
     def share(m, *others):
         factor = after(hidden, *others) if others else hidden
         if m == 0:
-            block = lax.dynamic_slice_in_dim(
-                down_weight, lax.axis_index("book") * width, width, 1
-            )
-            return jnp.dot(factor, block, preferred_element_type=f32)
+            total = 0.0
+            each = factor.shape[1] // 4
+            for step in range(4):
+                block = lax.dynamic_slice(
+                    down_weight, (step * each, lax.axis_index("book") * width), (each, width)
+                )
+                part = lax.slice_in_dim(factor, step * each, (step + 1) * each, axis=1)
+                total = total + jnp.dot(part, block, preferred_element_type=f32)
+                total = lax.optimization_barrier(total)
+            return total
         return share_products(factor, down_weight, width, m)
 
     rows = pack(*after((in_proj[0], embedding[0], qkv_weight[0]), first))
@@ -484,7 +490,7 @@
     last = lax.optimization_barrier(share(0, came, parts[1][0][1]))
     sums[0] = last + residual.astype(f32)
     for m in range(books - 3, 0, -2):
-        near_came = swap(after(sums.pop(m).astype(bf16), onward, last), "book", 1)
+        near_came = swap(after(sums.pop(m).astype(bf16), onward), "book", 1)
         sums[m ^ 1] = sums[m ^ 1] + near_came.astype(f32)
     sums[(books - 2) ^ 2] = sums[(books - 2) ^ 2] + far_came.astype(f32)
     distance = 2

time: 120 us -> 116 us (0.967)
  waiting for transfers between devices: 63 us -> 54.3 us
  matrix products: 2.86 us -> 6.33 us
    ppermute x18, waiting for transfers between devices: 63 us -> 54.3 us  [swap(): lax.ppermute(value, axis, [(i, i ^ distance) for i in range(lax.axis_size...]
    dot_general x1 -> x4, matrix products: 2.86 us -> 6.33 us  [share(): total = total + jnp.dot(part, block, preferred_element_type=f32)]
  transfers between devices with their start and end apart: 18 -> 18, of which waited for: 9 -> 6; matrix products, arithmetic and copies ran while one was open for 5% -> 8% of each run, Pallas kernels for 15% -> 15%
where the time goes in v13:
time: 116 us
  waiting for transfers between devices  54.3 us (47%)
  Pallas kernels  27.6 us (24%)
  starting transfers between devices  23.2 us (20%)
  matrix products  6.33 us (5%)
  other arithmetic  3.18 us (3%)
  local copies, waits for them, and re-layouts  1.18 us (1%)
    ppermute x18, waiting for transfers between devices, swap(): lax.ppermute(value, axis, [(i, i ^ distance) for i in range(lax.axis_size...  54.3 us
    ppermute x18, starting transfers between devices, swap(): lax.ppermute(value, axis, [(i, i ^ distance) for i in range(lax.axis_size...  23.2 us
    pallas_call x1, Pallas kernels, project_early(): pl.pallas_call(functools.partial(early_kernel, books, early, pieces, size...  7.91 us
    pallas_call x2, Pallas kernels, share_products(): pl.pallas_call(functools.partial(share_kernel, partner), out_shape=jax.Sh...  7.24 us
    dot_general x4, matrix products, share(): total = total + jnp.dot(part, block, preferred_element_type=f32)  6.33 us
    pallas_call x1, Pallas kernels, first_products(): pl.pallas_call(first_kernel, out_shape=[jax.ShapeDtypeStruct((frames_here...  3.73 us
    pallas_call x1, Pallas kernels, project_late(): pl.pallas_call(functools.partial(late_kernel, books, late), out_shape=[ja...  3.61 us
    pallas_call x1, Pallas kernels, cut_rows(): pl.pallas_call(functools.partial(cut_kernel, cut), out_shape=[jax.ShapeDt...  2.66 us
  transfers between devices with their start and end apart: 18, of which 6 were waited for; matrix products, arithmetic and copies ran while one was open for 8% of the time, Pallas kernels for 15%

profile of v13, /device:TPU:0, one launch (start us, length us, event | category | flops | bytes accessed | tf_op | source)
XLA Modules:
  0.0 116.1 jit_solution(12740262746707992051)
XLA Ops:
  0.0 3.7 %hidden_and_first_products.1 = (bf16[256,1536]{1,0:T(8,128)(2,1)}, bf16[256,1024]{1,0:T(8,128)(2,1)S(1)}) custom-call(bf16[256,1536]{1,0:T(8,128)(2,1)} %gate_ref.1, bf16[256,1536]{1,0:T(8,128)(2,1)} %up_ref.1, bf16[1536,4096]{1,0:T(8,128)(2,1)} %down_ref.5), custom_call_target="tpu_custom_call" | custom-call | tf_op jit(solution)/shard_map/hidden_and_first_products/pallas_call | solution.py:47
  4.5 2.7 %collective-permute-start = (bf16[256,1024]{1,0:T(8,128)(2,1)S(1)}, bf16[256,1024]{1,0:T(8,128)(2,1)}, u32[]{:S(2)}, u32[]{:S(2)}) collective-permute-start(bf16[256,1024]{1,0:T(8,128)(2,1)S(1)} %get-tuple-element.30), channel_id=1, source_target_pairs={{0,1},{1,0},{2,3},{3,2},{4,5},{5,4},{6,7},{7,6},{8,9},{9,8},{10,11... | collective-permute-start | bytes 1572872 | tf_op jit(solution)/shard_map/ppermute | solution.py:428
  7.1 1.5 %collective-permute-start.6 = (bf16[832,1024]{1,0:T(8,128)(2,1)S(1)}, bf16[832,1024]{1,0:T(8,128)(2,1)}, u32[]{:S(2)}, u32[]{:S(2)}) collective-permute-start(bf16[832,1024]{1,0:T(8,128)(2,1)S(1)} %pack_weight_rows.1.refs_3_), channel_id=1, source_target_pairs={{0,16},{4,20},{8,24},{12,28},{16,0},{20,4},{24,8},{28,12},{1,17},{... | collective-permute-start | bytes 5111816 | tf_op jit(solution)/shard_map/ppermute | solution.py:428
  11.3 3.6 %share_products.3 = f32[256,1024]{1,0:T(8,128)} custom-call(bf16[256,1536]{1,0:T(8,128)(2,1)S(1)} %copy-done, bf16[1536,4096]{1,0:T(8,128)(2,1)} %down_ref.5), custom_call_target="tpu_custom_call" | custom-call | tf_op jit(solution)/shard_map/share_products/pallas_call | solution.py:91
  14.9 3.6 %share_products.2 = f32[256,1024]{1,0:T(8,128)} custom-call(bf16[256,1536]{1,0:T(8,128)(2,1)S(1)} %copy-done, bf16[1536,4096]{1,0:T(8,128)(2,1)} %down_ref.5), custom_call_target="tpu_custom_call" | custom-call | tf_op jit(solution)/shard_map/share_products/pallas_call | solution.py:91
  19.9 1.6 %add_convert_fusion.1 = bf16[256,1024]{1,0:T(8,128)(2,1)S(1)} fusion(f32[256,1024]{1,0:T(8,128)} %share_products.3, bf16[256,1024]{1,0:T(8,128)(2,1)} %collective-permute-done), kind=kLoop, calls=%fused_computation.4 | loop fusion | flops 786432 | bytes 2097152 | tf_op jit(solution)/shard_map/convert_element_type | solution.py:488
  21.5 2.7 %collective-permute-start.3 = (bf16[256,1024]{1,0:T(8,128)(2,1)S(1)}, bf16[256,1024]{1,0:T(8,128)(2,1)S(1)}, u32[]{:S(2)}, u32[]{:S(2)}) collective-permute-start(bf16[256,1024]{1,0:T(8,128)(2,1)S(1)} %add_convert_fusion.1), channel_id=1, source_target_pairs={{0,2},{1,3},{2,0},{3,1},{4,6},{5,7},{6,4},{7,5},{8,10},{9,11},{10,... | collective-permute-start | bytes 1572872 | tf_op jit(solution)/shard_map/ppermute | solution.py:428
  24.2 1.5 %collective-permute-start.2 = (bf16[256,1024]{1,0:T(8,128)(2,1)S(1)}, bf16[256,1024]{1,0:T(8,128)(2,1)S(1)}, u32[]{:S(2)}, u32[]{:S(2)}) collective-permute-start(bf16[256,1024]{1,0:T(8,128)(2,1)S(1)} %convert_element_type.22), channel_id=1, source_target_pairs={{0,1},{1,0},{2,3},{3,2},{4,5},{5,4},{6,7},{7,6},{8,9},{9,8},{10,11... | collective-permute-start | bytes 1572872 | tf_op jit(solution)/shard_map/ppermute | solution.py:428
  25.7 1.6 %fusion.3 = f32[256,1024]{1,0:T(8,128)S(1)} fusion(bf16[1536,4096]{1,0:T(8,128)(2,1)} %down_ref.5, s32[]{:T(128)S(6)} %select_n.2, bf16[256,1536]{1,0:T(8,128)(2,1)S(1)} %copy-done.1), kind=kOutput, calls=%fused_computation.8 | convolution fusion | flops 201326592 | bytes 2031620 | tf_op jit(solution)/shard_map/dot_general | solution.py:470
  27.3 1.6 %convolution_add_fusion.2 = f32[256,1024]{1,0:T(8,128)S(1)} fusion(f32[256,1024]{1,0:T(8,128)S(1)} %fusion.3, bf16[1536,4096]{1,0:T(8,128)(2,1)} %down_ref.5, s32[]{:T(128)S(6)} %select_n.2, bf16[256,1536]{1,0:T(8,128)(2,1)S(1)} %copy-done.1), kind=kOutput, calls=%fused_computation.2 | convolution fusion | flops 201588736 | bytes 3080196 | tf_op jit(solution)/shard_map/dot_general | solution.py:470
  28.9 1.6 %convolution_add_fusion.1 = f32[256,1024]{1,0:T(8,128)S(1)} fusion(f32[256,1024]{1,0:T(8,128)S(1)} %convolution_add_fusion.2, bf16[1536,4096]{1,0:T(8,128)(2,1)} %down_ref.5, s32[]{:T(128)S(6)} %select_n.2, bf16[256,1536]{1,0:T(8,128)(2,1)S(1)} %copy-done.1), kind=kOutput, calls=%fused_computation.1 | convolution fusion | flops 201588736 | bytes 3080196 | tf_op jit(solution)/shard_map/dot_general | solution.py:470
  30.5 1.6 %convolution_add_fusion = f32[256,1024]{1,0:T(8,128)S(1)} fusion(f32[256,1024]{1,0:T(8,128)S(1)} %convolution_add_fusion.1, bf16[1536,4096]{1,0:T(8,128)(2,1)} %down_ref.5, s32[]{:T(128)S(6)} %select_n.2, bf16[256,1536]{1,0:T(8,128)(2,1)S(1)} %copy-done.1), kind=kOutput, calls=%fused_computation | convolution fusion | flops 201588736 | bytes 3080196 | tf_op jit(solution)/shard_map/dot_general | solution.py:470
  32.1 15.5 %collective-permute-done.2 = bf16[256,1024]{1,0:T(8,128)(2,1)S(1)} collective-permute-done((bf16[256,1024]{1,0:T(8,128)(2,1)S(1)}, bf16[256,1024]{1,0:T(8,128)(2,1)S(1)}, u32[]{:S(2)}, u32[]{:S(2)}) %collective-permute-start.2) | collective-permute-done | bytes 524320 | tf_op jit(solution)/shard_map/ppermute | solution.py:428
  48.5 2.7 %cut_rows.1 = (bf16[384,1024]{1,0:T(8,128)(2,1)}, bf16[448,1024]{1,0:T(8,128)(2,1)}) custom-call(bf16[832,1024]{1,0:T(8,128)(2,1)} %collective-permute-done.6.upper_from.refs_7_, bf16[832,1024]{1,0:T(8,128)(2,1)} %collective-permute-done.5.lower_from.refs_5_), custom_call_target="tpu_custom_call" | custom-call | tf_op jit(solution)/shard_map/cut_rows/pallas_call | solution.py:161
  55.6 2.3 %collective-permute-start.9 = (bf16[256,1024]{1,0:T(8,128)(2,1)S(1)}, bf16[256,1024]{1,0:T(8,128)(2,1)S(1)}, u32[]{:S(2)}, u32[]{:S(2)}) collective-permute-start(bf16[256,1024]{1,0:T(8,128)(2,1)S(1)} %add_convert_fusion.refs_0_), channel_id=1, source_target_pairs={{0,1},{1,0},{2,3},{3,2},{4,5},{5,4},{6,7},{7,6},{8,9},{9,8},{10,11... | collective-permute-start | bytes 1572872 | tf_op jit(solution)/shard_map/ppermute | solution.py:428
  57.9 15.9 %collective-permute-done.12.refs_10_ = bf16[448,1024]{1,0:T(8,128)(2,1)S(1)} collective-permute-done((bf16[448,1024]{1,0:T(8,128)(2,1)}, bf16[448,1024]{1,0:T(8,128)(2,1)S(1)}, u32[]{:S(2)}, u32[]{:S(2)}) %collective-permute-start.12) | collective-permute-done | bytes 917536 | tf_op jit(solution)/shard_map/ppermute | solution.py:428
  74.3 5.3 %collective-permute-done.4.refs_2_ = bf16[256,1024]{1,0:T(8,128)(2,1)S(1)} collective-permute-done((bf16[256,1024]{1,0:T(8,128)(2,1)S(1)}, bf16[256,1024]{1,0:T(8,128)(2,1)S(1)}, u32[]{:S(2)}, u32[]{:S(2)}) %collective-permute-start.4) | collective-permute-done | bytes 524320 | tf_op jit(solution)/shard_map/ppermute | solution.py:428
  80.2 7.9 %early_products_and_lookup.1 = (f32[256,1024]{1,0:T(8,128)S(1)}, f32[256,1]{1,0:T(8,128)S(1)}, bf16[1,1024,1024]{2,1,0:T(8,128)(2,1)}, bf16[256,1024]{1,0:T(8,128)(2,1)S(1)}, bf16[1024,1536]{1,0:T(8,128)(2,1)}) custom-call(s32[1,256]{1,0:T(1,128)S(1)} %bitcast.7, bf16[1,4096]{1,0:T(2,128)(2,1)S(1)} %broadcast_in_dim.3.gain_ref, ...), custom_call_target="tpu_custom_call" | custom-call | tf_op jit(solution)/shard_map/early_products_and_lookup/pallas_call | solution.py:288
  88.1 4.4 %collective-permute-done.10.refs_0_ = bf16[256,1024]{1,0:T(8,128)(2,1)S(1)} collective-permute-done((bf16[256,1024]{1,0:T(8,128)(2,1)S(1)}, bf16[256,1024]{1,0:T(8,128)(2,1)S(1)}, u32[]{:S(2)}, u32[]{:S(2)}) %collective-permute-start.10) | collective-permute-done | bytes 524320 | tf_op jit(solution)/shard_map/ppermute | solution.py:428
  92.5 3.6 %late_products_and_qkv.1 = (bf16[64,1536]{1,0:T(8,128)(2,1)S(1)}, bf16[64,1536]{1,0:T(8,128)(2,1)S(1)}, bf16[64,1536]{1,0:T(8,128)(2,1)S(1)}, bf16[64,1536]{1,0:T(8,128)(2,1)S(1)}) custom-call(bf16[1,4096]{1,0:T(2,128)(2,1)S(1)} %broadcast_in_dim.3.gain_ref, bf16[256,1024]{1,0:T(8,128)(2,1)S(1)} %collective-permute-done.10.refs_0_, ...), custom_call_target="tpu_custom_call" | custom-call | tf_op jit(solution)/shard_map/late_products_and_qkv/pallas_call | solution.py:349
  96.7 3.4 %collective-permute-start.16 = (bf16[64,1536]{1,0:T(8,128)(2,1)S(1)}, bf16[64,1536]{1,0:T(8,128)(2,1)S(1)}, u32[]{:S(2)}, u32[]{:S(2)}) collective-permute-start(bf16[64,1536]{1,0:T(8,128)(2,1)S(1)} %get-tuple-element.51), channel_id=1, source_target_pairs={{0,2},{1,3},{2,0},{3,1},{4,6},{5,7},{6,4},{7,5},{8,10},{9,11},{10,... | collective-permute-start | bytes 589832 | tf_op jit(solution)/shard_map/ppermute | solution.py:428
  100.6 3.2 %collective-permute-done.15.refs_1_ = bf16[64,1536]{1,0:T(8,128)(2,1)S(1)} collective-permute-done((bf16[64,1536]{1,0:T(8,128)(2,1)S(1)}, bf16[64,1536]{1,0:T(8,128)(2,1)S(1)}, u32[]{:S(2)}, u32[]{:S(2)}) %collective-permute-start.15) | collective-permute-done | bytes 196640 | tf_op jit(solution)/shard_map/ppermute | solution.py:428
  103.8 10.0 %collective-permute-done.16.refs_2_ = bf16[64,1536]{1,0:T(8,128)(2,1)S(1)} collective-permute-done((bf16[64,1536]{1,0:T(8,128)(2,1)S(1)}, bf16[64,1536]{1,0:T(8,128)(2,1)S(1)}, u32[]{:S(2)}, u32[]{:S(2)}) %collective-permute-start.16) | collective-permute-done | bytes 196640 | tf_op jit(solution)/shard_map/ppermute | solution.py:428
  113.8 2.3 %attend_books.1 = bf16[64,4,512]{2,1,0:T(4,128)(2,1)} custom-call(bf16[64,1536]{1,0:T(8,128)(2,1)S(1)} %get-tuple-element.49.refs_0_, bf16[64,1536]{1,0:T(8,128)(2,1)S(1)} %collective-permute-done.15.refs_1_, bf16[64,1536]{1,0:T(8,128)(2,1)S(1)} %collective-permute-done.16.refs_2_, bf16[64,1536]{1,0:T(8,128)(2,1)S(1)} %collective-permute-done.17.refs_3_), custom_call_target="tpu_custom_call" | custom-call | tf_op jit(solution)/shard_map/attend_books/pallas_call | solution.py:416
  (46 shorter events, 12.2 us)
Async XLA Ops:
  0.0 3.8 %copy-start.2 = (bf16[1,512,1024]{2,1,0:T(8,128)(2,1)S(1)}, bf16[1,512,1024]{2,1,0:T(8,128)(2,1)}, u32[]{:S(2)}) copy-start(bf16[1,512,1024]{2,1,0:T(8,128)(2,1)} %param.15) | copy-start | bytes 3145732
  4.0 21.7 %collective-permute-start.1 = (bf16[832,1024]{1,0:T(8,128)(2,1)S(1)}, bf16[832,1024]{1,0:T(8,128)(2,1)}, u32[]{:S(2)}, u32[]{:S(2)}) collective-permute-start(bf16[832,1024]{1,0:T(8,128)(2,1)S(1)} %pack_weight_rows.1.refs_3_), channel_id=1, source_target_pairs={{0,4},{4,0},{8,12},{12,8},{16,20},{20,16},{24,28},{28,24},{1,5},{5... | collective-permute-start | bytes 5111816 | tf_op jit(solution)/shard_map/ppermute | solution.py:428
  4.5 15.4 %collective-permute-start = (bf16[256,1024]{1,0:T(8,128)(2,1)S(1)}, bf16[256,1024]{1,0:T(8,128)(2,1)}, u32[]{:S(2)}, u32[]{:S(2)}) collective-permute-start(bf16[256,1024]{1,0:T(8,128)(2,1)S(1)} %get-tuple-element.30), channel_id=1, source_target_pairs={{0,1},{1,0},{2,3},{3,2},{4,5},{5,4},{6,7},{7,6},{8,9},{9,8},{10,11... | collective-permute-start | bytes 1572872 | tf_op jit(solution)/shard_map/ppermute | solution.py:428
  7.1 40.7 %collective-permute-start.6 = (bf16[832,1024]{1,0:T(8,128)(2,1)S(1)}, bf16[832,1024]{1,0:T(8,128)(2,1)}, u32[]{:S(2)}, u32[]{:S(2)}) collective-permute-start(bf16[832,1024]{1,0:T(8,128)(2,1)S(1)} %pack_weight_rows.1.refs_3_), channel_id=1, source_target_pairs={{0,16},{4,20},{8,24},{12,28},{16,0},{20,4},{24,8},{28,12},{1,17},{... | collective-permute-start | bytes 5111816 | tf_op jit(solution)/shard_map/ppermute | solution.py:428
  8.7 39.2 %collective-permute-start.5 = (bf16[832,1024]{1,0:T(8,128)(2,1)S(1)}, bf16[832,1024]{1,0:T(8,128)(2,1)}, u32[]{:S(2)}, u32[]{:S(2)}) collective-permute-start(bf16[832,1024]{1,0:T(8,128)(2,1)S(1)} %pack_weight_rows.1.refs_3_), channel_id=1, source_target_pairs={{0,8},{4,12},{8,0},{12,4},{16,24},{20,28},{24,16},{28,20},{1,9},{5... | collective-permute-start | bytes 5111816 | tf_op jit(solution)/shard_map/ppermute | solution.py:428
  14.9 10.8 %copy-start.1 = (bf16[256,1536]{1,0:T(8,128)(2,1)S(1)}, bf16[256,1536]{1,0:T(8,128)(2,1)}, u32[]{:S(2)}) copy-start(bf16[256,1536]{1,0:T(8,128)(2,1)} %get-tuple-element.36.hidden_ref) | copy-start | bytes 2359300
  18.6 61.6 %copy-start.8 = (bf16[4096]{0:T(1024)(128)(2,1)S(1)}, bf16[4096]{0:T(1024)(128)(2,1)}, u32[]{:S(2)}) copy-start(bf16[4096]{0:T(1024)(128)(2,1)} %param.14) | copy-start | bytes 24580
  18.6 61.6 %copy-start.6 = (s32[256,1]{0,1:T(1,128)S(1)}, s32[256,1]{0,1:T(1,128)}, u32[]{:S(2)}) copy-start(s32[256,1]{0,1:T(1,128)} %param.17) | copy-start | bytes 3076
  19.9 27.6 %copy-start.7 = (bf16[256,1024]{1,0:T(8,128)(2,1)S(1)}, bf16[256,1024]{1,0:T(8,128)(2,1)}, u32[]{:S(2)}) copy-start(bf16[256,1024]{1,0:T(8,128)(2,1)} %param.13) | copy-start | bytes 1572868
  21.5 26.1 %collective-permute-start.3 = (bf16[256,1024]{1,0:T(8,128)(2,1)S(1)}, bf16[256,1024]{1,0:T(8,128)(2,1)S(1)}, u32[]{:S(2)}, u32[]{:S(2)}) collective-permute-start(bf16[256,1024]{1,0:T(8,128)(2,1)S(1)} %add_convert_fusion.1), channel_id=1, source_target_pairs={{0,2},{1,3},{2,0},{3,1},{4,6},{5,7},{6,4},{7,5},{8,10},{9,11},{10,... | collective-permute-start | bytes 1572872 | tf_op jit(solution)/shard_map/ppermute | solution.py:428
  24.2 23.4 %collective-permute-start.2 = (bf16[256,1024]{1,0:T(8,128)(2,1)S(1)}, bf16[256,1024]{1,0:T(8,128)(2,1)S(1)}, u32[]{:S(2)}, u32[]{:S(2)}) collective-permute-start(bf16[256,1024]{1,0:T(8,128)(2,1)S(1)} %convert_element_type.22), channel_id=1, source_target_pairs={{0,1},{1,0},{2,3},{3,2},{4,5},{5,4},{6,7},{7,6},{8,9},{9,8},{10,11... | collective-permute-start | bytes 1572872 | tf_op jit(solution)/shard_map/ppermute | solution.py:428
  30.4 62.1 %copy-start.5 = (bf16[1,1024]{1,0:T(2,128)(2,1)S(1)}, bf16[1,1024]{1,0:T(2,128)(2,1)}, u32[]{:S(2)}) copy-start(bf16[1,1024]{1,0:T(2,128)(2,1)} %refs_5_.1) | copy-start | bytes 6148
  47.9 7.7 %collective-permute-start.7 = (bf16[832,1024]{1,0:T(8,128)(2,1)}, bf16[832,1024]{1,0:T(8,128)(2,1)}, u32[]{:S(2)}, u32[]{:S(2)}) collective-permute-start(bf16[832,1024]{1,0:T(8,128)(2,1)} %collective-permute-done.5.lower_from.refs_5_), channel_id=1, source_target_pairs={{0,4},{4,0},{8,12},{12,8},{16,20},{20,16},{24,28},{28,24},{1,5},{5... | collective-permute-start | bytes 5111816 | tf_op jit(solution)/shard_map/ppermute | solution.py:428
  48.0 7.6 %collective-permute-start.8 = (bf16[832,1024]{1,0:T(8,128)(2,1)}, bf16[832,1024]{1,0:T(8,128)(2,1)}, u32[]{:S(2)}, u32[]{:S(2)}) collective-permute-start(bf16[832,1024]{1,0:T(8,128)(2,1)} %collective-permute-done.6.upper_from.refs_7_), channel_id=1, source_target_pairs={{0,4},{4,0},{8,12},{12,8},{16,20},{20,16},{24,28},{28,24},{1,5},{5... | collective-permute-start | bytes 5111816 | tf_op jit(solution)/shard_map/ppermute | solution.py:428
  51.1 22.6 %collective-permute-start.12 = (bf16[448,1024]{1,0:T(8,128)(2,1)}, bf16[448,1024]{1,0:T(8,128)(2,1)S(1)}, u32[]{:S(2)}, u32[]{:S(2)}) collective-permute-start(bf16[448,1024]{1,0:T(8,128)(2,1)} %get-tuple-element.43), channel_id=1, source_target_pairs={{0,16},{4,20},{8,24},{12,28},{16,0},{20,4},{24,8},{28,12},{1,17},{... | collective-permute-start | bytes 2752520 | tf_op jit(solution)/shard_map/ppermute | solution.py:428
  52.6 21.1 %collective-permute-start.11 = (bf16[384,1024]{1,0:T(8,128)(2,1)}, bf16[384,1024]{1,0:T(8,128)(2,1)S(1)}, u32[]{:S(2)}, u32[]{:S(2)}) collective-permute-start(bf16[384,1024]{1,0:T(8,128)(2,1)} %get-tuple-element.42), channel_id=1, source_target_pairs={{0,8},{4,12},{8,0},{12,4},{16,24},{20,28},{24,16},{28,20},{1,9},{5... | collective-permute-start | bytes 2359304 | tf_op jit(solution)/shard_map/ppermute | solution.py:428
  54.1 25.5 %collective-permute-start.4 = (bf16[256,1024]{1,0:T(8,128)(2,1)S(1)}, bf16[256,1024]{1,0:T(8,128)(2,1)S(1)}, u32[]{:S(2)}, u32[]{:S(2)}) collective-permute-start(bf16[256,1024]{1,0:T(8,128)(2,1)S(1)} %add_convert_fusion.refs_0_), channel_id=1, source_target_pairs={{0,2},{1,3},{2,0},{3,1},{4,6},{5,7},{6,4},{7,5},{8,10},{9,11},{10,... | collective-permute-start | bytes 1572872 | tf_op jit(solution)/shard_map/ppermute | solution.py:428
  55.6 24.0 %collective-permute-start.9 = (bf16[256,1024]{1,0:T(8,128)(2,1)S(1)}, bf16[256,1024]{1,0:T(8,128)(2,1)S(1)}, u32[]{:S(2)}, u32[]{:S(2)}) collective-permute-start(bf16[256,1024]{1,0:T(8,128)(2,1)S(1)} %add_convert_fusion.refs_0_), channel_id=1, source_target_pairs={{0,1},{1,0},{2,3},{3,2},{4,5},{5,4},{6,7},{7,6},{8,9},{9,8},{10,11... | collective-permute-start | bytes 1572872 | tf_op jit(solution)/shard_map/ppermute | solution.py:428
  73.7 6.4 %collective-permute-start.14 = (bf16[448,1024]{1,0:T(8,128)(2,1)S(1)}, bf16[448,1024]{1,0:T(8,128)(2,1)S(1)}, u32[]{:S(2)}, u32[]{:S(2)}) collective-permute-start(bf16[448,1024]{1,0:T(8,128)(2,1)S(1)} %collective-permute-done.12.refs_10_), channel_id=1, source_target_pairs={{0,4},{4,0},{8,12},{12,8},{16,20},{20,16},{24,28},{28,24},{1,5},{5... | collective-permute-start | bytes 2752520 | tf_op jit(solution)/shard_map/ppermute | solution.py:428
  73.7 6.4 %collective-permute-start.13 = (bf16[384,1024]{1,0:T(8,128)(2,1)S(1)}, bf16[384,1024]{1,0:T(8,128)(2,1)S(1)}, u32[]{:S(2)}, u32[]{:S(2)}) collective-permute-start(bf16[384,1024]{1,0:T(8,128)(2,1)S(1)} %collective-permute-done.11.refs_9_), channel_id=1, source_target_pairs={{0,4},{4,0},{8,12},{12,8},{16,20},{20,16},{24,28},{28,24},{1,5},{5... | collective-permute-start | bytes 2359304 | tf_op jit(solution)/shard_map/ppermute | solution.py:428
  79.6 12.9 %collective-permute-start.10 = (bf16[256,1024]{1,0:T(8,128)(2,1)S(1)}, bf16[256,1024]{1,0:T(8,128)(2,1)S(1)}, u32[]{:S(2)}, u32[]{:S(2)}) collective-permute-start(bf16[256,1024]{1,0:T(8,128)(2,1)S(1)} %collective-permute-done.4.refs_2_), channel_id=1, source_target_pairs={{0,1},{1,0},{2,3},{3,2},{4,5},{5,4},{6,7},{7,6},{8,9},{9,8},{10,11... | collective-permute-start | bytes 1572872 | tf_op jit(solution)/shard_map/ppermute | solution.py:428
  96.1 7.7 %collective-permute-start.15 = (bf16[64,1536]{1,0:T(8,128)(2,1)S(1)}, bf16[64,1536]{1,0:T(8,128)(2,1)S(1)}, u32[]{:S(2)}, u32[]{:S(2)}) collective-permute-start(bf16[64,1536]{1,0:T(8,128)(2,1)S(1)} %get-tuple-element.50), channel_id=1, source_target_pairs={{0,1},{1,0},{2,3},{3,2},{4,5},{5,4},{6,7},{7,6},{8,9},{9,8},{10,11... | collective-permute-start | bytes 589832 | tf_op jit(solution)/shard_map/ppermute | solution.py:428
  96.7 17.1 %collective-permute-start.16 = (bf16[64,1536]{1,0:T(8,128)(2,1)S(1)}, bf16[64,1536]{1,0:T(8,128)(2,1)S(1)}, u32[]{:S(2)}, u32[]{:S(2)}) collective-permute-start(bf16[64,1536]{1,0:T(8,128)(2,1)S(1)} %get-tuple-element.51), channel_id=1, source_target_pairs={{0,2},{1,3},{2,0},{3,1},{4,6},{5,7},{6,4},{7,5},{8,10},{9,11},{10,... | collective-permute-start | bytes 589832 | tf_op jit(solution)/shard_map/ppermute | solution.py:428
  100.1 13.7 %collective-permute-start.17 = (bf16[64,1536]{1,0:T(8,128)(2,1)S(1)}, bf16[64,1536]{1,0:T(8,128)(2,1)S(1)}, u32[]{:S(2)}, u32[]{:S(2)}) collective-permute-start(bf16[64,1536]{1,0:T(8,128)(2,1)S(1)} %get-tuple-element.52), channel_id=1, source_target_pairs={{0,3},{1,2},{2,1},{3,0},{4,7},{5,6},{6,5},{7,4},{8,11},{9,10},{10,... | collective-permute-start | bytes 589832 | tf_op jit(solution)/shard_map/ppermute | solution.py:428
  (3 other events, 8.6 us)

commit v14 on v13

--- a/solution.py
+++ b/solution.py
@@ -81,7 +81,7 @@
         total = total + jnp.dot(
             hidden_ref[:, pl.ds(step * each, each)], held[step], preferred_element_type=f32
         )
-    out_ref[...] = total
+    out_ref[...] = total.astype(out_ref.dtype)
 
 
 def share_products(hidden, down, width, partner):
@@ -90,7 +90,7 @@
     vmem = pl.BlockSpec(memory_space=pltpu.VMEM)
     return pl.pallas_call(
         functools.partial(share_kernel, partner),
-        out_shape=jax.ShapeDtypeStruct((frames_here, width), f32),
+        out_shape=jax.ShapeDtypeStruct((frames_here, width), bf16 if partner % 2 else f32),
         in_specs=[vmem, pl.BlockSpec(memory_space=pl.ANY)],
         out_specs=vmem,
         scratch_shapes=[

time: 116 us -> 116 us (level)
  waiting for transfers between devices: 54.3 us -> 56.5 us
  other arithmetic: 3.18 us -> 1.83 us
    ppermute x18, waiting for transfers between devices: 54.3 us -> 56.5 us  [swap(): lax.ppermute(value, axis, [(i, i ^ distance) for i in range(lax.axis_size...]
    convert_element_type x1 -> x0, other arithmetic: 1.3 us -> none  [per_device(): near_came = swap(after(sums.pop(m).astype(bf16), onward), 'book', 1)]
  transfers between devices with their start and end apart: 18 -> 18, of which waited for: 6 -> 7; matrix products, arithmetic and copies ran while one was open for 8% -> 7% of each run, Pallas kernels for 15% -> 15%
where the time goes in v14:
time: 116 us
  waiting for transfers between devices  56.5 us (49%)
  Pallas kernels  27.7 us (24%)
  starting transfers between devices  23.5 us (20%)
  matrix products  6.29 us (5%)
  other arithmetic  1.83 us (2%)
    ppermute x18, waiting for transfers between devices, swap(): lax.ppermute(value, axis, [(i, i ^ distance) for i in range(lax.axis_size...  56.5 us
    ppermute x18, starting transfers between devices, swap(): lax.ppermute(value, axis, [(i, i ^ distance) for i in range(lax.axis_size...  23.5 us
    pallas_call x1, Pallas kernels, project_early(): pl.pallas_call(functools.partial(early_kernel, books, early, pieces, size...  7.91 us
    pallas_call x2, Pallas kernels, share_products(): pl.pallas_call(functools.partial(share_kernel, partner), out_shape=jax.Sh...  7.34 us
    dot_general x4, matrix products, share(): total = total + jnp.dot(part, block, preferred_element_type=f32)  6.29 us
    pallas_call x1, Pallas kernels, first_products(): pl.pallas_call(first_kernel, out_shape=[jax.ShapeDtypeStruct((frames_here...  3.74 us
    pallas_call x1, Pallas kernels, project_late(): pl.pallas_call(functools.partial(late_kernel, books, late), out_shape=[ja...  3.61 us
    pallas_call x1, Pallas kernels, cut_rows(): pl.pallas_call(functools.partial(cut_kernel, cut), out_shape=[jax.ShapeDt...  2.63 us
  transfers between devices with their start and end apart: 18, of which 7 were waited for; matrix products, arithmetic and copies ran while one was open for 7% of the time, Pallas kernels for 15%

profile of v14, /device:TPU:0, one launch (start us, length us, event | category | flops | bytes accessed | tf_op | source)
XLA Modules:
  0.0 116.0 jit_solution(2819609057442318721)
XLA Ops:
  0.0 3.7 %hidden_and_first_products.1 = (bf16[256,1536]{1,0:T(8,128)(2,1)}, bf16[256,1024]{1,0:T(8,128)(2,1)S(1)}) custom-call(bf16[256,1536]{1,0:T(8,128)(2,1)} %gate_ref.1, bf16[256,1536]{1,0:T(8,128)(2,1)} %up_ref.1, bf16[1536,4096]{1,0:T(8,128)(2,1)} %down_ref.5), custom_call_target="tpu_custom_call" | custom-call | tf_op jit(solution)/shard_map/hidden_and_first_products/pallas_call | solution.py:47
  4.5 2.7 %collective-permute-start = (bf16[256,1024]{1,0:T(8,128)(2,1)S(1)}, bf16[256,1024]{1,0:T(8,128)(2,1)}, u32[]{:S(2)}, u32[]{:S(2)}) collective-permute-start(bf16[256,1024]{1,0:T(8,128)(2,1)S(1)} %get-tuple-element.30), channel_id=1, source_target_pairs={{0,1},{1,0},{2,3},{3,2},{4,5},{5,4},{6,7},{7,6},{8,9},{9,8},{10,11... | collective-permute-start | bytes 1572872 | tf_op jit(solution)/shard_map/ppermute | solution.py:428
  10.2 3.7 %share_products.2 = bf16[256,1024]{1,0:T(8,128)(2,1)S(1)} custom-call(bf16[256,1536]{1,0:T(8,128)(2,1)} %get-tuple-element.36.hidden_ref, bf16[1536,4096]{1,0:T(8,128)(2,1)} %down_ref.5), custom_call_target="tpu_custom_call" | custom-call | tf_op jit(solution)/shard_map/share_products/pallas_call | solution.py:91
  13.9 3.6 %share_products.3 = f32[256,1024]{1,0:T(8,128)} custom-call(bf16[256,1536]{1,0:T(8,128)(2,1)S(1)} %copy-done, bf16[1536,4096]{1,0:T(8,128)(2,1)} %down_ref.5), custom_call_target="tpu_custom_call" | custom-call | tf_op jit(solution)/shard_map/share_products/pallas_call | solution.py:91
  17.6 2.2 %collective-permute-done = bf16[256,1024]{1,0:T(8,128)(2,1)} collective-permute-done((bf16[256,1024]{1,0:T(8,128)(2,1)S(1)}, bf16[256,1024]{1,0:T(8,128)(2,1)}, u32[]{:S(2)}, u32[]{:S(2)}) %collective-permute-start) | collective-permute-done | bytes 524320 | tf_op jit(solution)/shard_map/ppermute | solution.py:428
  21.3 2.8 %collective-permute-start.3 = (bf16[256,1024]{1,0:T(8,128)(2,1)S(1)}, bf16[256,1024]{1,0:T(8,128)(2,1)S(1)}, u32[]{:S(2)}, u32[]{:S(2)}) collective-permute-start(bf16[256,1024]{1,0:T(8,128)(2,1)S(1)} %add_convert_fusion.1), channel_id=1, source_target_pairs={{0,2},{1,3},{2,0},{3,1},{4,6},{5,7},{6,4},{7,5},{8,10},{9,11},{10,... | collective-permute-start | bytes 1572872 | tf_op jit(solution)/shard_map/ppermute | solution.py:428
  24.1 1.6 %collective-permute-start.2 = (bf16[256,1024]{1,0:T(8,128)(2,1)S(1)}, bf16[256,1024]{1,0:T(8,128)(2,1)S(1)}, u32[]{:S(2)}, u32[]{:S(2)}) collective-permute-start(bf16[256,1024]{1,0:T(8,128)(2,1)S(1)} %share_products.2), channel_id=1, source_target_pairs={{0,1},{1,0},{2,3},{3,2},{4,5},{5,4},{6,7},{7,6},{8,9},{9,8},{10,11... | collective-permute-start | bytes 1572872 | tf_op jit(solution)/shard_map/ppermute | solution.py:428
  25.7 1.6 %fusion.3 = f32[256,1024]{1,0:T(8,128)S(1)} fusion(bf16[1536,4096]{1,0:T(8,128)(2,1)} %down_ref.5, s32[]{:T(128)S(6)} %select_n.2, bf16[256,1536]{1,0:T(8,128)(2,1)S(1)} %copy-done), kind=kOutput, calls=%fused_computation.8 | convolution fusion | flops 201326592 | bytes 2031620 | tf_op jit(solution)/shard_map/dot_general | solution.py:470
  27.3 1.6 %convolution_add_fusion.2 = f32[256,1024]{1,0:T(8,128)S(1)} fusion(f32[256,1024]{1,0:T(8,128)S(1)} %fusion.3, bf16[1536,4096]{1,0:T(8,128)(2,1)} %down_ref.5, s32[]{:T(128)S(6)} %select_n.2, bf16[256,1536]{1,0:T(8,128)(2,1)S(1)} %copy-done), kind=kOutput, calls=%fused_computation.2 | convolution fusion | flops 201588736 | bytes 3080196 | tf_op jit(solution)/shard_map/dot_general | solution.py:470
  28.9 1.6 %convolution_add_fusion.1 = f32[256,1024]{1,0:T(8,128)S(1)} fusion(f32[256,1024]{1,0:T(8,128)S(1)} %convolution_add_fusion.2, bf16[1536,4096]{1,0:T(8,128)(2,1)} %down_ref.5, s32[]{:T(128)S(6)} %select_n.2, bf16[256,1536]{1,0:T(8,128)(2,1)S(1)} %copy-done), kind=kOutput, calls=%fused_computation.1 | convolution fusion | flops 201588736 | bytes 3080196 | tf_op jit(solution)/shard_map/dot_general | solution.py:470
  30.4 1.6 %convolution_add_fusion = f32[256,1024]{1,0:T(8,128)S(1)} fusion(f32[256,1024]{1,0:T(8,128)S(1)} %convolution_add_fusion.1, bf16[1536,4096]{1,0:T(8,128)(2,1)} %down_ref.5, s32[]{:T(128)S(6)} %select_n.2, bf16[256,1536]{1,0:T(8,128)(2,1)S(1)} %copy-done), kind=kOutput, calls=%fused_computation | convolution fusion | flops 201588736 | bytes 3080196 | tf_op jit(solution)/shard_map/dot_general | solution.py:470
  32.0 15.4 %collective-permute-done.2 = bf16[256,1024]{1,0:T(8,128)(2,1)S(1)} collective-permute-done((bf16[256,1024]{1,0:T(8,128)(2,1)S(1)}, bf16[256,1024]{1,0:T(8,128)(2,1)S(1)}, u32[]{:S(2)}, u32[]{:S(2)}) %collective-permute-start.2) | collective-permute-done | bytes 524320 | tf_op jit(solution)/shard_map/ppermute | solution.py:428
  48.4 2.6 %cut_rows.1 = (bf16[384,1024]{1,0:T(8,128)(2,1)}, bf16[448,1024]{1,0:T(8,128)(2,1)}) custom-call(bf16[832,1024]{1,0:T(8,128)(2,1)} %collective-permute-done.6.upper_from.refs_7_, bf16[832,1024]{1,0:T(8,128)(2,1)} %collective-permute-done.5.lower_from.refs_5_), custom_call_target="tpu_custom_call" | custom-call | tf_op jit(solution)/shard_map/cut_rows/pallas_call | solution.py:161
  51.0 1.6 %collective-permute-start.12 = (bf16[448,1024]{1,0:T(8,128)(2,1)}, bf16[448,1024]{1,0:T(8,128)(2,1)S(1)}, u32[]{:S(2)}, u32[]{:S(2)}) collective-permute-start(bf16[448,1024]{1,0:T(8,128)(2,1)} %get-tuple-element.43), channel_id=1, source_target_pairs={{0,16},{4,20},{8,24},{12,28},{16,0},{20,4},{24,8},{28,12},{1,17},{... | collective-permute-start | bytes 2752520 | tf_op jit(solution)/shard_map/ppermute | solution.py:428
  55.6 2.3 %collective-permute-start.9 = (bf16[256,1024]{1,0:T(8,128)(2,1)S(1)}, bf16[256,1024]{1,0:T(8,128)(2,1)S(1)}, u32[]{:S(2)}, u32[]{:S(2)}) collective-permute-start(bf16[256,1024]{1,0:T(8,128)(2,1)S(1)} %add_convert_fusion.refs_0_), channel_id=1, source_target_pairs={{0,1},{1,0},{2,3},{3,2},{4,5},{5,4},{6,7},{7,6},{8,9},{9,8},{10,11... | collective-permute-start | bytes 1572872 | tf_op jit(solution)/shard_map/ppermute | solution.py:428
  57.9 15.8 %collective-permute-done.12.refs_10_ = bf16[448,1024]{1,0:T(8,128)(2,1)S(1)} collective-permute-done((bf16[448,1024]{1,0:T(8,128)(2,1)}, bf16[448,1024]{1,0:T(8,128)(2,1)S(1)}, u32[]{:S(2)}, u32[]{:S(2)}) %collective-permute-start.12) | collective-permute-done | bytes 917536 | tf_op jit(solution)/shard_map/ppermute | solution.py:428
  74.2 5.4 %collective-permute-done.4.refs_2_ = bf16[256,1024]{1,0:T(8,128)(2,1)S(1)} collective-permute-done((bf16[256,1024]{1,0:T(8,128)(2,1)S(1)}, bf16[256,1024]{1,0:T(8,128)(2,1)S(1)}, u32[]{:S(2)}, u32[]{:S(2)}) %collective-permute-start.4) | collective-permute-done | bytes 524320 | tf_op jit(solution)/shard_map/ppermute | solution.py:428
  80.2 7.9 %early_products_and_lookup.1 = (f32[256,1024]{1,0:T(8,128)S(1)}, f32[256,1]{1,0:T(8,128)S(1)}, bf16[1,1024,1024]{2,1,0:T(8,128)(2,1)}, bf16[256,1024]{1,0:T(8,128)(2,1)S(1)}, bf16[1024,1536]{1,0:T(8,128)(2,1)}) custom-call(s32[1,256]{1,0:T(1,128)S(1)} %bitcast.7, bf16[1,4096]{1,0:T(2,128)(2,1)S(1)} %broadcast_in_dim.3.gain_ref, ...), custom_call_target="tpu_custom_call" | custom-call | tf_op jit(solution)/shard_map/early_products_and_lookup/pallas_call | solution.py:288
  88.1 4.4 %collective-permute-done.10.refs_0_ = bf16[256,1024]{1,0:T(8,128)(2,1)S(1)} collective-permute-done((bf16[256,1024]{1,0:T(8,128)(2,1)S(1)}, bf16[256,1024]{1,0:T(8,128)(2,1)S(1)}, u32[]{:S(2)}, u32[]{:S(2)}) %collective-permute-start.10) | collective-permute-done | bytes 524320 | tf_op jit(solution)/shard_map/ppermute | solution.py:428
  92.5 3.6 %late_products_and_qkv.1 = (bf16[64,1536]{1,0:T(8,128)(2,1)S(1)}, bf16[64,1536]{1,0:T(8,128)(2,1)S(1)}, bf16[64,1536]{1,0:T(8,128)(2,1)S(1)}, bf16[64,1536]{1,0:T(8,128)(2,1)S(1)}) custom-call(bf16[1,4096]{1,0:T(2,128)(2,1)S(1)} %broadcast_in_dim.3.gain_ref, bf16[256,1024]{1,0:T(8,128)(2,1)S(1)} %collective-permute-done.10.refs_0_, ...), custom_call_target="tpu_custom_call" | custom-call | tf_op jit(solution)/shard_map/late_products_and_qkv/pallas_call | solution.py:349
  96.7 3.4 %collective-permute-start.16 = (bf16[64,1536]{1,0:T(8,128)(2,1)S(1)}, bf16[64,1536]{1,0:T(8,128)(2,1)S(1)}, u32[]{:S(2)}, u32[]{:S(2)}) collective-permute-start(bf16[64,1536]{1,0:T(8,128)(2,1)S(1)} %get-tuple-element.51), channel_id=1, source_target_pairs={{0,2},{1,3},{2,0},{3,1},{4,6},{5,7},{6,4},{7,5},{8,10},{9,11},{10,... | collective-permute-start | bytes 589832 | tf_op jit(solution)/shard_map/ppermute | solution.py:428
  100.6 3.2 %collective-permute-done.15.refs_1_ = bf16[64,1536]{1,0:T(8,128)(2,1)S(1)} collective-permute-done((bf16[64,1536]{1,0:T(8,128)(2,1)S(1)}, bf16[64,1536]{1,0:T(8,128)(2,1)S(1)}, u32[]{:S(2)}, u32[]{:S(2)}) %collective-permute-start.15) | collective-permute-done | bytes 196640 | tf_op jit(solution)/shard_map/ppermute | solution.py:428
  103.8 10.0 %collective-permute-done.16.refs_2_ = bf16[64,1536]{1,0:T(8,128)(2,1)S(1)} collective-permute-done((bf16[64,1536]{1,0:T(8,128)(2,1)S(1)}, bf16[64,1536]{1,0:T(8,128)(2,1)S(1)}, u32[]{:S(2)}, u32[]{:S(2)}) %collective-permute-start.16) | collective-permute-done | bytes 196640 | tf_op jit(solution)/shard_map/ppermute | solution.py:428
  113.8 2.3 %attend_books.1 = bf16[64,4,512]{2,1,0:T(4,128)(2,1)} custom-call(bf16[64,1536]{1,0:T(8,128)(2,1)S(1)} %get-tuple-element.49.refs_0_, bf16[64,1536]{1,0:T(8,128)(2,1)S(1)} %collective-permute-done.15.refs_1_, bf16[64,1536]{1,0:T(8,128)(2,1)S(1)} %collective-permute-done.16.refs_2_, bf16[64,1536]{1,0:T(8,128)(2,1)S(1)} %collective-permute-done.17.refs_3_), custom_call_target="tpu_custom_call" | custom-call | tf_op jit(solution)/shard_map/attend_books/pallas_call | solution.py:416
  (43 shorter events, 11.3 us)
Async XLA Ops:
  0.0 3.8 %copy-start.1 = (bf16[1,512,1024]{2,1,0:T(8,128)(2,1)S(1)}, bf16[1,512,1024]{2,1,0:T(8,128)(2,1)}, u32[]{:S(2)}) copy-start(bf16[1,512,1024]{2,1,0:T(8,128)(2,1)} %param.15) | copy-start | bytes 3145732
  3.8 10.2 %copy-start = (bf16[256,1536]{1,0:T(8,128)(2,1)S(1)}, bf16[256,1536]{1,0:T(8,128)(2,1)}, u32[]{:S(2)}) copy-start(bf16[256,1536]{1,0:T(8,128)(2,1)} %get-tuple-element.36.hidden_ref) | copy-start | bytes 2359300
  4.0 21.7 %collective-permute-start.1 = (bf16[832,1024]{1,0:T(8,128)(2,1)S(1)}, bf16[832,1024]{1,0:T(8,128)(2,1)}, u32[]{:S(2)}, u32[]{:S(2)}) collective-permute-start(bf16[832,1024]{1,0:T(8,128)(2,1)S(1)} %pack_weight_rows.1.refs_3_), channel_id=1, source_target_pairs={{0,4},{4,0},{8,12},{12,8},{16,20},{20,16},{24,28},{28,24},{1,5},{5... | collective-permute-start | bytes 5111816 | tf_op jit(solution)/shard_map/ppermute | solution.py:428
  4.5 15.3 %collective-permute-start = (bf16[256,1024]{1,0:T(8,128)(2,1)S(1)}, bf16[256,1024]{1,0:T(8,128)(2,1)}, u32[]{:S(2)}, u32[]{:S(2)}) collective-permute-start(bf16[256,1024]{1,0:T(8,128)(2,1)S(1)} %get-tuple-element.30), channel_id=1, source_target_pairs={{0,1},{1,0},{2,3},{3,2},{4,5},{5,4},{6,7},{7,6},{8,9},{9,8},{10,11... | collective-permute-start | bytes 1572872 | tf_op jit(solution)/shard_map/ppermute | solution.py:428
  7.2 40.6 %collective-permute-start.6 = (bf16[832,1024]{1,0:T(8,128)(2,1)S(1)}, bf16[832,1024]{1,0:T(8,128)(2,1)}, u32[]{:S(2)}, u32[]{:S(2)}) collective-permute-start(bf16[832,1024]{1,0:T(8,128)(2,1)S(1)} %pack_weight_rows.1.refs_3_), channel_id=1, source_target_pairs={{0,16},{4,20},{8,24},{12,28},{16,0},{20,4},{24,8},{28,12},{1,17},{... | collective-permute-start | bytes 5111816 | tf_op jit(solution)/shard_map/ppermute | solution.py:428
  8.7 39.1 %collective-permute-start.5 = (bf16[832,1024]{1,0:T(8,128)(2,1)S(1)}, bf16[832,1024]{1,0:T(8,128)(2,1)}, u32[]{:S(2)}, u32[]{:S(2)}) collective-permute-start(bf16[832,1024]{1,0:T(8,128)(2,1)S(1)} %pack_weight_rows.1.refs_3_), channel_id=1, source_target_pairs={{0,8},{4,12},{8,0},{12,4},{16,24},{20,28},{24,16},{28,20},{1,9},{5... | collective-permute-start | bytes 5111816 | tf_op jit(solution)/shard_map/ppermute | solution.py:428
  17.5 62.6 %copy-start.7 = (bf16[4096]{0:T(1024)(128)(2,1)S(1)}, bf16[4096]{0:T(1024)(128)(2,1)}, u32[]{:S(2)}) copy-start(bf16[4096]{0:T(1024)(128)(2,1)} %param.14) | copy-start | bytes 24580
  17.5 62.6 %copy-start.5 = (s32[256,1]{0,1:T(1,128)S(1)}, s32[256,1]{0,1:T(1,128)}, u32[]{:S(2)}) copy-start(s32[256,1]{0,1:T(1,128)} %param.17) | copy-start | bytes 3076
  17.6 29.9 %copy-start.6 = (bf16[256,1024]{1,0:T(8,128)(2,1)S(1)}, bf16[256,1024]{1,0:T(8,128)(2,1)}, u32[]{:S(2)}) copy-start(bf16[256,1024]{1,0:T(8,128)(2,1)} %param.13) | copy-start | bytes 1572868
  21.3 26.2 %collective-permute-start.3 = (bf16[256,1024]{1,0:T(8,128)(2,1)S(1)}, bf16[256,1024]{1,0:T(8,128)(2,1)S(1)}, u32[]{:S(2)}, u32[]{:S(2)}) collective-permute-start(bf16[256,1024]{1,0:T(8,128)(2,1)S(1)} %add_convert_fusion.1), channel_id=1, source_target_pairs={{0,2},{1,3},{2,0},{3,1},{4,6},{5,7},{6,4},{7,5},{8,10},{9,11},{10,... | collective-permute-start | bytes 1572872 | tf_op jit(solution)/shard_map/ppermute | solution.py:428
  24.1 23.3 %collective-permute-start.2 = (bf16[256,1024]{1,0:T(8,128)(2,1)S(1)}, bf16[256,1024]{1,0:T(8,128)(2,1)S(1)}, u32[]{:S(2)}, u32[]{:S(2)}) collective-permute-start(bf16[256,1024]{1,0:T(8,128)(2,1)S(1)} %share_products.2), channel_id=1, source_target_pairs={{0,1},{1,0},{2,3},{3,2},{4,5},{5,4},{6,7},{7,6},{8,9},{9,8},{10,11... | collective-permute-start | bytes 1572872 | tf_op jit(solution)/shard_map/ppermute | solution.py:428
  30.4 62.1 %copy-start.4 = (bf16[1,1024]{1,0:T(2,128)(2,1)S(1)}, bf16[1,1024]{1,0:T(2,128)(2,1)}, u32[]{:S(2)}) copy-start(bf16[1,1024]{1,0:T(2,128)(2,1)} %refs_5_.1) | copy-start | bytes 6148
  47.8 7.8 %collective-permute-start.7 = (bf16[832,1024]{1,0:T(8,128)(2,1)}, bf16[832,1024]{1,0:T(8,128)(2,1)}, u32[]{:S(2)}, u32[]{:S(2)}) collective-permute-start(bf16[832,1024]{1,0:T(8,128)(2,1)} %collective-permute-done.5.lower_from.refs_5_), channel_id=1, source_target_pairs={{0,4},{4,0},{8,12},{12,8},{16,20},{20,16},{24,28},{28,24},{1,5},{5... | collective-permute-start | bytes 5111816 | tf_op jit(solution)/shard_map/ppermute | solution.py:428
  47.9 7.7 %collective-permute-start.8 = (bf16[832,1024]{1,0:T(8,128)(2,1)}, bf16[832,1024]{1,0:T(8,128)(2,1)}, u32[]{:S(2)}, u32[]{:S(2)}) collective-permute-start(bf16[832,1024]{1,0:T(8,128)(2,1)} %collective-permute-done.6.upper_from.refs_7_), channel_id=1, source_target_pairs={{0,4},{4,0},{8,12},{12,8},{16,20},{20,16},{24,28},{28,24},{1,5},{5... | collective-permute-start | bytes 5111816 | tf_op jit(solution)/shard_map/ppermute | solution.py:428
  51.0 22.6 %collective-permute-start.12 = (bf16[448,1024]{1,0:T(8,128)(2,1)}, bf16[448,1024]{1,0:T(8,128)(2,1)S(1)}, u32[]{:S(2)}, u32[]{:S(2)}) collective-permute-start(bf16[448,1024]{1,0:T(8,128)(2,1)} %get-tuple-element.43), channel_id=1, source_target_pairs={{0,16},{4,20},{8,24},{12,28},{16,0},{20,4},{24,8},{28,12},{1,17},{... | collective-permute-start | bytes 2752520 | tf_op jit(solution)/shard_map/ppermute | solution.py:428
  52.6 21.0 %collective-permute-start.11 = (bf16[384,1024]{1,0:T(8,128)(2,1)}, bf16[384,1024]{1,0:T(8,128)(2,1)S(1)}, u32[]{:S(2)}, u32[]{:S(2)}) collective-permute-start(bf16[384,1024]{1,0:T(8,128)(2,1)} %get-tuple-element.42), channel_id=1, source_target_pairs={{0,8},{4,12},{8,0},{12,4},{16,24},{20,28},{24,16},{28,20},{1,9},{5... | collective-permute-start | bytes 2359304 | tf_op jit(solution)/shard_map/ppermute | solution.py:428
  54.1 25.5 %collective-permute-start.4 = (bf16[256,1024]{1,0:T(8,128)(2,1)S(1)}, bf16[256,1024]{1,0:T(8,128)(2,1)S(1)}, u32[]{:S(2)}, u32[]{:S(2)}) collective-permute-start(bf16[256,1024]{1,0:T(8,128)(2,1)S(1)} %add_convert_fusion.refs_0_), channel_id=1, source_target_pairs={{0,2},{1,3},{2,0},{3,1},{4,6},{5,7},{6,4},{7,5},{8,10},{9,11},{10,... | collective-permute-start | bytes 1572872 | tf_op jit(solution)/shard_map/ppermute | solution.py:428
  55.6 24.0 %collective-permute-start.9 = (bf16[256,1024]{1,0:T(8,128)(2,1)S(1)}, bf16[256,1024]{1,0:T(8,128)(2,1)S(1)}, u32[]{:S(2)}, u32[]{:S(2)}) collective-permute-start(bf16[256,1024]{1,0:T(8,128)(2,1)S(1)} %add_convert_fusion.refs_0_), channel_id=1, source_target_pairs={{0,1},{1,0},{2,3},{3,2},{4,5},{5,4},{6,7},{7,6},{8,9},{9,8},{10,11... | collective-permute-start | bytes 1572872 | tf_op jit(solution)/shard_map/ppermute | solution.py:428
  73.6 6.5 %collective-permute-start.14 = (bf16[448,1024]{1,0:T(8,128)(2,1)S(1)}, bf16[448,1024]{1,0:T(8,128)(2,1)S(1)}, u32[]{:S(2)}, u32[]{:S(2)}) collective-permute-start(bf16[448,1024]{1,0:T(8,128)(2,1)S(1)} %collective-permute-done.12.refs_10_), channel_id=1, source_target_pairs={{0,4},{4,0},{8,12},{12,8},{16,20},{20,16},{24,28},{28,24},{1,5},{5... | collective-permute-start | bytes 2752520 | tf_op jit(solution)/shard_map/ppermute | solution.py:428
  73.7 6.5 %collective-permute-start.13 = (bf16[384,1024]{1,0:T(8,128)(2,1)S(1)}, bf16[384,1024]{1,0:T(8,128)(2,1)S(1)}, u32[]{:S(2)}, u32[]{:S(2)}) collective-permute-start(bf16[384,1024]{1,0:T(8,128)(2,1)S(1)} %collective-permute-done.11.refs_9_), channel_id=1, source_target_pairs={{0,4},{4,0},{8,12},{12,8},{16,20},{20,16},{24,28},{28,24},{1,5},{5... | collective-permute-start | bytes 2359304 | tf_op jit(solution)/shard_map/ppermute | solution.py:428
  79.6 12.9 %collective-permute-start.10 = (bf16[256,1024]{1,0:T(8,128)(2,1)S(1)}, bf16[256,1024]{1,0:T(8,128)(2,1)S(1)}, u32[]{:S(2)}, u32[]{:S(2)}) collective-permute-start(bf16[256,1024]{1,0:T(8,128)(2,1)S(1)} %collective-permute-done.4.refs_2_), channel_id=1, source_target_pairs={{0,1},{1,0},{2,3},{3,2},{4,5},{5,4},{6,7},{7,6},{8,9},{9,8},{10,11... | collective-permute-start | bytes 1572872 | tf_op jit(solution)/shard_map/ppermute | solution.py:428
  96.1 7.6 %collective-permute-start.15 = (bf16[64,1536]{1,0:T(8,128)(2,1)S(1)}, bf16[64,1536]{1,0:T(8,128)(2,1)S(1)}, u32[]{:S(2)}, u32[]{:S(2)}) collective-permute-start(bf16[64,1536]{1,0:T(8,128)(2,1)S(1)} %get-tuple-element.50), channel_id=1, source_target_pairs={{0,1},{1,0},{2,3},{3,2},{4,5},{5,4},{6,7},{7,6},{8,9},{9,8},{10,11... | collective-permute-start | bytes 589832 | tf_op jit(solution)/shard_map/ppermute | solution.py:428
  96.7 17.1 %collective-permute-start.16 = (bf16[64,1536]{1,0:T(8,128)(2,1)S(1)}, bf16[64,1536]{1,0:T(8,128)(2,1)S(1)}, u32[]{:S(2)}, u32[]{:S(2)}) collective-permute-start(bf16[64,1536]{1,0:T(8,128)(2,1)S(1)} %get-tuple-element.51), channel_id=1, source_target_pairs={{0,2},{1,3},{2,0},{3,1},{4,6},{5,7},{6,4},{7,5},{8,10},{9,11},{10,... | collective-permute-start | bytes 589832 | tf_op jit(solution)/shard_map/ppermute | solution.py:428
  100.0 13.7 %collective-permute-start.17 = (bf16[64,1536]{1,0:T(8,128)(2,1)S(1)}, bf16[64,1536]{1,0:T(8,128)(2,1)S(1)}, u32[]{:S(2)}, u32[]{:S(2)}) collective-permute-start(bf16[64,1536]{1,0:T(8,128)(2,1)S(1)} %get-tuple-element.52), channel_id=1, source_target_pairs={{0,3},{1,2},{2,1},{3,0},{4,7},{5,6},{6,5},{7,4},{8,11},{9,10},{10,... | collective-permute-start | bytes 589832 | tf_op jit(solution)/shard_map/ppermute | solution.py:428
  (2 other events, 7.5 us)

commit v15 on v14

--- a/solution.py
+++ b/solution.py
@@ -143,32 +143,6 @@
         compiler_params=pltpu.CompilerParams(vmem_limit_bytes=4 * 2**20),
         name="pack_weight_rows",
     )(proj, table, qkv)
-
-
-def cut_kernel(cut, upper_from, lower_from, upper_ref, lower_ref, sems):
-    upper = pltpu.make_async_copy(upper_from.at[pl.ds(0, cut)], upper_ref, sems.at[0])
-    lower = pltpu.make_async_copy(
-        lower_from.at[pl.ds(cut, lower_ref.shape[0])], lower_ref, sems.at[1]
-    )
-    upper.start()
-    lower.start()
-    upper.wait()
-    lower.wait()
-
-
-def cut_rows(upper_from, lower_from, cut):
-    rows, depth = upper_from.shape
-    return pl.pallas_call(
-        functools.partial(cut_kernel, cut),
-        out_shape=[
-            jax.ShapeDtypeStruct((cut, depth), bf16),
-            jax.ShapeDtypeStruct((rows - cut, depth), bf16),
-        ],
-        in_specs=[pl.BlockSpec(memory_space=pl.ANY)] * 2,
-        out_specs=[pl.BlockSpec(memory_space=pltpu.VMEM)] * 2,
-        scratch_shapes=[pltpu.SemaphoreType.DMA((2,))],
-        name="cut_rows",
-    )(upper_from, lower_from)
 
 
 def is_late(m):
@@ -512,9 +486,8 @@
         if n in near:
             continue
         if len(sides) == 2 and 0 < cut < proj_rows:
-            upper, lower = cut_rows(parts[n ^ sides[0]][0][1], parts[n ^ sides[1]][0][1], cut)
-            upper = swap(upper, "frames", sides[0])
-            lower = swap(lower, "frames", sides[1])
+            upper = swap(parts[n ^ sides[0]][0][1][:cut], "frames", sides[0])
+            lower = swap(parts[n ^ sides[1]][0][1][cut:], "frames", sides[1])
             parts[n] = [(0, upper), (cut, lower)]
         else:
             parts[n] = [(0, swap(rows, "frames", n))]

time: 116 us -> 116 us (level)
  Pallas kernels: 27.7 us -> 25.1 us
  local copies, waits for them, and re-layouts: 0.05 us -> 2.48 us
    pallas_call x1 -> x0, Pallas kernels: 2.63 us -> none  [cut_rows(): pl.pallas_call(functools.partial(cut_kernel, cut), out_shape=[jax.ShapeDt...]
    slice x0 -> x2, local copies, waits for them, and re-layouts: none -> 2.42 us  [the longest x1 1.24 us: per_device(): lower = swap(parts[n ^ sides[1]][0][1][cut:], 'frames', sides[1])]
  transfers between devices with their start and end apart: 18 -> 18, of which waited for: 7 -> 7; matrix products, arithmetic and copies ran while one was open for 7% -> 9% of each run, Pallas kernels for 15% -> 13%
where the time goes in v15:
time: 116 us
  waiting for transfers between devices  56.3 us (49%)
  Pallas kernels  25.1 us (22%)
  starting transfers between devices  23.6 us (20%)
  matrix products  6.33 us (5%)
  local copies, waits for them, and re-layouts  2.48 us (2%)
  other arithmetic  1.83 us (2%)
    ppermute x18, waiting for transfers between devices, swap(): lax.ppermute(value, axis, [(i, i ^ distance) for i in range(lax.axis_size...  56.3 us
    ppermute x18, starting transfers between devices, swap(): lax.ppermute(value, axis, [(i, i ^ distance) for i in range(lax.axis_size...  23.6 us
    pallas_call x1, Pallas kernels, project_early(): pl.pallas_call(functools.partial(early_kernel, books, early, pieces, size...  7.91 us
    pallas_call x2, Pallas kernels, share_products(): pl.pallas_call(functools.partial(share_kernel, partner), out_shape=jax.Sh...  7.37 us
    dot_general x4, matrix products, share(): total = total + jnp.dot(part, block, preferred_element_type=f32)  6.33 us
    pallas_call x1, Pallas kernels, first_products(): pl.pallas_call(first_kernel, out_shape=[jax.ShapeDtypeStruct((frames_here...  3.75 us
    pallas_call x1, Pallas kernels, project_late(): pl.pallas_call(functools.partial(late_kernel, books, late), out_shape=[ja...  3.62 us
  transfers between devices with their start and end apart: 18, of which 7 were waited for; matrix products, arithmetic and copies ran while one was open for 9% of the time, Pallas kernels for 13%

profile of v15, /device:TPU:0, one launch (start us, length us, event | category | flops | bytes accessed | tf_op | source)
XLA Modules:
  0.0 115.9 jit_solution(4425866786426488194)
XLA Ops:
  0.0 3.7 %hidden_and_first_products.1 = (bf16[256,1536]{1,0:T(8,128)(2,1)}, bf16[256,1024]{1,0:T(8,128)(2,1)S(1)}) custom-call(bf16[256,1536]{1,0:T(8,128)(2,1)} %gate_ref.1, bf16[256,1536]{1,0:T(8,128)(2,1)} %up_ref.1, bf16[1536,4096]{1,0:T(8,128)(2,1)} %down_ref.5), custom_call_target="tpu_custom_call" | custom-call | tf_op jit(solution)/shard_map/hidden_and_first_products/pallas_call | solution.py:47
  4.5 2.7 %collective-permute-start = (bf16[256,1024]{1,0:T(8,128)(2,1)S(1)}, bf16[256,1024]{1,0:T(8,128)(2,1)}, u32[]{:S(2)}, u32[]{:S(2)}) collective-permute-start(bf16[256,1024]{1,0:T(8,128)(2,1)S(1)} %get-tuple-element.28), channel_id=1, source_target_pairs={{0,1},{1,0},{2,3},{3,2},{4,5},{5,4},{6,7},{7,6},{8,9},{9,8},{10,11... | collective-permute-start | bytes 1572872 | tf_op jit(solution)/shard_map/ppermute | solution.py:402
  10.2 3.7 %share_products.2 = bf16[256,1024]{1,0:T(8,128)(2,1)S(1)} custom-call(bf16[256,1536]{1,0:T(8,128)(2,1)} %get-tuple-element.34.hidden_ref, bf16[1536,4096]{1,0:T(8,128)(2,1)} %down_ref.5), custom_call_target="tpu_custom_call" | custom-call | tf_op jit(solution)/shard_map/share_products/pallas_call | solution.py:91
  13.9 3.6 %share_products.3 = f32[256,1024]{1,0:T(8,128)} custom-call(bf16[256,1536]{1,0:T(8,128)(2,1)S(1)} %copy-done, bf16[1536,4096]{1,0:T(8,128)(2,1)} %down_ref.5), custom_call_target="tpu_custom_call" | custom-call | tf_op jit(solution)/shard_map/share_products/pallas_call | solution.py:91
  17.6 2.2 %collective-permute-done = bf16[256,1024]{1,0:T(8,128)(2,1)} collective-permute-done((bf16[256,1024]{1,0:T(8,128)(2,1)S(1)}, bf16[256,1024]{1,0:T(8,128)(2,1)}, u32[]{:S(2)}, u32[]{:S(2)}) %collective-permute-start) | collective-permute-done | bytes 524320 | tf_op jit(solution)/shard_map/ppermute | solution.py:402
  21.3 2.8 %collective-permute-start.3 = (bf16[256,1024]{1,0:T(8,128)(2,1)S(1)}, bf16[256,1024]{1,0:T(8,128)(2,1)S(1)}, u32[]{:S(2)}, u32[]{:S(2)}) collective-permute-start(bf16[256,1024]{1,0:T(8,128)(2,1)S(1)} %add_convert_fusion.1), channel_id=1, source_target_pairs={{0,2},{1,3},{2,0},{3,1},{4,6},{5,7},{6,4},{7,5},{8,10},{9,11},{10,... | collective-permute-start | bytes 1572872 | tf_op jit(solution)/shard_map/ppermute | solution.py:402
  24.1 1.6 %collective-permute-start.2 = (bf16[256,1024]{1,0:T(8,128)(2,1)S(1)}, bf16[256,1024]{1,0:T(8,128)(2,1)S(1)}, u32[]{:S(2)}, u32[]{:S(2)}) collective-permute-start(bf16[256,1024]{1,0:T(8,128)(2,1)S(1)} %share_products.2), channel_id=1, source_target_pairs={{0,1},{1,0},{2,3},{3,2},{4,5},{5,4},{6,7},{7,6},{8,9},{9,8},{10,11... | collective-permute-start | bytes 1572872 | tf_op jit(solution)/shard_map/ppermute | solution.py:402
  25.7 1.6 %fusion.3 = f32[256,1024]{1,0:T(8,128)S(1)} fusion(bf16[1536,4096]{1,0:T(8,128)(2,1)} %down_ref.5, s32[]{:T(128)S(6)} %select_n.2, bf16[256,1536]{1,0:T(8,128)(2,1)S(1)} %copy-done), kind=kOutput, calls=%fused_computation.8 | convolution fusion | flops 201326592 | bytes 2031620 | tf_op jit(solution)/shard_map/dot_general | solution.py:444
  27.3 1.6 %convolution_add_fusion.2 = f32[256,1024]{1,0:T(8,128)S(1)} fusion(f32[256,1024]{1,0:T(8,128)S(1)} %fusion.3, bf16[1536,4096]{1,0:T(8,128)(2,1)} %down_ref.5, s32[]{:T(128)S(6)} %select_n.2, bf16[256,1536]{1,0:T(8,128)(2,1)S(1)} %copy-done), kind=kOutput, calls=%fused_computation.2 | convolution fusion | flops 201588736 | bytes 3080196 | tf_op jit(solution)/shard_map/dot_general | solution.py:444
  28.9 1.6 %convolution_add_fusion.1 = f32[256,1024]{1,0:T(8,128)S(1)} fusion(f32[256,1024]{1,0:T(8,128)S(1)} %convolution_add_fusion.2, bf16[1536,4096]{1,0:T(8,128)(2,1)} %down_ref.5, s32[]{:T(128)S(6)} %select_n.2, bf16[256,1536]{1,0:T(8,128)(2,1)S(1)} %copy-done), kind=kOutput, calls=%fused_computation.1 | convolution fusion | flops 201588736 | bytes 3080196 | tf_op jit(solution)/shard_map/dot_general | solution.py:444
  30.5 1.6 %convolution_add_fusion = f32[256,1024]{1,0:T(8,128)S(1)} fusion(f32[256,1024]{1,0:T(8,128)S(1)} %convolution_add_fusion.1, bf16[1536,4096]{1,0:T(8,128)(2,1)} %down_ref.5, s32[]{:T(128)S(6)} %select_n.2, bf16[256,1536]{1,0:T(8,128)(2,1)S(1)} %copy-done), kind=kOutput, calls=%fused_computation | convolution fusion | flops 201588736 | bytes 3080196 | tf_op jit(solution)/shard_map/dot_general | solution.py:444
  32.1 15.4 %collective-permute-done.2 = bf16[256,1024]{1,0:T(8,128)(2,1)S(1)} collective-permute-done((bf16[256,1024]{1,0:T(8,128)(2,1)S(1)}, bf16[256,1024]{1,0:T(8,128)(2,1)S(1)}, u32[]{:S(2)}, u32[]{:S(2)}) %collective-permute-start.2) | collective-permute-done | bytes 524320 | tf_op jit(solution)/shard_map/ppermute | solution.py:402
  49.6 1.6 %collective-permute-start.12 = (bf16[448,1024]{1,0:T(8,128)(2,1)S(1)}, bf16[448,1024]{1,0:T(8,128)(2,1)S(1)}, u32[]{:S(2)}, u32[]{:S(2)}) collective-permute-start(bf16[448,1024]{1,0:T(8,128)(2,1)S(1)} %slice.23), channel_id=1, source_target_pairs={{0,16},{4,20},{8,24},{12,28},{16,0},{20,4},{24,8},{28,12},{1,17},{... | collective-permute-start | bytes 2752520 | tf_op jit(solution)/shard_map/ppermute | solution.py:402
  52.4 1.6 %collective-permute-start.11 = (bf16[384,1024]{1,0:T(8,128)(2,1)S(1)}, bf16[384,1024]{1,0:T(8,128)(2,1)S(1)}, u32[]{:S(2)}, u32[]{:S(2)}) collective-permute-start(bf16[384,1024]{1,0:T(8,128)(2,1)S(1)} %slice.22), channel_id=1, source_target_pairs={{0,8},{4,12},{8,0},{12,4},{16,24},{20,28},{24,16},{28,20},{1,9},{5... | collective-permute-start | bytes 2359304 | tf_op jit(solution)/shard_map/ppermute | solution.py:402
  55.5 2.3 %collective-permute-start.9 = (bf16[256,1024]{1,0:T(8,128)(2,1)S(1)}, bf16[256,1024]{1,0:T(8,128)(2,1)S(1)}, u32[]{:S(2)}, u32[]{:S(2)}) collective-permute-start(bf16[256,1024]{1,0:T(8,128)(2,1)S(1)} %add_convert_fusion.refs_0_), channel_id=1, source_target_pairs={{0,1},{1,0},{2,3},{3,2},{4,5},{5,4},{6,7},{7,6},{8,9},{9,8},{10,11... | collective-permute-start | bytes 1572872 | tf_op jit(solution)/shard_map/ppermute | solution.py:402
  57.8 14.2 %collective-permute-done.12.refs_10_ = bf16[448,1024]{1,0:T(8,128)(2,1)S(1)} collective-permute-done((bf16[448,1024]{1,0:T(8,128)(2,1)S(1)}, bf16[448,1024]{1,0:T(8,128)(2,1)S(1)}, u32[]{:S(2)}, u32[]{:S(2)}) %collective-permute-start.12) | collective-permute-done | bytes 917536 | tf_op jit(solution)/shard_map/ppermute | solution.py:402
  72.6 6.9 %collective-permute-done.4.refs_2_ = bf16[256,1024]{1,0:T(8,128)(2,1)S(1)} collective-permute-done((bf16[256,1024]{1,0:T(8,128)(2,1)S(1)}, bf16[256,1024]{1,0:T(8,128)(2,1)S(1)}, u32[]{:S(2)}, u32[]{:S(2)}) %collective-permute-start.4) | collective-permute-done | bytes 524320 | tf_op jit(solution)/shard_map/ppermute | solution.py:402
  80.1 7.9 %early_products_and_lookup.1 = (f32[256,1024]{1,0:T(8,128)S(1)}, f32[256,1]{1,0:T(8,128)S(1)}, bf16[1,1024,1024]{2,1,0:T(8,128)(2,1)}, bf16[256,1024]{1,0:T(8,128)(2,1)S(1)}, bf16[1024,1536]{1,0:T(8,128)(2,1)}) custom-call(s32[1,256]{1,0:T(1,128)S(1)} %bitcast.7, bf16[1,4096]{1,0:T(2,128)(2,1)S(1)} %broadcast_in_dim.3.gain_ref, ...), custom_call_target="tpu_custom_call" | custom-call | tf_op jit(solution)/shard_map/early_products_and_lookup/pallas_call | solution.py:262
  88.0 4.4 %collective-permute-done.10.refs_0_ = bf16[256,1024]{1,0:T(8,128)(2,1)S(1)} collective-permute-done((bf16[256,1024]{1,0:T(8,128)(2,1)S(1)}, bf16[256,1024]{1,0:T(8,128)(2,1)S(1)}, u32[]{:S(2)}, u32[]{:S(2)}) %collective-permute-start.10) | collective-permute-done | bytes 524320 | tf_op jit(solution)/shard_map/ppermute | solution.py:402
  92.4 3.6 %late_products_and_qkv.1 = (bf16[64,1536]{1,0:T(8,128)(2,1)S(1)}, bf16[64,1536]{1,0:T(8,128)(2,1)S(1)}, bf16[64,1536]{1,0:T(8,128)(2,1)S(1)}, bf16[64,1536]{1,0:T(8,128)(2,1)S(1)}) custom-call(bf16[1,4096]{1,0:T(2,128)(2,1)S(1)} %broadcast_in_dim.3.gain_ref, bf16[256,1024]{1,0:T(8,128)(2,1)S(1)} %collective-permute-done.10.refs_0_, ...), custom_call_target="tpu_custom_call" | custom-call | tf_op jit(solution)/shard_map/late_products_and_qkv/pallas_call | solution.py:323
  96.5 3.4 %collective-permute-start.16 = (bf16[64,1536]{1,0:T(8,128)(2,1)S(1)}, bf16[64,1536]{1,0:T(8,128)(2,1)S(1)}, u32[]{:S(2)}, u32[]{:S(2)}) collective-permute-start(bf16[64,1536]{1,0:T(8,128)(2,1)S(1)} %get-tuple-element.47), channel_id=1, source_target_pairs={{0,2},{1,3},{2,0},{3,1},{4,6},{5,7},{6,4},{7,5},{8,10},{9,11},{10,... | collective-permute-start | bytes 589832 | tf_op jit(solution)/shard_map/ppermute | solution.py:402
  100.5 3.2 %collective-permute-done.15.refs_1_ = bf16[64,1536]{1,0:T(8,128)(2,1)S(1)} collective-permute-done((bf16[64,1536]{1,0:T(8,128)(2,1)S(1)}, bf16[64,1536]{1,0:T(8,128)(2,1)S(1)}, u32[]{:S(2)}, u32[]{:S(2)}) %collective-permute-start.15) | collective-permute-done | bytes 196640 | tf_op jit(solution)/shard_map/ppermute | solution.py:402
  103.6 10.0 %collective-permute-done.16.refs_2_ = bf16[64,1536]{1,0:T(8,128)(2,1)S(1)} collective-permute-done((bf16[64,1536]{1,0:T(8,128)(2,1)S(1)}, bf16[64,1536]{1,0:T(8,128)(2,1)S(1)}, u32[]{:S(2)}, u32[]{:S(2)}) %collective-permute-start.16) | collective-permute-done | bytes 196640 | tf_op jit(solution)/shard_map/ppermute | solution.py:402
  113.7 2.3 %attend_books.1 = bf16[64,4,512]{2,1,0:T(4,128)(2,1)} custom-call(bf16[64,1536]{1,0:T(8,128)(2,1)S(1)} %get-tuple-element.45.refs_0_, bf16[64,1536]{1,0:T(8,128)(2,1)S(1)} %collective-permute-done.15.refs_1_, bf16[64,1536]{1,0:T(8,128)(2,1)S(1)} %collective-permute-done.16.refs_2_, bf16[64,1536]{1,0:T(8,128)(2,1)S(1)} %collective-permute-done.17.refs_3_), custom_call_target="tpu_custom_call" | custom-call | tf_op jit(solution)/shard_map/attend_books/pallas_call | solution.py:390
  (48 shorter events, 12.2 us)
Async XLA Ops:
  4.0 21.7 %collective-permute-start.1 = (bf16[832,1024]{1,0:T(8,128)(2,1)S(1)}, bf16[832,1024]{1,0:T(8,128)(2,1)}, u32[]{:S(2)}, u32[]{:S(2)}) collective-permute-start(bf16[832,1024]{1,0:T(8,128)(2,1)S(1)} %pack_weight_rows.1.refs_3_), channel_id=1, source_target_pairs={{0,4},{4,0},{8,12},{12,8},{16,20},{20,16},{24,28},{28,24},{1,5},{5... | collective-permute-start | bytes 5111816 | tf_op jit(solution)/shard_map/ppermute | solution.py:402
  4.5 15.3 %collective-permute-start = (bf16[256,1024]{1,0:T(8,128)(2,1)S(1)}, bf16[256,1024]{1,0:T(8,128)(2,1)}, u32[]{:S(2)}, u32[]{:S(2)}) collective-permute-start(bf16[256,1024]{1,0:T(8,128)(2,1)S(1)} %get-tuple-element.28), channel_id=1, source_target_pairs={{0,1},{1,0},{2,3},{3,2},{4,5},{5,4},{6,7},{7,6},{8,9},{9,8},{10,11... | collective-permute-start | bytes 1572872 | tf_op jit(solution)/shard_map/ppermute | solution.py:402
  7.2 40.6 %collective-permute-start.6 = (bf16[832,1024]{1,0:T(8,128)(2,1)S(1)}, bf16[832,1024]{1,0:T(8,128)(2,1)}, u32[]{:S(2)}, u32[]{:S(2)}) collective-permute-start(bf16[832,1024]{1,0:T(8,128)(2,1)S(1)} %pack_weight_rows.1.refs_3_), channel_id=1, source_target_pairs={{0,16},{4,20},{8,24},{12,28},{16,0},{20,4},{24,8},{28,12},{1,17},{... | collective-permute-start | bytes 5111816 | tf_op jit(solution)/shard_map/ppermute | solution.py:402
  8.7 39.1 %collective-permute-start.5 = (bf16[832,1024]{1,0:T(8,128)(2,1)S(1)}, bf16[832,1024]{1,0:T(8,128)(2,1)}, u32[]{:S(2)}, u32[]{:S(2)}) collective-permute-start(bf16[832,1024]{1,0:T(8,128)(2,1)S(1)} %pack_weight_rows.1.refs_3_), channel_id=1, source_target_pairs={{0,8},{4,12},{8,0},{12,4},{16,24},{20,28},{24,16},{28,20},{1,9},{5... | collective-permute-start | bytes 5111816 | tf_op jit(solution)/shard_map/ppermute | solution.py:402
  17.6 62.4 %copy-start.9 = (bf16[4096]{0:T(1024)(128)(2,1)S(1)}, bf16[4096]{0:T(1024)(128)(2,1)}, u32[]{:S(2)}) copy-start(bf16[4096]{0:T(1024)(128)(2,1)} %param.14) | copy-start | bytes 24580
  17.6 62.5 %copy-start.5 = (s32[256,1]{0,1:T(1,128)S(1)}, s32[256,1]{0,1:T(1,128)}, u32[]{:S(2)}) copy-start(s32[256,1]{0,1:T(1,128)} %param.17) | copy-start | bytes 3076
  17.6 29.9 %copy-start.8 = (bf16[256,1024]{1,0:T(8,128)(2,1)S(1)}, bf16[256,1024]{1,0:T(8,128)(2,1)}, u32[]{:S(2)}) copy-start(bf16[256,1024]{1,0:T(8,128)(2,1)} %param.13) | copy-start | bytes 1572868
  21.3 26.2 %collective-permute-start.3 = (bf16[256,1024]{1,0:T(8,128)(2,1)S(1)}, bf16[256,1024]{1,0:T(8,128)(2,1)S(1)}, u32[]{:S(2)}, u32[]{:S(2)}) collective-permute-start(bf16[256,1024]{1,0:T(8,128)(2,1)S(1)} %add_convert_fusion.1), channel_id=1, source_target_pairs={{0,2},{1,3},{2,0},{3,1},{4,6},{5,7},{6,4},{7,5},{8,10},{9,11},{10,... | collective-permute-start | bytes 1572872 | tf_op jit(solution)/shard_map/ppermute | solution.py:402
  24.1 23.3 %collective-permute-start.2 = (bf16[256,1024]{1,0:T(8,128)(2,1)S(1)}, bf16[256,1024]{1,0:T(8,128)(2,1)S(1)}, u32[]{:S(2)}, u32[]{:S(2)}) collective-permute-start(bf16[256,1024]{1,0:T(8,128)(2,1)S(1)} %share_products.2), channel_id=1, source_target_pairs={{0,1},{1,0},{2,3},{3,2},{4,5},{5,4},{6,7},{7,6},{8,9},{9,8},{10,11... | collective-permute-start | bytes 1572872 | tf_op jit(solution)/shard_map/ppermute | solution.py:402
  30.5 61.9 %copy-start.4 = (bf16[1,1024]{1,0:T(2,128)(2,1)S(1)}, bf16[1,1024]{1,0:T(2,128)(2,1)}, u32[]{:S(2)}) copy-start(bf16[1,1024]{1,0:T(2,128)(2,1)} %refs_5_.1) | copy-start | bytes 6148
  47.8 7.6 %collective-permute-start.7 = (bf16[832,1024]{1,0:T(8,128)(2,1)}, bf16[832,1024]{1,0:T(8,128)(2,1)S(1)}, u32[]{:S(2)}, u32[]{:S(2)}) collective-permute-start(bf16[832,1024]{1,0:T(8,128)(2,1)} %collective-permute-done.5.refs_5_), channel_id=1, source_target_pairs={{0,4},{4,0},{8,12},{12,8},{16,20},{20,16},{24,28},{28,24},{1,5},{5... | collective-permute-start | bytes 5111816 | tf_op jit(solution)/shard_map/ppermute | solution.py:402
  47.9 7.5 %collective-permute-start.8 = (bf16[832,1024]{1,0:T(8,128)(2,1)}, bf16[832,1024]{1,0:T(8,128)(2,1)S(1)}, u32[]{:S(2)}, u32[]{:S(2)}) collective-permute-start(bf16[832,1024]{1,0:T(8,128)(2,1)} %collective-permute-done.6.refs_7_), channel_id=1, source_target_pairs={{0,4},{4,0},{8,12},{12,8},{16,20},{20,16},{24,28},{28,24},{1,5},{5... | collective-permute-start | bytes 5111816 | tf_op jit(solution)/shard_map/ppermute | solution.py:402
  49.6 22.4 %collective-permute-start.12 = (bf16[448,1024]{1,0:T(8,128)(2,1)S(1)}, bf16[448,1024]{1,0:T(8,128)(2,1)S(1)}, u32[]{:S(2)}, u32[]{:S(2)}) collective-permute-start(bf16[448,1024]{1,0:T(8,128)(2,1)S(1)} %slice.23), channel_id=1, source_target_pairs={{0,16},{4,20},{8,24},{12,28},{16,0},{20,4},{24,8},{28,12},{1,17},{... | collective-permute-start | bytes 2752520 | tf_op jit(solution)/shard_map/ppermute | solution.py:402
  52.4 19.6 %collective-permute-start.11 = (bf16[384,1024]{1,0:T(8,128)(2,1)S(1)}, bf16[384,1024]{1,0:T(8,128)(2,1)S(1)}, u32[]{:S(2)}, u32[]{:S(2)}) collective-permute-start(bf16[384,1024]{1,0:T(8,128)(2,1)S(1)} %slice.22), channel_id=1, source_target_pairs={{0,8},{4,12},{8,0},{12,4},{16,24},{20,28},{24,16},{28,20},{1,9},{5... | collective-permute-start | bytes 2359304 | tf_op jit(solution)/shard_map/ppermute | solution.py:402
  54.0 25.5 %collective-permute-start.4 = (bf16[256,1024]{1,0:T(8,128)(2,1)S(1)}, bf16[256,1024]{1,0:T(8,128)(2,1)S(1)}, u32[]{:S(2)}, u32[]{:S(2)}) collective-permute-start(bf16[256,1024]{1,0:T(8,128)(2,1)S(1)} %add_convert_fusion.refs_0_), channel_id=1, source_target_pairs={{0,2},{1,3},{2,0},{3,1},{4,6},{5,7},{6,4},{7,5},{8,10},{9,11},{10,... | collective-permute-start | bytes 1572872 | tf_op jit(solution)/shard_map/ppermute | solution.py:402
  55.5 24.6 %copy-start.6 = (bf16[832,1024]{1,0:T(8,128)(2,1)}, bf16[832,1024]{1,0:T(8,128)(2,1)S(1)}, u32[]{:S(2)}) copy-start(bf16[832,1024]{1,0:T(8,128)(2,1)S(1)} %collective-permute-done.7.refs_6_) | copy-start | bytes 5111812
  55.5 24.6 %copy-start.7 = (bf16[832,1024]{1,0:T(8,128)(2,1)}, bf16[832,1024]{1,0:T(8,128)(2,1)S(1)}, u32[]{:S(2)}) copy-start(bf16[832,1024]{1,0:T(8,128)(2,1)S(1)} %collective-permute-done.8.refs_8_) | copy-start | bytes 5111812
  55.5 24.0 %collective-permute-start.9 = (bf16[256,1024]{1,0:T(8,128)(2,1)S(1)}, bf16[256,1024]{1,0:T(8,128)(2,1)S(1)}, u32[]{:S(2)}, u32[]{:S(2)}) collective-permute-start(bf16[256,1024]{1,0:T(8,128)(2,1)S(1)} %add_convert_fusion.refs_0_), channel_id=1, source_target_pairs={{0,1},{1,0},{2,3},{3,2},{4,5},{5,4},{6,7},{7,6},{8,9},{9,8},{10,11... | collective-permute-start | bytes 1572872 | tf_op jit(solution)/shard_map/ppermute | solution.py:402
  72.0 8.0 %collective-permute-start.14 = (bf16[448,1024]{1,0:T(8,128)(2,1)S(1)}, bf16[448,1024]{1,0:T(8,128)(2,1)S(1)}, u32[]{:S(2)}, u32[]{:S(2)}) collective-permute-start(bf16[448,1024]{1,0:T(8,128)(2,1)S(1)} %collective-permute-done.12.refs_10_), channel_id=1, source_target_pairs={{0,4},{4,0},{8,12},{12,8},{16,20},{20,16},{24,28},{28,24},{1,5},{5... | collective-permute-start | bytes 2752520 | tf_op jit(solution)/shard_map/ppermute | solution.py:402
  72.1 8.0 %collective-permute-start.13 = (bf16[384,1024]{1,0:T(8,128)(2,1)S(1)}, bf16[384,1024]{1,0:T(8,128)(2,1)S(1)}, u32[]{:S(2)}, u32[]{:S(2)}) collective-permute-start(bf16[384,1024]{1,0:T(8,128)(2,1)S(1)} %collective-permute-done.11.refs_9_), channel_id=1, source_target_pairs={{0,4},{4,0},{8,12},{12,8},{16,20},{20,16},{24,28},{28,24},{1,5},{5... | collective-permute-start | bytes 2359304 | tf_op jit(solution)/shard_map/ppermute | solution.py:402
  79.5 12.9 %collective-permute-start.10 = (bf16[256,1024]{1,0:T(8,128)(2,1)S(1)}, bf16[256,1024]{1,0:T(8,128)(2,1)S(1)}, u32[]{:S(2)}, u32[]{:S(2)}) collective-permute-start(bf16[256,1024]{1,0:T(8,128)(2,1)S(1)} %collective-permute-done.4.refs_2_), channel_id=1, source_target_pairs={{0,1},{1,0},{2,3},{3,2},{4,5},{5,4},{6,7},{7,6},{8,9},{9,8},{10,11... | collective-permute-start | bytes 1572872 | tf_op jit(solution)/shard_map/ppermute | solution.py:402
  96.0 7.6 %collective-permute-start.15 = (bf16[64,1536]{1,0:T(8,128)(2,1)S(1)}, bf16[64,1536]{1,0:T(8,128)(2,1)S(1)}, u32[]{:S(2)}, u32[]{:S(2)}) collective-permute-start(bf16[64,1536]{1,0:T(8,128)(2,1)S(1)} %get-tuple-element.46), channel_id=1, source_target_pairs={{0,1},{1,0},{2,3},{3,2},{4,5},{5,4},{6,7},{7,6},{8,9},{9,8},{10,11... | collective-permute-start | bytes 589832 | tf_op jit(solution)/shard_map/ppermute | solution.py:402
  96.5 17.1 %collective-permute-start.16 = (bf16[64,1536]{1,0:T(8,128)(2,1)S(1)}, bf16[64,1536]{1,0:T(8,128)(2,1)S(1)}, u32[]{:S(2)}, u32[]{:S(2)}) collective-permute-start(bf16[64,1536]{1,0:T(8,128)(2,1)S(1)} %get-tuple-element.47), channel_id=1, source_target_pairs={{0,2},{1,3},{2,0},{3,1},{4,6},{5,7},{6,4},{7,5},{8,10},{9,11},{10,... | collective-permute-start | bytes 589832 | tf_op jit(solution)/shard_map/ppermute | solution.py:402
  99.9 13.7 %collective-permute-start.17 = (bf16[64,1536]{1,0:T(8,128)(2,1)S(1)}, bf16[64,1536]{1,0:T(8,128)(2,1)S(1)}, u32[]{:S(2)}, u32[]{:S(2)}) collective-permute-start(bf16[64,1536]{1,0:T(8,128)(2,1)S(1)} %get-tuple-element.48), channel_id=1, source_target_pairs={{0,3},{1,2},{2,1},{3,0},{4,7},{5,6},{6,5},{7,4},{8,11},{9,10},{10,... | collective-permute-start | bytes 589832 | tf_op jit(solution)/shard_map/ppermute | solution.py:402
  (4 other events, 21.5 us)

commit v16 on v14

--- a/solution.py
+++ b/solution.py
@@ -388,22 +388,25 @@
     same_head = (head_of_row == head_of_column).astype(f32).astype(bf16)
     keys_all = [inner[j, :, width : 2 * width].astype(f32) for j in range(books)]
     values_all = [inner[j, :, 2 * width :].astype(f32) for j in range(books)]
+    pairs = [(k, j) for k in range(books) for j in range(k + 1)]
+    queries = [inner[k, :, :width].astype(f32) * HD ** (-0.5) for k in range(books)]
+    products = jnp.concatenate([queries[k] * keys_all[j] for k, j in pairs], axis=0)
+    high = products.astype(bf16)
+    low = (products - high.astype(f32)).astype(bf16)
+    both = jnp.dot(
+        jnp.concatenate([high, low], axis=0), same_head, preferred_element_type=f32
+    )
+    every = both[: len(pairs) * rows] + both[len(pairs) * rows :]
     contexts = []
     for k in range(books):
-        query = inner[k, :, :width].astype(f32) * HD ** (-0.5)
-        products = jnp.concatenate([query * keys_all[j] for j in range(k + 1)], axis=0)
-        high = products.astype(bf16)
-        low = (products - high.astype(f32)).astype(bf16)
-        scores = jnp.dot(high, same_head, preferred_element_type=f32) + jnp.dot(
-            low, same_head, preferred_element_type=f32
-        )
-        scores = [scores[j * rows : (j + 1) * rows] for j in range(k + 1)]
+        first = pairs.index((k, 0))
+        scores = [every[(first + j) * rows : (first + j + 1) * rows] for j in range(k + 1)]
         peak = functools.reduce(jnp.maximum, scores)
         expo = [jnp.exp(score - peak) for score in scores]
-        total = functools.reduce(jnp.add, expo)
+        share = 1.0 / functools.reduce(jnp.add, expo)
         context = 0.0
         for j in range(k + 1):
-            probability = (expo[j] / total).astype(bf16).astype(f32)
+            probability = (expo[j] * share).astype(bf16).astype(f32)
             context = context + probability * values_all[j]
         contexts.append(context)
     out_ref[...] = jnp.stack(contexts, axis=1).astype(bf16)

time: 116 us -> 116 us (level)
  no operation moved by 1% of the time
where the time goes in v16:
time: 116 us
  waiting for transfers between devices  56.5 us (49%)
  Pallas kernels  27.7 us (24%)
  starting transfers between devices  23.5 us (20%)
  matrix products  6.29 us (5%)
  other arithmetic  1.83 us (2%)
    ppermute x18, waiting for transfers between devices, swap(): lax.ppermute(value, axis, [(i, i ^ distance) for i in range(lax.axis_size...  56.5 us
    ppermute x18, starting transfers between devices, swap(): lax.ppermute(value, axis, [(i, i ^ distance) for i in range(lax.axis_size...  23.5 us
    pallas_call x1, Pallas kernels, project_early(): pl.pallas_call(functools.partial(early_kernel, books, early, pieces, size...  7.91 us
    pallas_call x2, Pallas kernels, share_products(): pl.pallas_call(functools.partial(share_kernel, partner), out_shape=jax.Sh...  7.34 us
    dot_general x4, matrix products, share(): total = total + jnp.dot(part, block, preferred_element_type=f32)  6.29 us
    pallas_call x1, Pallas kernels, first_products(): pl.pallas_call(first_kernel, out_shape=[jax.ShapeDtypeStruct((frames_here...  3.74 us
    pallas_call x1, Pallas kernels, project_late(): pl.pallas_call(functools.partial(late_kernel, books, late), out_shape=[ja...  3.61 us
    pallas_call x1, Pallas kernels, cut_rows(): pl.pallas_call(functools.partial(cut_kernel, cut), out_shape=[jax.ShapeDt...  2.63 us
  transfers between devices with their start and end apart: 18, of which 7 were waited for; matrix products, arithmetic and copies ran while one was open for 7% of the time, Pallas kernels for 15%

profile of v16, /device:TPU:0, one launch (start us, length us, event | category | flops | bytes accessed | tf_op | source)
XLA Modules:
  0.0 116.1 jit_solution(17858722986768417307)
XLA Ops:
  0.0 3.7 %hidden_and_first_products.1 = (bf16[256,1536]{1,0:T(8,128)(2,1)}, bf16[256,1024]{1,0:T(8,128)(2,1)S(1)}) custom-call(bf16[256,1536]{1,0:T(8,128)(2,1)} %gate_ref.1, bf16[256,1536]{1,0:T(8,128)(2,1)} %up_ref.1, bf16[1536,4096]{1,0:T(8,128)(2,1)} %down_ref.5), custom_call_target="tpu_custom_call" | custom-call | tf_op jit(solution)/shard_map/hidden_and_first_products/pallas_call | solution.py:47
  4.5 2.7 %collective-permute-start = (bf16[256,1024]{1,0:T(8,128)(2,1)S(1)}, bf16[256,1024]{1,0:T(8,128)(2,1)}, u32[]{:S(2)}, u32[]{:S(2)}) collective-permute-start(bf16[256,1024]{1,0:T(8,128)(2,1)S(1)} %get-tuple-element.30), channel_id=1, source_target_pairs={{0,1},{1,0},{2,3},{3,2},{4,5},{5,4},{6,7},{7,6},{8,9},{9,8},{10,11... | collective-permute-start | bytes 1572872 | tf_op jit(solution)/shard_map/ppermute | solution.py:431
  10.2 3.7 %share_products.2 = bf16[256,1024]{1,0:T(8,128)(2,1)S(1)} custom-call(bf16[256,1536]{1,0:T(8,128)(2,1)} %get-tuple-element.36.hidden_ref, bf16[1536,4096]{1,0:T(8,128)(2,1)} %down_ref.5), custom_call_target="tpu_custom_call" | custom-call | tf_op jit(solution)/shard_map/share_products/pallas_call | solution.py:91
  13.9 3.6 %share_products.3 = f32[256,1024]{1,0:T(8,128)} custom-call(bf16[256,1536]{1,0:T(8,128)(2,1)S(1)} %copy-done, bf16[1536,4096]{1,0:T(8,128)(2,1)} %down_ref.5), custom_call_target="tpu_custom_call" | custom-call | tf_op jit(solution)/shard_map/share_products/pallas_call | solution.py:91
  17.6 2.2 %collective-permute-done = bf16[256,1024]{1,0:T(8,128)(2,1)} collective-permute-done((bf16[256,1024]{1,0:T(8,128)(2,1)S(1)}, bf16[256,1024]{1,0:T(8,128)(2,1)}, u32[]{:S(2)}, u32[]{:S(2)}) %collective-permute-start) | collective-permute-done | bytes 524320 | tf_op jit(solution)/shard_map/ppermute | solution.py:431
  21.3 2.8 %collective-permute-start.3 = (bf16[256,1024]{1,0:T(8,128)(2,1)S(1)}, bf16[256,1024]{1,0:T(8,128)(2,1)S(1)}, u32[]{:S(2)}, u32[]{:S(2)}) collective-permute-start(bf16[256,1024]{1,0:T(8,128)(2,1)S(1)} %add_convert_fusion.1), channel_id=1, source_target_pairs={{0,2},{1,3},{2,0},{3,1},{4,6},{5,7},{6,4},{7,5},{8,10},{9,11},{10,... | collective-permute-start | bytes 1572872 | tf_op jit(solution)/shard_map/ppermute | solution.py:431
  24.1 1.6 %collective-permute-start.2 = (bf16[256,1024]{1,0:T(8,128)(2,1)S(1)}, bf16[256,1024]{1,0:T(8,128)(2,1)S(1)}, u32[]{:S(2)}, u32[]{:S(2)}) collective-permute-start(bf16[256,1024]{1,0:T(8,128)(2,1)S(1)} %share_products.2), channel_id=1, source_target_pairs={{0,1},{1,0},{2,3},{3,2},{4,5},{5,4},{6,7},{7,6},{8,9},{9,8},{10,11... | collective-permute-start | bytes 1572872 | tf_op jit(solution)/shard_map/ppermute | solution.py:431
  25.7 1.6 %fusion.3 = f32[256,1024]{1,0:T(8,128)S(1)} fusion(bf16[1536,4096]{1,0:T(8,128)(2,1)} %down_ref.5, s32[]{:T(128)S(6)} %select_n.2, bf16[256,1536]{1,0:T(8,128)(2,1)S(1)} %copy-done), kind=kOutput, calls=%fused_computation.8 | convolution fusion | flops 201326592 | bytes 2031620 | tf_op jit(solution)/shard_map/dot_general | solution.py:473
  27.3 1.6 %convolution_add_fusion.2 = f32[256,1024]{1,0:T(8,128)S(1)} fusion(f32[256,1024]{1,0:T(8,128)S(1)} %fusion.3, bf16[1536,4096]{1,0:T(8,128)(2,1)} %down_ref.5, s32[]{:T(128)S(6)} %select_n.2, bf16[256,1536]{1,0:T(8,128)(2,1)S(1)} %copy-done), kind=kOutput, calls=%fused_computation.2 | convolution fusion | flops 201588736 | bytes 3080196 | tf_op jit(solution)/shard_map/dot_general | solution.py:473
  28.9 1.6 %convolution_add_fusion.1 = f32[256,1024]{1,0:T(8,128)S(1)} fusion(f32[256,1024]{1,0:T(8,128)S(1)} %convolution_add_fusion.2, bf16[1536,4096]{1,0:T(8,128)(2,1)} %down_ref.5, s32[]{:T(128)S(6)} %select_n.2, bf16[256,1536]{1,0:T(8,128)(2,1)S(1)} %copy-done), kind=kOutput, calls=%fused_computation.1 | convolution fusion | flops 201588736 | bytes 3080196 | tf_op jit(solution)/shard_map/dot_general | solution.py:473
  30.4 1.6 %convolution_add_fusion = f32[256,1024]{1,0:T(8,128)S(1)} fusion(f32[256,1024]{1,0:T(8,128)S(1)} %convolution_add_fusion.1, bf16[1536,4096]{1,0:T(8,128)(2,1)} %down_ref.5, s32[]{:T(128)S(6)} %select_n.2, bf16[256,1536]{1,0:T(8,128)(2,1)S(1)} %copy-done), kind=kOutput, calls=%fused_computation | convolution fusion | flops 201588736 | bytes 3080196 | tf_op jit(solution)/shard_map/dot_general | solution.py:473
  32.0 15.4 %collective-permute-done.2 = bf16[256,1024]{1,0:T(8,128)(2,1)S(1)} collective-permute-done((bf16[256,1024]{1,0:T(8,128)(2,1)S(1)}, bf16[256,1024]{1,0:T(8,128)(2,1)S(1)}, u32[]{:S(2)}, u32[]{:S(2)}) %collective-permute-start.2) | collective-permute-done | bytes 524320 | tf_op jit(solution)/shard_map/ppermute | solution.py:431
  48.4 2.6 %cut_rows.1 = (bf16[384,1024]{1,0:T(8,128)(2,1)}, bf16[448,1024]{1,0:T(8,128)(2,1)}) custom-call(bf16[832,1024]{1,0:T(8,128)(2,1)} %collective-permute-done.6.upper_from.refs_7_, bf16[832,1024]{1,0:T(8,128)(2,1)} %collective-permute-done.5.lower_from.refs_5_), custom_call_target="tpu_custom_call" | custom-call | tf_op jit(solution)/shard_map/cut_rows/pallas_call | solution.py:161
  51.0 1.6 %collective-permute-start.12 = (bf16[448,1024]{1,0:T(8,128)(2,1)}, bf16[448,1024]{1,0:T(8,128)(2,1)S(1)}, u32[]{:S(2)}, u32[]{:S(2)}) collective-permute-start(bf16[448,1024]{1,0:T(8,128)(2,1)} %get-tuple-element.43), channel_id=1, source_target_pairs={{0,16},{4,20},{8,24},{12,28},{16,0},{20,4},{24,8},{28,12},{1,17},{... | collective-permute-start | bytes 2752520 | tf_op jit(solution)/shard_map/ppermute | solution.py:431
  55.6 2.3 %collective-permute-start.9 = (bf16[256,1024]{1,0:T(8,128)(2,1)S(1)}, bf16[256,1024]{1,0:T(8,128)(2,1)S(1)}, u32[]{:S(2)}, u32[]{:S(2)}) collective-permute-start(bf16[256,1024]{1,0:T(8,128)(2,1)S(1)} %add_convert_fusion.refs_0_), channel_id=1, source_target_pairs={{0,1},{1,0},{2,3},{3,2},{4,5},{5,4},{6,7},{7,6},{8,9},{9,8},{10,11... | collective-permute-start | bytes 1572872 | tf_op jit(solution)/shard_map/ppermute | solution.py:431
  57.9 15.8 %collective-permute-done.12.refs_10_ = bf16[448,1024]{1,0:T(8,128)(2,1)S(1)} collective-permute-done((bf16[448,1024]{1,0:T(8,128)(2,1)}, bf16[448,1024]{1,0:T(8,128)(2,1)S(1)}, u32[]{:S(2)}, u32[]{:S(2)}) %collective-permute-start.12) | collective-permute-done | bytes 917536 | tf_op jit(solution)/shard_map/ppermute | solution.py:431
  74.2 5.4 %collective-permute-done.4.refs_2_ = bf16[256,1024]{1,0:T(8,128)(2,1)S(1)} collective-permute-done((bf16[256,1024]{1,0:T(8,128)(2,1)S(1)}, bf16[256,1024]{1,0:T(8,128)(2,1)S(1)}, u32[]{:S(2)}, u32[]{:S(2)}) %collective-permute-start.4) | collective-permute-done | bytes 524320 | tf_op jit(solution)/shard_map/ppermute | solution.py:431
  80.2 7.9 %early_products_and_lookup.1 = (f32[256,1024]{1,0:T(8,128)S(1)}, f32[256,1]{1,0:T(8,128)S(1)}, bf16[1,1024,1024]{2,1,0:T(8,128)(2,1)}, bf16[256,1024]{1,0:T(8,128)(2,1)S(1)}, bf16[1024,1536]{1,0:T(8,128)(2,1)}) custom-call(s32[1,256]{1,0:T(1,128)S(1)} %bitcast.7, bf16[1,4096]{1,0:T(2,128)(2,1)S(1)} %broadcast_in_dim.3.gain_ref, ...), custom_call_target="tpu_custom_call" | custom-call | tf_op jit(solution)/shard_map/early_products_and_lookup/pallas_call | solution.py:288
  88.1 4.4 %collective-permute-done.10.refs_0_ = bf16[256,1024]{1,0:T(8,128)(2,1)S(1)} collective-permute-done((bf16[256,1024]{1,0:T(8,128)(2,1)S(1)}, bf16[256,1024]{1,0:T(8,128)(2,1)S(1)}, u32[]{:S(2)}, u32[]{:S(2)}) %collective-permute-start.10) | collective-permute-done | bytes 524320 | tf_op jit(solution)/shard_map/ppermute | solution.py:431
  92.5 3.6 %late_products_and_qkv.1 = (bf16[64,1536]{1,0:T(8,128)(2,1)S(1)}, bf16[64,1536]{1,0:T(8,128)(2,1)S(1)}, bf16[64,1536]{1,0:T(8,128)(2,1)S(1)}, bf16[64,1536]{1,0:T(8,128)(2,1)S(1)}) custom-call(bf16[1,4096]{1,0:T(2,128)(2,1)S(1)} %broadcast_in_dim.3.gain_ref, bf16[256,1024]{1,0:T(8,128)(2,1)S(1)} %collective-permute-done.10.refs_0_, ...), custom_call_target="tpu_custom_call" | custom-call | tf_op jit(solution)/shard_map/late_products_and_qkv/pallas_call | solution.py:349
  96.7 3.4 %collective-permute-start.16 = (bf16[64,1536]{1,0:T(8,128)(2,1)S(1)}, bf16[64,1536]{1,0:T(8,128)(2,1)S(1)}, u32[]{:S(2)}, u32[]{:S(2)}) collective-permute-start(bf16[64,1536]{1,0:T(8,128)(2,1)S(1)} %get-tuple-element.51), channel_id=1, source_target_pairs={{0,2},{1,3},{2,0},{3,1},{4,6},{5,7},{6,4},{7,5},{8,10},{9,11},{10,... | collective-permute-start | bytes 589832 | tf_op jit(solution)/shard_map/ppermute | solution.py:431
  100.6 3.2 %collective-permute-done.15.refs_1_ = bf16[64,1536]{1,0:T(8,128)(2,1)S(1)} collective-permute-done((bf16[64,1536]{1,0:T(8,128)(2,1)S(1)}, bf16[64,1536]{1,0:T(8,128)(2,1)S(1)}, u32[]{:S(2)}, u32[]{:S(2)}) %collective-permute-start.15) | collective-permute-done | bytes 196640 | tf_op jit(solution)/shard_map/ppermute | solution.py:431
  103.8 10.0 %collective-permute-done.16.refs_2_ = bf16[64,1536]{1,0:T(8,128)(2,1)S(1)} collective-permute-done((bf16[64,1536]{1,0:T(8,128)(2,1)S(1)}, bf16[64,1536]{1,0:T(8,128)(2,1)S(1)}, u32[]{:S(2)}, u32[]{:S(2)}) %collective-permute-start.16) | collective-permute-done | bytes 196640 | tf_op jit(solution)/shard_map/ppermute | solution.py:431
  113.8 2.3 %attend_books.1 = bf16[64,4,512]{2,1,0:T(4,128)(2,1)} custom-call(bf16[64,1536]{1,0:T(8,128)(2,1)S(1)} %get-tuple-element.49.refs_0_, bf16[64,1536]{1,0:T(8,128)(2,1)S(1)} %collective-permute-done.15.refs_1_, bf16[64,1536]{1,0:T(8,128)(2,1)S(1)} %collective-permute-done.16.refs_2_, bf16[64,1536]{1,0:T(8,128)(2,1)S(1)} %collective-permute-done.17.refs_3_), custom_call_target="tpu_custom_call" | custom-call | tf_op jit(solution)/shard_map/attend_books/pallas_call | solution.py:419
  (43 shorter events, 11.3 us)
Async XLA Ops:
  0.0 3.8 %copy-start.1 = (bf16[1,512,1024]{2,1,0:T(8,128)(2,1)S(1)}, bf16[1,512,1024]{2,1,0:T(8,128)(2,1)}, u32[]{:S(2)}) copy-start(bf16[1,512,1024]{2,1,0:T(8,128)(2,1)} %param.15) | copy-start | bytes 3145732
  3.8 10.2 %copy-start = (bf16[256,1536]{1,0:T(8,128)(2,1)S(1)}, bf16[256,1536]{1,0:T(8,128)(2,1)}, u32[]{:S(2)}) copy-start(bf16[256,1536]{1,0:T(8,128)(2,1)} %get-tuple-element.36.hidden_ref) | copy-start | bytes 2359300
  4.0 21.7 %collective-permute-start.1 = (bf16[832,1024]{1,0:T(8,128)(2,1)S(1)}, bf16[832,1024]{1,0:T(8,128)(2,1)}, u32[]{:S(2)}, u32[]{:S(2)}) collective-permute-start(bf16[832,1024]{1,0:T(8,128)(2,1)S(1)} %pack_weight_rows.1.refs_3_), channel_id=1, source_target_pairs={{0,4},{4,0},{8,12},{12,8},{16,20},{20,16},{24,28},{28,24},{1,5},{5... | collective-permute-start | bytes 5111816 | tf_op jit(solution)/shard_map/ppermute | solution.py:431
  4.5 15.3 %collective-permute-start = (bf16[256,1024]{1,0:T(8,128)(2,1)S(1)}, bf16[256,1024]{1,0:T(8,128)(2,1)}, u32[]{:S(2)}, u32[]{:S(2)}) collective-permute-start(bf16[256,1024]{1,0:T(8,128)(2,1)S(1)} %get-tuple-element.30), channel_id=1, source_target_pairs={{0,1},{1,0},{2,3},{3,2},{4,5},{5,4},{6,7},{7,6},{8,9},{9,8},{10,11... | collective-permute-start | bytes 1572872 | tf_op jit(solution)/shard_map/ppermute | solution.py:431
  7.2 40.6 %collective-permute-start.6 = (bf16[832,1024]{1,0:T(8,128)(2,1)S(1)}, bf16[832,1024]{1,0:T(8,128)(2,1)}, u32[]{:S(2)}, u32[]{:S(2)}) collective-permute-start(bf16[832,1024]{1,0:T(8,128)(2,1)S(1)} %pack_weight_rows.1.refs_3_), channel_id=1, source_target_pairs={{0,16},{4,20},{8,24},{12,28},{16,0},{20,4},{24,8},{28,12},{1,17},{... | collective-permute-start | bytes 5111816 | tf_op jit(solution)/shard_map/ppermute | solution.py:431
  8.7 39.1 %collective-permute-start.5 = (bf16[832,1024]{1,0:T(8,128)(2,1)S(1)}, bf16[832,1024]{1,0:T(8,128)(2,1)}, u32[]{:S(2)}, u32[]{:S(2)}) collective-permute-start(bf16[832,1024]{1,0:T(8,128)(2,1)S(1)} %pack_weight_rows.1.refs_3_), channel_id=1, source_target_pairs={{0,8},{4,12},{8,0},{12,4},{16,24},{20,28},{24,16},{28,20},{1,9},{5... | collective-permute-start | bytes 5111816 | tf_op jit(solution)/shard_map/ppermute | solution.py:431
  17.5 62.6 %copy-start.7 = (bf16[4096]{0:T(1024)(128)(2,1)S(1)}, bf16[4096]{0:T(1024)(128)(2,1)}, u32[]{:S(2)}) copy-start(bf16[4096]{0:T(1024)(128)(2,1)} %param.14) | copy-start | bytes 24580
  17.5 62.6 %copy-start.5 = (s32[256,1]{0,1:T(1,128)S(1)}, s32[256,1]{0,1:T(1,128)}, u32[]{:S(2)}) copy-start(s32[256,1]{0,1:T(1,128)} %param.17) | copy-start | bytes 3076
  17.6 29.9 %copy-start.6 = (bf16[256,1024]{1,0:T(8,128)(2,1)S(1)}, bf16[256,1024]{1,0:T(8,128)(2,1)}, u32[]{:S(2)}) copy-start(bf16[256,1024]{1,0:T(8,128)(2,1)} %param.13) | copy-start | bytes 1572868
  21.3 26.2 %collective-permute-start.3 = (bf16[256,1024]{1,0:T(8,128)(2,1)S(1)}, bf16[256,1024]{1,0:T(8,128)(2,1)S(1)}, u32[]{:S(2)}, u32[]{:S(2)}) collective-permute-start(bf16[256,1024]{1,0:T(8,128)(2,1)S(1)} %add_convert_fusion.1), channel_id=1, source_target_pairs={{0,2},{1,3},{2,0},{3,1},{4,6},{5,7},{6,4},{7,5},{8,10},{9,11},{10,... | collective-permute-start | bytes 1572872 | tf_op jit(solution)/shard_map/ppermute | solution.py:431
  24.1 23.3 %collective-permute-start.2 = (bf16[256,1024]{1,0:T(8,128)(2,1)S(1)}, bf16[256,1024]{1,0:T(8,128)(2,1)S(1)}, u32[]{:S(2)}, u32[]{:S(2)}) collective-permute-start(bf16[256,1024]{1,0:T(8,128)(2,1)S(1)} %share_products.2), channel_id=1, source_target_pairs={{0,1},{1,0},{2,3},{3,2},{4,5},{5,4},{6,7},{7,6},{8,9},{9,8},{10,11... | collective-permute-start | bytes 1572872 | tf_op jit(solution)/shard_map/ppermute | solution.py:431
  30.4 62.1 %copy-start.4 = (bf16[1,1024]{1,0:T(2,128)(2,1)S(1)}, bf16[1,1024]{1,0:T(2,128)(2,1)}, u32[]{:S(2)}) copy-start(bf16[1,1024]{1,0:T(2,128)(2,1)} %refs_5_.1) | copy-start | bytes 6148
  47.8 7.8 %collective-permute-start.7 = (bf16[832,1024]{1,0:T(8,128)(2,1)}, bf16[832,1024]{1,0:T(8,128)(2,1)}, u32[]{:S(2)}, u32[]{:S(2)}) collective-permute-start(bf16[832,1024]{1,0:T(8,128)(2,1)} %collective-permute-done.5.lower_from.refs_5_), channel_id=1, source_target_pairs={{0,4},{4,0},{8,12},{12,8},{16,20},{20,16},{24,28},{28,24},{1,5},{5... | collective-permute-start | bytes 5111816 | tf_op jit(solution)/shard_map/ppermute | solution.py:431
  47.9 7.7 %collective-permute-start.8 = (bf16[832,1024]{1,0:T(8,128)(2,1)}, bf16[832,1024]{1,0:T(8,128)(2,1)}, u32[]{:S(2)}, u32[]{:S(2)}) collective-permute-start(bf16[832,1024]{1,0:T(8,128)(2,1)} %collective-permute-done.6.upper_from.refs_7_), channel_id=1, source_target_pairs={{0,4},{4,0},{8,12},{12,8},{16,20},{20,16},{24,28},{28,24},{1,5},{5... | collective-permute-start | bytes 5111816 | tf_op jit(solution)/shard_map/ppermute | solution.py:431
  51.0 22.6 %collective-permute-start.12 = (bf16[448,1024]{1,0:T(8,128)(2,1)}, bf16[448,1024]{1,0:T(8,128)(2,1)S(1)}, u32[]{:S(2)}, u32[]{:S(2)}) collective-permute-start(bf16[448,1024]{1,0:T(8,128)(2,1)} %get-tuple-element.43), channel_id=1, source_target_pairs={{0,16},{4,20},{8,24},{12,28},{16,0},{20,4},{24,8},{28,12},{1,17},{... | collective-permute-start | bytes 2752520 | tf_op jit(solution)/shard_map/ppermute | solution.py:431
  52.6 21.0 %collective-permute-start.11 = (bf16[384,1024]{1,0:T(8,128)(2,1)}, bf16[384,1024]{1,0:T(8,128)(2,1)S(1)}, u32[]{:S(2)}, u32[]{:S(2)}) collective-permute-start(bf16[384,1024]{1,0:T(8,128)(2,1)} %get-tuple-element.42), channel_id=1, source_target_pairs={{0,8},{4,12},{8,0},{12,4},{16,24},{20,28},{24,16},{28,20},{1,9},{5... | collective-permute-start | bytes 2359304 | tf_op jit(solution)/shard_map/ppermute | solution.py:431
  54.1 25.5 %collective-permute-start.4 = (bf16[256,1024]{1,0:T(8,128)(2,1)S(1)}, bf16[256,1024]{1,0:T(8,128)(2,1)S(1)}, u32[]{:S(2)}, u32[]{:S(2)}) collective-permute-start(bf16[256,1024]{1,0:T(8,128)(2,1)S(1)} %add_convert_fusion.refs_0_), channel_id=1, source_target_pairs={{0,2},{1,3},{2,0},{3,1},{4,6},{5,7},{6,4},{7,5},{8,10},{9,11},{10,... | collective-permute-start | bytes 1572872 | tf_op jit(solution)/shard_map/ppermute | solution.py:431
  55.6 24.0 %collective-permute-start.9 = (bf16[256,1024]{1,0:T(8,128)(2,1)S(1)}, bf16[256,1024]{1,0:T(8,128)(2,1)S(1)}, u32[]{:S(2)}, u32[]{:S(2)}) collective-permute-start(bf16[256,1024]{1,0:T(8,128)(2,1)S(1)} %add_convert_fusion.refs_0_), channel_id=1, source_target_pairs={{0,1},{1,0},{2,3},{3,2},{4,5},{5,4},{6,7},{7,6},{8,9},{9,8},{10,11... | collective-permute-start | bytes 1572872 | tf_op jit(solution)/shard_map/ppermute | solution.py:431
  73.6 6.5 %collective-permute-start.14 = (bf16[448,1024]{1,0:T(8,128)(2,1)S(1)}, bf16[448,1024]{1,0:T(8,128)(2,1)S(1)}, u32[]{:S(2)}, u32[]{:S(2)}) collective-permute-start(bf16[448,1024]{1,0:T(8,128)(2,1)S(1)} %collective-permute-done.12.refs_10_), channel_id=1, source_target_pairs={{0,4},{4,0},{8,12},{12,8},{16,20},{20,16},{24,28},{28,24},{1,5},{5... | collective-permute-start | bytes 2752520 | tf_op jit(solution)/shard_map/ppermute | solution.py:431
  73.7 6.5 %collective-permute-start.13 = (bf16[384,1024]{1,0:T(8,128)(2,1)S(1)}, bf16[384,1024]{1,0:T(8,128)(2,1)S(1)}, u32[]{:S(2)}, u32[]{:S(2)}) collective-permute-start(bf16[384,1024]{1,0:T(8,128)(2,1)S(1)} %collective-permute-done.11.refs_9_), channel_id=1, source_target_pairs={{0,4},{4,0},{8,12},{12,8},{16,20},{20,16},{24,28},{28,24},{1,5},{5... | collective-permute-start | bytes 2359304 | tf_op jit(solution)/shard_map/ppermute | solution.py:431
  79.6 12.9 %collective-permute-start.10 = (bf16[256,1024]{1,0:T(8,128)(2,1)S(1)}, bf16[256,1024]{1,0:T(8,128)(2,1)S(1)}, u32[]{:S(2)}, u32[]{:S(2)}) collective-permute-start(bf16[256,1024]{1,0:T(8,128)(2,1)S(1)} %collective-permute-done.4.refs_2_), channel_id=1, source_target_pairs={{0,1},{1,0},{2,3},{3,2},{4,5},{5,4},{6,7},{7,6},{8,9},{9,8},{10,11... | collective-permute-start | bytes 1572872 | tf_op jit(solution)/shard_map/ppermute | solution.py:431
  96.1 7.6 %collective-permute-start.15 = (bf16[64,1536]{1,0:T(8,128)(2,1)S(1)}, bf16[64,1536]{1,0:T(8,128)(2,1)S(1)}, u32[]{:S(2)}, u32[]{:S(2)}) collective-permute-start(bf16[64,1536]{1,0:T(8,128)(2,1)S(1)} %get-tuple-element.50), channel_id=1, source_target_pairs={{0,1},{1,0},{2,3},{3,2},{4,5},{5,4},{6,7},{7,6},{8,9},{9,8},{10,11... | collective-permute-start | bytes 589832 | tf_op jit(solution)/shard_map/ppermute | solution.py:431
  96.7 17.1 %collective-permute-start.16 = (bf16[64,1536]{1,0:T(8,128)(2,1)S(1)}, bf16[64,1536]{1,0:T(8,128)(2,1)S(1)}, u32[]{:S(2)}, u32[]{:S(2)}) collective-permute-start(bf16[64,1536]{1,0:T(8,128)(2,1)S(1)} %get-tuple-element.51), channel_id=1, source_target_pairs={{0,2},{1,3},{2,0},{3,1},{4,6},{5,7},{6,4},{7,5},{8,10},{9,11},{10,... | collective-permute-start | bytes 589832 | tf_op jit(solution)/shard_map/ppermute | solution.py:431
  100.0 13.7 %collective-permute-start.17 = (bf16[64,1536]{1,0:T(8,128)(2,1)S(1)}, bf16[64,1536]{1,0:T(8,128)(2,1)S(1)}, u32[]{:S(2)}, u32[]{:S(2)}) collective-permute-start(bf16[64,1536]{1,0:T(8,128)(2,1)S(1)} %get-tuple-element.52), channel_id=1, source_target_pairs={{0,3},{1,2},{2,1},{3,0},{4,7},{5,6},{6,5},{7,4},{8,11},{9,10},{10,... | collective-permute-start | bytes 589832 | tf_op jit(solution)/shard_map/ppermute | solution.py:431
  (2 other events, 7.5 us)
